TPU v7x, 32 devices: a whole 2x2x4 slice. The times are simulated.
32 devices in a mesh: ctx: 8 (over y, x, core), head: 4 (over z).
Axes of the slice: x: 2, y: 2, z: 4, core: 2. Of those that a mesh axis runs over, the one named last changes fastest.
Arguments:
- query_input: bfloat16 [4096, 4096], P('ctx', 'head'), may hold values from -96 to 96
- key_input: bfloat16 [4096, 4096], P('ctx', 'head'), may hold values from -6 to 6
- value_input: bfloat16 [4096, 4096], P('ctx', 'head'), may hold values from -6 to 6
- out_weight: bfloat16 [4096, 4096], P('head'), may hold values from -0.125 to 0.125
- out_cotangent: bfloat16 [4096, 4096], P('ctx', 'head'), may hold values from -6 to 6
Outputs:
- mixed: float32 [4096, 4096], P('ctx', 'head')
- grad_q: float32 [4096, 4096], P('ctx', 'head')
- grad_k: float32 [4096, 4096], P('ctx', 'head')
- grad_v: float32 [4096, 4096], P('ctx', 'head')
- weight_grad: float32 [4096, 4096], P('head', 'ctx')
- level_max: float32 [5, 32], P(None, 'head')
All inputs are finite; a program needn't handle non-finite values.
Results may differ from a plain program's by a relative error of at most 0.04.
Values may be sent and summed in bfloat16 or wider, within the bound.
No kernel may reach another device: no remote copies, remote signals or barrier semaphores. Data moves between devices by JAX's collectives and lax.ppermute only.
A program may use at most 128 MiB of HBM per device.

v0:
```python
import functools
import math

import jax
import jax.numpy as jnp
from jax import lax
from jax.experimental import pallas as pl
from jax.experimental.pallas import tpu as pltpu
from jax.sharding import PartitionSpec as P

DH = 128
BLK = 128
LEVELS = 5
SCALE = DH ** (-0.5)
LOG_TWO = math.log(2.0)
F32 = jnp.float32
BF16 = jnp.bfloat16
VMEM_LIMIT = 48 * 1024 * 1024


def dot_nn(a, b):
    return lax.dot_general(a, b, (((1,), (0,)), ((), ())), preferred_element_type=F32)


def dot_nt(a, b):
    return lax.dot_general(a, b, (((1,), (1,)), ((), ())), preferred_element_type=F32)


def dot_tn(a, b):
    return lax.dot_general(a, b, (((0,), (0,)), ((), ())), preferred_element_type=F32)


def pool_matrix(level, rows, tokens):
    row = lax.broadcasted_iota(jnp.int32, (rows, tokens), 0)
    token = lax.broadcasted_iota(jnp.int32, (rows, tokens), 1)
    return jnp.where(lax.shift_right_logical(token, level) == row, 0.5**level, 0.0).astype(BF16)


def pooled(level, tensor):
    tokens = tensor.shape[0]
    return dot_nn(pool_matrix(level, tokens >> level, tokens), tensor).astype(BF16)


def expand_two(scratch, base, value):
    rows = value.shape[0]
    scratch[pl.ds(base, rows, stride=2), :] = value
    scratch[pl.ds(base + 1, rows, stride=2), :] = value
    return scratch[pl.ds(base, 2 * rows), :]


def pool_kernel(k_ref, v_ref, two_ref, three_ref, four_ref):
    k = k_ref[...]
    v = v_ref[...]
    for level, out in ((2, two_ref), (3, three_ref), (4, four_ref)):
        rows = k.shape[0] >> level
        out[pl.ds(0, rows), :] = pooled(level, k)
        out[pl.ds(rows, rows), :] = pooled(level, v)


def pool_call(key, value):
    tokens, width = key.shape
    step = 256
    spec = pl.BlockSpec((tokens, step), lambda i: (0, i))
    rows = [2 * (tokens >> level) for level in (2, 3, 4)]
    return pl.pallas_call(
        pool_kernel,
        grid=(width // step,),
        in_specs=[spec, spec],
        out_specs=[pl.BlockSpec((r, step), lambda i: (0, i)) for r in rows],
        out_shape=[jax.ShapeDtypeStruct((r, width), BF16) for r in rows],
        compiler_params=pltpu.CompilerParams(vmem_limit_bytes=VMEM_LIMIT),
        cost_estimate=pl.CostEstimate(
            flops=4 * 224 * tokens * width, bytes_accessed=6 * tokens * width, transcendentals=0
        ),
        name="pool_keys",
    )(key, value)


def gather_rows(refs):
    keys = []
    values = []
    for ref in refs:
        half = ref.shape[0] // 2
        keys.append(ref[pl.ds(0, half), :])
        values.append(ref[pl.ds(half, half), :])
    if len(refs) == 1:
        return keys[0], values[0]
    return jnp.concatenate(keys, 0), jnp.concatenate(values, 0)


def level_block(q, k, v, shift):
    scores = dot_nt(q, k) * SCALE + shift
    peak = jnp.max(scores, axis=-1, keepdims=True)
    weights = jnp.exp(scores - peak)
    total = jnp.sum(weights, axis=-1, keepdims=True)
    mean = dot_nn(weights.astype(BF16), v) / total
    return peak, peak + jnp.log(total), mean


def forward_kernel(
    q_ref, k_ref, v_ref, t2, t3a, t3b, t4a, t4b, t4c, t4d, attn_ref, lse_ref, top_ref, lse_s, out_s
):
    head = pl.program_id(0)
    q = q_ref[...]
    k = k_ref[...]
    v = v_ref[...]
    tokens = q.shape[0]
    tops = []
    state = None
    base = 0
    for level in range(LEVELS - 1, -1, -1):
        shift = level * LOG_TWO
        if level >= 2:
            refs = {2: (t2,), 3: (t3a, t3b), 4: (t4a, t4b, t4c, t4d)}[level]
            keys, values = gather_rows(refs)
            peak, lse, mean = level_block(pooled(level, q), keys, values, shift)
        else:
            parts = []
            if level == 1:
                qc, kc, vc = pooled(1, q), pooled(1, k), pooled(1, v)
                for b in range(2):
                    mine = slice(b * BLK, (b + 1) * BLK)
                    other = slice((1 - b) * BLK, (2 - b) * BLK)
                    parts.append(level_block(qc[mine], kc[other], vc[other], shift))
            else:
                for b in range(tokens // (2 * BLK)):
                    both = slice(b * 2 * BLK, (b + 1) * 2 * BLK)
                    parts.append(level_block(q[both], k[both], v[both], 0.0))
            peak, lse, mean = [jnp.concatenate(p, 0) for p in zip(*parts)]
        tops.append((level, jnp.max(peak) - shift))
        lse = jnp.broadcast_to(lse, mean.shape)
        if state is None:
            state = (lse, mean)
            continue
        rows = mean.shape[0]
        other_lse = expand_two(lse_s, base, state[0])
        other_mean = expand_two(out_s, base, state[1])
        base += rows
        top = jnp.maximum(lse, other_lse)
        mine = jnp.exp(lse - top)
        other = jnp.exp(other_lse - top)
        total = mine + other
        state = (top + jnp.log(total), (mine * mean + other * other_mean) / total)
    attn_ref[...] = state[1].astype(BF16)
    lane = lax.broadcasted_iota(jnp.int32, state[0].shape, 1)
    lse_ref[...] = jnp.where(lane == head, state[0], lse_ref[...])
    row = lax.broadcasted_iota(jnp.int32, (8, 128), 0)
    tile = jnp.zeros((8, 128), F32)
    for level, value in tops:
        tile = jnp.where(row == level, value, tile)
    top_ref[0] = tile


def forward_call(query, key, value, received):
    tokens, width = query.shape
    heads = width // DH
    spec = pl.BlockSpec((tokens, DH), lambda h: (0, h))
    extra = [pl.BlockSpec((r.shape[0], DH), lambda h: (0, h)) for r in received]
    grown = tokens + tokens // 2 + tokens // 4 + tokens // 8
    return pl.pallas_call(
        forward_kernel,
        grid=(heads,),
        in_specs=[spec, spec, spec] + extra,
        out_specs=[
            spec,
            pl.BlockSpec((tokens, 128), lambda h: (0, 0)),
            pl.BlockSpec((1, 8, 128), lambda h: (h, 0, 0)),
        ],
        out_shape=[
            jax.ShapeDtypeStruct((tokens, width), BF16),
            jax.ShapeDtypeStruct((tokens, 128), F32),
            jax.ShapeDtypeStruct((heads, 8, 128), F32),
        ],
        scratch_shapes=[pltpu.VMEM((grown, 128), F32), pltpu.VMEM((grown, 128), F32)],
        compiler_params=pltpu.CompilerParams(vmem_limit_bytes=VMEM_LIMIT),
        cost_estimate=pl.CostEstimate(
            flops=8 * 376 * tokens * width, bytes_accessed=10 * tokens * width, transcendentals=0
        ),
        name="attention_forward",
    )(query, key, value, *received)


def backward_block(q, k, v, shift, lse, grad, scalar):
    weights = jnp.exp(dot_nt(q, k) * SCALE + (shift - lse))
    grad_scores = (weights * (dot_nt(grad, v) - scalar)).astype(BF16)
    grad_q = dot_nn(grad_scores, k) * SCALE
    grad_k = dot_tn(grad_scores, q) * SCALE
    grad_v = dot_tn(weights.astype(BF16), grad)
    return grad_q, grad_k, grad_v


def backward_kernel(
    q_ref, k_ref, v_ref, attn_ref, grad_ref, lse_ref, t2, t3a, t3b, t4a, t4b, t4c, t4d,
    gq_ref, gk_ref, gv_ref, r2, r3a, r3b, r4a, r4b, r4c, r4d,
    lse_s, grad_s, scal_s, gq_s, gk_s, gv_s,
):
    head = pl.program_id(0)
    q = q_ref[...]
    k = k_ref[...]
    v = v_ref[...]
    grad = grad_ref[...]
    tokens = q.shape[0]
    grad_f = grad.astype(F32)
    lane = lax.broadcasted_iota(jnp.int32, (tokens, 128), 1)
    lse = jnp.sum(jnp.where(lane == head, lse_ref[...], 0.0), axis=-1, keepdims=True)
    scalar = jnp.sum(grad_f * attn_ref[...].astype(F32), axis=-1, keepdims=True)
    lse_s[pl.ds(0, tokens), :] = jnp.broadcast_to(lse, (tokens, 128))
    scal_s[pl.ds(0, tokens), :] = jnp.broadcast_to(scalar, (tokens, 128))
    grad_s[pl.ds(0, tokens), :] = grad_f
    base = 0
    rows = tokens
    places = {}
    for level in range(1, LEVELS):
        half = rows // 2
        even = pl.ds(base, half, stride=2)
        odd = pl.ds(base + 1, half, stride=2)
        lse_even, lse_odd = lse_s[even, :], lse_s[odd, :]
        least = jnp.minimum(lse_even, lse_odd)
        factor_even = jnp.exp(least - lse_even)
        factor_odd = jnp.exp(least - lse_odd)
        nxt = pl.ds(base + rows, half)
        lse_s[nxt, :] = least
        grad_s[nxt, :] = factor_even * grad_s[even, :] + factor_odd * grad_s[odd, :]
        scal_s[nxt, :] = factor_even * scal_s[even, :] + factor_odd * scal_s[odd, :]
        places[level] = nxt
        base += rows
        rows = half
    grad_q = None
    up = 0
    for level in range(LEVELS - 1, -1, -1):
        shift = level * LOG_TWO
        if level >= 2:
            refs = {2: (t2,), 3: (t3a, t3b), 4: (t4a, t4b, t4c, t4d)}[level]
            outs = {2: (r2,), 3: (r3a, r3b), 4: (r4a, r4b, r4c, r4d)}[level]
            keys, values = gather_rows(refs)
            place = places[level]
            part_q, part_k, part_v = backward_block(
                pooled(level, q), keys, values, shift,
                lse_s[place, :], grad_s[place, :].astype(BF16), scal_s[place, :],
            )
            piece = BLK // len(outs)
            for i, out in enumerate(outs):
                out[pl.ds(0, piece), :] = part_k[i * piece : (i + 1) * piece].astype(BF16)
                out[pl.ds(piece, piece), :] = part_v[i * piece : (i + 1) * piece].astype(BF16)
        elif level == 1:
            place = places[level]
            qc, kc, vc = pooled(1, q), pooled(1, k), pooled(1, v)
            low, gr, sc = lse_s[place, :], grad_s[place, :].astype(BF16), scal_s[place, :]
            parts = []
            for b in range(2):
                mine = slice(b * BLK, (b + 1) * BLK)
                other = slice((1 - b) * BLK, (2 - b) * BLK)
                parts.append(
                    backward_block(qc[mine], kc[other], vc[other], shift, low[mine], gr[mine], sc[mine])
                )
            part_q = jnp.concatenate([parts[0][0], parts[1][0]], 0)
            part_k = jnp.concatenate([parts[1][1], parts[0][1]], 0)
            part_v = jnp.concatenate([parts[1][2], parts[0][2]], 0)
            coarse_k = expand_two(gk_s, 0, part_k * 0.5)
            coarse_v = expand_two(gv_s, 0, part_v * 0.5)
        if level == 0:
            for b in range(tokens // (2 * BLK)):
                both = slice(b * 2 * BLK, (b + 1) * 2 * BLK)
                part_q, part_k, part_v = backward_block(
                    q[both], k[both], v[both], 0.0, lse[both], grad[both], scalar[both]
                )
                here = pl.ds(b * 2 * BLK, 2 * BLK)
                gq_ref[here, :] = part_q + grad_q[both]
                gk_ref[here, :] = part_k + coarse_k[both]
                gv_ref[here, :] = part_v + coarse_v[both]
        else:
            grad_q = part_q if grad_q is None else part_q + grad_q
            rows = grad_q.shape[0]
            grad_q = expand_two(gq_s, up, grad_q * 0.5)
            up += 2 * rows


def backward_call(query, key, value, attn, grad, lse, received):
    tokens, width = query.shape
    heads = width // DH
    spec = pl.BlockSpec((tokens, DH), lambda h: (0, h))
    extra = [pl.BlockSpec((r.shape[0], DH), lambda h: (0, h)) for r in received]
    full = jax.ShapeDtypeStruct((tokens, width), F32)
    scratch = pltpu.VMEM((2 * tokens, 128), F32)
    return pl.pallas_call(
        backward_kernel,
        grid=(heads,),
        in_specs=[spec] * 5 + [pl.BlockSpec((tokens, 128), lambda h: (0, 0))] + extra,
        out_specs=[spec] * 3 + extra,
        out_shape=[full] * 3 + [jax.ShapeDtypeStruct(r.shape, BF16) for r in received],
        scratch_shapes=[scratch] * 6,
        compiler_params=pltpu.CompilerParams(vmem_limit_bytes=VMEM_LIMIT),
        cost_estimate=pl.CostEstimate(
            flops=20 * 376 * tokens * width, bytes_accessed=24 * tokens * width, transcendentals=0
        ),
        name="attention_backward",
    )(query, key, value, attn, grad, lse, *received)


def finish_kernel(gk_ref, gv_ref, t2, t3a, t3b, t4a, t4b, t4c, t4d, ok_ref, ov_ref, k_s, v_s):
    for part, local, out, scr in ((0, gk_ref, ok_ref, k_s), (1, gv_ref, ov_ref, v_s)):
        state = None
        base = 0
        for refs in ((t4a, t4b, t4c, t4d), (t3a, t3b), (t2,)):
            rows = refs[0].shape[0] // 2
            here = pl.ds(part * rows, rows)
            total = refs[0][here, :].astype(F32)
            for ref in refs[1:]:
                total = total + ref[here, :].astype(F32)
            state = total if state is None else total + state
            state = expand_two(scr, base, state * 0.5)
            base += 2 * rows
        state = expand_two(scr, base, state * 0.5)
        out[...] = local[...] + state


def finish_call(grad_k, grad_v, returned):
    tokens, width = grad_k.shape
    step = 128
    spec = pl.BlockSpec((tokens, step), lambda h: (0, h))
    extra = [pl.BlockSpec((r.shape[0], step), lambda h: (0, h)) for r in returned]
    full = jax.ShapeDtypeStruct((tokens, width), F32)
    scratch = pltpu.VMEM((2 * tokens, step), F32)
    return pl.pallas_call(
        finish_kernel,
        grid=(width // step,),
        in_specs=[spec, spec] + extra,
        out_specs=[spec, spec],
        out_shape=[full, full],
        scratch_shapes=[scratch, scratch],
        compiler_params=pltpu.CompilerParams(vmem_limit_bytes=VMEM_LIMIT),
        cost_estimate=pl.CostEstimate(
            flops=8 * tokens * width, bytes_accessed=18 * tokens * width, transcendentals=0
        ),
        name="add_returned",
    )(grad_k, grad_v, *returned)


def swap(value, axis, mask):
    return lax.ppermute(value, axis, [(i, i ^ mask) for i in range(lax.axis_size(axis))])


def shift(value, axis, pairs):
    return lax.ppermute(value, axis, pairs)


def per_device(query, key, value, out_weight, cotangent):
    tokens, width = query.shape
    model = out_weight.shape[1]
    count = lax.axis_size("head")
    ctx_count = lax.axis_size("ctx")
    column = model // ctx_count
    me = lax.axis_index("ctx")
    z = lax.axis_index("head")

    right, left = cotangent, cotangent
    from_left, from_right = [], []
    for step in range(1, count):
        right = shift(right, "head", [(i, i + 1) for i in range(step - 1, count - 1)])
        left = shift(left, "head", [(i, i - 1) for i in range(1, count - step + 1)])
        from_left.append(right)
        from_right.append(left)

    sent = pool_call(key, value)
    masks = (1, 2, 3, 4, 5, 6, 7)
    which = (0, 1, 1, 2, 2, 2, 2)
    received = [swap(sent[w], "ctx", m) for m, w in zip(masks, which)]
    attn, lse, tops = forward_call(query, key, value, received)

    level_max = jnp.transpose(tops[:, :LEVELS, 0])
    mask = 1
    while mask < ctx_count:
        level_max = jnp.maximum(level_max, swap(level_max, "ctx", mask))
        mask *= 2

    product = dot_nn(attn, out_weight).astype(BF16)

    def chunk(index):
        return lax.dynamic_slice(product, (0, lax.rem(index + count, count) * width), (tokens, width))

    to_left, to_right = None, None
    for step in range(1, count):
        piece = chunk(z + step)
        to_left = piece if to_left is None else (to_left.astype(F32) + piece).astype(BF16)
        to_left = shift(to_left, "head", [(i, i - 1) for i in range(count - step, count)])
        piece = chunk(z - step)
        to_right = piece if to_right is None else (to_right.astype(F32) + piece).astype(BF16)
        to_right = shift(to_right, "head", [(i, i + 1) for i in range(0, step)])
    mixed = chunk(z).astype(F32) + to_left.astype(F32) + to_right.astype(F32)

    whole = jnp.zeros((tokens, model), BF16)
    whole = lax.dynamic_update_slice(whole, cotangent, (0, z * width))
    for step in range(1, count):
        got = jnp.where(step <= z, from_left[step - 1], from_right[count - step - 1])
        whole = lax.dynamic_update_slice(whole, got, (0, lax.rem(z - step + count, count) * width))

    attn_other = swap(attn, "ctx", 1)
    terms = []
    chips = ctx_count // 2
    for i in range(chips):
        mine = lax.dynamic_slice(whole, (0, (me ^ (2 * i)) * column), (tokens, column))
        theirs = lax.dynamic_slice(whole, (0, (me ^ (2 * i) ^ 1) * column), (tokens, column))
        theirs = swap(theirs, "ctx", 1)
        term = dot_tn(attn, mine) + dot_tn(attn_other, theirs)
        terms.append(term if i == 0 else swap(term.astype(BF16), "ctx", 2 * i))
    weight_grad = terms[0]
    for term in terms[1:]:
        weight_grad = weight_grad + term.astype(F32)

    grad_attn = dot_nt(whole, out_weight).astype(BF16)
    outs = backward_call(query, key, value, attn, grad_attn, lse, received)
    grad_q, grad_k, grad_v = outs[:3]
    returned = [swap(part, "ctx", m) for m, part in zip(masks, outs[3:])]
    grad_k, grad_v = finish_call(grad_k, grad_v, returned)
    return mixed, grad_q, grad_k, grad_v, weight_grad, level_max


def solution(mesh):
    tokens = P("ctx", "head")
    return jax.shard_map(
        per_device,
        mesh=mesh,
        in_specs=(tokens, tokens, tokens, P("head", None), tokens),
        out_specs=(tokens, tokens, tokens, tokens, P("head", "ctx"), P(None, "head")),
        check_vma=False,
    )
```

profile of v0, /device:TPU:0, one launch (start us, length us, event | category | flops | bytes accessed | tf_op | source)
XLA Modules:
  0.0 263.6 jit_solution(15748921781004212079)
XLA Ops:
  3.1 2.7 %pool_keys.1 = (bf16[256,1024]{1,0:T(8,128)(2,1)S(1)}, bf16[128,1024]{1,0:T(8,128)(2,1)}, bf16[64,1024]{1,0:T(8,128)(2,1)}) custom-call(bf16[512,1024]{1,0:T(8,128)(2,1)S(1)} %copy-done.2, bf16[512,1024]{1,0:T(8,128)(2,1)S(1)} %copy-done.4), custom_call_target="tpu_custom_call" | custom-call | flops 469762048 | bytes 3145728 | tf_op jit(solution)/shard_map/pool_keys/pallas_call | solution.py:65
  6.2 2.5 collective-permute-start.3
  8.9 1.7 collective-permute-start.1
  10.6 2.7 %collective-permute-done.3.t4a = bf16[64,1024]{1,0:T(8,128)(2,1)S(1)} collective-permute-done((bf16[64,1024]{1,0:T(8,128)(2,1)}, bf16[64,1024]{1,0:T(8,128)(2,1)S(1)}, u32[]{:S(2)}, u32[]{:S(2)}) %collective-permute-start.3) | collective-permute-done | bytes 131104 | tf_op jit(solution)/shard_map/ppermute | solution.py:340
  13.9 2.9 %collective-permute-start.5 = (bf16[64,1024]{1,0:T(8,128)(2,1)}, bf16[64,1024]{1,0:T(8,128)(2,1)}, u32[]{:S(2)}, u32[]{:S(2)}) collective-permute-start(bf16[64,1024]{1,0:T(8,128)(2,1)} %get-tuple-element.26), channel_id=1, source_target_pairs={{0,24},{4,28},{8,16},{12,20},{16,8},{20,12},{24,0},{28,4},{1,25},{... | collective-permute-start | bytes 393224 | tf_op jit(solution)/shard_map/ppermute | solution.py:340
  17.5 1.5 collective-permute-start.6
  19.0 8.9 %collective-permute-done.5.t4c = bf16[64,1024]{1,0:T(8,128)(2,1)} collective-permute-done((bf16[64,1024]{1,0:T(8,128)(2,1)}, bf16[64,1024]{1,0:T(8,128)(2,1)}, u32[]{:S(2)}, u32[]{:S(2)}) %collective-permute-start.5) | collective-permute-done | bytes 131104 | tf_op jit(solution)/shard_map/ppermute | solution.py:340
  29.4 5.3 %collective-permute-start.13 = (bf16[512,1024]{1,0:T(8,128)(2,1)}, bf16[512,1024]{1,0:T(8,128)(2,1)}, u32[]{:S(2)}, u32[]{:S(2)}) collective-permute-start(bf16[512,1024]{1,0:T(8,128)(2,1)} %param.9), channel_id=1, source_target_pairs={{0,1},{1,2},{2,3},{4,5},{5,6},{6,7},{8,9},{9,10},{10,11},{12,13},{... | collective-permute-start | bytes 3145736 | tf_op jit(solution)/shard_map/ppermute | solution.py:344
  37.8 22.5 %attention_forward.1 = (bf16[512,1024]{1,0:T(8,128)(2,1)}, f32[512,128]{1,0:T(8,128)S(1)}, f32[8,8,128]{2,1,0:T(8,128)S(1)}) custom-call(bf16[512,1024]{1,0:T(8,128)(2,1)S(1)} %copy-done.6, bf16[512,1024]{1,0:T(8,128)(2,1)S(1)} %copy-done.3, bf16[512,1024]{1,0:T(8,128)(2,1)S(1)} %copy-done.5, bf16[256,1024]{1,0:T(8,128)(2,1)S(1)} %collective-permute-done.t2, ...), custom_call_target="tpu_custom_call" | custom-call | flops 1577058304 | bytes 5242880 | tf_op jit(solution)/shard_map/attention_forward/pallas_call | solution.py:160
  60.3 8.3 %convolution_convert_fusion = bf16[512,4096]{1,0:T(8,128)(2,1)S(1)} fusion(bf16[512,1024]{1,0:T(8,128)(2,1)} %get-tuple-element.27.attn_ref, bf16[1024,4096]{1,0:T(8,128)(2,1)} %param.8), kind=kOutput, calls=%fused_computation | convolution fusion | flops 4297064448 | bytes 13631488 | tf_op jit(solution)/shard_map/dot_general | solution.py:22
  68.6 1.4 constant_dynamic-slice_fusion.5
  70.9 3.5 %collective-permute-start.10 = (bf16[512,1024]{1,0:T(8,128)(2,1)}, bf16[512,1024]{1,0:T(8,128)(2,1)}, u32[]{:S(2)}, u32[]{:S(2)}) collective-permute-start(bf16[512,1024]{1,0:T(8,128)(2,1)} %get-tuple-element.63), channel_id=1, source_target_pairs={{0,1},{4,5},{8,9},{12,13},{16,17},{20,21},{24,25},{28,29}} | collective-permute-start | bytes 3145736 | tf_op jit(solution)/shard_map/ppermute | solution.py:344
  74.4 1.7 collective-permute-start.7
  76.1 1.3 collective-permute-start.15
  77.4 1.6 collective-permute-start.17
  79.1 16.6 %collective-permute-done.10 = bf16[512,1024]{1,0:T(8,128)(2,1)} collective-permute-done((bf16[512,1024]{1,0:T(8,128)(2,1)}, bf16[512,1024]{1,0:T(8,128)(2,1)}, u32[]{:S(2)}, u32[]{:S(2)}) %collective-permute-start.10) | collective-permute-done | bytes 1048608 | tf_op jit(solution)/shard_map/ppermute | solution.py:344
  95.6 4.5 %add_convert_fusion.6 = (bf16[512,1024]{1,0:T(8,128)(2,1)}, bf16[512,1024]{1,0:T(8,128)(2,1)}) fusion(bf16[512,1024]{1,0:T(8,128)(2,1)} %collective-permute-done.7, bf16[512,4096]{1,0:T(8,128)(2,1)} %copy-done.21, s32[]{:T(128)S(6)} %select_n.73, s32[]{:T(128)S(6)} %select_n.76, bf16[512,1024]{1,0:T(8,128)(2,1)} %collective-permute-done.10), kind=kLoop, calls=%fused_computation.9 | loop fusion | flops 4194304 | bytes 6291464 | tf_op jit(solution)/shard_map/convert_element_type | solution.py:384
  100.1 5.5 %collective-permute-start.11 = (bf16[512,1024]{1,0:T(8,128)(2,1)}, bf16[512,1024]{1,0:T(8,128)(2,1)}, u32[]{:S(2)}, u32[]{:S(2)}) collective-permute-start(bf16[512,1024]{1,0:T(8,128)(2,1)} %get-tuple-element.61), channel_id=1, source_target_pairs={{0,1},{1,2},{4,5},{5,6},{8,9},{9,10},{12,13},{13,14},{16,17},{17,1... | collective-permute-start | bytes 3145736 | tf_op jit(solution)/shard_map/ppermute | solution.py:344
  105.6 1.6 collective-permute-start.8
  110.0 1.9 copy-done.18
  112.0 1.6 collective-permute-start.18
  113.6 1.5 collective-permute-start.35
  115.1 2.1 collective-permute-done.35
  117.2 8.7 %collective-permute-done.11 = bf16[512,1024]{1,0:T(8,128)(2,1)} collective-permute-done((bf16[512,1024]{1,0:T(8,128)(2,1)}, bf16[512,1024]{1,0:T(8,128)(2,1)}, u32[]{:S(2)}, u32[]{:S(2)}) %collective-permute-start.11) | collective-permute-done | bytes 1048608 | tf_op jit(solution)/shard_map/ppermute | solution.py:344
  126.4 4.5 %add_convert_fusion.5 = (bf16[512,1024]{1,0:T(8,128)(2,1)}, bf16[512,1024]{1,0:T(8,128)(2,1)}) fusion(bf16[512,1024]{1,0:T(8,128)(2,1)} %collective-permute-done.8, bf16[512,4096]{1,0:T(8,128)(2,1)} %copy-done.21, s32[]{:T(128)S(6)} %select_n.74, s32[]{:T(128)S(6)} %select_n.77, bf16[512,1024]{1,0:T(8,128)(2,1)} %collective-permute-done.11), kind=kLoop, calls=%fused_computation.8 | loop fusion | flops 4194304 | bytes 6291464 | tf_op jit(solution)/shard_map/convert_element_type | solution.py:384
  130.9 1.6 collective-permute-done.16
  132.9 1.6 select_dynamic-update-slice_fusion.1
  134.6 1.6 select_dynamic-update-slice_fusion
  136.7 9.4 %convolution_convert_fusion.1.grad_ref = bf16[512,1024]{1,0:T(8,128)(2,1)} fusion(bf16[512,4096]{1,0:T(8,128)(2,1)S(1)} %select_dynamic-update-slice_fusion, bf16[1024,4096]{1,0:T(8,128)(2,1)} %param.8), kind=kOutput, calls=%fused_computation.10 | convolution fusion | flops 4295491584 | bytes 13631488 | tf_op jit(solution)/shard_map/dot_general | solution.py:26
  146.5 25.3 %attention_backward.1 = (f32[512,1024]{1,0:T(8,128)}, f32[512,1024]{1,0:T(8,128)}, f32[512,1024]{1,0:T(8,128)}, bf16[256,1024]{1,0:T(8,128)(2,1)S(1)}, bf16[128,...) custom-call(bf16[512,1024]{1,0:T(8,128)(2,1)S(1)} %copy-done.7, ...), custom_call_target="tpu_custom_call" | custom-call | flops 3942645760 | bytes 12582912 | tf_op jit(solution)/shard_map/attention_backward/pallas_call | solution.py:285
  173.3 2.0 add_convert_fusion.2
  175.3 1.4 collective-permute-start.23
  177.4 3.0 %add_convert_fusion.1 = bf16[1024,512]{1,0:T(8,128)(2,1)} fusion(f32[1024,512]{1,0:T(8,128)S(1)} %fusion.11, bf16[512,1024]{1,0:T(8,128)(2,1)} %get-tuple-element.27.attn_ref, bf16[512,4096]{1,0:T(8,128)(2,1)S(1)} %select_dynamic-update-slice_fusion, s32[]{:T(128)S(6)} %select_n.89), kind=kOutput, calls=%fused_computation.3 | convolution fusion | flops 537919488 | bytes 4718596 | tf_op jit(solution)/shard_map/dot_general | solution.py:30
  180.7 1.5 collective-permute-start.20
  185.1 7.5 %collective-permute-done.24.t4c = bf16[64,1024]{1,0:T(8,128)(2,1)S(1)} collective-permute-done((bf16[64,1024]{1,0:T(8,128)(2,1)S(1)}, bf16[64,1024]{1,0:T(8,128)(2,1)S(1)}, u32[]{:S(2)}, u32[]{:S(2)}) %collective-permute-start.24) | collective-permute-done | bytes 131104 | tf_op jit(solution)/shard_map/ppermute | solution.py:340
  192.6 8.2 %collective-permute-start.12 = (bf16[512,1024]{1,0:T(8,128)(2,1)}, bf16[512,1024]{1,0:T(8,128)(2,1)}, u32[]{:S(2)}, u32[]{:S(2)}) collective-permute-start(bf16[512,1024]{1,0:T(8,128)(2,1)} %get-tuple-element.59), channel_id=1, source_target_pairs={{0,1},{1,2},{2,3},{4,5},{5,6},{6,7},{8,9},{9,10},{10,11},{12,13},{... | collective-permute-start | bytes 3145736 | tf_op jit(solution)/shard_map/ppermute | solution.py:344
  200.7 1.5 collective-permute-start.9
  202.4 3.0 %add_convert_fusion = bf16[1024,512]{1,0:T(8,128)(2,1)} fusion(f32[1024,512]{1,0:T(8,128)S(1)} %fusion.12, bf16[512,1024]{1,0:T(8,128)(2,1)} %get-tuple-element.27.attn_ref, bf16[512,4096]{1,0:T(8,128)(2,1)S(1)} %select_dynamic-update-slice_fusion, s32[]{:T(128)S(6)} %select_n.91), kind=kOutput, calls=%fused_computation.2 | convolution fusion | flops 537919488 | bytes 4718596 | tf_op jit(solution)/shard_map/dot_general | solution.py:30
  205.3 5.6 %collective-permute-done.21.t3b = bf16[128,1024]{1,0:T(8,128)(2,1)S(1)} collective-permute-done((bf16[128,1024]{1,0:T(8,128)(2,1)S(1)}, bf16[128,1024]{1,0:T(8,128)(2,1)S(1)}, u32[]{:S(2)}, u32[]{:S(2)}) %collective-permute-start.21) | collective-permute-done | bytes 262176 | tf_op jit(solution)/shard_map/ppermute | solution.py:340
  211.5 1.5 collective-permute-start.31
  213.0 1.3 collective-permute-start.33
  215.1 2.2 fusion.3
  217.8 4.4 %add_returned.1 = (f32[512,1024]{1,0:T(8,128)}, f32[512,1024]{1,0:T(8,128)}) custom-call(f32[512,1024]{1,0:T(8,128)S(1)} %copy-done, f32[512,1024]{1,0:T(8,128)S(1)} %copy-done.1, bf16[256,1024]{1,0:T(8,128)(2,1)S(1)} %collective-permute-done.19.t2, bf16[128,1024]{1,0:T(8,128)(2,1)S(1)} %collective-permute-done.20.t3a, ...), custom_call_target="tpu_custom_call" | custom-call | flops 4194304 | bytes 9437184 | tf_op jit(solution)/shard_map/add_returned/pallas_call | solution.py:324
  222.9 3.4 %collective-permute-done.9 = bf16[512,1024]{1,0:T(8,128)(2,1)} collective-permute-done((bf16[512,1024]{1,0:T(8,128)(2,1)}, bf16[512,1024]{1,0:T(8,128)(2,1)}, u32[]{:S(2)}, u32[]{:S(2)}) %collective-permute-start.9) | collective-permute-done | bytes 1048608 | tf_op jit(solution)/shard_map/ppermute | solution.py:344
  226.3 3.8 %convert_add_fusion.1 = f32[512,1024]{1,0:T(8,128)} fusion(bf16[512,1024]{1,0:T(8,128)(2,1)} %collective-permute-done.12, bf16[512,1024]{1,0:T(8,128)(2,1)} %collective-permute-done.9, bf16[512,4096]{1,0:T(8,128)(2,1)} %copy-done.21, s32[]{:T(128)S(6)} %select_n.71), kind=kLoop, calls=%fused_computation.5 | loop fusion | flops 2621440 | bytes 5242884 | tf_op jit(solution)/shard_map/add | solution.py:389
  230.1 6.9 %collective-permute-done.29 = bf16[1024,512]{1,0:T(8,128)(2,1)} collective-permute-done((bf16[1024,512]{1,0:T(8,128)(2,1)S(1)}, bf16[1024,512]{1,0:T(8,128)(2,1)}, u32[]{:S(2)}, u32[]{:S(2)}) %collective-permute-start.29) | collective-permute-done | bytes 1048608 | tf_op jit(solution)/shard_map/ppermute | solution.py:340
  237.0 22.8 %collective-permute-done.33 = bf16[1024,512]{1,0:T(8,128)(2,1)} collective-permute-done((bf16[1024,512]{1,0:T(8,128)(2,1)}, bf16[1024,512]{1,0:T(8,128)(2,1)}, u32[]{:S(2)}, u32[]{:S(2)}) %collective-permute-start.33) | collective-permute-done | bytes 1048608 | tf_op jit(solution)/shard_map/ppermute | solution.py:340
  259.7 3.9 %convert_add_fusion = f32[1024,512]{1,0:T(8,128)} fusion(bf16[1024,512]{1,0:T(8,128)(2,1)} %collective-permute-done.33, bf16[1024,512]{1,0:T(8,128)(2,1)} %collective-permute-done.31, bf16[1024,512]{1,0:T(8,128)(2,1)} %collective-permute-done.29, f32[1024,512]{1,0:T(8,128)S(1)} %fusion.3, f32[1024,512]{1,0:T(8,128)S(1)} %fusion.9), kind=kLoop, calls=%fused_computation.1 | loop fusion | flops 3670016 | bytes 9437184 | tf_op jit(solution)/shard_map/add | solution.py:408
  (102 shorter events, 22.3 us)
Async XLA Ops:
  3.1 31.7 %copy-start.3 = (bf16[512,1024]{1,0:T(8,128)(2,1)S(1)}, bf16[512,1024]{1,0:T(8,128)(2,1)}, u32[]{:S(2)}) copy-start(bf16[512,1024]{1,0:T(8,128)(2,1)} %k_ref.5) | copy-start | bytes 3145732
  3.1 31.7 %copy-start.5 = (bf16[512,1024]{1,0:T(8,128)(2,1)S(1)}, bf16[512,1024]{1,0:T(8,128)(2,1)}, u32[]{:S(2)}) copy-start(bf16[512,1024]{1,0:T(8,128)(2,1)} %v_ref.5) | copy-start | bytes 3145732
  5.8 29.0 %collective-permute-start = (bf16[256,1024]{1,0:T(8,128)(2,1)S(1)}, bf16[256,1024]{1,0:T(8,128)(2,1)S(1)}, u32[]{:S(2)}, u32[]{:S(2)}) collective-permute-start(bf16[256,1024]{1,0:T(8,128)(2,1)S(1)} %get-tuple-element.24), channel_id=1, source_target_pairs={{0,4},{4,0},{8,12},{12,8},{16,20},{20,16},{24,28},{28,24},{1,5},{5... | collective-permute-start | bytes 1572872 | tf_op jit(solution)/shard_map/ppermute | solution.py:340
  6.2 7.1 %collective-permute-start.3 = (bf16[64,1024]{1,0:T(8,128)(2,1)}, bf16[64,1024]{1,0:T(8,128)(2,1)S(1)}, u32[]{:S(2)}, u32[]{:S(2)}) collective-permute-start(bf16[64,1024]{1,0:T(8,128)(2,1)} %get-tuple-element.26), channel_id=1, source_target_pairs={{0,16},{4,20},{8,24},{12,28},{16,0},{20,4},{24,8},{28,12},{1,17},{... | collective-permute-start | bytes 393224 | tf_op jit(solution)/shard_map/ppermute | solution.py:340
  8.7 8.1 %collective-permute-start.4 = (bf16[64,1024]{1,0:T(8,128)(2,1)}, bf16[64,1024]{1,0:T(8,128)(2,1)S(1)}, u32[]{:S(2)}, u32[]{:S(2)}) collective-permute-start(bf16[64,1024]{1,0:T(8,128)(2,1)} %get-tuple-element.26), channel_id=1, source_target_pairs={{0,20},{4,16},{8,28},{12,24},{16,4},{20,0},{24,12},{28,8},{1,21},{... | collective-permute-start | bytes 393224 | tf_op jit(solution)/shard_map/ppermute | solution.py:340
  8.9 25.9 %collective-permute-start.1 = (bf16[128,1024]{1,0:T(8,128)(2,1)}, bf16[128,1024]{1,0:T(8,128)(2,1)S(1)}, u32[]{:S(2)}, u32[]{:S(2)}) collective-permute-start(bf16[128,1024]{1,0:T(8,128)(2,1)} %get-tuple-element.25), channel_id=1, source_target_pairs={{0,8},{4,12},{8,0},{12,4},{16,24},{20,28},{24,16},{28,20},{1,9},{5... | collective-permute-start | bytes 786440 | tf_op jit(solution)/shard_map/ppermute | solution.py:340
  10.6 24.2 %collective-permute-start.2 = (bf16[128,1024]{1,0:T(8,128)(2,1)}, bf16[128,1024]{1,0:T(8,128)(2,1)}, u32[]{:S(2)}, u32[]{:S(2)}) collective-permute-start(bf16[128,1024]{1,0:T(8,128)(2,1)} %get-tuple-element.25), channel_id=1, source_target_pairs={{0,12},{4,8},{8,4},{12,0},{16,28},{20,24},{24,20},{28,16},{1,13},{... | collective-permute-start | bytes 786440 | tf_op jit(solution)/shard_map/ppermute | solution.py:340
  13.9 14.0 %collective-permute-start.5 = (bf16[64,1024]{1,0:T(8,128)(2,1)}, bf16[64,1024]{1,0:T(8,128)(2,1)}, u32[]{:S(2)}, u32[]{:S(2)}) collective-permute-start(bf16[64,1024]{1,0:T(8,128)(2,1)} %get-tuple-element.26), channel_id=1, source_target_pairs={{0,24},{4,28},{8,16},{12,20},{16,8},{20,12},{24,0},{28,4},{1,25},{... | collective-permute-start | bytes 393224 | tf_op jit(solution)/shard_map/ppermute | solution.py:340
  17.5 12.0 %collective-permute-start.6 = (bf16[64,1024]{1,0:T(8,128)(2,1)}, bf16[64,1024]{1,0:T(8,128)(2,1)}, u32[]{:S(2)}, u32[]{:S(2)}) collective-permute-start(bf16[64,1024]{1,0:T(8,128)(2,1)} %get-tuple-element.26), channel_id=1, source_target_pairs={{0,28},{4,24},{8,20},{12,16},{16,12},{20,8},{24,4},{28,0},{1,29},{... | collective-permute-start | bytes 393224 | tf_op jit(solution)/shard_map/ppermute | solution.py:340
  27.9 48.2 %collective-permute-start.14 = (bf16[512,1024]{1,0:T(8,128)(2,1)}, bf16[512,1024]{1,0:T(8,128)(2,1)}, u32[]{:S(2)}, u32[]{:S(2)}) collective-permute-start(bf16[512,1024]{1,0:T(8,128)(2,1)} %param.9), channel_id=1, source_target_pairs={{1,0},{2,1},{3,2},{5,4},{6,5},{7,6},{9,8},{10,9},{11,10},{13,12},{... | collective-permute-start | bytes 3145736 | tf_op jit(solution)/shard_map/ppermute | solution.py:344
  29.4 48.0 %collective-permute-start.13 = (bf16[512,1024]{1,0:T(8,128)(2,1)}, bf16[512,1024]{1,0:T(8,128)(2,1)}, u32[]{:S(2)}, u32[]{:S(2)}) collective-permute-start(bf16[512,1024]{1,0:T(8,128)(2,1)} %param.9), channel_id=1, source_target_pairs={{0,1},{1,2},{2,3},{4,5},{5,6},{6,7},{8,9},{9,10},{10,11},{12,13},{... | collective-permute-start | bytes 3145736 | tf_op jit(solution)/shard_map/ppermute | solution.py:344
  60.3 8.3 %copy-start.14 = (f32[512,128]{1,0:T(8,128)}, f32[512,128]{1,0:T(8,128)S(1)}, u32[]{:S(2)}) copy-start(f32[512,128]{1,0:T(8,128)S(1)} %get-tuple-element.28.lse_ref) | copy-start | bytes 786436
  70.9 24.7 %collective-permute-start.10 = (bf16[512,1024]{1,0:T(8,128)(2,1)}, bf16[512,1024]{1,0:T(8,128)(2,1)}, u32[]{:S(2)}, u32[]{:S(2)}) collective-permute-start(bf16[512,1024]{1,0:T(8,128)(2,1)} %get-tuple-element.63), channel_id=1, source_target_pairs={{0,1},{4,5},{8,9},{12,13},{16,17},{20,21},{24,25},{28,29}} | collective-permute-start | bytes 3145736 | tf_op jit(solution)/shard_map/ppermute | solution.py:344
  74.4 21.2 %collective-permute-start.7 = (bf16[512,1024]{1,0:T(8,128)(2,1)S(1)}, bf16[512,1024]{1,0:T(8,128)(2,1)}, u32[]{:S(2)}, u32[]{:S(2)}) collective-permute-start(bf16[512,1024]{1,0:T(8,128)(2,1)S(1)} %get-tuple-element.62), channel_id=1, source_target_pairs={{3,2},{7,6},{11,10},{15,14},{19,18},{23,22},{27,26},{31,30}} | collective-permute-start | bytes 3145736 | tf_op jit(solution)/shard_map/ppermute | solution.py:344
  76.1 31.1 %collective-permute-start.15 = (bf16[512,1024]{1,0:T(8,128)(2,1)}, bf16[512,1024]{1,0:T(8,128)(2,1)}, u32[]{:S(2)}, u32[]{:S(2)}) collective-permute-start(bf16[512,1024]{1,0:T(8,128)(2,1)} %collective-permute-done.14), channel_id=1, source_target_pairs={{1,0},{2,1},{5,4},{6,5},{9,8},{10,9},{13,12},{14,13},{17,16},{18,1... | collective-permute-start | bytes 3145736 | tf_op jit(solution)/shard_map/ppermute | solution.py:344
  77.4 34.5 %collective-permute-start.17 = (bf16[512,1024]{1,0:T(8,128)(2,1)}, bf16[512,1024]{1,0:T(8,128)(2,1)}, u32[]{:S(2)}, u32[]{:S(2)}) collective-permute-start(bf16[512,1024]{1,0:T(8,128)(2,1)} %collective-permute-done.13), channel_id=1, source_target_pairs={{1,2},{2,3},{5,6},{6,7},{9,10},{10,11},{13,14},{14,15},{17,18},{18... | collective-permute-start | bytes 3145736 | tf_op jit(solution)/shard_map/ppermute | solution.py:344
  100.1 25.8 %collective-permute-start.11 = (bf16[512,1024]{1,0:T(8,128)(2,1)}, bf16[512,1024]{1,0:T(8,128)(2,1)}, u32[]{:S(2)}, u32[]{:S(2)}) collective-permute-start(bf16[512,1024]{1,0:T(8,128)(2,1)} %get-tuple-element.61), channel_id=1, source_target_pairs={{0,1},{1,2},{4,5},{5,6},{8,9},{9,10},{12,13},{13,14},{16,17},{17,1... | collective-permute-start | bytes 3145736 | tf_op jit(solution)/shard_map/ppermute | solution.py:344
  105.6 20.8 %collective-permute-start.8 = (bf16[512,1024]{1,0:T(8,128)(2,1)}, bf16[512,1024]{1,0:T(8,128)(2,1)}, u32[]{:S(2)}, u32[]{:S(2)}) collective-permute-start(bf16[512,1024]{1,0:T(8,128)(2,1)} %get-tuple-element.60), channel_id=1, source_target_pairs={{2,1},{3,2},{6,5},{7,6},{10,9},{11,10},{14,13},{15,14},{18,17},{19... | collective-permute-start | bytes 3145736 | tf_op jit(solution)/shard_map/ppermute | solution.py:344
  107.2 25.3 %collective-permute-start.16 = (bf16[512,1024]{1,0:T(8,128)(2,1)}, bf16[512,1024]{1,0:T(8,128)(2,1)S(1)}, u32[]{:S(2)}, u32[]{:S(2)}) collective-permute-start(bf16[512,1024]{1,0:T(8,128)(2,1)} %collective-permute-done.15), channel_id=1, source_target_pairs={{1,0},{5,4},{9,8},{13,12},{17,16},{21,20},{25,24},{29,28}} | collective-permute-start | bytes 3145736 | tf_op jit(solution)/shard_map/ppermute | solution.py:344
  112.0 1.7 collective-permute-start.34
  112.0 22.6 %collective-permute-start.18 = (bf16[512,1024]{1,0:T(8,128)(2,1)}, bf16[512,1024]{1,0:T(8,128)(2,1)}, u32[]{:S(2)}, u32[]{:S(2)}) collective-permute-start(bf16[512,1024]{1,0:T(8,128)(2,1)} %collective-permute-done.17), channel_id=1, source_target_pairs={{2,3},{6,7},{10,11},{14,15},{18,19},{22,23},{26,27},{30,31}} | collective-permute-start | bytes 3145736 | tf_op jit(solution)/shard_map/ppermute | solution.py:344
  113.6 3.6 %collective-permute-start.35 = (f32[5,8]{0,1:T(8,128)S(1)}, f32[5,8]{0,1:T(8,128)S(1)}, u32[]{:S(2)}, u32[]{:S(2)}) collective-permute-start(f32[5,8]{0,1:T(8,128)S(1)} %bitcast_maximum_fusion), channel_id=1, source_target_pairs={{0,8},{4,12},{8,0},{12,4},{16,24},{20,28},{24,16},{28,20},{1,9},{5... | collective-permute-start | bytes 488 | tf_op jit(solution)/shard_map/ppermute | solution.py:340
  117.2 54.6 %collective-permute-start.26 = (bf16[512,1024]{1,0:T(8,128)(2,1)}, bf16[512,1024]{1,0:T(8,128)(2,1)S(1)}, u32[]{:S(2)}, u32[]{:S(2)}) collective-permute-start(bf16[512,1024]{1,0:T(8,128)(2,1)} %get-tuple-element.27.attn_ref), channel_id=1, source_target_pairs={{0,4},{4,0},{8,12},{12,8},{16,20},{20,16},{24,28},{28,24},{1,5},{5... | collective-permute-start | bytes 3145736 | tf_op jit(solution)/shard_map/ppermute | solution.py:340
  117.2 15.3 %copy-start.19 = (bf16[512,4096]{1,0:T(8,128)(2,1)S(1)}, bf16[512,4096]{1,0:T(8,128)(2,1)}, u32[]{:S(2)}) copy-start(bf16[512,4096]{1,0:T(8,128)(2,1)} %copy-done.18) | copy-start | bytes 12582916
  125.9 54.4 %collective-permute-start.36 = (f32[5,8]{0,1:T(8,128)S(1)}, f32[5,8]{0,1:T(8,128)S(1)}, u32[]{:S(2)}, u32[]{:S(2)}) collective-permute-start(f32[5,8]{0,1:T(8,128)S(1)} %max.10), channel_id=1, source_target_pairs={{0,16},{4,20},{8,24},{12,28},{16,0},{20,4},{24,8},{28,12},{1,17},{... | collective-permute-start | bytes 488 | tf_op jit(solution)/shard_map/ppermute | solution.py:340
  136.3 66.1 %copy-start.20 = (bf16[512,4096]{1,0:T(8,128)(2,1)}, bf16[512,4096]{1,0:T(8,128)(2,1)S(1)}, u32[]{:S(2)}) copy-start(bf16[512,4096]{1,0:T(8,128)(2,1)S(1)} %select_dynamic-update-slice_fusion) | copy-start | bytes 12582916
  136.5 10.0 %copy-start.7 = (bf16[512,1024]{1,0:T(8,128)(2,1)S(1)}, bf16[512,1024]{1,0:T(8,128)(2,1)}, u32[]{:S(2)}) copy-start(bf16[512,1024]{1,0:T(8,128)(2,1)} %q_ref.3) | copy-start | bytes 3145732
  136.6 10.0 %copy-start.10 = (bf16[64,1024]{1,0:T(8,128)(2,1)S(1)}, bf16[64,1024]{1,0:T(8,128)(2,1)}, u32[]{:S(2)}) copy-start(bf16[64,1024]{1,0:T(8,128)(2,1)} %copy-done.8) | copy-start | bytes 393220
  136.6 10.0 %copy-start.13 = (bf16[64,1024]{1,0:T(8,128)(2,1)S(1)}, bf16[64,1024]{1,0:T(8,128)(2,1)}, u32[]{:S(2)}) copy-start(bf16[64,1024]{1,0:T(8,128)(2,1)} %copy-done.11) | copy-start | bytes 393220
  136.6 10.0 %copy-start.15 = (f32[512,128]{1,0:T(8,128)S(1)}, f32[512,128]{1,0:T(8,128)}, u32[]{:S(2)}) copy-start(f32[512,128]{1,0:T(8,128)} %copy-done.14) | copy-start | bytes 786436
  136.6 35.4 %collective-permute-start.28 = (bf16[512,512]{1,0:T(8,128)(2,1)S(1)}, bf16[512,512]{1,0:T(8,128)(2,1)S(1)}, u32[]{:S(2)}, u32[]{:S(2)}) collective-permute-start(bf16[512,512]{1,0:T(8,128)(2,1)S(1)} %get-tuple-element.57), channel_id=1, source_target_pairs={{0,4},{4,0},{8,12},{12,8},{16,20},{20,16},{24,28},{28,24},{1,5},{5... | collective-permute-start | bytes 1572872 | tf_op jit(solution)/shard_map/ppermute | solution.py:340
  146.0 29.2 %collective-permute-start.30 = (bf16[512,512]{1,0:T(8,128)(2,1)S(1)}, bf16[512,512]{1,0:T(8,128)(2,1)S(1)}, u32[]{:S(2)}, u32[]{:S(2)}) collective-permute-start(bf16[512,512]{1,0:T(8,128)(2,1)S(1)} %get-tuple-element.56), channel_id=1, source_target_pairs={{0,4},{4,0},{8,12},{12,8},{16,20},{20,16},{24,28},{28,24},{1,5},{5... | collective-permute-start | bytes 1572872 | tf_op jit(solution)/shard_map/ppermute | solution.py:340
  146.0 37.3 %collective-permute-start.32 = (bf16[512,512]{1,0:T(8,128)(2,1)S(1)}, bf16[512,512]{1,0:T(8,128)(2,1)S(1)}, u32[]{:S(2)}, u32[]{:S(2)}) collective-permute-start(bf16[512,512]{1,0:T(8,128)(2,1)S(1)} %get-tuple-element.55), channel_id=1, source_target_pairs={{0,4},{4,0},{8,12},{12,8},{16,20},{20,16},{24,28},{28,24},{1,5},{5... | collective-permute-start | bytes 1572872 | tf_op jit(solution)/shard_map/ppermute | solution.py:340
  171.9 12.5 %copy-start.16 = (bf16[512,1024]{1,0:T(8,128)(2,1)}, bf16[512,1024]{1,0:T(8,128)(2,1)S(1)}, u32[]{:S(2)}) copy-start(bf16[512,1024]{1,0:T(8,128)(2,1)S(1)} %collective-permute-done.26) | copy-start | bytes 3145732
  171.9 39.6 %collective-permute-start.27 = (bf16[512,512]{1,0:T(8,128)(2,1)S(1)}, bf16[512,512]{1,0:T(8,128)(2,1)S(1)}, u32[]{:S(2)}, u32[]{:S(2)}) collective-permute-start(bf16[512,512]{1,0:T(8,128)(2,1)S(1)} %get-tuple-element.54), channel_id=1, source_target_pairs={{0,4},{4,0},{8,12},{12,8},{16,20},{20,16},{24,28},{28,24},{1,5},{5... | collective-permute-start | bytes 1572872 | tf_op jit(solution)/shard_map/ppermute | solution.py:340
  172.0 8.7 %collective-permute-start.22 = (bf16[64,1024]{1,0:T(8,128)(2,1)S(1)}, bf16[64,1024]{1,0:T(8,128)(2,1)S(1)}, u32[]{:S(2)}, u32[]{:S(2)}) collective-permute-start(bf16[64,1024]{1,0:T(8,128)(2,1)S(1)} %get-tuple-element.35), channel_id=1, source_target_pairs={{0,16},{4,20},{8,24},{12,28},{16,0},{20,4},{24,8},{28,12},{1,17},{... | collective-permute-start | bytes 393224 | tf_op jit(solution)/shard_map/ppermute | solution.py:340
  175.3 6.9 %collective-permute-start.23 = (bf16[64,1024]{1,0:T(8,128)(2,1)S(1)}, bf16[64,1024]{1,0:T(8,128)(2,1)S(1)}, u32[]{:S(2)}, u32[]{:S(2)}) collective-permute-start(bf16[64,1024]{1,0:T(8,128)(2,1)S(1)} %get-tuple-element.36), channel_id=1, source_target_pairs={{0,20},{4,16},{8,28},{12,24},{16,4},{20,0},{24,12},{28,8},{1,21},{... | collective-permute-start | bytes 393224 | tf_op jit(solution)/shard_map/ppermute | solution.py:340
  180.3 32.7 %collective-permute-start.19 = (bf16[256,1024]{1,0:T(8,128)(2,1)S(1)}, bf16[256,1024]{1,0:T(8,128)(2,1)S(1)}, u32[]{:S(2)}, u32[]{:S(2)}) collective-permute-start(bf16[256,1024]{1,0:T(8,128)(2,1)S(1)} %get-tuple-element.32), channel_id=1, source_target_pairs={{0,4},{4,0},{8,12},{12,8},{16,20},{20,16},{24,28},{28,24},{1,5},{5... | collective-permute-start | bytes 1572872 | tf_op jit(solution)/shard_map/ppermute | solution.py:340
  180.7 21.6 %collective-permute-start.20 = (bf16[128,1024]{1,0:T(8,128)(2,1)S(1)}, bf16[128,1024]{1,0:T(8,128)(2,1)S(1)}, u32[]{:S(2)}, u32[]{:S(2)}) collective-permute-start(bf16[128,1024]{1,0:T(8,128)(2,1)S(1)} %get-tuple-element.33), channel_id=1, source_target_pairs={{0,8},{4,12},{8,0},{12,4},{16,24},{20,28},{24,16},{28,20},{1,9},{5... | collective-permute-start | bytes 786440 | tf_op jit(solution)/shard_map/ppermute | solution.py:340
  182.2 10.4 %collective-permute-start.24 = (bf16[64,1024]{1,0:T(8,128)(2,1)S(1)}, bf16[64,1024]{1,0:T(8,128)(2,1)S(1)}, u32[]{:S(2)}, u32[]{:S(2)}) collective-permute-start(bf16[64,1024]{1,0:T(8,128)(2,1)S(1)} %get-tuple-element.37), channel_id=1, source_target_pairs={{0,24},{4,28},{8,16},{12,20},{16,8},{20,12},{24,0},{28,4},{1,25},{... | collective-permute-start | bytes 393224 | tf_op jit(solution)/shard_map/ppermute | solution.py:340
  183.3 17.4 %collective-permute-start.25 = (bf16[64,1024]{1,0:T(8,128)(2,1)S(1)}, bf16[64,1024]{1,0:T(8,128)(2,1)S(1)}, u32[]{:S(2)}, u32[]{:S(2)}) collective-permute-start(bf16[64,1024]{1,0:T(8,128)(2,1)S(1)} %get-tuple-element.38), channel_id=1, source_target_pairs={{0,28},{4,24},{8,20},{12,16},{16,12},{20,8},{24,4},{28,0},{1,29},{... | collective-permute-start | bytes 393224 | tf_op jit(solution)/shard_map/ppermute | solution.py:340
  192.6 30.3 %collective-permute-start.12 = (bf16[512,1024]{1,0:T(8,128)(2,1)}, bf16[512,1024]{1,0:T(8,128)(2,1)}, u32[]{:S(2)}, u32[]{:S(2)}) collective-permute-start(bf16[512,1024]{1,0:T(8,128)(2,1)} %get-tuple-element.59), channel_id=1, source_target_pairs={{0,1},{1,2},{2,3},{4,5},{5,6},{6,7},{8,9},{9,10},{10,11},{12,13},{... | collective-permute-start | bytes 3145736 | tf_op jit(solution)/shard_map/ppermute | solution.py:344
  200.7 25.5 %collective-permute-start.9 = (bf16[512,1024]{1,0:T(8,128)(2,1)}, bf16[512,1024]{1,0:T(8,128)(2,1)}, u32[]{:S(2)}, u32[]{:S(2)}) collective-permute-start(bf16[512,1024]{1,0:T(8,128)(2,1)} %get-tuple-element.58), channel_id=1, source_target_pairs={{1,0},{2,1},{3,2},{5,4},{6,5},{7,6},{9,8},{10,9},{11,10},{13,12},{... | collective-permute-start | bytes 3145736 | tf_op jit(solution)/shard_map/ppermute | solution.py:344
  202.3 8.6 %collective-permute-start.21 = (bf16[128,1024]{1,0:T(8,128)(2,1)S(1)}, bf16[128,1024]{1,0:T(8,128)(2,1)S(1)}, u32[]{:S(2)}, u32[]{:S(2)}) collective-permute-start(bf16[128,1024]{1,0:T(8,128)(2,1)S(1)} %get-tuple-element.34), channel_id=1, source_target_pairs={{0,12},{4,8},{8,4},{12,0},{16,28},{20,24},{24,20},{28,16},{1,13},{... | collective-permute-start | bytes 786440 | tf_op jit(solution)/shard_map/ppermute | solution.py:340
  210.9 26.1 %collective-permute-start.29 = (bf16[1024,512]{1,0:T(8,128)(2,1)S(1)}, bf16[1024,512]{1,0:T(8,128)(2,1)}, u32[]{:S(2)}, u32[]{:S(2)}) collective-permute-start(bf16[1024,512]{1,0:T(8,128)(2,1)S(1)} %add_convert_fusion.2), channel_id=1, source_target_pairs={{0,8},{4,12},{8,0},{12,4},{16,24},{20,28},{24,16},{28,20},{1,9},{5... | collective-permute-start | bytes 3145736 | tf_op jit(solution)/shard_map/ppermute | solution.py:340
  211.5 25.5 %collective-permute-start.31 = (bf16[1024,512]{1,0:T(8,128)(2,1)}, bf16[1024,512]{1,0:T(8,128)(2,1)}, u32[]{:S(2)}, u32[]{:S(2)}) collective-permute-start(bf16[1024,512]{1,0:T(8,128)(2,1)} %add_convert_fusion.1), channel_id=1, source_target_pairs={{0,16},{4,20},{8,24},{12,28},{16,0},{20,4},{24,8},{28,12},{1,17},{... | collective-permute-start | bytes 3145736 | tf_op jit(solution)/shard_map/ppermute | solution.py:340
  213.0 46.7 %collective-permute-start.33 = (bf16[1024,512]{1,0:T(8,128)(2,1)}, bf16[1024,512]{1,0:T(8,128)(2,1)}, u32[]{:S(2)}, u32[]{:S(2)}) collective-permute-start(bf16[1024,512]{1,0:T(8,128)(2,1)} %add_convert_fusion), channel_id=1, source_target_pairs={{0,24},{4,28},{8,16},{12,20},{16,8},{20,12},{24,0},{28,4},{1,25},{... | collective-permute-start | bytes 3145736 | tf_op jit(solution)/shard_map/ppermute | solution.py:340
  217.8 4.4 %copy-start.17 = (bf16[512,1024]{1,0:T(8,128)(2,1)S(1)}, bf16[512,1024]{1,0:T(8,128)(2,1)}, u32[]{:S(2)}) copy-start(bf16[512,1024]{1,0:T(8,128)(2,1)} %copy-done.16) | copy-start | bytes 3145732
  (12 other events, 17.3 us)
where the time goes:
time: 265 us; the launch traced here: 264 us
  waiting for transfers between devices  87.2 us (33%)
  starting transfers between devices  55.7 us (21%)
  Pallas kernels  54.8 us (21%)
  matrix products  30.7 us (12%)
  other arithmetic  20.4 us (8%)
  local copies, waits for them, and re-layouts  13.8 us (5%)
    ppermute x25, waiting for transfers between devices, swap(): lax.ppermute(value, axis, [(i, i ^ mask) for i in range(lax.axis_size(axi...  56.8 us
    ppermute x12, starting transfers between devices, shift(): return lax.ppermute(value, axis, pairs)  34.4 us
    ppermute x12, waiting for transfers between devices, shift(): return lax.ppermute(value, axis, pairs)  30.3 us
    pallas_call x1, Pallas kernels, backward_call(): pl.pallas_call(backward_kernel, grid=(heads,), in_specs=[spec] * 5 + [pl....  25.3 us
    pallas_call x1, Pallas kernels, forward_call(): pl.pallas_call(forward_kernel, grid=(heads,), in_specs=[spec, spec, spec]...  22.5 us
    ppermute x25, starting transfers between devices, swap(): lax.ppermute(value, axis, [(i, i ^ mask) for i in range(lax.axis_size(axi...  21.3 us
    dot_general x8, matrix products, dot_tn(): lax.dot_general(a, b, (((0,), (0,)), ((), ())), preferred_element_type=F32)  13.1 us
    unnamed x47, local copies, waits for them, and re-layouts  11.4 us
  transfers between devices with their start and end apart: 37, of which 12 were waited for; matrix products, arithmetic and copies ran while one was open for 19% of the time, Pallas kernels for 20%

commit v1 on v0

v1 whole, which is shorter than its diff:
```python
import functools
import math

import jax
import jax.numpy as jnp
from jax import lax
from jax.experimental import pallas as pl
from jax.experimental.pallas import tpu as pltpu
from jax.sharding import PartitionSpec as P

DH = 128
BLK = 128
LEVELS = 5
SCALE = DH ** (-0.5)
LOG_TWO = math.log(2.0)
F32 = jnp.float32
BF16 = jnp.bfloat16
VMEM_LIMIT = 60 * 1024 * 1024


def dot_nn(a, b):
    return lax.dot_general(a, b, (((1,), (0,)), ((), ())), preferred_element_type=F32)


def dot_nt(a, b):
    return lax.dot_general(a, b, (((1,), (1,)), ((), ())), preferred_element_type=F32)


def dot_tn(a, b):
    return lax.dot_general(a, b, (((0,), (0,)), ((), ())), preferred_element_type=F32)


def pool_matrix(level, rows, tokens):
    row = lax.broadcasted_iota(jnp.int32, (rows, tokens), 0)
    token = lax.broadcasted_iota(jnp.int32, (rows, tokens), 1)
    return jnp.where(lax.shift_right_logical(token, level) == row, 0.5**level, 0.0).astype(BF16)


def pooled(level, tensor):
    tokens = tensor.shape[0]
    return dot_nn(pool_matrix(level, tokens >> level, tokens), tensor).astype(BF16)


def pool_kernel(k_ref, v_ref, two_ref, three_ref, four_ref):
    k = k_ref[...]
    v = v_ref[...]
    for level, out in ((2, two_ref), (3, three_ref), (4, four_ref)):
        rows = k.shape[0] >> level
        out[pl.ds(0, rows), :] = pooled(level, k)
        out[pl.ds(rows, rows), :] = pooled(level, v)


def pool_call(key, value):
    tokens, width = key.shape
    step = 256
    spec = pl.BlockSpec((tokens, step), lambda i: (0, i))
    rows = [2 * (tokens >> level) for level in (2, 3, 4)]
    return pl.pallas_call(
        pool_kernel,
        grid=(width // step,),
        in_specs=[spec, spec],
        out_specs=[pl.BlockSpec((r, step), lambda i: (0, i)) for r in rows],
        out_shape=[jax.ShapeDtypeStruct((r, width), BF16) for r in rows],
        compiler_params=pltpu.CompilerParams(vmem_limit_bytes=VMEM_LIMIT),
        name="pool_keys",
    )(key, value)


def fill_pool(pool, tokens):
    base = 0
    for level in range(1, LEVELS):
        rows = tokens >> level
        pool[pl.ds(base, rows), :] = pool_matrix(level, rows, tokens)
        base += rows


def expand_two(scratch, base, value):
    rows = value.shape[0]
    scratch[pl.ds(base, rows, stride=2), :] = value
    scratch[pl.ds(base + 1, rows, stride=2), :] = value
    return scratch[pl.ds(base, 2 * rows), :]


def partner_rows(near, three, four_a, four_b, columns):
    def cut(ref, base, half):
        return ref[pl.ds(base, half), columns], ref[pl.ds(base + half, half), columns]

    two = BLK
    join = lambda *pairs: tuple(jnp.concatenate(p, 0) for p in zip(*pairs))
    return {
        2: cut(near, 0, two),
        3: join(cut(three, 0, two // 2), cut(near, 2 * two, two // 2)),
        4: join(
            cut(four_a, 0, two // 4),
            cut(four_b, 0, two // 4),
            cut(near, 3 * two, two // 4),
            cut(near, 3 * two + two // 2, two // 4),
        ),
    }


def coarse_slices(tokens):
    base = 0
    found = {}
    for level in range(1, LEVELS):
        rows = tokens >> level
        found[level] = slice(base, base + rows)
        base += rows
    return found


def forward_kernel(
    q_ref, k_ref, v_ref, near, three, four_a, four_b, *rest, extra
):
    attn_ref, lse_ref, top_ref, pool, peak_s, total_s, summed_s = rest[extra:]
    tokens, width = q_ref.shape

    @pl.when(pl.program_id(0) == 0)
    def _():
        fill_pool(pool, tokens)

    q_all = dot_nn(pool[...], q_ref[...]).astype(BF16)
    half = pl.ds(0, tokens // 2)
    k_one = dot_nn(pool[half, :], k_ref[...]).astype(BF16)
    v_one = dot_nn(pool[half, :], v_ref[...]).astype(BF16)
    where = coarse_slices(tokens)
    heads = range(width // DH)
    columns = [pl.ds(h * DH, DH) for h in heads]
    lanes = [slice(h * DH, (h + 1) * DH) for h in heads]
    work = []
    for h in heads:
        partner = partner_rows(near, three, four_a, four_b, columns[h])
        for level in range(LEVELS - 1, -1, -1):
            if level >= 2:
                work.append((h, level, q_all[where[level], lanes[h]], *partner[level]))
            elif level == 1:
                qc, kc, vc = q_all[where[1], lanes[h]], k_one[:, lanes[h]], v_one[:, lanes[h]]
                for b in range(2):
                    mine = slice(b * BLK, (b + 1) * BLK)
                    other = slice((1 - b) * BLK, (2 - b) * BLK)
                    work.append((h, 1, qc[mine], kc[other], vc[other]))
            else:
                for b in range(tokens // (2 * BLK)):
                    both = pl.ds(b * 2 * BLK, 2 * BLK)
                    work.append(
                        (h, 0, q_ref[both, columns[h]], k_ref[both, columns[h]], v_ref[both, columns[h]])
                    )
    scores = [dot_nt(q, k) * SCALE for _, _, q, k, _ in work]
    peaks = [jnp.max(s, axis=-1, keepdims=True) for s in scores]
    weights = [jnp.exp(s - p).astype(BF16) for s, p in zip(scores, peaks)]
    sums = [
        dot_nn(w, jnp.concatenate([item[4], jnp.ones_like(item[4])], 1))
        for w, item in zip(weights, work)
    ]

    def joined(h, level, values):
        return jnp.concatenate([x for x, item in zip(values, work) if item[:2] == (h, level)], 0)

    row = lax.broadcasted_iota(jnp.int32, (8, 128), 0)
    tiles = [jnp.zeros((8, 128), F32) for _ in heads]
    state = {}
    base = 0
    for level in range(LEVELS - 1, -1, -1):
        rows = tokens >> level
        for h in heads:
            peak = joined(h, level, peaks)
            total = joined(h, level, sums)
            tiles[h] = jnp.where(row == level, jnp.max(peak), tiles[h])
            peak = jnp.broadcast_to(peak + level * LOG_TWO, (rows, DH))
            total, summed = total[:, DH:], total[:, :DH]
            if level < LEVELS - 1:
                place = h * 2 * tokens + base
                peak_up, total_up, summed_up = [
                    expand_two(scratch, place, value)
                    for scratch, value in zip((peak_s, total_s, summed_s), state[h])
                ]
                top = jnp.maximum(peak, peak_up)
                mine = jnp.exp(peak - top)
                other = jnp.exp(peak_up - top)
                total = mine * total + other * total_up
                summed = mine * summed + other * summed_up
                peak = top
            state[h] = (peak, total, summed)
        if level < LEVELS - 1:
            base += rows
    for h in heads:
        peak, total, summed = state[h]
        attn_ref[:, columns[h]] = (summed / total).astype(BF16)
        lse_ref[:, columns[h]] = peak + jnp.log(total)
        top_ref[h] = tiles[h]


def forward_call(query, key, value, received, after=(), step=2):
    tokens, width = query.shape
    heads = width // DH
    spec = pl.BlockSpec((tokens, step * DH), lambda h: (0, h))
    others = [pl.BlockSpec((r.shape[0], step * DH), lambda h: (0, h)) for r in received]
    others += [pl.BlockSpec(memory_space=pl.ANY)] * len(after)
    return pl.pallas_call(
        functools.partial(forward_kernel, extra=len(after)),
        grid=(heads // step,),
        in_specs=[spec, spec, spec] + others,
        out_specs=[spec, spec, pl.BlockSpec((step, 8, 128), lambda h: (h, 0, 0))],
        out_shape=[
            jax.ShapeDtypeStruct((tokens, width), BF16),
            jax.ShapeDtypeStruct((tokens, width), F32),
            jax.ShapeDtypeStruct((heads, 8, 128), F32),
        ],
        scratch_shapes=[
            pltpu.VMEM((tokens - tokens // 16, tokens), BF16),
            pltpu.VMEM((step * 2 * tokens, 128), F32),
            pltpu.VMEM((step * 2 * tokens, 128), F32),
            pltpu.VMEM((step * 2 * tokens, 128), F32),
        ],
        compiler_params=pltpu.CompilerParams(vmem_limit_bytes=VMEM_LIMIT),
        name="attention_forward",
    )(query, key, value, *received, *after)


def backward_kernel(
    q_ref, k_ref, v_ref, attn_ref, grad_ref, lse_ref, near, three, four_a, four_b, *rest, extra
):
    gq_ref, gk_ref, gv_ref, far, keep, pool, lse_s, grad_s, scal_s, gq_s, gk_s, gv_s = rest[extra:]
    tokens, width = q_ref.shape

    @pl.when(pl.program_id(0) == 0)
    def _():
        fill_pool(pool, tokens)

    q_all = dot_nn(pool[...], q_ref[...]).astype(BF16)
    half_rows = pl.ds(0, tokens // 2)
    k_one = dot_nn(pool[half_rows, :], k_ref[...]).astype(BF16)
    v_one = dot_nn(pool[half_rows, :], v_ref[...]).astype(BF16)
    where = coarse_slices(tokens)
    heads = range(width // DH)
    columns = [pl.ds(h * DH, DH) for h in heads]
    lanes = [slice(h * DH, (h + 1) * DH) for h in heads]
    scalars = []
    for h in heads:
        grad_f = grad_ref[:, columns[h]].astype(F32)
        scalar = jnp.sum(grad_f * attn_ref[:, columns[h]].astype(F32), axis=-1, keepdims=True)
        scalars.append(scalar)
        first = pl.ds(h * 2 * tokens, tokens)
        lse_s[first, :] = lse_ref[:, columns[h]]
        scal_s[first, :] = jnp.broadcast_to(scalar, (tokens, 128))
        grad_s[first, :] = grad_f
    places = {}
    base = 0
    rows = tokens
    for level in range(1, LEVELS):
        half = rows // 2
        for h in heads:
            start = h * 2 * tokens + base
            even = pl.ds(start, half, stride=2)
            odd = pl.ds(start + 1, half, stride=2)
            lse_even, lse_odd = lse_s[even, :], lse_s[odd, :]
            least = jnp.minimum(lse_even, lse_odd)
            factor_even = jnp.exp(least - lse_even)
            factor_odd = jnp.exp(least - lse_odd)
            summed = factor_even * grad_s[even, :] + factor_odd * grad_s[odd, :]
            summed_scalar = factor_even * scal_s[even, :] + factor_odd * scal_s[odd, :]
            if level < LEVELS - 1:
                nxt = pl.ds(start + rows, half)
                lse_s[nxt, :] = least
                grad_s[nxt, :] = summed
                scal_s[nxt, :] = summed_scalar
            places[h, level] = (least, summed.astype(BF16), summed_scalar)
        base += rows
        rows = half
    work = []
    for h in heads:
        partner = partner_rows(near, three, four_a, four_b, columns[h])
        for level in range(LEVELS - 1, -1, -1):
            if level >= 2:
                work.append(
                    (h, level, q_all[where[level], lanes[h]], *partner[level], *places[h, level])
                )
            elif level == 1:
                low, gr, sc = places[h, 1]
                qc, kc, vc = q_all[where[1], lanes[h]], k_one[:, lanes[h]], v_one[:, lanes[h]]
                for b in range(2):
                    mine = slice(b * BLK, (b + 1) * BLK)
                    other = slice((1 - b) * BLK, (2 - b) * BLK)
                    work.append((h, 1, qc[mine], kc[other], vc[other], low[mine], gr[mine], sc[mine]))
            else:
                for b in range(tokens // (2 * BLK)):
                    both = pl.ds(b * 2 * BLK, 2 * BLK)
                    part = slice(b * 2 * BLK, (b + 1) * 2 * BLK)
                    low = lse_ref[both, columns[h]]
                    work.append((
                        h, 0, q_ref[both, columns[h]], k_ref[both, columns[h]], v_ref[both, columns[h]],
                        jnp.concatenate([low, low], 1), grad_ref[both, columns[h]], scalars[h][part],
                    ))
    scores = [dot_nt(item[2], item[3]) for item in work]
    grads = [dot_nt(item[6], item[4]) for item in work]
    weights = [
        jnp.exp(s * SCALE + (item[1] * LOG_TWO - item[5])) for s, item in zip(scores, work)
    ]
    grad_scores = [
        (w * (g - item[7])).astype(BF16) for w, g, item in zip(weights, grads, work)
    ]
    weights = [w.astype(BF16) for w in weights]
    parts_q = [dot_nn(s, item[3]) * SCALE for s, item in zip(grad_scores, work)]
    parts_k = [dot_tn(s, item[2]) * SCALE for s, item in zip(grad_scores, work)]
    parts_v = [dot_tn(w, item[6]) for w, item in zip(weights, work)]
    found = {}
    for item, *parts in zip(work, parts_q, parts_k, parts_v):
        found.setdefault(item[:2], []).append(parts)
    state = {}
    up = 0
    for level in range(LEVELS - 1, -1, -1):
        rows = tokens >> level
        for h in heads:
            parts = found[h, level]
            if level >= 2:
                part_q, part_k, part_v = parts[0]
                part_k = part_k.astype(BF16)
                part_v = part_v.astype(BF16)
                outs = {
                    2: ((far, 0),),
                    3: ((keep, 0), (far, 2 * BLK)),
                    4: ((keep, BLK), (keep, BLK + BLK // 2), (far, 3 * BLK), (far, 3 * BLK + BLK // 2)),
                }[level]
                piece = BLK // len(outs)
                for i, (out, at) in enumerate(outs):
                    out[pl.ds(at, piece), columns[h]] = part_k[i * piece : (i + 1) * piece]
                    out[pl.ds(at + piece, piece), columns[h]] = part_v[i * piece : (i + 1) * piece]
            elif level == 1:
                part_q = jnp.concatenate([parts[0][0], parts[1][0]], 0)
                part_k = jnp.concatenate([parts[1][1], parts[0][1]], 0)
                part_v = jnp.concatenate([parts[1][2], parts[0][2]], 0)
                coarse_k = expand_two(gk_s, h * tokens, part_k * 0.5)
                coarse_v = expand_two(gv_s, h * tokens, part_v * 0.5)
                state[h, "k"], state[h, "v"] = coarse_k, coarse_v
            if level == 0:
                for b, (part_q, part_k, part_v) in enumerate(parts):
                    both = slice(b * 2 * BLK, (b + 1) * 2 * BLK)
                    here = pl.ds(b * 2 * BLK, 2 * BLK)
                    gq_ref[here, columns[h]] = part_q + state[h, "q"][both]
                    gk_ref[here, columns[h]] = part_k + state[h, "k"][both]
                    gv_ref[here, columns[h]] = part_v + state[h, "v"][both]
            else:
                grad_q = part_q if level == LEVELS - 1 else part_q + state[h, "q"]
                state[h, "q"] = expand_two(gq_s, h * 2 * tokens + up, grad_q * 0.5)
        up += 2 * rows


def backward_call(query, key, value, attn, grad, lse, received, after=(), step=2):
    tokens, width = query.shape
    heads = width // DH
    spec = pl.BlockSpec((tokens, step * DH), lambda h: (0, h))
    others = [pl.BlockSpec((r.shape[0], step * DH), lambda h: (0, h)) for r in received]
    others += [pl.BlockSpec(memory_space=pl.ANY)] * len(after)
    full = jax.ShapeDtypeStruct((tokens, width), F32)
    outs = [spec, pl.BlockSpec((tokens // 2, step * DH), lambda h: (0, h))]
    return pl.pallas_call(
        functools.partial(backward_kernel, extra=len(after)),
        grid=(heads // step,),
        in_specs=[spec] * 6 + others,
        out_specs=[spec] * 3 + outs,
        out_shape=[full] * 3
        + [jax.ShapeDtypeStruct((tokens, width), BF16), jax.ShapeDtypeStruct((tokens // 2, width), BF16)],
        scratch_shapes=[pltpu.VMEM((tokens - tokens // 16, tokens), BF16)]
        + [pltpu.VMEM((step * 2 * tokens, 128), F32)] * 6,
        compiler_params=pltpu.CompilerParams(vmem_limit_bytes=VMEM_LIMIT),
        name="attention_backward",
    )(query, key, value, attn, grad, lse, *received, *after)


def finish_kernel(gk_ref, gv_ref, near, three, four, ok_ref, ov_ref, k_s, v_s):
    for part, local, out, scr in ((0, gk_ref, ok_ref, k_s), (1, gv_ref, ov_ref, v_s)):
        state = None
        base = 0
        for ref, rows in ((four, BLK // 4), (three, BLK // 2), (near, BLK)):
            total = ref[pl.ds(part * rows, rows), :].astype(F32)
            state = total if state is None else total + state
            state = expand_two(scr, base, state * 0.5)
            base += 2 * rows
        state = expand_two(scr, base, state * 0.5)
        out[...] = local[...] + state


def finish_call(grad_k, grad_v, near, three, four):
    tokens, width = grad_k.shape
    step = 128
    spec = pl.BlockSpec((tokens, step), lambda h: (0, h))
    rows = (2 * BLK, BLK, BLK // 2)
    extra = [pl.BlockSpec((r, step), lambda h: (0, h)) for r in rows]
    full = jax.ShapeDtypeStruct((tokens, width), F32)
    scratch = pltpu.VMEM((2 * tokens, step), F32)
    return pl.pallas_call(
        finish_kernel,
        grid=(width // step,),
        in_specs=[spec, spec] + extra,
        out_specs=[spec, spec],
        out_shape=[full, full],
        scratch_shapes=[scratch, scratch],
        compiler_params=pltpu.CompilerParams(vmem_limit_bytes=VMEM_LIMIT),
        name="add_returned",
    )(grad_k, grad_v, near, three, four)


def assemble_kernel(core_ref, *refs, pairs, column):
    count = len(pairs)
    sources = refs[: sum(pairs)]
    outs = refs[sum(pairs) :]
    whole, mine_ref, send_ref = outs[:count], outs[count], outs[count + 1]
    first = core_ref[0] == 0
    at = 0
    for index, number in enumerate(pairs):
        chunk = sources[at][...]
        if number == 2:
            chunk = chunk + sources[at + 1][...]
        at += number
        whole[index][...] = chunk
        width = chunk.shape[1]
        for group in range(width // (2 * column)):
            low = chunk[:, 2 * group * column : (2 * group + 1) * column]
            high = chunk[:, (2 * group + 1) * column : (2 * group + 2) * column]
            here = pl.ds(index * width // 2 + group * column, column)
            mine_ref[:, here] = jnp.where(first, low, high)
            send_ref[:, here] = jnp.where(first, high, low)


def assemble_call(chunks, core, column):
    flat = [array for chunk in chunks for array in chunk]
    tokens, width = flat[0].shape
    count = len(chunks)
    rows = 128
    spec = pl.BlockSpec((rows, width), lambda i: (i, 0))
    half = pl.BlockSpec((rows, count * width // 2), lambda i: (i, 0))
    outs = pl.pallas_call(
        functools.partial(assemble_kernel, pairs=tuple(len(c) for c in chunks), column=column),
        grid=(tokens // rows,),
        in_specs=[pl.BlockSpec(memory_space=pltpu.SMEM)] + [spec] * len(flat),
        out_specs=[spec] * count + [half, half],
        out_shape=[jax.ShapeDtypeStruct((tokens, width), BF16)] * count
        + [jax.ShapeDtypeStruct((tokens, count * width // 2), BF16)] * 2,
        compiler_params=pltpu.CompilerParams(vmem_limit_bytes=VMEM_LIMIT),
        name="assemble",
    )(core.reshape(1).astype(jnp.int32), *flat)
    return outs[:count], outs[count], outs[count + 1]


def term_order(chips):
    top = chips // 2
    groups = {(1, 0): [], (1, 1): [], (0, 1): [], (0, 0): []}
    for i in range(chips):
        groups[i & 1, int(i & top != 0)].append(i)
    return [i for key in ((1, 0), (1, 1), (0, 1), (0, 0)) for i in groups[key]]


def term_kernel(place_ref, turned_ref, mine_ref, theirs_ref, a_send, a_keep, b_send, b_keep, *, chips):
    step = pl.program_id(0)
    tokens = mine_ref.shape[0]
    half = turned_ref.shape[0] // 2

    def rows(start):
        here = pl.ds(start, half)
        return dot_nn(turned_ref[here, pl.ds(0, tokens)], mine_ref[...]) + dot_nn(
            turned_ref[here, pl.ds(tokens, tokens)], theirs_ref[...]
        )

    top = rows(0).astype(BF16)
    bottom = rows(half).astype(BF16)

    @pl.when(step < chips // 2)
    def _():
        a_send[0] = top

    @pl.when(step >= chips // 2)
    def _():
        a_keep[0] = top

    middle = jnp.logical_and(step >= chips // 4, step < 3 * chips // 4)

    @pl.when(middle)
    def _():
        b_send[0] = bottom

    @pl.when(jnp.logical_not(middle))
    def _():
        b_keep[0] = bottom


def term_call(turned, mine, theirs, place, column):
    features = turned.shape[0]
    tokens = mine.shape[0]
    chips = place.shape[0]
    half, quarter = chips // 2, chips // 4
    source = pl.BlockSpec((tokens, column), lambda i, p: (0, p[i]))
    shape = (1, features // 2, column)
    outs = [
        pl.BlockSpec(shape, lambda i, p: (jnp.minimum(i, half - 1), 0, 0)),
        pl.BlockSpec(shape, lambda i, p: (jnp.maximum(i - half, 0), 0, 0)),
        pl.BlockSpec(shape, lambda i, p: (jnp.clip(i - quarter, 0, half - 1), 0, 0)),
        pl.BlockSpec(
            shape,
            lambda i, p: (jnp.where(i < 3 * quarter, jnp.minimum(i, quarter - 1), i - half), 0, 0),
        ),
    ]
    return pl.pallas_call(
        functools.partial(term_kernel, chips=chips),
        grid_spec=pltpu.PrefetchScalarGridSpec(
            num_scalar_prefetch=1,
            grid=(chips,),
            in_specs=[pl.BlockSpec((features, 2 * tokens), lambda i, p: (0, 0)), source, source],
            out_specs=outs,
        ),
        out_shape=[jax.ShapeDtypeStruct((half, features // 2, column), BF16)] * 4,
        compiler_params=pltpu.CompilerParams(vmem_limit_bytes=VMEM_LIMIT),
        name="weight_terms",
    )(place, turned, mine, theirs)


def halve(sent, kept, bits, mask_of):
    for n, bit in enumerate(bits):
        arrived = swap(sent[1], "ctx", mask_of(bit))
        names = [i ^ bit for i in sent[0]]
        parts = {}
        for k, i in enumerate(kept[0]):
            parts[i] = kept[1][k].astype(F32) + arrived[names.index(i)].astype(F32)
        if n + 1 == len(bits):
            return parts[0]
        cut = lambda flag: [i for i in kept[0] if (i & bits[n + 1] != 0) == flag]
        pack = lambda names: (names, jnp.stack([parts[i].astype(BF16) for i in names]))
        sent, kept = pack(cut(True)), pack(cut(False))


def swap(value, axis, mask):
    return lax.ppermute(value, axis, [(i, i ^ mask) for i in range(lax.axis_size(axis))])


def per_device(query, key, value, out_weight, cotangent):
    tokens, width = query.shape
    model = out_weight.shape[1]
    count = lax.axis_size("head")
    ctx_count = lax.axis_size("ctx")
    column = model // ctx_count
    me = lax.axis_index("ctx")
    z = lax.axis_index("head")

    right, left = cotangent, cotangent
    from_left, from_right = [None], [None]
    for step in range(1, count):
        right = lax.ppermute(right, "head", [(i, i + 1) for i in range(step - 1, count - 1)])
        left = lax.ppermute(left, "head", [(i, i - 1) for i in range(1, count - step + 1)])
        from_left.append(right)
        from_right.append(left)

    two, three, four = pool_call(key, value)
    three = swap(three, "ctx", 2)
    four_a = swap(four, "ctx", 4)
    four_b = swap(four, "ctx", 6)
    near = swap(jnp.concatenate([two, three, four_a, four_b], 0), "ctx", 1)
    received = (near, three, four_a, four_b)

    weights = [
        lax.dynamic_slice(
            out_weight, (0, lax.rem(z - s + count, count) * width), (out_weight.shape[0], width)
        )
        for s in range(count)
    ]

    attn, lse, tops = forward_call(query, key, value, received)
    level_max = jnp.max(lax.all_gather(jnp.transpose(tops[:, :LEVELS, 0]), "ctx"), axis=0)
    attn_other = swap(attn, "ctx", 1)
    turned = jnp.concatenate([attn.T, attn_other.T], 1)

    to_left = to_right = None
    for step in range(1, count):
        piece = dot_nn(attn, weights[count - step])
        to_left = (piece if to_left is None else piece + to_left).astype(BF16)
        to_left = lax.ppermute(to_left, "head", [(i, i - 1) for i in range(count - step, count)])
        piece = dot_nn(attn, weights[step])
        to_right = (piece if to_right is None else piece + to_right).astype(BF16)
        to_right = lax.ppermute(to_right, "head", [(i, i + 1) for i in range(0, step)])
    mixed = dot_nn(attn, weights[0]) + to_left + to_right

    core = me % 2
    early = [s for s in range(count) if s not in (1, count - 1)]
    late = sorted({1, count - 1})
    grad_attn = None
    mine, theirs = [], []
    for group in (early, late):
        chunks = [(cotangent,) if s == 0 else (from_left[s], from_right[count - s]) for s in group]
        whole, here, send = assemble_call(chunks, core, column)
        mine.append(here)
        theirs.append(swap(send, "ctx", 1))
        for s, chunk in zip(group, whole):
            part = dot_nt(chunk, weights[s])
            grad_attn = part if grad_attn is None else grad_attn + part
    grad_attn = grad_attn.astype(BF16)

    chips = ctx_count // 2
    per_chunk = chips // count
    slots = {s: n for n, s in enumerate(early + late)}
    slot = jnp.array([slots[s] for s in range(count)], jnp.int32)
    order = term_order(chips)
    chip = jnp.bitwise_xor(me // 2, jnp.array(order, jnp.int32))
    place = slot[lax.rem(z - chip // per_chunk + count, count)] * per_chunk + chip % per_chunk
    terms = term_call(
        turned, jnp.concatenate(mine, 1), jnp.concatenate(theirs, 1), place.astype(jnp.int32), column
    )
    half, quarter = chips // 2, chips // 4
    bits = [1 << n for n in range(chips.bit_length() - 1)]
    mask_of = lambda bit: 2 * bit
    top_rows = halve((order[:half], terms[0]), (order[half:], terms[1]), bits, mask_of)
    bottom_rows = halve(
        (order[quarter : 3 * quarter], terms[2]),
        (order[:quarter] + order[3 * quarter :], terms[3]),
        bits[::-1],
        mask_of,
    )
    weight_grad = jnp.concatenate([top_rows, bottom_rows], 0)

    outs = backward_call(query, key, value, attn, grad_attn, lse, received, after=terms)
    grad_q, grad_k, grad_v, far, keep = outs
    far = swap(far, "ctx", 1)
    half = tokens // 2
    keep = (keep.astype(F32) + far[half:].astype(F32)).astype(BF16)
    third = BLK + BLK // 2
    sent = jnp.concatenate([keep[:BLK], keep[third:]], 0)
    back = swap(sent, "ctx", 2)
    back_four = swap((keep[BLK:third].astype(F32) + back[BLK:].astype(F32)).astype(BF16), "ctx", 4)
    grad_k, grad_v = finish_call(grad_k, grad_v, far, back, back_four)
    return mixed, grad_q, grad_k, grad_v, weight_grad, level_max


def solution(mesh):
    tokens = P("ctx", "head")
    return jax.shard_map(
        per_device,
        mesh=mesh,
        in_specs=(tokens, tokens, tokens, P("head", None), tokens),
        out_specs=(tokens, tokens, tokens, tokens, P("head", "ctx"), P(None, "head")),
        check_vma=False,
    )
```

time: 265 us -> 235 us (0.89)
  waiting for transfers between devices: 87.2 us -> 41.4 us
  blocking collectives: 0 us -> 27 us
  starting transfers between devices: 55.7 us -> 45.6 us
  local copies, waits for them, and re-layouts: 13.8 us -> 4.5 us
  other arithmetic: 20.4 us -> 28.3 us
    ppermute x25 -> x14, waiting for transfers between devices: 56.8 us -> 13.4 us  [swap(): lax.ppermute(value, axis, [(i, i ^ mask) for i in range(lax.axis_size(axi...]
    all_gather x0 -> x1, blocking collectives: none -> 27 us  [per_device(): lax.all_gather(jnp.transpose(tops[:, :LEVELS, 0]), 'ctx')]
    dot_general x8 -> x0, matrix products: 13.1 us -> none  [dot_tn(): lax.dot_general(a, b, (((0,), (0,)), ((), ())), preferred_element_type=F32)]
    concatenate x0 -> x6, other arithmetic: none -> 11.2 us  [the longest x1 3.12 us: per_device(): turned = jnp.concatenate([attn.T, attn_other.T], 1)]
    unnamed x47 -> x48, local copies, waits for them, and re-layouts: 11.4 us -> 1.72 us
    ppermute x25 -> x14, starting transfers between devices: 21.3 us -> 12.4 us  [swap(): lax.ppermute(value, axis, [(i, i ^ mask) for i in range(lax.axis_size(axi...]
    dot_general x1 -> x4, matrix products: 8.29 us -> 16.5 us  [dot_nn(): lax.dot_general(a, b, (((1,), (0,)), ((), ())), preferred_element_type=F32)]
    dot_general x1 -> x4, matrix products: 9.36 us -> 16 us  [dot_nt(): lax.dot_general(a, b, (((1,), (1,)), ((), ())), preferred_element_type=F32)]
  transfers between devices with their start and end apart: 37 -> 26, of which waited for: 12 -> 7; matrix products, arithmetic and copies ran while one was open for 19% -> 26% of each run, Pallas kernels for 20% -> 21%
where the time goes in v1:
time: 235 us; the launch traced here: 233 us
  Pallas kernels  52.8 us (22%)
  starting transfers between devices  45.6 us (19%)
  waiting for transfers between devices  41.4 us (18%)
  matrix products  32.5 us (14%)
  other arithmetic  28.3 us (12%)
  blocking collectives  27 us (11%)
  local copies, waits for them, and re-layouts  4.5 us (2%)
    all_gather x1, blocking collectives, per_device(): lax.all_gather(jnp.transpose(tops[:, :LEVELS, 0]), 'ctx')  27 us
    ppermute x3, starting transfers between devices, per_device(): lax.ppermute(to_right, 'head', [(i, i + 1) for i in range(0, step)])  16.6 us
    dot_general x4, matrix products, dot_nn(): lax.dot_general(a, b, (((1,), (0,)), ((), ())), preferred_element_type=F32)  16.5 us
    dot_general x4, matrix products, dot_nt(): lax.dot_general(a, b, (((1,), (1,)), ((), ())), preferred_element_type=F32)  16 us
    ppermute x3, waiting for transfers between devices, per_device(): lax.ppermute(right, 'head', [(i, i + 1) for i in range(step - 1, count -...  14.2 us
    ppermute x3, waiting for transfers between devices, per_device(): lax.ppermute(left, 'head', [(i, i - 1) for i in range(1, count - step + 1)])  13.7 us
    ppermute x14, waiting for transfers between devices, swap(): lax.ppermute(value, axis, [(i, i ^ mask) for i in range(lax.axis_size(axi...  13.4 us
    ppermute x14, starting transfers between devices, swap(): lax.ppermute(value, axis, [(i, i ^ mask) for i in range(lax.axis_size(axi...  12.4 us
  transfers between devices with their start and end apart: 26, of which 7 were waited for; matrix products, arithmetic and copies ran while one was open for 26% of the time, Pallas kernels for 21%

profile of v1, /device:TPU:0, one launch (start us, length us, event | category | flops | bytes accessed | tf_op | source)
XLA Modules:
  0.0 233.2 jit_solution(15969310538248047287)
XLA Ops:
  0.6 4.2 %pool_keys.1 = (bf16[256,1024]{1,0:T(8,128)(2,1)}, bf16[128,1024]{1,0:T(8,128)(2,1)}, bf16[64,1024]{1,0:T(8,128)(2,1)}) custom-call(bf16[512,1024]{1,0:T(8,128)(2,1)} %k_ref.5, bf16[512,1024]{1,0:T(8,128)(2,1)} %v_ref.5), custom_call_target="tpu_custom_call" | custom-call | tf_op jit(solution)/shard_map/pool_keys/pallas_call | solution.py:58
  4.8 2.9 %collective-permute-start = (bf16[128,1024]{1,0:T(8,128)(2,1)}, bf16[128,1024]{1,0:T(8,128)(2,1)S(1)}, u32[]{:S(2)}, u32[]{:S(2)}) collective-permute-start(bf16[128,1024]{1,0:T(8,128)(2,1)} %get-tuple-element.32), channel_id=1, source_target_pairs={{0,8},{4,12},{8,0},{12,4},{16,24},{20,28},{24,16},{28,20},{1,9},{5... | collective-permute-start | bytes 786440 | tf_op jit(solution)/shard_map/ppermute | solution.py:531
  7.8 1.5 collective-permute-start.2
  9.3 4.9 %collective-permute-start.10 = (bf16[512,1024]{1,0:T(8,128)(2,1)S(1)}, bf16[512,1024]{1,0:T(8,128)(2,1)}, u32[]{:S(2)}, u32[]{:S(2)}) collective-permute-start(bf16[512,1024]{1,0:T(8,128)(2,1)S(1)} %copy-done.14), channel_id=1, source_target_pairs={{0,1},{1,2},{2,3},{4,5},{5,6},{6,7},{8,9},{9,10},{10,11},{12,13},{... | collective-permute-start | bytes 3145736 | tf_op jit(solution)/shard_map/ppermute | solution.py:546
  14.2 1.3 collective-permute-start.12
  15.5 2.8 %collective-permute-done.2.four_b = bf16[64,1024]{1,0:T(8,128)(2,1)S(1)} collective-permute-done((bf16[64,1024]{1,0:T(8,128)(2,1)}, bf16[64,1024]{1,0:T(8,128)(2,1)S(1)}, u32[]{:S(2)}, u32[]{:S(2)}) %collective-permute-start.2) | collective-permute-done | bytes 131104 | tf_op jit(solution)/shard_map/ppermute | solution.py:531
  18.3 2.3 pad_maximum_fusion.4
  20.6 14.2 %collective-permute-done.10.refs_0_ = bf16[512,1024]{1,0:T(8,128)(2,1)} collective-permute-done((bf16[512,1024]{1,0:T(8,128)(2,1)S(1)}, bf16[512,1024]{1,0:T(8,128)(2,1)}, u32[]{:S(2)}, u32[]{:S(2)}) %collective-permute-start.10) | collective-permute-done | bytes 1048608 | tf_op jit(solution)/shard_map/ppermute | solution.py:546
  34.8 1.6 collective-permute-start.11
  36.4 3.6 %collective-permute-done.12.refs_3_ = bf16[512,1024]{1,0:T(8,128)(2,1)} collective-permute-done((bf16[512,1024]{1,0:T(8,128)(2,1)S(1)}, bf16[512,1024]{1,0:T(8,128)(2,1)}, u32[]{:S(2)}, u32[]{:S(2)}) %collective-permute-start.12) | collective-permute-done | bytes 1048608 | tf_op jit(solution)/shard_map/ppermute | solution.py:547
  40.0 1.3 collective-permute-start.13
  42.3 10.8 %attention_forward.1 = (bf16[512,1024]{1,0:T(8,128)(2,1)}, f32[512,1024]{1,0:T(8,128)}, f32[8,8,128]{2,1,0:T(8,128)}) custom-call(bf16[512,1024]{1,0:T(8,128)(2,1)} %q_ref.3, bf16[512,1024]{1,0:T(8,128)(2,1)} %k_ref.5, bf16[512,1024]{1,0:T(8,128)(2,1)} %v_ref.5, bf16[512,1024]{1,0:T(8,128)(2,1)} %copy-done.5, bf16[128,1024]{1,0:T(8,128)(2,1)} %copy-done.7, ...), custom_call_target="tpu_custom_call" | custom-call | tf_op jit(solution)/shard_map/attention_forward/pallas_call | solution.py:199
  53.2 4.9 %fusion.27 = (bf16[512,1024]{1,0:T(8,128)(2,1)}, f32[512,1024]{1,0:T(8,128)}) fusion(bf16[512,1024]{1,0:T(8,128)(2,1)} %get-tuple-element.34.attn_ref, bf16[1024,4096]{1,0:T(8,128)(2,1)} %param.10, s32[]{:T(128)S(6)} %select_n.37), kind=kOutput, calls=%fused_computation.51 | convolution fusion | flops 1074266112 | bytes 6291460 | tf_op jit(solution)/shard_map/dot_general | solution.py:22
  58.1 1.6 collective-permute-start.4
  60.9 1.4 copy.19
  62.3 2.8 %fusion.6 = f32[512,1024]{1,0:T(8,128)S(1)} fusion(bf16[512,1024]{1,0:T(8,128)(2,1)S(1)} %copy-done.3, bf16[1024,4096]{1,0:T(8,128)(2,1)} %param.10, s32[]{:T(128)S(6)} %select_n.36), kind=kOutput, calls=%fused_computation.17 | convolution fusion | flops 1073741824 | bytes 5242884 | tf_op jit(solution)/shard_map/dot_general | solution.py:22
  65.2 4.4 %assemble.2 = (bf16[512,1024]{1,0:T(8,128)(2,1)}, bf16[512,1024]{1,0:T(8,128)(2,1)}, bf16[512,1024]{1,0:T(8,128)(2,1)}, bf16[512,1024]{1,0:T(8,128)(2,1)}) custom-call(s32[1]{0:T(128)} %bitcast.core_ref, bf16[512,1024]{1,0:T(8,128)(2,1)} %refs_0_.1, bf16[512,1024]{1,0:T(8,128)(2,1)} %collective-permute-done.11.refs_1_, ...), custom_call_target="tpu_custom_call" | custom-call | tf_op jit(solution)/shard_map/assemble/pallas_call | solution.py:432
  70.1 1.6 collective-permute-start.15
  73.0 4.5 %fusion.4 = f32[512,1024]{1,0:T(8,128)} fusion(bf16[512,1024]{1,0:T(8,128)(2,1)} %get-tuple-element.36, bf16[1024,4096]{1,0:T(8,128)(2,1)} %param.10, s32[]{:T(128)S(6)} %select_n.36), kind=kOutput, calls=%fused_computation.15 | convolution fusion | flops 1073741824 | bytes 5242884 | tf_op jit(solution)/shard_map/dot_general | solution.py:26
  77.6 2.6 %add_convert_fusion.4 = bf16[512,1024]{1,0:T(8,128)(2,1)} fusion(f32[512,1024]{1,0:T(8,128)S(1)} %fusion.6, bf16[512,1024]{1,0:T(8,128)(2,1)} %collective-permute-done.4), kind=kLoop, calls=%fused_computation.10 | loop fusion | flops 1572864 | bytes 4194304 | tf_op jit(solution)/shard_map/convert_element_type | solution.py:573
  80.2 1.6 collective-permute-start.5
  81.8 4.2 %fusion.12 = f32[512,1024]{1,0:T(8,128)} fusion(bf16[512,1024]{1,0:T(8,128)(2,1)S(1)} %copy-done.23, bf16[1024,4096]{1,0:T(8,128)(2,1)} %param.10, s32[]{:T(128)S(6)} %select_n.34), kind=kOutput, calls=%fused_computation.23 | convolution fusion | flops 1073741824 | bytes 5242884 | tf_op jit(solution)/shard_map/dot_general | solution.py:26
  86.0 3.1 %pad_maximum_fusion.turned_ref = bf16[1024,1024]{1,0:T(8,128)(2,1)} fusion(bf16[1024,512]{1,0:T(8,128)(2,1)} %bitcast.2, bf16[1024,512]{1,0:T(8,128)(2,1)} %bitcast.1), kind=kLoop, calls=%fused_computation.1 | loop fusion | flops 4194304 | bytes 4194304 | tf_op jit(solution)/shard_map/concatenate | solution.py:568
  89.1 10.2 %collective-permute-done.14.refs_1_ = bf16[512,1024]{1,0:T(8,128)(2,1)} collective-permute-done((bf16[512,1024]{1,0:T(8,128)(2,1)}, bf16[512,1024]{1,0:T(8,128)(2,1)}, u32[]{:S(2)}, u32[]{:S(2)}) %collective-permute-start.14) | collective-permute-done | bytes 1048608 | tf_op jit(solution)/shard_map/ppermute | solution.py:547
  99.3 4.7 %assemble.3 = (bf16[512,1024]{1,0:T(8,128)(2,1)}, bf16[512,1024]{1,0:T(8,128)(2,1)}, bf16[512,1024]{1,0:T(8,128)(2,1)}, bf16[512,1024]{1,0:T(8,128)(2,1)}) custom-call(s32[1]{0:T(128)} %bitcast.core_ref, bf16[512,1024]{1,0:T(8,128)(2,1)} %collective-permute-done.10.refs_0_, bf16[512,1024]{1,0:T(8,128)(2,1)} %collective-permute-done.14.refs_1_, ...), custom_call_target="tpu_custom_call" | custom-call | tf_op jit(solution)/shard_map/assemble/pallas_call | solution.py:432
  104.0 3.3 %fusion.8 = f32[512,1024]{1,0:T(8,128)S(1)} fusion(bf16[512,1024]{1,0:T(8,128)(2,1)} %get-tuple-element.37, bf16[1024,4096]{1,0:T(8,128)(2,1)} %param.10, s32[]{:T(128)S(6)} %select_n.35), kind=kOutput, calls=%fused_computation.19 | convolution fusion | flops 1073741824 | bytes 5242884 | tf_op jit(solution)/shard_map/dot_general | solution.py:26
  107.3 1.5 pad_maximum_fusion.1.mine_ref
  108.9 4.6 %add_convert_fusion.3 = (bf16[512,1024]{1,0:T(8,128)(2,1)}, bf16[512,1024]{1,0:T(8,128)(2,1)}) fusion(bf16[512,1024]{1,0:T(8,128)(2,1)} %collective-permute-done.5, bf16[512,1024]{1,0:T(8,128)(2,1)S(1)} %copy-done.3, bf16[1024,4096]{1,0:T(8,128)(2,1)} %param.10, s32[]{:T(128)S(6)} %select_n.35), kind=kOutput, calls=%fused_computation.9 | convolution fusion | flops 1075838976 | bytes 6291460 | tf_op jit(solution)/shard_map/dot_general | solution.py:22
  113.5 9.6 %collective-permute-start.7 = (bf16[512,1024]{1,0:T(8,128)(2,1)}, bf16[512,1024]{1,0:T(8,128)(2,1)}, u32[]{:S(2)}, u32[]{:S(2)}) collective-permute-start(bf16[512,1024]{1,0:T(8,128)(2,1)} %get-tuple-element.57), channel_id=1, source_target_pairs={{0,1},{4,5},{8,9},{12,13},{16,17},{20,21},{24,25},{28,29}} | collective-permute-start | bytes 3145736 | tf_op jit(solution)/shard_map/ppermute | solution.py:577
  123.1 3.9 %add_convert_fusion.grad_ref = bf16[512,1024]{1,0:T(8,128)(2,1)} fusion(f32[512,1024]{1,0:T(8,128)S(1)} %fusion.8, f32[512,1024]{1,0:T(8,128)S(1)} %copy-done.11, f32[512,1024]{1,0:T(8,128)S(1)} %copy-done.10, bf16[512,1024]{1,0:T(8,128)(2,1)S(1)} %copy-done.17, bf16[1024,4096]{1,0:T(8,128)(2,1)} %param.10, s32[]{:T(128)S(6)} %select_n.37), kind=kOutput, calls=%fused_computation.5 | convolution fusion | flops 1075838976 | bytes 10485764 | tf_op jit(solution)/shard_map/dot_general | solution.py:26
  126.9 2.7 %pad_maximum_fusion.2.theirs_ref = bf16[512,2048]{1,0:T(8,128)(2,1)} fusion(bf16[512,1024]{1,0:T(8,128)(2,1)S(1)} %collective-permute-done.18, bf16[512,1024]{1,0:T(8,128)(2,1)} %collective-permute-done.17), kind=kLoop, calls=%fused_computation.3 | loop fusion | flops 4194304 | bytes 4194304 | tf_op jit(solution)/shard_map/concatenate | solution.py:603
  129.7 9.7 %weight_terms.1 = (bf16[2,512,512]{2,1,0:T(8,128)(2,1)}, bf16[2,512,512]{2,1,0:T(8,128)(2,1)}, bf16[2,512,512]{2,1,0:T(8,128)(2,1)}, bf16[2,512,512]{2,1,0:T(8,128)(2,1)}) custom-call(s32[4]{0:T(128)} %gather_fusion, bf16[1024,1024]{1,0:T(8,128)(2,1)} %pad_maximum_fusion.turned_ref, bf16[512,2048]{1,0:T(8,128)(2,1)} %pad_maximum_fusion.1.mine_ref, ...), custom_call_target="tpu_custom_call" | custom-call | tf_op jit(solution)/shard_map/weight_terms/pallas_call | solution.py:502
  139.4 12.1 %attention_backward.1 = (f32[512,1024]{1,0:T(8,128)}, f32[512,1024]{1,0:T(8,128)}, f32[512,1024]{1,0:T(8,128)}, bf16[512,1024]{1,0:T(8,128)(2,1)}, bf16[256,1024]{1,0:T(8,128)(2,1)}) custom-call(bf16[512,1024]{1,0:T(8,128)(2,1)} %q_ref.3, bf16[512,1024]{1,0:T(8,128)(2,1)} %k_ref.5, bf16[512,1024]{1,0:T(8,128)(2,1)} %v_ref.5, ...), custom_call_target="tpu_custom_call" | custom-call | tf_op jit(solution)/shard_map/attention_backward/pallas_call | solution.py:356
  151.6 1.6 collective-permute-start.22
  153.1 2.5 %add_convert_fusion.2 = bf16[512,1024]{1,0:T(8,128)(2,1)} fusion(f32[512,1024]{1,0:T(8,128)S(1)} %fusion.6, bf16[512,1024]{1,0:T(8,128)(2,1)} %collective-permute-done.7), kind=kLoop, calls=%fused_computation.8 | loop fusion | flops 1572864 | bytes 4194304 | tf_op jit(solution)/shard_map/convert_element_type | solution.py:576
  155.7 2.4 %collective-permute-start.8 = (bf16[512,1024]{1,0:T(8,128)(2,1)}, bf16[512,1024]{1,0:T(8,128)(2,1)}, u32[]{:S(2)}, u32[]{:S(2)}) collective-permute-start(bf16[512,1024]{1,0:T(8,128)(2,1)} %add_convert_fusion.2), channel_id=1, source_target_pairs={{0,1},{1,2},{4,5},{5,6},{8,9},{9,10},{12,13},{13,14},{16,17},{17,1... | collective-permute-start | bytes 3145736 | tf_op jit(solution)/shard_map/ppermute | solution.py:577
  158.1 4.2 %fusion.14 = f32[512,1024]{1,0:T(8,128)} fusion(bf16[512,1024]{1,0:T(8,128)(2,1)S(1)} %copy-done.4, bf16[1024,4096]{1,0:T(8,128)(2,1)} %param.10, s32[]{:T(128)S(6)} %select_n.34), kind=kOutput, calls=%fused_computation.25 | convolution fusion | flops 1073741824 | bytes 5242884 | tf_op jit(solution)/shard_map/dot_general | solution.py:22
  162.3 1.5 collective-permute-start.24
  164.0 27.0 %all-gather.1 = f32[8,5,8]{2,1,0:T(8,128)S(1)} all-gather(f32[1,5,8]{2,1,0:T(8,128)S(1)} %bitcast.18), channel_id=2, replica_groups=mesh['ctx'=8,'head'=4] {'ctx'}, dimensions={0}, use_global_device_ids=true | all-gather | bytes 1440 | tf_op jit(solution)/shard_map/all_gather | solution.py:566
  193.2 1.7 add_convert_fusion.7
  194.9 1.6 collective-permute-start.23
  196.5 1.5 collective-permute-start.20
  198.1 2.7 %add_convert_fusion.1 = bf16[512,1024]{1,0:T(8,128)(2,1)} fusion(f32[512,1024]{1,0:T(8,128)S(1)} %copy-done.9, bf16[512,1024]{1,0:T(8,128)(2,1)} %collective-permute-done.8), kind=kLoop, calls=%fused_computation.7 | loop fusion | flops 1572864 | bytes 4194304 | tf_op jit(solution)/shard_map/convert_element_type | solution.py:576
  200.8 4.6 %collective-permute-start.9 = (bf16[512,1024]{1,0:T(8,128)(2,1)}, bf16[512,1024]{1,0:T(8,128)(2,1)S(1)}, u32[]{:S(2)}, u32[]{:S(2)}) collective-permute-start(bf16[512,1024]{1,0:T(8,128)(2,1)} %add_convert_fusion.1), channel_id=1, source_target_pairs={{0,1},{1,2},{2,3},{4,5},{5,6},{6,7},{8,9},{9,10},{10,11},{12,13},{... | collective-permute-start | bytes 3145736 | tf_op jit(solution)/shard_map/ppermute | solution.py:577
  210.3 9.4 %collective-permute-done.25 = bf16[1,512,512]{2,1,0:T(8,128)(2,1)S(1)} collective-permute-done((bf16[1,512,512]{2,1,0:T(8,128)(2,1)S(1)}, bf16[1,512,512]{2,1,0:T(8,128)(2,1)S(1)}, u32[]{:S(2)}, u32[]{:S(2)}) %collective-permute-start.25) | collective-permute-done | bytes 524320 | tf_op jit(solution)/shard_map/ppermute | solution.py:531
  221.0 1.5 pad_maximum_fusion.3
  223.1 7.0 %add_returned.1 = (f32[512,1024]{1,0:T(8,128)}, f32[512,1024]{1,0:T(8,128)}) custom-call(f32[512,1024]{1,0:T(8,128)} %get-tuple-element.49.gk_ref, f32[512,1024]{1,0:T(8,128)} %get-tuple-element.50.gv_ref, bf16[512,1024]{1,0:T(8,128)(2,1)} %copy-done.6, bf16[192,1024]{1,0:T(8,128)(2,1)} %copy-done.18, bf16[64,1024]{1,0:T(8,128)(2,1)} %copy-done.20), custom_call_target="tpu_custom_call" | custom-call | tf_op jit(solution)/shard_map/add_returned/pallas_call | solution.py:391
  230.1 3.1 %convert_add_fusion = f32[512,1024]{1,0:T(8,128)} fusion(bf16[512,1024]{1,0:T(8,128)(2,1)S(1)} %collective-permute-done.9, f32[512,1024]{1,0:T(8,128)S(1)} %copy-done.8, bf16[512,1024]{1,0:T(8,128)(2,1)} %collective-permute-done.6), kind=kLoop, calls=%fused_computation.6 | loop fusion | flops 2097152 | bytes 6291456 | tf_op jit(solution)/shard_map/add | solution.py:578
  (93 shorter events, 13.3 us)
Async XLA Ops:
  0.6 8.7 %copy-start.14 = (bf16[512,1024]{1,0:T(8,128)(2,1)S(1)}, bf16[512,1024]{1,0:T(8,128)(2,1)}, u32[]{:S(2)}) copy-start(bf16[512,1024]{1,0:T(8,128)(2,1)} %refs_0_.1) | copy-start | bytes 3145732
  4.8 13.5 %collective-permute-start = (bf16[128,1024]{1,0:T(8,128)(2,1)}, bf16[128,1024]{1,0:T(8,128)(2,1)S(1)}, u32[]{:S(2)}, u32[]{:S(2)}) collective-permute-start(bf16[128,1024]{1,0:T(8,128)(2,1)} %get-tuple-element.32), channel_id=1, source_target_pairs={{0,8},{4,12},{8,0},{12,4},{16,24},{20,28},{24,16},{28,20},{1,9},{5... | collective-permute-start | bytes 786440 | tf_op jit(solution)/shard_map/ppermute | solution.py:531
  7.8 10.5 %collective-permute-start.2 = (bf16[64,1024]{1,0:T(8,128)(2,1)}, bf16[64,1024]{1,0:T(8,128)(2,1)S(1)}, u32[]{:S(2)}, u32[]{:S(2)}) collective-permute-start(bf16[64,1024]{1,0:T(8,128)(2,1)} %get-tuple-element.33), channel_id=1, source_target_pairs={{0,24},{4,28},{8,16},{12,20},{16,8},{20,12},{24,0},{28,4},{1,25},{... | collective-permute-start | bytes 393224 | tf_op jit(solution)/shard_map/ppermute | solution.py:531
  9.3 9.0 %collective-permute-start.1 = (bf16[64,1024]{1,0:T(8,128)(2,1)}, bf16[64,1024]{1,0:T(8,128)(2,1)S(1)}, u32[]{:S(2)}, u32[]{:S(2)}) collective-permute-start(bf16[64,1024]{1,0:T(8,128)(2,1)} %get-tuple-element.33), channel_id=1, source_target_pairs={{0,16},{4,20},{8,24},{12,28},{16,0},{20,4},{24,8},{28,12},{1,17},{... | collective-permute-start | bytes 393224 | tf_op jit(solution)/shard_map/ppermute | solution.py:531
  9.3 25.5 %collective-permute-start.10 = (bf16[512,1024]{1,0:T(8,128)(2,1)S(1)}, bf16[512,1024]{1,0:T(8,128)(2,1)}, u32[]{:S(2)}, u32[]{:S(2)}) collective-permute-start(bf16[512,1024]{1,0:T(8,128)(2,1)S(1)} %copy-done.14), channel_id=1, source_target_pairs={{0,1},{1,2},{2,3},{4,5},{5,6},{6,7},{8,9},{9,10},{10,11},{12,13},{... | collective-permute-start | bytes 3145736 | tf_op jit(solution)/shard_map/ppermute | solution.py:546
  14.2 25.8 %collective-permute-start.12 = (bf16[512,1024]{1,0:T(8,128)(2,1)S(1)}, bf16[512,1024]{1,0:T(8,128)(2,1)}, u32[]{:S(2)}, u32[]{:S(2)}) collective-permute-start(bf16[512,1024]{1,0:T(8,128)(2,1)S(1)} %copy-done.14), channel_id=1, source_target_pairs={{1,0},{2,1},{3,2},{5,4},{6,5},{7,6},{9,8},{10,9},{11,10},{13,12},{... | collective-permute-start | bytes 3145736 | tf_op jit(solution)/shard_map/ppermute | solution.py:547
  18.3 23.0 %copy-start.12 = (bf16[64,1024]{1,0:T(8,128)(2,1)}, bf16[64,1024]{1,0:T(8,128)(2,1)S(1)}, u32[]{:S(2)}) copy-start(bf16[64,1024]{1,0:T(8,128)(2,1)S(1)} %collective-permute-done.2.four_b) | copy-start | bytes 393220
  18.3 23.0 %copy-start.13 = (bf16[64,1024]{1,0:T(8,128)(2,1)}, bf16[64,1024]{1,0:T(8,128)(2,1)S(1)}, u32[]{:S(2)}) copy-start(bf16[64,1024]{1,0:T(8,128)(2,1)S(1)} %collective-permute-done.1.four_a) | copy-start | bytes 393220
  18.3 23.0 %copy-start.7 = (bf16[128,1024]{1,0:T(8,128)(2,1)}, bf16[128,1024]{1,0:T(8,128)(2,1)S(1)}, u32[]{:S(2)}) copy-start(bf16[128,1024]{1,0:T(8,128)(2,1)S(1)} %collective-permute-done.three) | copy-start | bytes 786436
  20.6 20.7 %collective-permute-start.3 = (bf16[512,1024]{1,0:T(8,128)(2,1)}, bf16[512,1024]{1,0:T(8,128)(2,1)S(1)}, u32[]{:S(2)}, u32[]{:S(2)}) collective-permute-start(bf16[512,1024]{1,0:T(8,128)(2,1)} %pad_maximum_fusion.4), channel_id=1, source_target_pairs={{0,4},{4,0},{8,12},{12,8},{16,20},{20,16},{24,28},{28,24},{1,5},{5... | collective-permute-start | bytes 3145736 | tf_op jit(solution)/shard_map/ppermute | solution.py:531
  34.8 30.4 %collective-permute-start.11 = (bf16[512,1024]{1,0:T(8,128)(2,1)}, bf16[512,1024]{1,0:T(8,128)(2,1)}, u32[]{:S(2)}, u32[]{:S(2)}) collective-permute-start(bf16[512,1024]{1,0:T(8,128)(2,1)} %collective-permute-done.10.refs_0_), channel_id=1, source_target_pairs={{1,2},{2,3},{5,6},{6,7},{9,10},{10,11},{13,14},{14,15},{17,18},{18... | collective-permute-start | bytes 3145736 | tf_op jit(solution)/shard_map/ppermute | solution.py:546
  40.0 25.2 %collective-permute-start.13 = (bf16[512,1024]{1,0:T(8,128)(2,1)}, bf16[512,1024]{1,0:T(8,128)(2,1)}, u32[]{:S(2)}, u32[]{:S(2)}) collective-permute-start(bf16[512,1024]{1,0:T(8,128)(2,1)} %collective-permute-done.12.refs_3_), channel_id=1, source_target_pairs={{1,0},{2,1},{5,4},{6,5},{9,8},{10,9},{13,12},{14,13},{17,16},{18,1... | collective-permute-start | bytes 3145736 | tf_op jit(solution)/shard_map/ppermute | solution.py:547
  53.1 6.6 %copy-start.22 = (s32[4]{0:T(128)S(1)}, s32[4]{0:T(128)}, u32[]{:S(2)}) copy-start(s32[4]{0:T(128)} %constant.89.clone) | copy-start | bytes 52
  53.1 6.6 %copy-start = (s32[4]{0:T(128)S(1)}, s32[4]{0:T(128)}, u32[]{:S(2)}) copy-start(s32[4]{0:T(128)} %constant.88.clone) | copy-start | bytes 52
  53.2 7.8 %copy-start.3 = (bf16[512,1024]{1,0:T(8,128)(2,1)S(1)}, bf16[512,1024]{1,0:T(8,128)(2,1)}, u32[]{:S(2)}) copy-start(bf16[512,1024]{1,0:T(8,128)(2,1)} %get-tuple-element.34.attn_ref) | copy-start | bytes 3145732
  58.1 19.5 %collective-permute-start.4 = (bf16[512,1024]{1,0:T(8,128)(2,1)}, bf16[512,1024]{1,0:T(8,128)(2,1)}, u32[]{:S(2)}, u32[]{:S(2)}) collective-permute-start(bf16[512,1024]{1,0:T(8,128)(2,1)} %get-tuple-element.58), channel_id=1, source_target_pairs={{3,2},{7,6},{11,10},{15,14},{19,18},{23,22},{27,26},{31,30}} | collective-permute-start | bytes 3145736 | tf_op jit(solution)/shard_map/ppermute | solution.py:574
  62.3 23.7 %collective-permute-start.16 = (bf16[512,1024]{0,1:T(8,128)(2,1)}, bf16[512,1024]{0,1:T(8,128)(2,1)}, u32[]{:S(2)}, u32[]{:S(2)}) collective-permute-start(bf16[512,1024]{0,1:T(8,128)(2,1)} %copy.19), channel_id=1, source_target_pairs={{0,4},{4,0},{8,12},{12,8},{16,20},{20,16},{24,28},{28,24},{1,5},{5... | collective-permute-start | bytes 3145736 | tf_op jit(solution)/shard_map/ppermute | solution.py:531
  69.6 57.4 %collective-permute-start.17 = (bf16[512,1024]{1,0:T(8,128)(2,1)}, bf16[512,1024]{1,0:T(8,128)(2,1)}, u32[]{:S(2)}, u32[]{:S(2)}) collective-permute-start(bf16[512,1024]{1,0:T(8,128)(2,1)} %get-tuple-element.42), channel_id=1, source_target_pairs={{0,4},{4,0},{8,12},{12,8},{16,20},{20,16},{24,28},{28,24},{1,5},{5... | collective-permute-start | bytes 3145736 | tf_op jit(solution)/shard_map/ppermute | solution.py:531
  70.1 19.0 %collective-permute-start.15 = (bf16[512,1024]{1,0:T(8,128)(2,1)}, bf16[512,1024]{1,0:T(8,128)(2,1)}, u32[]{:S(2)}, u32[]{:S(2)}) collective-permute-start(bf16[512,1024]{1,0:T(8,128)(2,1)} %collective-permute-done.11.refs_1_), channel_id=1, source_target_pairs={{2,3},{6,7},{10,11},{14,15},{18,19},{22,23},{26,27},{30,31}} | collective-permute-start | bytes 3145736 | tf_op jit(solution)/shard_map/ppermute | solution.py:546
  71.7 27.6 %collective-permute-start.14 = (bf16[512,1024]{1,0:T(8,128)(2,1)}, bf16[512,1024]{1,0:T(8,128)(2,1)}, u32[]{:S(2)}, u32[]{:S(2)}) collective-permute-start(bf16[512,1024]{1,0:T(8,128)(2,1)} %collective-permute-done.13.refs_2_), channel_id=1, source_target_pairs={{1,0},{5,4},{9,8},{13,12},{17,16},{21,20},{25,24},{29,28}} | collective-permute-start | bytes 3145736 | tf_op jit(solution)/shard_map/ppermute | solution.py:547
  77.5 4.2 %copy-start.23 = (bf16[512,1024]{1,0:T(8,128)(2,1)S(1)}, bf16[512,1024]{1,0:T(8,128)(2,1)}, u32[]{:S(2)}) copy-start(bf16[512,1024]{1,0:T(8,128)(2,1)} %get-tuple-element.35) | copy-start | bytes 3145732
  80.2 28.7 %collective-permute-start.5 = (bf16[512,1024]{1,0:T(8,128)(2,1)}, bf16[512,1024]{1,0:T(8,128)(2,1)}, u32[]{:S(2)}, u32[]{:S(2)}) collective-permute-start(bf16[512,1024]{1,0:T(8,128)(2,1)} %add_convert_fusion.4), channel_id=1, source_target_pairs={{2,1},{3,2},{6,5},{7,6},{10,9},{11,10},{14,13},{15,14},{18,17},{19... | collective-permute-start | bytes 3145736 | tf_op jit(solution)/shard_map/ppermute | solution.py:574
  103.9 23.0 %collective-permute-start.18 = (bf16[512,1024]{1,0:T(8,128)(2,1)}, bf16[512,1024]{1,0:T(8,128)(2,1)S(1)}, u32[]{:S(2)}, u32[]{:S(2)}) collective-permute-start(bf16[512,1024]{1,0:T(8,128)(2,1)} %get-tuple-element.43), channel_id=1, source_target_pairs={{0,4},{4,0},{8,12},{12,8},{16,20},{20,16},{24,28},{28,24},{1,5},{5... | collective-permute-start | bytes 3145736 | tf_op jit(solution)/shard_map/ppermute | solution.py:531
  103.9 3.4 %copy-start.15 = (bf16[512,1024]{1,0:T(8,128)(2,1)S(1)}, bf16[512,1024]{1,0:T(8,128)(2,1)}, u32[]{:S(2)}) copy-start(bf16[512,1024]{1,0:T(8,128)(2,1)} %get-tuple-element.40) | copy-start | bytes 3145732
  104.0 3.4 %copy-start.16 = (bf16[512,1024]{1,0:T(8,128)(2,1)S(1)}, bf16[512,1024]{1,0:T(8,128)(2,1)}, u32[]{:S(2)}) copy-start(bf16[512,1024]{1,0:T(8,128)(2,1)} %get-tuple-element.41) | copy-start | bytes 3145732
  108.9 14.2 %copy-start.10 = (f32[512,1024]{1,0:T(8,128)S(1)}, f32[512,1024]{1,0:T(8,128)}, u32[]{:S(2)}) copy-start(f32[512,1024]{1,0:T(8,128)} %fusion.4) | copy-start | bytes 6291460
  108.9 14.2 %copy-start.11 = (f32[512,1024]{1,0:T(8,128)S(1)}, f32[512,1024]{1,0:T(8,128)}, u32[]{:S(2)}) copy-start(f32[512,1024]{1,0:T(8,128)} %fusion.12) | copy-start | bytes 6291460
  108.9 14.2 %copy-start.17 = (bf16[512,1024]{1,0:T(8,128)(2,1)S(1)}, bf16[512,1024]{1,0:T(8,128)(2,1)}, u32[]{:S(2)}) copy-start(bf16[512,1024]{1,0:T(8,128)(2,1)} %get-tuple-element.38) | copy-start | bytes 3145732
  113.5 39.7 %collective-permute-start.7 = (bf16[512,1024]{1,0:T(8,128)(2,1)}, bf16[512,1024]{1,0:T(8,128)(2,1)}, u32[]{:S(2)}, u32[]{:S(2)}) collective-permute-start(bf16[512,1024]{1,0:T(8,128)(2,1)} %get-tuple-element.57), channel_id=1, source_target_pairs={{0,1},{4,5},{8,9},{12,13},{16,17},{20,21},{24,25},{28,29}} | collective-permute-start | bytes 3145736 | tf_op jit(solution)/shard_map/ppermute | solution.py:577
  151.5 6.6 %copy-start.4 = (bf16[512,1024]{1,0:T(8,128)(2,1)S(1)}, bf16[512,1024]{1,0:T(8,128)(2,1)}, u32[]{:S(2)}) copy-start(bf16[512,1024]{1,0:T(8,128)(2,1)} %get-tuple-element.34.attn_ref) | copy-start | bytes 3145732
  151.5 41.4 %collective-permute-start.19 = (bf16[512,1024]{1,0:T(8,128)(2,1)}, bf16[512,1024]{1,0:T(8,128)(2,1)S(1)}, u32[]{:S(2)}, u32[]{:S(2)}) collective-permute-start(bf16[512,1024]{1,0:T(8,128)(2,1)} %get-tuple-element.51), channel_id=1, source_target_pairs={{0,4},{4,0},{8,12},{12,8},{16,20},{20,16},{24,28},{28,24},{1,5},{5... | collective-permute-start | bytes 3145736 | tf_op jit(solution)/shard_map/ppermute | solution.py:531
  151.6 41.6 %collective-permute-start.22 = (bf16[2,512,512]{2,1,0:T(8,128)(2,1)}, bf16[2,512,512]{2,1,0:T(8,128)(2,1)}, u32[]{:S(2)}, u32[]{:S(2)}) collective-permute-start(bf16[2,512,512]{2,1,0:T(8,128)(2,1)} %get-tuple-element.44.rest_0_), channel_id=1, source_target_pairs={{0,8},{4,12},{8,0},{12,4},{16,24},{20,28},{24,16},{28,20},{1,9},{5... | collective-permute-start | bytes 3145736 | tf_op jit(solution)/shard_map/ppermute | solution.py:531
  155.7 8.1 %copy-start.21 = (f32[8,8,128]{2,1,0:T(8,128)S(1)}, f32[8,8,128]{2,1,0:T(8,128)}, u32[]{:S(2)}) copy-start(f32[8,8,128]{2,1,0:T(8,128)} %get-tuple-element.55) | copy-start | bytes 98308
  155.7 37.2 %copy-start.19 = (bf16[256,1024]{1,0:T(8,128)(2,1)S(1)}, bf16[256,1024]{1,0:T(8,128)(2,1)}, u32[]{:S(2)}) copy-start(bf16[256,1024]{1,0:T(8,128)(2,1)} %get-tuple-element.52) | copy-start | bytes 1572868
  155.7 42.4 %collective-permute-start.8 = (bf16[512,1024]{1,0:T(8,128)(2,1)}, bf16[512,1024]{1,0:T(8,128)(2,1)}, u32[]{:S(2)}, u32[]{:S(2)}) collective-permute-start(bf16[512,1024]{1,0:T(8,128)(2,1)} %add_convert_fusion.2), channel_id=1, source_target_pairs={{0,1},{1,2},{4,5},{5,6},{8,9},{9,10},{12,13},{13,14},{16,17},{17,1... | collective-permute-start | bytes 3145736 | tf_op jit(solution)/shard_map/ppermute | solution.py:577
  162.3 30.9 %copy-start.2 = (bf16[2,512,512]{2,1,0:T(8,128)(2,1)S(1)}, bf16[2,512,512]{2,1,0:T(8,128)(2,1)}, u32[]{:S(2)}) copy-start(bf16[2,512,512]{2,1,0:T(8,128)(2,1)} %get-tuple-element.45.rest_1_) | copy-start | bytes 3145732
  162.3 43.1 %collective-permute-start.24 = (bf16[2,512,512]{2,1,0:T(8,128)(2,1)}, bf16[2,512,512]{2,1,0:T(8,128)(2,1)}, u32[]{:S(2)}, u32[]{:S(2)}) collective-permute-start(bf16[2,512,512]{2,1,0:T(8,128)(2,1)} %get-tuple-element.46.rest_2_), channel_id=1, source_target_pairs={{0,16},{4,20},{8,24},{12,28},{16,0},{20,4},{24,8},{28,12},{1,17},{... | collective-permute-start | bytes 3145736 | tf_op jit(solution)/shard_map/ppermute | solution.py:531
  191.6 38.5 %collective-permute-start.6 = (bf16[512,1024]{1,0:T(8,128)(2,1)}, bf16[512,1024]{1,0:T(8,128)(2,1)}, u32[]{:S(2)}, u32[]{:S(2)}) collective-permute-start(bf16[512,1024]{1,0:T(8,128)(2,1)} %get-tuple-element.56), channel_id=1, source_target_pairs={{1,0},{2,1},{3,2},{5,4},{6,5},{7,6},{9,8},{10,9},{11,10},{13,12},{... | collective-permute-start | bytes 3145736 | tf_op jit(solution)/shard_map/ppermute | solution.py:574
  192.9 3.6 %copy-start.6 = (bf16[512,1024]{1,0:T(8,128)(2,1)}, bf16[512,1024]{1,0:T(8,128)(2,1)S(1)}, u32[]{:S(2)}) copy-start(bf16[512,1024]{1,0:T(8,128)(2,1)S(1)} %collective-permute-done.19.near) | copy-start | bytes 3145732
  192.9 5.2 %copy-start.9 = (f32[512,1024]{1,0:T(8,128)S(1)}, f32[512,1024]{1,0:T(8,128)}, u32[]{:S(2)}) copy-start(f32[512,1024]{1,0:T(8,128)} %get-tuple-element.59) | copy-start | bytes 6291460
  194.9 14.2 %collective-permute-start.23 = (bf16[1,512,512]{2,1,0:T(8,128)(2,1)S(1)}, bf16[1,512,512]{2,1,0:T(8,128)(2,1)S(1)}, u32[]{:S(2)}, u32[]{:S(2)}) collective-permute-start(bf16[1,512,512]{2,1,0:T(8,128)(2,1)S(1)} %add_convert_fusion.7), channel_id=1, source_target_pairs={{0,16},{4,20},{8,24},{12,28},{16,0},{20,4},{24,8},{28,12},{1,17},{... | collective-permute-start | bytes 1572872 | tf_op jit(solution)/shard_map/ppermute | solution.py:531
  196.5 11.1 %collective-permute-start.20 = (bf16[192,1024]{1,0:T(8,128)(2,1)S(1)}, bf16[192,1024]{1,0:T(8,128)(2,1)S(1)}, u32[]{:S(2)}, u32[]{:S(2)}) collective-permute-start(bf16[192,1024]{1,0:T(8,128)(2,1)S(1)} %pad_maximum_fusion.5), channel_id=1, source_target_pairs={{0,8},{4,12},{8,0},{12,4},{16,24},{20,28},{24,16},{28,20},{1,9},{5... | collective-permute-start | bytes 1179656 | tf_op jit(solution)/shard_map/ppermute | solution.py:531
  198.1 7.3 %copy-start.1 = (bf16[2,512,512]{2,1,0:T(8,128)(2,1)S(1)}, bf16[2,512,512]{2,1,0:T(8,128)(2,1)}, u32[]{:S(2)}) copy-start(bf16[2,512,512]{2,1,0:T(8,128)(2,1)} %get-tuple-element.47.rest_3_) | copy-start | bytes 3145732
  200.8 29.3 %collective-permute-start.9 = (bf16[512,1024]{1,0:T(8,128)(2,1)}, bf16[512,1024]{1,0:T(8,128)(2,1)S(1)}, u32[]{:S(2)}, u32[]{:S(2)}) collective-permute-start(bf16[512,1024]{1,0:T(8,128)(2,1)} %add_convert_fusion.1), channel_id=1, source_target_pairs={{0,1},{1,2},{2,3},{4,5},{5,6},{6,7},{8,9},{9,10},{10,11},{12,13},{... | collective-permute-start | bytes 3145736 | tf_op jit(solution)/shard_map/ppermute | solution.py:577
  206.6 13.1 %collective-permute-start.25 = (bf16[1,512,512]{2,1,0:T(8,128)(2,1)S(1)}, bf16[1,512,512]{2,1,0:T(8,128)(2,1)S(1)}, u32[]{:S(2)}, u32[]{:S(2)}) collective-permute-start(bf16[1,512,512]{2,1,0:T(8,128)(2,1)S(1)} %add_convert_fusion.5), channel_id=1, source_target_pairs={{0,8},{4,12},{8,0},{12,4},{16,24},{20,28},{24,16},{28,20},{1,9},{5... | collective-permute-start | bytes 1572872 | tf_op jit(solution)/shard_map/ppermute | solution.py:531
  207.7 13.3 %copy-start.18 = (bf16[192,1024]{1,0:T(8,128)(2,1)}, bf16[192,1024]{1,0:T(8,128)(2,1)S(1)}, u32[]{:S(2)}) copy-start(bf16[192,1024]{1,0:T(8,128)(2,1)S(1)} %collective-permute-done.20.three) | copy-start | bytes 1179652
  207.7 14.7 %collective-permute-start.21 = (bf16[64,1024]{1,0:T(8,128)(2,1)S(1)}, bf16[64,1024]{1,0:T(8,128)(2,1)S(1)}, u32[]{:S(2)}, u32[]{:S(2)}) collective-permute-start(bf16[64,1024]{1,0:T(8,128)(2,1)S(1)} %add_convert_fusion.10), channel_id=1, source_target_pairs={{0,16},{4,20},{8,24},{12,28},{16,0},{20,4},{24,8},{28,12},{1,17},{... | collective-permute-start | bytes 393224 | tf_op jit(solution)/shard_map/ppermute | solution.py:531
  223.1 7.0 %copy-start.8 = (f32[512,1024]{1,0:T(8,128)S(1)}, f32[512,1024]{1,0:T(8,128)}, u32[]{:S(2)}) copy-start(f32[512,1024]{1,0:T(8,128)} %fusion.14) | copy-start | bytes 6291460
  (2 other events, 1.6 us)

commit v2 on v1

--- a/solution.py
+++ b/solution.py
@@ -36,42 +36,62 @@
     return jnp.where(lax.shift_right_logical(token, level) == row, 0.5**level, 0.0).astype(BF16)
 
 
-def pooled(level, tensor):
-    tokens = tensor.shape[0]
-    return dot_nn(pool_matrix(level, tokens >> level, tokens), tensor).astype(BF16)
-
-
-def pool_kernel(k_ref, v_ref, two_ref, three_ref, four_ref):
-    k = k_ref[...]
-    v = v_ref[...]
-    for level, out in ((2, two_ref), (3, three_ref), (4, four_ref)):
-        rows = k.shape[0] >> level
-        out[pl.ds(0, rows), :] = pooled(level, k)
-        out[pl.ds(rows, rows), :] = pooled(level, v)
-
-
-def pool_call(key, value):
-    tokens, width = key.shape
-    step = 256
-    spec = pl.BlockSpec((tokens, step), lambda i: (0, i))
-    rows = [2 * (tokens >> level) for level in (2, 3, 4)]
-    return pl.pallas_call(
-        pool_kernel,
-        grid=(width // step,),
-        in_specs=[spec, spec],
-        out_specs=[pl.BlockSpec((r, step), lambda i: (0, i)) for r in rows],
-        out_shape=[jax.ShapeDtypeStruct((r, width), BF16) for r in rows],
-        compiler_params=pltpu.CompilerParams(vmem_limit_bytes=VMEM_LIMIT),
-        name="pool_keys",
-    )(key, value)
-
-
 def fill_pool(pool, tokens):
     base = 0
     for level in range(1, LEVELS):
         rows = tokens >> level
         pool[pl.ds(base, rows), :] = pool_matrix(level, rows, tokens)
         base += rows
+
+
+def pool_kernel(k_ref, v_ref, near_ref, three_ref, four_ref):
+    tokens = k_ref.shape[0]
+    matrix = jnp.concatenate([pool_matrix(l, tokens >> l, tokens) for l in (2, 3, 4)], 0)
+    for part, ref in enumerate((k_ref, v_ref)):
+        rows = dot_nn(matrix, ref[...]).astype(BF16)
+        base = 0
+        for level, out in ((2, near_ref), (3, three_ref), (4, four_ref)):
+            size = tokens >> level
+            out[pl.ds(part * size, size), :] = rows[base : base + size]
+            base += size
+
+
+def pool_call(key, value):
+    tokens, width = key.shape
+    step = min(512, width)
+    spec = pl.BlockSpec((tokens, step), lambda i: (0, i))
+    rows = [2 * (tokens >> level) for level in (2, 3, 4)]
+    return pl.pallas_call(
+        pool_kernel,
+        grid=(width // step,),
+        in_specs=[spec, spec],
+        out_specs=[pl.BlockSpec((r, step), lambda i: (0, i)) for r in rows],
+        out_shape=[jax.ShapeDtypeStruct((r, width), BF16) for r in (tokens, *rows[1:])],
+        compiler_params=pltpu.CompilerParams(vmem_limit_bytes=VMEM_LIMIT),
+        name="pool_keys",
+    )(key, value)
+
+
+def lower_kernel(near_in, three_ref, four_a, four_b, near_out):
+    base = 0
+    for ref in (three_ref, four_a, four_b):
+        near_out[pl.ds(base, ref.shape[0]), :] = ref[...]
+        base += ref.shape[0]
+
+
+def lower_call(near, three, four_a, four_b):
+    tokens, width = near.shape
+    spec = lambda r: pl.BlockSpec((r.shape[0], width), lambda i: (0, 0))
+    return pl.pallas_call(
+        lower_kernel,
+        grid=(1,),
+        in_specs=[pl.BlockSpec(memory_space=pl.ANY), spec(three), spec(four_a), spec(four_b)],
+        out_specs=pl.BlockSpec((tokens // 2, width), lambda i: (1, 0)),
+        out_shape=jax.ShapeDtypeStruct((tokens, width), BF16),
+        input_output_aliases={0: 0},
+        compiler_params=pltpu.CompilerParams(vmem_limit_bytes=VMEM_LIMIT),
+        name="lower_rows",
+    )(near, three, four_a, four_b)
 
 
 def expand_two(scratch, base, value):
@@ -112,7 +132,7 @@
 def forward_kernel(
     q_ref, k_ref, v_ref, near, three, four_a, four_b, *rest, extra
 ):
-    attn_ref, lse_ref, top_ref, pool, peak_s, total_s, summed_s = rest[extra:]
+    attn_ref, turned_ref, lse_ref, top_ref, pool, peak_s, total_s, summed_s = rest[extra:]
     tokens, width = q_ref.shape
 
     @pl.when(pl.program_id(0) == 0)
@@ -185,12 +205,14 @@
             base += rows
     for h in heads:
         peak, total, summed = state[h]
-        attn_ref[:, columns[h]] = (summed / total).astype(BF16)
+        attn = (summed / total).astype(BF16)
+        attn_ref[:, columns[h]] = attn
+        turned_ref[columns[h], :] = attn.T
         lse_ref[:, columns[h]] = peak + jnp.log(total)
         top_ref[h] = tiles[h]
 
 
-def forward_call(query, key, value, received, after=(), step=2):
+def forward_call(query, key, value, received, after=(), step=4):
     tokens, width = query.shape
     heads = width // DH
     spec = pl.BlockSpec((tokens, step * DH), lambda h: (0, h))
@@ -200,9 +222,15 @@
         functools.partial(forward_kernel, extra=len(after)),
         grid=(heads // step,),
         in_specs=[spec, spec, spec] + others,
-        out_specs=[spec, spec, pl.BlockSpec((step, 8, 128), lambda h: (h, 0, 0))],
+        out_specs=[
+            spec,
+            pl.BlockSpec((step * DH, tokens), lambda h: (h, 0)),
+            spec,
+            pl.BlockSpec((step, 8, 128), lambda h: (h, 0, 0)),
+        ],
         out_shape=[
             jax.ShapeDtypeStruct((tokens, width), BF16),
+            jax.ShapeDtypeStruct((width, tokens), BF16),
             jax.ShapeDtypeStruct((tokens, width), F32),
             jax.ShapeDtypeStruct((heads, 8, 128), F32),
         ],
@@ -220,7 +248,7 @@
 def backward_kernel(
     q_ref, k_ref, v_ref, attn_ref, grad_ref, lse_ref, near, three, four_a, four_b, *rest, extra
 ):
-    gq_ref, gk_ref, gv_ref, far, keep, pool, lse_s, grad_s, scal_s, gq_s, gk_s, gv_s = rest[extra:]
+    gq_ref, gk_ref, gv_ref, far, keep, four, pool, lse_s, grad_s, scal_s, gq_s, gk_s, gv_s = rest[extra:]
     tokens, width = q_ref.shape
 
     @pl.when(pl.program_id(0) == 0)
@@ -319,7 +347,7 @@
                 outs = {
                     2: ((far, 0),),
                     3: ((keep, 0), (far, 2 * BLK)),
-                    4: ((keep, BLK), (keep, BLK + BLK // 2), (far, 3 * BLK), (far, 3 * BLK + BLK // 2)),
+                    4: ((four, 0), (keep, BLK), (far, 3 * BLK + BLK // 2), (far, 3 * BLK)),
                 }[level]
                 piece = BLK // len(outs)
                 for i, (out, at) in enumerate(outs):
@@ -352,14 +380,15 @@
     others = [pl.BlockSpec((r.shape[0], step * DH), lambda h: (0, h)) for r in received]
     others += [pl.BlockSpec(memory_space=pl.ANY)] * len(after)
     full = jax.ShapeDtypeStruct((tokens, width), F32)
-    outs = [spec, pl.BlockSpec((tokens // 2, step * DH), lambda h: (0, h))]
+    back_rows = (tokens, BLK + BLK // 2, BLK // 2)
+    outs = [pl.BlockSpec((r, step * DH), lambda h: (0, h)) for r in back_rows]
     return pl.pallas_call(
         functools.partial(backward_kernel, extra=len(after)),
         grid=(heads // step,),
         in_specs=[spec] * 6 + others,
         out_specs=[spec] * 3 + outs,
         out_shape=[full] * 3
-        + [jax.ShapeDtypeStruct((tokens, width), BF16), jax.ShapeDtypeStruct((tokens // 2, width), BF16)],
+        + [jax.ShapeDtypeStruct((r, width), BF16) for r in back_rows],
         scratch_shapes=[pltpu.VMEM((tokens - tokens // 16, tokens), BF16)]
         + [pltpu.VMEM((step * 2 * tokens, 128), F32)] * 6,
         compiler_params=pltpu.CompilerParams(vmem_limit_bytes=VMEM_LIMIT),
@@ -368,26 +397,33 @@
 
 
 def finish_kernel(gk_ref, gv_ref, near, three, four, ok_ref, ov_ref, k_s, v_s):
-    for part, local, out, scr in ((0, gk_ref, ok_ref, k_s), (1, gv_ref, ov_ref, v_s)):
-        state = None
-        base = 0
-        for ref, rows in ((four, BLK // 4), (three, BLK // 2), (near, BLK)):
-            total = ref[pl.ds(part * rows, rows), :].astype(F32)
-            state = total if state is None else total + state
-            state = expand_two(scr, base, state * 0.5)
-            base += 2 * rows
-        state = expand_two(scr, base, state * 0.5)
-        out[...] = local[...] + state
+    heads = range(gk_ref.shape[1] // DH)
+    tokens = gk_ref.shape[0]
+    state = {}
+    base = 0
+    for ref, rows in ((four, BLK // 4), (three, BLK // 2), (near, BLK), (None, 2 * BLK)):
+        for h in heads:
+            for part, scr in ((0, k_s), (1, v_s)):
+                total = state.get((h, part))
+                if ref is not None:
+                    own = ref[pl.ds(part * rows, rows), pl.ds(h * DH, DH)].astype(F32)
+                    total = own if total is None else total + own
+                state[h, part] = expand_two(scr, h * 2 * tokens + base, total * 0.5)
+        base += 2 * rows
+    for h in heads:
+        here = pl.ds(h * DH, DH)
+        ok_ref[:, here] = gk_ref[:, here] + state[h, 0]
+        ov_ref[:, here] = gv_ref[:, here] + state[h, 1]
 
 
 def finish_call(grad_k, grad_v, near, three, four):
     tokens, width = grad_k.shape
-    step = 128
+    step = 2 * DH
     spec = pl.BlockSpec((tokens, step), lambda h: (0, h))
     rows = (2 * BLK, BLK, BLK // 2)
     extra = [pl.BlockSpec((r, step), lambda h: (0, h)) for r in rows]
     full = jax.ShapeDtypeStruct((tokens, width), F32)
-    scratch = pltpu.VMEM((2 * tokens, step), F32)
+    scratch = pltpu.VMEM((2 * 2 * tokens, DH), F32)
     return pl.pallas_call(
         finish_kernel,
         grid=(width // step,),
@@ -400,19 +436,18 @@
     )(grad_k, grad_v, near, three, four)
 
 
-def assemble_kernel(core_ref, *refs, pairs, column):
-    count = len(pairs)
+def chunk_of(refs, number):
+    return refs[0][...] if number == 1 else refs[0][...] + refs[1][...]
+
+
+def split_kernel(core_ref, *refs, pairs, column, extra):
     sources = refs[: sum(pairs)]
-    outs = refs[sum(pairs) :]
-    whole, mine_ref, send_ref = outs[:count], outs[count], outs[count + 1]
+    mine_ref, send_ref = refs[sum(pairs) + extra :]
     first = core_ref[0] == 0
     at = 0
     for index, number in enumerate(pairs):
-        chunk = sources[at][...]
-        if number == 2:
-            chunk = chunk + sources[at + 1][...]
+        chunk = chunk_of(sources[at:], number)
         at += number
-        whole[index][...] = chunk
         width = chunk.shape[1]
         for group in range(width // (2 * column)):
             low = chunk[:, 2 * group * column : (2 * group + 1) * column]
@@ -422,24 +457,131 @@
             send_ref[:, here] = jnp.where(first, high, low)
 
 
-def assemble_call(chunks, core, column):
+def split_call(chunks, core, column, after=()):
     flat = [array for chunk in chunks for array in chunk]
     tokens, width = flat[0].shape
     count = len(chunks)
-    rows = 128
+    rows = 256
     spec = pl.BlockSpec((rows, width), lambda i: (i, 0))
     half = pl.BlockSpec((rows, count * width // 2), lambda i: (i, 0))
-    outs = pl.pallas_call(
-        functools.partial(assemble_kernel, pairs=tuple(len(c) for c in chunks), column=column),
+    return pl.pallas_call(
+        functools.partial(
+            split_kernel, pairs=tuple(len(c) for c in chunks), column=column, extra=len(after)
+        ),
         grid=(tokens // rows,),
-        in_specs=[pl.BlockSpec(memory_space=pltpu.SMEM)] + [spec] * len(flat),
-        out_specs=[spec] * count + [half, half],
-        out_shape=[jax.ShapeDtypeStruct((tokens, width), BF16)] * count
-        + [jax.ShapeDtypeStruct((tokens, count * width // 2), BF16)] * 2,
-        compiler_params=pltpu.CompilerParams(vmem_limit_bytes=VMEM_LIMIT),
-        name="assemble",
-    )(core.reshape(1).astype(jnp.int32), *flat)
-    return outs[:count], outs[count], outs[count + 1]
+        in_specs=[pl.BlockSpec(memory_space=pltpu.SMEM)]
+        + [spec] * len(flat)
+        + [pl.BlockSpec(memory_space=pl.ANY)] * len(after),
+        out_specs=[half, half],
+        out_shape=[jax.ShapeDtypeStruct((tokens, count * width // 2), BF16)] * 2,
+        compiler_params=pltpu.CompilerParams(vmem_limit_bytes=VMEM_LIMIT),
+        name="split_columns",
+    )(core.reshape(1).astype(jnp.int32), *flat, *after)
+
+
+def grad_kernel(place_ref, *refs, pairs, has_sum):
+    total = sum(pairs)
+    count = len(pairs)
+    sources = refs[:total]
+    weights = refs[total : total + count]
+    out = refs[-1]
+    result = refs[total + count][...] if has_sum else None
+    at = 0
+    for index, number in enumerate(pairs):
+        part = dot_nt(chunk_of(sources[at:], number), weights[index][...])
+        result = part if result is None else result + part
+        at += number
+    out[...] = result.astype(out.dtype)
+
+
+def grad_call(chunks, out_weight, place, partial_sum, dtype):
+    flat = [array for chunk in chunks for array in chunk]
+    tokens, width = flat[0].shape
+    features = out_weight.shape[0]
+    step = 256
+    chunk_spec = pl.BlockSpec((tokens, width), lambda i, p: (0, 0))
+    out_spec = pl.BlockSpec((tokens, step), lambda i, p: (0, i))
+    weight_specs = [
+        pl.BlockSpec((step, width), lambda i, p, n=n: (i, p[n])) for n in range(len(chunks))
+    ]
+    sums = () if partial_sum is None else (partial_sum,)
+    return pl.pallas_call(
+        functools.partial(
+            grad_kernel, pairs=tuple(len(c) for c in chunks), has_sum=partial_sum is not None
+        ),
+        grid_spec=pltpu.PrefetchScalarGridSpec(
+            num_scalar_prefetch=1,
+            grid=(features // step,),
+            in_specs=[chunk_spec] * len(flat) + weight_specs + [out_spec] * len(sums),
+            out_specs=out_spec,
+        ),
+        out_shape=jax.ShapeDtypeStruct((tokens, features), dtype),
+        compiler_params=pltpu.CompilerParams(vmem_limit_bytes=VMEM_LIMIT),
+        name="grad_products",
+    )(place.astype(jnp.int32), *flat, *[out_weight] * len(chunks), *sums)
+
+
+def project_kernel(place_ref, attn_ref, left_w, right_w, *refs, has_sum):
+    left_out, right_out = refs[-2:]
+    left = dot_nn(attn_ref[...], left_w[...])
+    right = dot_nn(attn_ref[...], right_w[...])
+    if has_sum:
+        left = left + refs[0][...].astype(F32)
+        right = right + refs[1][...].astype(F32)
+    left_out[...] = left.astype(BF16)
+    right_out[...] = right.astype(BF16)
+
+
+def project_call(attn, out_weight, place, sums):
+    tokens, width = attn.shape
+    features = out_weight.shape[0]
+    step = 256
+    per = width // step
+    spec = pl.BlockSpec((tokens, step), lambda i, p: (0, i))
+    return pl.pallas_call(
+        functools.partial(project_kernel, has_sum=bool(sums)),
+        grid_spec=pltpu.PrefetchScalarGridSpec(
+            num_scalar_prefetch=1,
+            grid=(per,),
+            in_specs=[pl.BlockSpec((tokens, width), lambda i, p: (0, 0))]
+            + [pl.BlockSpec((features, step), lambda i, p, n=n: (0, p[n] * per + i)) for n in (0, 1)]
+            + [spec] * len(sums),
+            out_specs=[spec, spec],
+        ),
+        out_shape=[jax.ShapeDtypeStruct((tokens, width), BF16)] * 2,
+        compiler_params=pltpu.CompilerParams(vmem_limit_bytes=VMEM_LIMIT),
+        name="mixed_products",
+    )(place.astype(jnp.int32), attn, out_weight, out_weight, *sums)
+
+
+def mixed_kernel(place_ref, attn_ref, weight_ref, left_ref, right_ref, out_ref):
+    total = left_ref[...].astype(F32) + right_ref[...].astype(F32)
+    out_ref[...] = dot_nn(attn_ref[...], weight_ref[...]) + total
+
+
+def mixed_call(attn, out_weight, place, left, right):
+    tokens, width = attn.shape
+    features = out_weight.shape[0]
+    step = 256
+    per = width // step
+    spec = pl.BlockSpec((tokens, step), lambda i, p: (0, i))
+    return pl.pallas_call(
+        mixed_kernel,
+        grid_spec=pltpu.PrefetchScalarGridSpec(
+            num_scalar_prefetch=1,
+            grid=(per,),
+            in_specs=[
+                pl.BlockSpec((tokens, width), lambda i, p: (0, 0)),
+                pl.BlockSpec((features, step), lambda i, p: (0, p[0] * per + i)),
+                spec,
+                spec,
+            ],
+            out_specs=spec,
+        ),
+        out_shape=jax.ShapeDtypeStruct((tokens, width), F32),
+        compiler_params=pltpu.CompilerParams(vmem_limit_bytes=VMEM_LIMIT),
+        name="mixed_last",
+    )(place.astype(jnp.int32), attn, out_weight, left, right)
 
 
 def term_order(chips):
@@ -450,45 +592,53 @@
     return [i for key in ((1, 0), (1, 1), (0, 1), (0, 0)) for i in groups[key]]
 
 
-def term_kernel(place_ref, turned_ref, mine_ref, theirs_ref, a_send, a_keep, b_send, b_keep, *, chips):
+def term_kernel(
+    place_ref, own_ref, other_ref, mine_a, theirs_a, mine_b, theirs_b,
+    a_send, a_keep, b_send, b_keep, turned, both, *, chips, first,
+):
     step = pl.program_id(0)
-    tokens = mine_ref.shape[0]
-    half = turned_ref.shape[0] // 2
-
-    def rows(start):
-        here = pl.ds(start, half)
-        return dot_nn(turned_ref[here, pl.ds(0, tokens)], mine_ref[...]) + dot_nn(
-            turned_ref[here, pl.ds(tokens, tokens)], theirs_ref[...]
-        )
-
-    top = rows(0).astype(BF16)
-    bottom = rows(half).astype(BF16)
-
-    @pl.when(step < chips // 2)
+    features, tokens = own_ref.shape
+
+    @pl.when(step == 0)
     def _():
-        a_send[0] = top
-
-    @pl.when(step >= chips // 2)
+        turned[:, pl.ds(0, tokens)] = own_ref[...]
+        turned[:, pl.ds(tokens, tokens)] = other_ref[...]
+
+    is_first = place_ref[step] < first
+
+    @pl.when(is_first)
     def _():
-        a_keep[0] = top
-
-    middle = jnp.logical_and(step >= chips // 4, step < 3 * chips // 4)
-
-    @pl.when(middle)
+        both[pl.ds(0, tokens), :] = mine_a[...]
+        both[pl.ds(tokens, tokens), :] = theirs_a[...]
+
+    @pl.when(jnp.logical_not(is_first))
     def _():
-        b_send[0] = bottom
-
-    @pl.when(jnp.logical_not(middle))
-    def _():
-        b_keep[0] = bottom
-
-
-def term_call(turned, mine, theirs, place, column):
-    features = turned.shape[0]
-    tokens = mine.shape[0]
+        both[pl.ds(0, tokens), :] = mine_b[...]
+        both[pl.ds(tokens, tokens), :] = theirs_b[...]
+
+    half = features // 2
+    in_a = step < chips // 2
+    in_b = jnp.logical_and(step >= chips // 4, step < 3 * chips // 4)
+    for start, flag, send, keep in ((0, in_a, a_send, a_keep), (half, in_b, b_send, b_keep)):
+        rows = dot_nn(turned[pl.ds(start, half), :], both[...]).astype(BF16)
+
+        @pl.when(flag)
+        def _():
+            send[0] = rows
+
+        @pl.when(jnp.logical_not(flag))
+        def _():
+            keep[0] = rows
+
+
+def term_call(own, other, early, late, place, column):
+    features, tokens = own.shape
     chips = place.shape[0]
     half, quarter = chips // 2, chips // 4
-    source = pl.BlockSpec((tokens, column), lambda i, p: (0, p[i]))
+    first = early[0].shape[1] // column
+    whole = pl.BlockSpec((features, tokens), lambda i, p: (0, 0))
+    spec_a = pl.BlockSpec((tokens, column), lambda i, p: (0, jnp.minimum(p[i], first - 1)))
+    spec_b = pl.BlockSpec((tokens, column), lambda i, p: (0, jnp.maximum(p[i] - first, 0)))
     shape = (1, features // 2, column)
     outs = [
         pl.BlockSpec(shape, lambda i, p: (jnp.minimum(i, half - 1), 0, 0)),
@@ -500,31 +650,55 @@
         ),
     ]
     return pl.pallas_call(
-        functools.partial(term_kernel, chips=chips),
+        functools.partial(term_kernel, chips=chips, first=first),
         grid_spec=pltpu.PrefetchScalarGridSpec(
             num_scalar_prefetch=1,
             grid=(chips,),
-            in_specs=[pl.BlockSpec((features, 2 * tokens), lambda i, p: (0, 0)), source, source],
+            in_specs=[whole, whole, spec_a, spec_a, spec_b, spec_b],
             out_specs=outs,
+            scratch_shapes=[
+                pltpu.VMEM((features, 2 * tokens), BF16),
+                pltpu.VMEM((2 * tokens, column), BF16),
+            ],
         ),
         out_shape=[jax.ShapeDtypeStruct((half, features // 2, column), BF16)] * 4,
         compiler_params=pltpu.CompilerParams(vmem_limit_bytes=VMEM_LIMIT),
         name="weight_terms",
-    )(place, turned, mine, theirs)
-
-
-def halve(sent, kept, bits, mask_of):
+    )(place, own, other, *early, *late)
+
+
+def total_kernel(top_a, top_b, bottom_a, bottom_b, out):
+    half = top_a.shape[0]
+    out[pl.ds(0, half), :] = top_a[...].astype(F32) + top_b[...].astype(F32)
+    out[pl.ds(half, half), :] = bottom_a[...].astype(F32) + bottom_b[...].astype(F32)
+
+
+def total_call(top, bottom):
+    rows, column = top[0].shape
+    return pl.pallas_call(
+        total_kernel,
+        out_shape=jax.ShapeDtypeStruct((2 * rows, column), F32),
+        compiler_params=pltpu.CompilerParams(vmem_limit_bytes=VMEM_LIMIT),
+        name="weight_total",
+    )(*top, *bottom)
+
+
+def halve(sent, kept, bits):
     for n, bit in enumerate(bits):
-        arrived = swap(sent[1], "ctx", mask_of(bit))
+        arrived = swap(sent[1], "ctx", 2 * bit)
         names = [i ^ bit for i in sent[0]]
-        parts = {}
-        for k, i in enumerate(kept[0]):
-            parts[i] = kept[1][k].astype(F32) + arrived[names.index(i)].astype(F32)
         if n + 1 == len(bits):
-            return parts[0]
-        cut = lambda flag: [i for i in kept[0] if (i & bits[n + 1] != 0) == flag]
-        pack = lambda names: (names, jnp.stack([parts[i].astype(BF16) for i in names]))
-        sent, kept = pack(cut(True)), pack(cut(False))
+            return kept[1][0], arrived[0]
+
+        def added(flag):
+            here = [i for i in kept[0] if (i & bits[n + 1] != 0) == flag]
+            parts = [
+                kept[1][kept[0].index(i)].astype(F32) + arrived[names.index(i)].astype(F32)
+                for i in here
+            ]
+            return here, jnp.stack([p.astype(BF16) for p in parts])
+
+        sent, kept = added(True), added(False)
 
 
 def swap(value, axis, mask):
@@ -548,49 +722,40 @@
         from_left.append(right)
         from_right.append(left)
 
-    two, three, four = pool_call(key, value)
+    near, three, four = pool_call(key, value)
     three = swap(three, "ctx", 2)
     four_a = swap(four, "ctx", 4)
     four_b = swap(four, "ctx", 6)
-    near = swap(jnp.concatenate([two, three, four_a, four_b], 0), "ctx", 1)
+    near = swap(lower_call(near, three, four_a, four_b), "ctx", 1)
     received = (near, three, four_a, four_b)
 
-    weights = [
-        lax.dynamic_slice(
-            out_weight, (0, lax.rem(z - s + count, count) * width), (out_weight.shape[0], width)
-        )
-        for s in range(count)
-    ]
-
-    attn, lse, tops = forward_call(query, key, value, received)
-    level_max = jnp.max(lax.all_gather(jnp.transpose(tops[:, :LEVELS, 0]), "ctx"), axis=0)
-    attn_other = swap(attn, "ctx", 1)
-    turned = jnp.concatenate([attn.T, attn_other.T], 1)
-
-    to_left = to_right = None
+    attn, turned, lse, tops = forward_call(query, key, value, received)
+    turned_other = swap(turned, "ctx", 1)
+
+    def chunk(*distances):
+        return jnp.stack([lax.rem(z + d + count, count) for d in distances])
+
+    sums = ()
+    summed = []
     for step in range(1, count):
-        piece = dot_nn(attn, weights[count - step])
-        to_left = (piece if to_left is None else piece + to_left).astype(BF16)
-        to_left = lax.ppermute(to_left, "head", [(i, i - 1) for i in range(count - step, count)])
-        piece = dot_nn(attn, weights[step])
-        to_right = (piece if to_right is None else piece + to_right).astype(BF16)
-        to_right = lax.ppermute(to_right, "head", [(i, i + 1) for i in range(0, step)])
-    mixed = dot_nn(attn, weights[0]) + to_left + to_right
+        left, right = project_call(attn, out_weight, chunk(step, -step), sums)
+        left = lax.ppermute(left, "head", [(i, i - 1) for i in range(count - step, count)])
+        right = lax.ppermute(right, "head", [(i, i + 1) for i in range(0, step)])
+        sums = (left, right)
+        summed.append(sums)
+    mixed = mixed_call(attn, out_weight, chunk(0), *sums)
 
     core = me % 2
     early = [s for s in range(count) if s not in (1, count - 1)]
     late = sorted({1, count - 1})
     grad_attn = None
-    mine, theirs = [], []
+    columns = []
     for group in (early, late):
         chunks = [(cotangent,) if s == 0 else (from_left[s], from_right[count - s]) for s in group]
-        whole, here, send = assemble_call(chunks, core, column)
-        mine.append(here)
-        theirs.append(swap(send, "ctx", 1))
-        for s, chunk in zip(group, whole):
-            part = dot_nt(chunk, weights[s])
-            grad_attn = part if grad_attn is None else grad_attn + part
-    grad_attn = grad_attn.astype(BF16)
+        mine, send = split_call(chunks, core, column, after=() if group is early else summed[0])
+        columns.append((mine, swap(send, "ctx", 1)))
+        dtype = F32 if group is early else BF16
+        grad_attn = grad_call(chunks, out_weight, chunk(*[-s for s in group]), grad_attn, dtype)
 
     chips = ctx_count // 2
     per_chunk = chips // count
@@ -599,31 +764,31 @@
     order = term_order(chips)
     chip = jnp.bitwise_xor(me // 2, jnp.array(order, jnp.int32))
     place = slot[lax.rem(z - chip // per_chunk + count, count)] * per_chunk + chip % per_chunk
-    terms = term_call(
-        turned, jnp.concatenate(mine, 1), jnp.concatenate(theirs, 1), place.astype(jnp.int32), column
-    )
+    terms = term_call(turned, turned_other, *columns, place.astype(jnp.int32), column)
     half, quarter = chips // 2, chips // 4
     bits = [1 << n for n in range(chips.bit_length() - 1)]
-    mask_of = lambda bit: 2 * bit
-    top_rows = halve((order[:half], terms[0]), (order[half:], terms[1]), bits, mask_of)
-    bottom_rows = halve(
+    top = halve((order[:half], terms[0]), (order[half:], terms[1]), bits)
+    bottom = halve(
         (order[quarter : 3 * quarter], terms[2]),
         (order[:quarter] + order[3 * quarter :], terms[3]),
         bits[::-1],
-        mask_of,
     )
-    weight_grad = jnp.concatenate([top_rows, bottom_rows], 0)
+    weight_grad = total_call(top, bottom)
 
     outs = backward_call(query, key, value, attn, grad_attn, lse, received, after=terms)
-    grad_q, grad_k, grad_v, far, keep = outs
+    grad_q, grad_k, grad_v, far, keep, four = outs
     far = swap(far, "ctx", 1)
-    half = tokens // 2
-    keep = (keep.astype(F32) + far[half:].astype(F32)).astype(BF16)
     third = BLK + BLK // 2
-    sent = jnp.concatenate([keep[:BLK], keep[third:]], 0)
-    back = swap(sent, "ctx", 2)
-    back_four = swap((keep[BLK:third].astype(F32) + back[BLK:].astype(F32)).astype(BF16), "ctx", 4)
-    grad_k, grad_v = finish_call(grad_k, grad_v, far, back, back_four)
+    back = swap((keep.astype(F32) + far[2 * BLK : 2 * BLK + third]).astype(BF16), "ctx", 2)
+    four = four.astype(F32) + far[2 * BLK + third :] + back[BLK:]
+    four = swap(four.astype(BF16), "ctx", 4)
+    grad_k, grad_v = finish_call(grad_k, grad_v, far, back, four)
+
+    level_max = jnp.transpose(tops[:, :LEVELS, 0])
+    mask = 1
+    while mask < ctx_count:
+        level_max = jnp.maximum(level_max, swap(level_max, "ctx", mask))
+        mask *= 2
     return mixed, grad_q, grad_k, grad_v, weight_grad, level_max
 
 

time: 235 us -> 204 us (0.87)
  Pallas kernels: 52.8 us -> 95.6 us
  matrix products: 32.5 us -> 0 us
  blocking collectives: 27 us -> 0 us
  other arithmetic: 28.3 us -> 8.14 us
  starting transfers between devices: 45.6 us -> 49.6 us
    pallas_call x3 -> x11, Pallas kernels: 18.8 us -> 64.6 us  [the longest x3 21.3 us: project_call(): pl.pallas_call(functools.partial(project_kernel, has_sum=bool(sums)), gri...]
    dot_general x8 -> x0, matrix products: 32.5 us -> none  [the longest x4 16.5 us: dot_nn(): lax.dot_general(a, b, (((1,), (0,)), ((), ())), preferred_element_type=F32)]
    all_gather x1 -> x0, blocking collectives: 27 us -> none  [per_device(): lax.all_gather(jnp.transpose(tops[:, :LEVELS, 0]), 'ctx')]
    ppermute x6, waiting for transfers between devices: 0.02 us -> 14.6 us  [the longest x3 14.6 us: per_device(): right = lax.ppermute(right, 'head', [(i, i + 1) for i in range(0, step)])]
    ppermute x3, waiting for transfers between devices: 14.2 us -> 0.01 us  [per_device(): lax.ppermute(right, 'head', [(i, i + 1) for i in range(step - 1, count -...]
    concatenate x6 -> x0, other arithmetic: 11.2 us -> none  [the longest x1 3.12 us: per_device(): turned = jnp.concatenate([attn.T, attn_other.T], 1)]
    ppermute x14 -> x17, waiting for transfers between devices: 13.4 us -> 20.7 us  [swap(): lax.ppermute(value, axis, [(i, i ^ mask) for i in range(lax.axis_size(axi...]
    ppermute x3, waiting for transfers between devices: 13.7 us -> 7.22 us  [per_device(): lax.ppermute(left, 'head', [(i, i - 1) for i in range(1, count - step + 1)])]
  transfers between devices with their start and end apart: 26 -> 29, of which waited for: 7 -> 9; matrix products, arithmetic and copies ran while one was open for 26% -> 5% of each run, Pallas kernels for 21% -> 45%
where the time goes in v2:
time: 204 us; the launch traced here: 203 us
  Pallas kernels  95.6 us (47%)
  starting transfers between devices  49.6 us (24%)
  waiting for transfers between devices  42.6 us (21%)
  other arithmetic  8.14 us (4%)
  local copies, waits for them, and re-layouts  6.25 us (3%)
    pallas_call x3, Pallas kernels, project_call(): pl.pallas_call(functools.partial(project_kernel, has_sum=bool(sums)), gri...  21.3 us
    ppermute x17, waiting for transfers between devices, swap(): lax.ppermute(value, axis, [(i, i ^ mask) for i in range(lax.axis_size(axi...  20.7 us
    ppermute x17, starting transfers between devices, swap(): lax.ppermute(value, axis, [(i, i ^ mask) for i in range(lax.axis_size(axi...  16.3 us
    ppermute x3, starting transfers between devices, per_device(): right = lax.ppermute(right, 'head', [(i, i + 1) for i in range(0, step)])  15.7 us
    pallas_call x2, Pallas kernels, grad_call(): pl.pallas_call(functools.partial(grad_kernel, pairs=tuple((len(c) for c i...  15.6 us
    ppermute x3, waiting for transfers between devices, per_device(): right = lax.ppermute(right, 'head', [(i, i + 1) for i in range(0, step)])  14.6 us
    pallas_call x1, Pallas kernels, backward_call(): pl.pallas_call(functools.partial(backward_kernel, extra=len(after)), grid...  12.2 us
    pallas_call x1, Pallas kernels, term_call(): pl.pallas_call(functools.partial(term_kernel, chips=chips, first=first),...  11.2 us
  transfers between devices with their start and end apart: 29, of which 9 were waited for; matrix products, arithmetic and copies ran while one was open for 5% of the time, Pallas kernels for 45%

profile of v2, /device:TPU:0, one launch (start us, length us, event | category | flops | bytes accessed | tf_op | source)
XLA Modules:
  0.0 203.1 jit_solution(16801755183919575584)
XLA Ops:
  0.6 1.3 collective-permute-start.11
  1.9 6.6 %collective-permute-start.10 = (bf16[512,1024]{1,0:T(8,128)(2,1)}, bf16[512,1024]{1,0:T(8,128)(2,1)}, u32[]{:S(2)}, u32[]{:S(2)}) collective-permute-start(bf16[512,1024]{1,0:T(8,128)(2,1)} %refs_0_.3), channel_id=1, source_target_pairs={{0,1},{1,2},{2,3},{4,5},{5,6},{6,7},{8,9},{9,10},{10,11},{12,13},{... | collective-permute-start | bytes 3145736 | tf_op jit(solution)/shard_map/ppermute | solution.py:720
  8.5 2.8 %pool_keys.1 = (bf16[512,1024]{1,0:T(8,128)(2,1)}, bf16[128,1024]{1,0:T(8,128)(2,1)}, bf16[64,1024]{1,0:T(8,128)(2,1)}) custom-call(bf16[512,1024]{1,0:T(8,128)(2,1)} %k_ref.5, bf16[512,1024]{1,0:T(8,128)(2,1)} %v_ref.5), custom_call_target="tpu_custom_call" | custom-call | tf_op jit(solution)/shard_map/pool_keys/pallas_call | solution.py:64
  11.3 1.9 collective-permute-start
  13.2 1.5 collective-permute-start.1
  14.8 3.6 %collective-permute-done.1.four_a = bf16[64,1024]{1,0:T(8,128)(2,1)S(1)} collective-permute-done((bf16[64,1024]{1,0:T(8,128)(2,1)}, bf16[64,1024]{1,0:T(8,128)(2,1)S(1)}, u32[]{:S(2)}, u32[]{:S(2)}) %collective-permute-start.1) | collective-permute-done | bytes 131104 | tf_op jit(solution)/shard_map/ppermute | solution.py:705
  18.4 4.8 %collective-permute-done.2.four_b = bf16[64,1024]{1,0:T(8,128)(2,1)S(1)} collective-permute-done((bf16[64,1024]{1,0:T(8,128)(2,1)}, bf16[64,1024]{1,0:T(8,128)(2,1)S(1)}, u32[]{:S(2)}, u32[]{:S(2)}) %collective-permute-start.2) | collective-permute-done | bytes 131104 | tf_op jit(solution)/shard_map/ppermute | solution.py:705
  23.9 1.9 lower_rows.1
  25.8 3.2 %collective-permute-done.11.refs_3_ = bf16[512,1024]{1,0:T(8,128)(2,1)} collective-permute-done((bf16[512,1024]{1,0:T(8,128)(2,1)}, bf16[512,1024]{1,0:T(8,128)(2,1)}, u32[]{:S(2)}, u32[]{:S(2)}) %collective-permute-start.11) | collective-permute-done | bytes 1048608 | tf_op jit(solution)/shard_map/ppermute | solution.py:721
  29.0 1.3 collective-permute-start.12
  30.3 1.7 collective-permute-start.14
  32.6 1.0 copy-done.6
  33.6 10.9 %attention_forward.1 = (bf16[512,1024]{1,0:T(8,128)(2,1)}, bf16[1024,512]{1,0:T(8,128)(2,1)}, f32[512,1024]{1,0:T(8,128)}, f32[8,8,128]{2,1,0:T(8,128)}) custom-call(bf16[512,1024]{1,0:T(8,128)(2,1)} %q_ref.3, bf16[512,1024]{1,0:T(8,128)(2,1)} %k_ref.5, bf16[512,1024]{1,0:T(8,128)(2,1)} %v_ref.5, bf16[512,1024]{1,0:T(8,128)(2,1)} %copy-done.6, ...), custom_call_target="tpu_custom_call" | custom-call | tf_op jit(solution)/shard_map/attention_forward/pallas_call | solution.py:221
  44.5 6.7 %mixed_products.3 = (bf16[512,1024]{1,0:T(8,128)(2,1)}, bf16[512,1024]{1,0:T(8,128)(2,1)}) custom-call(s32[2]{0:T(128)} %pad_add_fusion.2.place_ref, bf16[512,1024]{1,0:T(8,128)(2,1)} %get-tuple-element.38.attn_ref, bf16[1024,4096]{1,0:T(8,128)(2,1)} %refs_5_.1, bf16[1024,4096]{1,0:T(8,128)(2,1)} %refs_5_.1), custom_call_target="tpu_custom_call" | custom-call | tf_op jit(solution)/shard_map/mixed_products/pallas_call | solution.py:541
  52.0 7.6 %collective-permute-start.5 = (bf16[512,1024]{1,0:T(8,128)(2,1)}, bf16[512,1024]{1,0:T(8,128)(2,1)S(1)}, u32[]{:S(2)}, u32[]{:S(2)}) collective-permute-start(bf16[512,1024]{1,0:T(8,128)(2,1)} %get-tuple-element.40), channel_id=1, source_target_pairs={{0,1},{4,5},{8,9},{12,13},{16,17},{20,21},{24,25},{28,29}} | collective-permute-start | bytes 3145736 | tf_op jit(solution)/shard_map/ppermute | solution.py:743
  59.6 1.3 collective-permute-start.13
  60.9 1.7 collective-permute-start.15
  62.7 2.9 %split_columns.2 = (bf16[512,1024]{1,0:T(8,128)(2,1)}, bf16[512,1024]{1,0:T(8,128)(2,1)}) custom-call(s32[1]{0:T(128)} %bitcast.7.core_ref, bf16[512,1024]{1,0:T(8,128)(2,1)} %refs_0_.3, bf16[512,1024]{1,0:T(8,128)(2,1)} %collective-permute-done.14.refs_1_, bf16[512,1024]{1,0:T(8,128)(2,1)} %copy-done.5), custom_call_target="tpu_custom_call" | custom-call | tf_op jit(solution)/shard_map/split_columns/pallas_call | solution.py:467
  66.2 14.6 %collective-permute-done.5.refs_1_.refs_5_ = bf16[512,1024]{1,0:T(8,128)(2,1)S(1)} collective-permute-done((bf16[512,1024]{1,0:T(8,128)(2,1)}, bf16[512,1024]{1,0:T(8,128)(2,1)S(1)}, u32[]{:S(2)}, u32[]{:S(2)}) %collective-permute-start.5) | collective-permute-done | bytes 1048608 | tf_op jit(solution)/shard_map/ppermute | solution.py:743
  80.8 4.0 %collective-permute-done.13.refs_1_ = bf16[512,1024]{1,0:T(8,128)(2,1)} collective-permute-done((bf16[512,1024]{1,0:T(8,128)(2,1)S(1)}, bf16[512,1024]{1,0:T(8,128)(2,1)}, u32[]{:S(2)}, u32[]{:S(2)}) %collective-permute-start.13) | collective-permute-done | bytes 1048608 | tf_op jit(solution)/shard_map/ppermute | solution.py:721
  84.8 3.3 %split_columns.3 = (bf16[512,1024]{1,0:T(8,128)(2,1)}, bf16[512,1024]{1,0:T(8,128)(2,1)}) custom-call(s32[1]{0:T(128)} %bitcast.7.core_ref, bf16[512,1024]{1,0:T(8,128)(2,1)} %collective-permute-done.10.refs_0_, bf16[512,1024]{1,0:T(8,128)(2,1)} %collective-permute-done.13.refs_1_, bf16[512,1024]{1,0:T(8,128)(2,1)} %collective-permute-done.15.refs_2_, ...), custom_call_target="tpu_custom_call" | custom-call | tf_op jit(solution)/shard_map/split_columns/pallas_call | solution.py:467
  88.1 1.2 gather_fusion
  91.2 7.4 %grad_products.2.refs_6_ = f32[512,1024]{1,0:T(8,128)} custom-call(s32[2]{0:T(128)} %pad_add_fusion.4.place_ref, bf16[512,1024]{1,0:T(8,128)(2,1)} %refs_0_.3, bf16[512,1024]{1,0:T(8,128)(2,1)} %collective-permute-done.14.refs_1_, bf16[512,1024]{1,0:T(8,128)(2,1)} %copy-done.5, bf16[1024,4096]{1,0:T(8,128)(2,1)} %refs_5_.1, bf16[1024,4096]{1,0:T(8,128)(2,1)} %refs_5_.1), custom_call_target="tpu_custom_call" | custom-call | tf_op jit(solution)/shard_map/grad_products/pallas_call | solution.py:508
  98.6 7.3 %mixed_products.4 = (bf16[512,1024]{1,0:T(8,128)(2,1)}, bf16[512,1024]{1,0:T(8,128)(2,1)}) custom-call(s32[2]{0:T(128)} %pad_add_fusion.1.place_ref, bf16[512,1024]{1,0:T(8,128)(2,1)} %get-tuple-element.38.attn_ref, bf16[1024,4096]{1,0:T(8,128)(2,1)} %refs_5_.1, bf16[1024,4096]{1,0:T(8,128)(2,1)} %refs_5_.1, bf16[512,1024]{1,0:T(8,128)(2,1)} %copy-done.1, ...), custom_call_target="tpu_custom_call" | custom-call | tf_op jit(solution)/shard_map/mixed_products/pallas_call | solution.py:541
  105.9 1.7 collective-permute-start.6
  107.6 2.3 %collective-permute-start.7 = (bf16[512,1024]{1,0:T(8,128)(2,1)}, bf16[512,1024]{1,0:T(8,128)(2,1)}, u32[]{:S(2)}, u32[]{:S(2)}) collective-permute-start(bf16[512,1024]{1,0:T(8,128)(2,1)} %get-tuple-element.42), channel_id=1, source_target_pairs={{0,1},{1,2},{4,5},{5,6},{8,9},{9,10},{12,13},{13,14},{16,17},{17,1... | collective-permute-start | bytes 3145736 | tf_op jit(solution)/shard_map/ppermute | solution.py:743
  109.9 8.1 %grad_products.3.grad_ref = bf16[512,1024]{1,0:T(8,128)(2,1)} custom-call(s32[2]{0:T(128)} %pad_add_fusion.3.place_ref, bf16[512,1024]{1,0:T(8,128)(2,1)} %collective-permute-done.10.refs_0_, bf16[512,1024]{1,0:T(8,128)(2,1)} %collective-permute-done.13.refs_1_, bf16[512,1024]{1,0:T(8,128)(2,1)} %collective-permute-done.15.refs_2_, ...), custom_call_target="tpu_custom_call" | custom-call | tf_op jit(solution)/shard_map/grad_products/pallas_call | solution.py:508
  119.0 11.2 %weight_terms.1 = (bf16[2,512,512]{2,1,0:T(8,128)(2,1)}, bf16[2,512,512]{2,1,0:T(8,128)(2,1)}, bf16[2,512,512]{2,1,0:T(8,128)(2,1)}, bf16[2,512,512]{2,1,0:T(8,128)(2,1)}) custom-call(s32[4]{0:T(128)} %gather_fusion, bf16[1024,512]{1,0:T(8,128)(2,1)} %get-tuple-element.46.own_ref, bf16[1024,512]{1,0:T(8,128)(2,1)} %collective-permute-done.16.other_ref, ...), custom_call_target="tpu_custom_call" | custom-call | tf_op jit(solution)/shard_map/weight_terms/pallas_call | solution.py:652
  130.3 12.2 %attention_backward.1 = (f32[512,1024]{1,0:T(8,128)}, f32[512,1024]{1,0:T(8,128)}, f32[512,1024]{1,0:T(8,128)}, bf16[512,1024]{1,0:T(8,128)(2,1)}, bf16[192,1024]{1,0:T(8,128)(2,1)}, /*index=5*/bf16[64,1024]{1,0:T(8,128)(2,1)}) custom-call(bf16[512,1024]{1,0:T(8,128)(2,1)} %q_ref.3, bf16[512,1024]{1,0:T(8,128)(2,1)} %k_ref.5, bf16[512,1024]{1,0:T(8,128)(2,1)} %v_ref.5, ...), custom_call_target="tpu_custom_call" | custom-call | tf_op jit(solution)/shard_map/attention_backward/pallas_call | solution.py:385
  143.0 1.7 collective-permute-start.22
  144.7 1.2 collective-permute-done.26
  145.9 1.5 collective-permute-start.24
  148.0 1.1 collective-permute-start.27
  149.1 7.3 %mixed_products.5 = (bf16[512,1024]{1,0:T(8,128)(2,1)}, bf16[512,1024]{1,0:T(8,128)(2,1)}) custom-call(s32[2]{0:T(128)} %pad_add_fusion.place_ref, bf16[512,1024]{1,0:T(8,128)(2,1)} %get-tuple-element.38.attn_ref, bf16[1024,4096]{1,0:T(8,128)(2,1)} %refs_5_.1, bf16[1024,4096]{1,0:T(8,128)(2,1)} %refs_5_.1, bf16[512,1024]{1,0:T(8,128)(2,1)} %collective-permute-done.6.refs_0_, ...), custom_call_target="tpu_custom_call" | custom-call | tf_op jit(solution)/shard_map/mixed_products/pallas_call | solution.py:541
  156.4 1.3 collective-permute-start.8
  157.7 5.8 %collective-permute-start.9 = (bf16[512,1024]{1,0:T(8,128)(2,1)}, bf16[512,1024]{1,0:T(8,128)(2,1)}, u32[]{:S(2)}, u32[]{:S(2)}) collective-permute-start(bf16[512,1024]{1,0:T(8,128)(2,1)} %get-tuple-element.44), channel_id=1, source_target_pairs={{0,1},{1,2},{2,3},{4,5},{5,6},{6,7},{8,9},{9,10},{10,11},{12,13},{... | collective-permute-start | bytes 3145736 | tf_op jit(solution)/shard_map/ppermute | solution.py:743
  163.7 4.8 %collective-permute-done.22 = bf16[2,512,512]{2,1,0:T(8,128)(2,1)} collective-permute-done((bf16[2,512,512]{2,1,0:T(8,128)(2,1)}, bf16[2,512,512]{2,1,0:T(8,128)(2,1)}, u32[]{:S(2)}, u32[]{:S(2)}) %collective-permute-start.22) | collective-permute-done | bytes 1048608 | tf_op jit(solution)/shard_map/ppermute | solution.py:705
  168.5 1.7 collective-permute-start.20
  170.2 2.5 %add_convert_fusion.2 = (bf16[1,512,512]{2,1,0:T(8,128)(2,1)}, bf16[512,512]{1,0:T(8,128)(2,1)}) fusion(bf16[2,512,512]{2,1,0:T(8,128)(2,1)} %collective-permute-done.22, bf16[2,512,512]{2,1,0:T(8,128)(2,1)S(1)} %copy-done.4), kind=kLoop, calls=%fused_computation.3 | loop fusion | flops 2097152 | bytes 3145728 | tf_op jit(solution)/shard_map/convert_element_type | solution.py:699
  172.7 1.5 collective-permute-start.23
  174.2 2.4 %add_convert_fusion = (bf16[1,512,512]{2,1,0:T(8,128)(2,1)S(1)}, bf16[512,512]{1,0:T(8,128)(2,1)}) fusion(bf16[2,512,512]{2,1,0:T(8,128)(2,1)} %collective-permute-done.24, bf16[2,512,512]{2,1,0:T(8,128)(2,1)S(1)} %copy-done.3), kind=kLoop, calls=%fused_computation.1 | loop fusion | flops 2097152 | bytes 3145728 | tf_op jit(solution)/shard_map/convert_element_type | solution.py:699
  176.9 2.8 %collective-permute-done.20.three = bf16[192,1024]{1,0:T(8,128)(2,1)S(1)} collective-permute-done((bf16[192,1024]{1,0:T(8,128)(2,1)S(1)}, bf16[192,1024]{1,0:T(8,128)(2,1)S(1)}, u32[]{:S(2)}, u32[]{:S(2)}) %collective-permute-start.20) | collective-permute-done | bytes 393248 | tf_op jit(solution)/shard_map/ppermute | solution.py:705
  179.7 2.4 %collective-permute-start.28 = (f32[5,8]{0,1:T(8,128)S(1)}, f32[5,8]{0,1:T(8,128)S(1)}, u32[]{:S(2)}, u32[]{:S(2)}) collective-permute-start(f32[5,8]{0,1:T(8,128)S(1)} %max.10), channel_id=1, source_target_pairs={{0,16},{4,20},{8,24},{12,28},{16,0},{20,4},{24,8},{28,12},{1,17},{... | collective-permute-start | bytes 488 | tf_op jit(solution)/shard_map/ppermute | solution.py:705
  182.1 3.6 %collective-permute-done.28 = f32[5,8]{0,1:T(8,128)S(1)} collective-permute-done((f32[5,8]{0,1:T(8,128)S(1)}, f32[5,8]{0,1:T(8,128)S(1)}, u32[]{:S(2)}, u32[]{:S(2)}) %collective-permute-start.28) | collective-permute-done | bytes 192 | tf_op jit(solution)/shard_map/ppermute | solution.py:705
  185.7 1.5 collective-permute-start.21
  187.9 5.4 %mixed_last.1 = f32[512,1024]{1,0:T(8,128)} custom-call(s32[1]{0:T(128)} %bitcast.place_ref, bf16[512,1024]{1,0:T(8,128)(2,1)} %get-tuple-element.38.attn_ref, bf16[1024,4096]{1,0:T(8,128)(2,1)} %refs_5_.1, bf16[512,1024]{1,0:T(8,128)(2,1)} %collective-permute-done.8.left_ref, bf16[512,1024]{1,0:T(8,128)(2,1)} %collective-permute-done.9.right_ref), custom_call_target="tpu_custom_call" | custom-call | tf_op jit(solution)/shard_map/mixed_last/pallas_call | solution.py:568
  194.3 3.0 %weight_total.1 = f32[1024,512]{1,0:T(8,128)} custom-call(bf16[512,512]{1,0:T(8,128)(2,1)} %get-tuple-element.79.top_a, bf16[512,512]{1,0:T(8,128)(2,1)} %bitcast.16, bf16[512,512]{1,0:T(8,128)(2,1)} %get-tuple-element.77.bottom_a, bf16[512,512]{1,0:T(8,128)(2,1)} %bitcast.17), custom_call_target="tpu_custom_call" | custom-call | tf_op jit(solution)/shard_map/weight_total/pallas_call | solution.py:678
  198.0 5.2 %add_returned.1 = (f32[512,1024]{1,0:T(8,128)}, f32[512,1024]{1,0:T(8,128)}) custom-call(f32[512,1024]{1,0:T(8,128)} %get-tuple-element.56.gk_ref, f32[512,1024]{1,0:T(8,128)} %get-tuple-element.57.gv_ref, bf16[512,1024]{1,0:T(8,128)(2,1)} %copy-done.8, bf16[192,1024]{1,0:T(8,128)(2,1)} %copy-done.13, bf16[64,1024]{1,0:T(8,128)(2,1)} %copy-done.17), custom_call_target="tpu_custom_call" | custom-call | tf_op jit(solution)/shard_map/add_returned/pallas_call | solution.py:427
  (84 shorter events, 9.7 us)
Async XLA Ops:
  0.6 28.4 %collective-permute-start.11 = (bf16[512,1024]{1,0:T(8,128)(2,1)}, bf16[512,1024]{1,0:T(8,128)(2,1)}, u32[]{:S(2)}, u32[]{:S(2)}) collective-permute-start(bf16[512,1024]{1,0:T(8,128)(2,1)} %refs_0_.3), channel_id=1, source_target_pairs={{1,0},{2,1},{3,2},{5,4},{6,5},{7,6},{9,8},{10,9},{11,10},{13,12},{... | collective-permute-start | bytes 3145736 | tf_op jit(solution)/shard_map/ppermute | solution.py:721
  1.9 28.4 %collective-permute-start.10 = (bf16[512,1024]{1,0:T(8,128)(2,1)}, bf16[512,1024]{1,0:T(8,128)(2,1)}, u32[]{:S(2)}, u32[]{:S(2)}) collective-permute-start(bf16[512,1024]{1,0:T(8,128)(2,1)} %refs_0_.3), channel_id=1, source_target_pairs={{0,1},{1,2},{2,3},{4,5},{5,6},{6,7},{8,9},{9,10},{10,11},{12,13},{... | collective-permute-start | bytes 3145736 | tf_op jit(solution)/shard_map/ppermute | solution.py:720
  11.3 11.9 %collective-permute-start = (bf16[128,1024]{1,0:T(8,128)(2,1)}, bf16[128,1024]{1,0:T(8,128)(2,1)S(1)}, u32[]{:S(2)}, u32[]{:S(2)}) collective-permute-start(bf16[128,1024]{1,0:T(8,128)(2,1)} %get-tuple-element.36), channel_id=1, source_target_pairs={{0,8},{4,12},{8,0},{12,4},{16,24},{20,28},{24,16},{28,20},{1,9},{5... | collective-permute-start | bytes 786440 | tf_op jit(solution)/shard_map/ppermute | solution.py:705
  13.2 5.2 %collective-permute-start.1 = (bf16[64,1024]{1,0:T(8,128)(2,1)}, bf16[64,1024]{1,0:T(8,128)(2,1)S(1)}, u32[]{:S(2)}, u32[]{:S(2)}) collective-permute-start(bf16[64,1024]{1,0:T(8,128)(2,1)} %get-tuple-element.37), channel_id=1, source_target_pairs={{0,16},{4,20},{8,24},{12,28},{16,0},{20,4},{24,8},{28,12},{1,17},{... | collective-permute-start | bytes 393224 | tf_op jit(solution)/shard_map/ppermute | solution.py:705
  14.7 8.4 %collective-permute-start.2 = (bf16[64,1024]{1,0:T(8,128)(2,1)}, bf16[64,1024]{1,0:T(8,128)(2,1)S(1)}, u32[]{:S(2)}, u32[]{:S(2)}) collective-permute-start(bf16[64,1024]{1,0:T(8,128)(2,1)} %get-tuple-element.37), channel_id=1, source_target_pairs={{0,24},{4,28},{8,16},{12,20},{16,8},{20,12},{24,0},{28,4},{1,25},{... | collective-permute-start | bytes 393224 | tf_op jit(solution)/shard_map/ppermute | solution.py:705
  18.4 4.8 %copy-start.9 = (bf16[64,1024]{1,0:T(8,128)(2,1)}, bf16[64,1024]{1,0:T(8,128)(2,1)S(1)}, u32[]{:S(2)}) copy-start(bf16[64,1024]{1,0:T(8,128)(2,1)S(1)} %collective-permute-done.1.four_a) | copy-start | bytes 393220
  23.2 0.7 copy-start.7
  25.8 6.8 %collective-permute-start.3 = (bf16[512,1024]{1,0:T(8,128)(2,1)}, bf16[512,1024]{1,0:T(8,128)(2,1)S(1)}, u32[]{:S(2)}, u32[]{:S(2)}) collective-permute-start(bf16[512,1024]{1,0:T(8,128)(2,1)} %lower_rows.1), channel_id=1, source_target_pairs={{0,4},{4,0},{8,12},{12,8},{16,20},{20,16},{24,28},{28,24},{1,5},{5... | collective-permute-start | bytes 3145736 | tf_op jit(solution)/shard_map/ppermute | solution.py:705
  29.0 30.6 %collective-permute-start.12 = (bf16[512,1024]{1,0:T(8,128)(2,1)}, bf16[512,1024]{1,0:T(8,128)(2,1)S(1)}, u32[]{:S(2)}, u32[]{:S(2)}) collective-permute-start(bf16[512,1024]{1,0:T(8,128)(2,1)} %collective-permute-done.11.refs_3_), channel_id=1, source_target_pairs={{1,0},{2,1},{5,4},{6,5},{9,8},{10,9},{13,12},{14,13},{17,16},{18,1... | collective-permute-start | bytes 3145736 | tf_op jit(solution)/shard_map/ppermute | solution.py:721
  30.3 30.6 %collective-permute-start.14 = (bf16[512,1024]{1,0:T(8,128)(2,1)}, bf16[512,1024]{1,0:T(8,128)(2,1)}, u32[]{:S(2)}, u32[]{:S(2)}) collective-permute-start(bf16[512,1024]{1,0:T(8,128)(2,1)} %collective-permute-done.10.refs_0_), channel_id=1, source_target_pairs={{1,2},{2,3},{5,6},{6,7},{9,10},{10,11},{13,14},{14,15},{17,18},{18... | collective-permute-start | bytes 3145736 | tf_op jit(solution)/shard_map/ppermute | solution.py:720
  32.6 1.0 copy-start.6
  51.2 14.4 %collective-permute-start.4 = (bf16[512,1024]{1,0:T(8,128)(2,1)}, bf16[512,1024]{1,0:T(8,128)(2,1)S(1)}, u32[]{:S(2)}, u32[]{:S(2)}) collective-permute-start(bf16[512,1024]{1,0:T(8,128)(2,1)} %get-tuple-element.39), channel_id=1, source_target_pairs={{3,2},{7,6},{11,10},{15,14},{19,18},{23,22},{27,26},{31,30}} | collective-permute-start | bytes 3145736 | tf_op jit(solution)/shard_map/ppermute | solution.py:742
  52.0 28.9 %collective-permute-start.5 = (bf16[512,1024]{1,0:T(8,128)(2,1)}, bf16[512,1024]{1,0:T(8,128)(2,1)S(1)}, u32[]{:S(2)}, u32[]{:S(2)}) collective-permute-start(bf16[512,1024]{1,0:T(8,128)(2,1)} %get-tuple-element.40), channel_id=1, source_target_pairs={{0,1},{4,5},{8,9},{12,13},{16,17},{20,21},{24,25},{28,29}} | collective-permute-start | bytes 3145736 | tf_op jit(solution)/shard_map/ppermute | solution.py:743
  59.6 3.0 %copy-start.5 = (bf16[512,1024]{1,0:T(8,128)(2,1)}, bf16[512,1024]{1,0:T(8,128)(2,1)S(1)}, u32[]{:S(2)}) copy-start(bf16[512,1024]{1,0:T(8,128)(2,1)S(1)} %collective-permute-done.12.refs_2_) | copy-start | bytes 3145732
  59.6 25.2 %collective-permute-start.13 = (bf16[512,1024]{1,0:T(8,128)(2,1)S(1)}, bf16[512,1024]{1,0:T(8,128)(2,1)}, u32[]{:S(2)}, u32[]{:S(2)}) collective-permute-start(bf16[512,1024]{1,0:T(8,128)(2,1)S(1)} %collective-permute-done.12.refs_2_), channel_id=1, source_target_pairs={{1,0},{5,4},{9,8},{13,12},{17,16},{21,20},{25,24},{29,28}} | collective-permute-start | bytes 3145736 | tf_op jit(solution)/shard_map/ppermute | solution.py:721
  60.9 23.9 %collective-permute-start.15 = (bf16[512,1024]{1,0:T(8,128)(2,1)}, bf16[512,1024]{1,0:T(8,128)(2,1)}, u32[]{:S(2)}, u32[]{:S(2)}) collective-permute-start(bf16[512,1024]{1,0:T(8,128)(2,1)} %collective-permute-done.14.refs_1_), channel_id=1, source_target_pairs={{2,3},{6,7},{10,11},{14,15},{18,19},{22,23},{26,27},{30,31}} | collective-permute-start | bytes 3145736 | tf_op jit(solution)/shard_map/ppermute | solution.py:720
  62.6 55.4 %collective-permute-start.16 = (bf16[1024,512]{1,0:T(8,128)(2,1)}, bf16[1024,512]{1,0:T(8,128)(2,1)}, u32[]{:S(2)}, u32[]{:S(2)}) collective-permute-start(bf16[1024,512]{1,0:T(8,128)(2,1)} %get-tuple-element.46.own_ref), channel_id=1, source_target_pairs={{0,4},{4,0},{8,12},{12,8},{16,20},{20,16},{24,28},{28,24},{1,5},{5... | collective-permute-start | bytes 3145736 | tf_op jit(solution)/shard_map/ppermute | solution.py:705
  65.6 19.2 %copy-start.1 = (bf16[512,1024]{1,0:T(8,128)(2,1)}, bf16[512,1024]{1,0:T(8,128)(2,1)S(1)}, u32[]{:S(2)}) copy-start(bf16[512,1024]{1,0:T(8,128)(2,1)S(1)} %collective-permute-done.4.refs_0_.refs_4_) | copy-start | bytes 3145732
  65.6 22.5 %copy-start.20 = (s32[4]{0:T(128)S(1)}, s32[4]{0:T(128)}, u32[]{:S(2)}) copy-start(s32[4]{0:T(128)} %constant.94.clone) | copy-start | bytes 52
  65.6 22.5 %copy-start = (s32[4]{0:T(128)S(1)}, s32[4]{0:T(128)}, u32[]{:S(2)}) copy-start(s32[4]{0:T(128)} %constant.93.clone) | copy-start | bytes 52
  65.6 52.4 %collective-permute-start.17 = (bf16[512,1024]{1,0:T(8,128)(2,1)}, bf16[512,1024]{1,0:T(8,128)(2,1)}, u32[]{:S(2)}, u32[]{:S(2)}) collective-permute-start(bf16[512,1024]{1,0:T(8,128)(2,1)} %get-tuple-element.48), channel_id=1, source_target_pairs={{0,4},{4,0},{8,12},{12,8},{16,20},{20,16},{24,28},{28,24},{1,5},{5... | collective-permute-start | bytes 3145736 | tf_op jit(solution)/shard_map/ppermute | solution.py:705
  80.8 4.0 %copy-start.2 = (bf16[512,1024]{1,0:T(8,128)(2,1)}, bf16[512,1024]{1,0:T(8,128)(2,1)S(1)}, u32[]{:S(2)}) copy-start(bf16[512,1024]{1,0:T(8,128)(2,1)S(1)} %collective-permute-done.5.refs_1_.refs_5_) | copy-start | bytes 3145732
  88.1 29.9 %collective-permute-start.18 = (bf16[512,1024]{1,0:T(8,128)(2,1)}, bf16[512,1024]{1,0:T(8,128)(2,1)S(1)}, u32[]{:S(2)}, u32[]{:S(2)}) collective-permute-start(bf16[512,1024]{1,0:T(8,128)(2,1)} %get-tuple-element.50), channel_id=1, source_target_pairs={{0,4},{4,0},{8,12},{12,8},{16,20},{20,16},{24,28},{28,24},{1,5},{5... | collective-permute-start | bytes 3145736 | tf_op jit(solution)/shard_map/ppermute | solution.py:705
  105.9 42.1 %collective-permute-start.6 = (bf16[512,1024]{1,0:T(8,128)(2,1)}, bf16[512,1024]{1,0:T(8,128)(2,1)}, u32[]{:S(2)}, u32[]{:S(2)}) collective-permute-start(bf16[512,1024]{1,0:T(8,128)(2,1)} %get-tuple-element.41), channel_id=1, source_target_pairs={{2,1},{3,2},{6,5},{7,6},{10,9},{11,10},{14,13},{15,14},{18,17},{19... | collective-permute-start | bytes 3145736 | tf_op jit(solution)/shard_map/ppermute | solution.py:742
  107.6 41.5 %collective-permute-start.7 = (bf16[512,1024]{1,0:T(8,128)(2,1)}, bf16[512,1024]{1,0:T(8,128)(2,1)}, u32[]{:S(2)}, u32[]{:S(2)}) collective-permute-start(bf16[512,1024]{1,0:T(8,128)(2,1)} %get-tuple-element.42), channel_id=1, source_target_pairs={{0,1},{1,2},{4,5},{5,6},{8,9},{9,10},{12,13},{13,14},{16,17},{17,1... | collective-permute-start | bytes 3145736 | tf_op jit(solution)/shard_map/ppermute | solution.py:743
  118.1 1.0 copy-start.11
  130.2 14.4 %copy-start.19 = (f32[8,8,128]{2,1,0:T(8,128)S(1)}, f32[8,8,128]{2,1,0:T(8,128)}, u32[]{:S(2)}) copy-start(f32[8,8,128]{2,1,0:T(8,128)} %get-tuple-element.63) | copy-start | bytes 98308
  130.2 15.7 %copy-start.12 = (bf16[2,512,512]{2,1,0:T(8,128)(2,1)S(1)}, bf16[2,512,512]{2,1,0:T(8,128)(2,1)}, u32[]{:S(2)}) copy-start(bf16[2,512,512]{2,1,0:T(8,128)(2,1)} %get-tuple-element.53.rest_2_) | copy-start | bytes 3145732
  142.4 15.3 %collective-permute-start.19 = (bf16[512,1024]{1,0:T(8,128)(2,1)}, bf16[512,1024]{1,0:T(8,128)(2,1)S(1)}, u32[]{:S(2)}, u32[]{:S(2)}) collective-permute-start(bf16[512,1024]{1,0:T(8,128)(2,1)} %get-tuple-element.58), channel_id=1, source_target_pairs={{0,4},{4,0},{8,12},{12,8},{16,20},{20,16},{24,28},{28,24},{1,5},{5... | collective-permute-start | bytes 3145736 | tf_op jit(solution)/shard_map/ppermute | solution.py:705
  143.0 25.5 %collective-permute-start.22 = (bf16[2,512,512]{2,1,0:T(8,128)(2,1)}, bf16[2,512,512]{2,1,0:T(8,128)(2,1)}, u32[]{:S(2)}, u32[]{:S(2)}) collective-permute-start(bf16[2,512,512]{2,1,0:T(8,128)(2,1)} %get-tuple-element.51.rest_0_), channel_id=1, source_target_pairs={{0,8},{4,12},{8,0},{12,4},{16,24},{20,28},{24,16},{28,20},{1,9},{5... | collective-permute-start | bytes 3145736 | tf_op jit(solution)/shard_map/ppermute | solution.py:705
  144.7 1.2 collective-permute-start.26
  145.9 26.8 %collective-permute-start.24 = (bf16[2,512,512]{2,1,0:T(8,128)(2,1)S(1)}, bf16[2,512,512]{2,1,0:T(8,128)(2,1)}, u32[]{:S(2)}, u32[]{:S(2)}) collective-permute-start(bf16[2,512,512]{2,1,0:T(8,128)(2,1)S(1)} %copy-done.12), channel_id=1, source_target_pairs={{0,16},{4,20},{8,24},{12,28},{16,0},{20,4},{24,8},{28,12},{1,17},{... | collective-permute-start | bytes 3145736 | tf_op jit(solution)/shard_map/ppermute | solution.py:705
  148.0 15.5 %copy-start.16 = (bf16[192,1024]{1,0:T(8,128)(2,1)S(1)}, bf16[192,1024]{1,0:T(8,128)(2,1)}, u32[]{:S(2)}) copy-start(bf16[192,1024]{1,0:T(8,128)(2,1)} %get-tuple-element.59) | copy-start | bytes 1179652
  148.0 22.1 %copy-start.4 = (bf16[2,512,512]{2,1,0:T(8,128)(2,1)S(1)}, bf16[2,512,512]{2,1,0:T(8,128)(2,1)}, u32[]{:S(2)}) copy-start(bf16[2,512,512]{2,1,0:T(8,128)(2,1)} %get-tuple-element.52.rest_1_) | copy-start | bytes 3145732
  148.0 28.5 %collective-permute-start.27 = (f32[5,8]{0,1:T(8,128)S(1)}, f32[5,8]{0,1:T(8,128)S(1)}, u32[]{:S(2)}, u32[]{:S(2)}) collective-permute-start(f32[5,8]{0,1:T(8,128)S(1)} %bitcast_maximum_fusion), channel_id=1, source_target_pairs={{0,8},{4,12},{8,0},{12,4},{16,24},{20,28},{24,16},{28,20},{1,9},{5... | collective-permute-start | bytes 488 | tf_op jit(solution)/shard_map/ppermute | solution.py:705
  156.4 31.5 %collective-permute-start.8 = (bf16[512,1024]{1,0:T(8,128)(2,1)}, bf16[512,1024]{1,0:T(8,128)(2,1)}, u32[]{:S(2)}, u32[]{:S(2)}) collective-permute-start(bf16[512,1024]{1,0:T(8,128)(2,1)} %get-tuple-element.43), channel_id=1, source_target_pairs={{1,0},{2,1},{3,2},{5,4},{6,5},{7,6},{9,8},{10,9},{11,10},{13,12},{... | collective-permute-start | bytes 3145736 | tf_op jit(solution)/shard_map/ppermute | solution.py:742
  157.7 24.4 %copy-start.8 = (bf16[512,1024]{1,0:T(8,128)(2,1)}, bf16[512,1024]{1,0:T(8,128)(2,1)S(1)}, u32[]{:S(2)}) copy-start(bf16[512,1024]{1,0:T(8,128)(2,1)S(1)} %collective-permute-done.19.near) | copy-start | bytes 3145732
  157.7 30.2 %collective-permute-start.9 = (bf16[512,1024]{1,0:T(8,128)(2,1)}, bf16[512,1024]{1,0:T(8,128)(2,1)}, u32[]{:S(2)}, u32[]{:S(2)}) collective-permute-start(bf16[512,1024]{1,0:T(8,128)(2,1)} %get-tuple-element.44), channel_id=1, source_target_pairs={{0,1},{1,2},{2,3},{4,5},{5,6},{6,7},{8,9},{9,10},{10,11},{12,13},{... | collective-permute-start | bytes 3145736 | tf_op jit(solution)/shard_map/ppermute | solution.py:743
  163.6 10.6 %copy-start.3 = (bf16[2,512,512]{2,1,0:T(8,128)(2,1)S(1)}, bf16[2,512,512]{2,1,0:T(8,128)(2,1)}, u32[]{:S(2)}) copy-start(bf16[2,512,512]{2,1,0:T(8,128)(2,1)} %get-tuple-element.54.rest_3_) | copy-start | bytes 3145732
  168.5 11.2 %collective-permute-start.20 = (bf16[192,1024]{1,0:T(8,128)(2,1)S(1)}, bf16[192,1024]{1,0:T(8,128)(2,1)S(1)}, u32[]{:S(2)}, u32[]{:S(2)}) collective-permute-start(bf16[192,1024]{1,0:T(8,128)(2,1)S(1)} %add_convert_fusion.4), channel_id=1, source_target_pairs={{0,8},{4,12},{8,0},{12,4},{16,24},{20,28},{24,16},{28,20},{1,9},{5... | collective-permute-start | bytes 1179656 | tf_op jit(solution)/shard_map/ppermute | solution.py:705
  172.7 9.4 %copy-start.18 = (bf16[64,1024]{1,0:T(8,128)(2,1)S(1)}, bf16[64,1024]{1,0:T(8,128)(2,1)}, u32[]{:S(2)}) copy-start(bf16[64,1024]{1,0:T(8,128)(2,1)} %get-tuple-element.60) | copy-start | bytes 393220
  172.7 20.7 %collective-permute-start.23 = (bf16[1,512,512]{2,1,0:T(8,128)(2,1)}, bf16[1,512,512]{2,1,0:T(8,128)(2,1)S(1)}, u32[]{:S(2)}, u32[]{:S(2)}) collective-permute-start(bf16[1,512,512]{2,1,0:T(8,128)(2,1)} %get-tuple-element.78), channel_id=1, source_target_pairs={{0,16},{4,20},{8,24},{12,28},{16,0},{20,4},{24,8},{28,12},{1,17},{... | collective-permute-start | bytes 1572872 | tf_op jit(solution)/shard_map/ppermute | solution.py:705
  176.6 16.8 %collective-permute-start.25 = (bf16[1,512,512]{2,1,0:T(8,128)(2,1)S(1)}, bf16[1,512,512]{2,1,0:T(8,128)(2,1)S(1)}, u32[]{:S(2)}, u32[]{:S(2)}) collective-permute-start(bf16[1,512,512]{2,1,0:T(8,128)(2,1)S(1)} %get-tuple-element.76), channel_id=1, source_target_pairs={{0,8},{4,12},{8,0},{12,4},{16,24},{20,28},{24,16},{28,20},{1,9},{5... | collective-permute-start | bytes 1572872 | tf_op jit(solution)/shard_map/ppermute | solution.py:705
  179.7 13.6 %copy-start.13 = (bf16[192,1024]{1,0:T(8,128)(2,1)}, bf16[192,1024]{1,0:T(8,128)(2,1)S(1)}, u32[]{:S(2)}) copy-start(bf16[192,1024]{1,0:T(8,128)(2,1)S(1)} %collective-permute-done.20.three) | copy-start | bytes 1179652
  179.7 6.0 %collective-permute-start.28 = (f32[5,8]{0,1:T(8,128)S(1)}, f32[5,8]{0,1:T(8,128)S(1)}, u32[]{:S(2)}, u32[]{:S(2)}) collective-permute-start(f32[5,8]{0,1:T(8,128)S(1)} %max.10), channel_id=1, source_target_pairs={{0,16},{4,20},{8,24},{12,28},{16,0},{20,4},{24,8},{28,12},{1,17},{... | collective-permute-start | bytes 488 | tf_op jit(solution)/shard_map/ppermute | solution.py:705
  185.7 11.6 %collective-permute-start.21 = (bf16[64,1024]{1,0:T(8,128)(2,1)S(1)}, bf16[64,1024]{1,0:T(8,128)(2,1)S(1)}, u32[]{:S(2)}, u32[]{:S(2)}) collective-permute-start(bf16[64,1024]{1,0:T(8,128)(2,1)S(1)} %add_convert_fusion.5), channel_id=1, source_target_pairs={{0,16},{4,20},{8,24},{12,28},{16,0},{20,4},{24,8},{28,12},{1,17},{... | collective-permute-start | bytes 393224 | tf_op jit(solution)/shard_map/ppermute | solution.py:705
  193.3 0.8 copy-start.14
  193.3 0.9 copy-start.15
  (2 other events, 1.3 us)

commit v3 on v2

--- a/solution.py
+++ b/solution.py
@@ -3,6 +3,7 @@
 
 import jax
 import jax.numpy as jnp
+import numpy as np
 from jax import lax
 from jax.experimental import pallas as pl
 from jax.experimental.pallas import tpu as pltpu
@@ -15,7 +16,10 @@
 LOG_TWO = math.log(2.0)
 F32 = jnp.float32
 BF16 = jnp.bfloat16
-VMEM_LIMIT = 60 * 1024 * 1024
+VMEM_LIMIT = 20 * 1024 * 1024
+
+
+OPT = {'fp': True, 'se': True, 'sl': True, 'g': True, 'b': True, 'lm': 1, 'sa': True, 'b3': True, 'bar': True}
 
 
 def dot_nn(a, b):
@@ -365,8 +369,8 @@
                     both = slice(b * 2 * BLK, (b + 1) * 2 * BLK)
                     here = pl.ds(b * 2 * BLK, 2 * BLK)
                     gq_ref[here, columns[h]] = part_q + state[h, "q"][both]
-                    gk_ref[here, columns[h]] = part_k + state[h, "k"][both]
-                    gv_ref[here, columns[h]] = part_v + state[h, "v"][both]
+                    gk_ref[here, columns[h]] = (part_k + state[h, "k"][both]).astype(BF16)
+                    gv_ref[here, columns[h]] = (part_v + state[h, "v"][both]).astype(BF16)
             else:
                 grad_q = part_q if level == LEVELS - 1 else part_q + state[h, "q"]
                 state[h, "q"] = expand_two(gq_s, h * 2 * tokens + up, grad_q * 0.5)
@@ -375,7 +379,7 @@
 
 def backward_call(query, key, value, attn, grad, lse, received, after=(), step=2):
     tokens, width = query.shape
-    heads = width // DH
+    steps = width // DH // step
     spec = pl.BlockSpec((tokens, step * DH), lambda h: (0, h))
     others = [pl.BlockSpec((r.shape[0], step * DH), lambda h: (0, h)) for r in received]
     others += [pl.BlockSpec(memory_space=pl.ANY)] * len(after)
@@ -384,10 +388,10 @@
     outs = [pl.BlockSpec((r, step * DH), lambda h: (0, h)) for r in back_rows]
     return pl.pallas_call(
         functools.partial(backward_kernel, extra=len(after)),
-        grid=(heads // step,),
+        grid=(steps,),
         in_specs=[spec] * 6 + others,
         out_specs=[spec] * 3 + outs,
-        out_shape=[full] * 3
+        out_shape=[full] + [jax.ShapeDtypeStruct((tokens, width), BF16)] * 2
         + [jax.ShapeDtypeStruct((r, width), BF16) for r in back_rows],
         scratch_shapes=[pltpu.VMEM((tokens - tokens // 16, tokens), BF16)]
         + [pltpu.VMEM((step * 2 * tokens, 128), F32)] * 6,
@@ -412,8 +416,8 @@
         base += 2 * rows
     for h in heads:
         here = pl.ds(h * DH, DH)
-        ok_ref[:, here] = gk_ref[:, here] + state[h, 0]
-        ov_ref[:, here] = gv_ref[:, here] + state[h, 1]
+        ok_ref[:, here] = gk_ref[:, here].astype(F32) + state[h, 0]
+        ov_ref[:, here] = gv_ref[:, here].astype(F32) + state[h, 1]
 
 
 def finish_call(grad_k, grad_v, near, three, four):
@@ -494,15 +498,15 @@
     out[...] = result.astype(out.dtype)
 
 
-def grad_call(chunks, out_weight, place, partial_sum, dtype):
+def grad_call(chunks, out_weight, place, distances, partial_sum, dtype, after=()):
     flat = [array for chunk in chunks for array in chunk]
     tokens, width = flat[0].shape
     features = out_weight.shape[0]
-    step = 256
+    step = min(512, features)
     chunk_spec = pl.BlockSpec((tokens, width), lambda i, p: (0, 0))
     out_spec = pl.BlockSpec((tokens, step), lambda i, p: (0, i))
     weight_specs = [
-        pl.BlockSpec((step, width), lambda i, p, n=n: (i, p[n])) for n in range(len(chunks))
+        pl.BlockSpec((step, width), lambda i, p, d=d: (i, p[d])) for d in distances
     ]
     sums = () if partial_sum is None else (partial_sum,)
     return pl.pallas_call(
@@ -512,133 +516,148 @@
         grid_spec=pltpu.PrefetchScalarGridSpec(
             num_scalar_prefetch=1,
             grid=(features // step,),
-            in_specs=[chunk_spec] * len(flat) + weight_specs + [out_spec] * len(sums),
+            in_specs=[chunk_spec] * len(flat)
+            + weight_specs
+            + [out_spec] * len(sums)
+            + [pl.BlockSpec(memory_space=pl.ANY)] * len(after),
             out_specs=out_spec,
         ),
         out_shape=jax.ShapeDtypeStruct((tokens, features), dtype),
         compiler_params=pltpu.CompilerParams(vmem_limit_bytes=VMEM_LIMIT),
         name="grad_products",
-    )(place.astype(jnp.int32), *flat, *[out_weight] * len(chunks), *sums)
-
-
-def project_kernel(place_ref, attn_ref, left_w, right_w, *refs, has_sum):
-    left_out, right_out = refs[-2:]
-    left = dot_nn(attn_ref[...], left_w[...])
-    right = dot_nn(attn_ref[...], right_w[...])
-    if has_sum:
-        left = left + refs[0][...].astype(F32)
-        right = right + refs[1][...].astype(F32)
-    left_out[...] = left.astype(BF16)
-    right_out[...] = right.astype(BF16)
-
-
-def project_call(attn, out_weight, place, sums):
+    )(place, *flat, *[out_weight] * len(chunks), *sums, *after)
+
+
+def product_kernel(place_ref, attn_ref, *refs, count):
+    for weight, out in zip(refs[:count], refs[-count:]):
+        out[...] = dot_nn(attn_ref[...], weight[...]).astype(out.dtype)
+
+
+def product_call(attn, out_weight, place, count, after=()):
     tokens, width = attn.shape
     features = out_weight.shape[0]
-    step = 256
+    step = min(256, width)
     per = width // step
     spec = pl.BlockSpec((tokens, step), lambda i, p: (0, i))
     return pl.pallas_call(
-        functools.partial(project_kernel, has_sum=bool(sums)),
+        functools.partial(product_kernel, count=count),
         grid_spec=pltpu.PrefetchScalarGridSpec(
             num_scalar_prefetch=1,
             grid=(per,),
             in_specs=[pl.BlockSpec((tokens, width), lambda i, p: (0, 0))]
-            + [pl.BlockSpec((features, step), lambda i, p, n=n: (0, p[n] * per + i)) for n in (0, 1)]
-            + [spec] * len(sums),
-            out_specs=[spec, spec],
+            + [
+                pl.BlockSpec((features, step), lambda i, p, d=d: (0, p[d] * per + i))
+                for d in range(count)
+            ]
+            + [pl.BlockSpec(memory_space=pl.ANY)] * len(after),
+            out_specs=[spec] * count,
         ),
+        out_shape=[jax.ShapeDtypeStruct((tokens, width), BF16)] * count,
+        compiler_params=pltpu.CompilerParams(vmem_limit_bytes=VMEM_LIMIT),
+        name="mixed_products",
+    )(place, attn, *[out_weight] * count, *after)
+
+
+def add_kernel(left_a, left_b, right_a, right_b, left, right):
+    left[...] = (left_a[...].astype(F32) + left_b[...].astype(F32)).astype(left.dtype)
+    right[...] = (right_a[...].astype(F32) + right_b[...].astype(F32)).astype(right.dtype)
+
+
+def add_call(left, right):
+    tokens, width = left[0].shape
+    spec = pl.BlockSpec((tokens // 2, width), lambda i: (i, 0))
+    return pl.pallas_call(
+        add_kernel,
+        grid=(2,),
+        in_specs=[spec] * 4,
+        out_specs=[spec] * 2,
         out_shape=[jax.ShapeDtypeStruct((tokens, width), BF16)] * 2,
         compiler_params=pltpu.CompilerParams(vmem_limit_bytes=VMEM_LIMIT),
-        name="mixed_products",
-    )(place.astype(jnp.int32), attn, out_weight, out_weight, *sums)
-
-
-def mixed_kernel(place_ref, attn_ref, weight_ref, left_ref, right_ref, out_ref):
-    total = left_ref[...].astype(F32) + right_ref[...].astype(F32)
-    out_ref[...] = dot_nn(attn_ref[...], weight_ref[...]) + total
-
-
-def mixed_call(attn, out_weight, place, left, right):
-    tokens, width = attn.shape
-    features = out_weight.shape[0]
-    step = 256
-    per = width // step
-    spec = pl.BlockSpec((tokens, step), lambda i, p: (0, i))
-    return pl.pallas_call(
-        mixed_kernel,
+        name="mixed_add",
+    )(*left, *right)
+
+
+def last_kernel(own, left, right, out):
+    out[...] = own[...].astype(F32) + left[...].astype(F32) + right[...].astype(F32)
+
+
+def last_call(own, left, right):
+    tokens, width = own.shape
+    spec = pl.BlockSpec((tokens // 4, width), lambda i: (i, 0))
+    return pl.pallas_call(
+        last_kernel,
+        grid=(4,),
+        in_specs=[spec] * 3,
+        out_specs=spec,
+        out_shape=jax.ShapeDtypeStruct((tokens, width), F32),
+        compiler_params=pltpu.CompilerParams(vmem_limit_bytes=VMEM_LIMIT),
+        name="mixed_last",
+    )(own, left, right)
+
+
+def term_kernel(place_ref, own_ref, other_ref, mine_ref, theirs_ref, out):
+    out[0] = (
+        dot_nn(own_ref[...], mine_ref[...]) + dot_nn(other_ref[...], theirs_ref[...])
+    ).astype(BF16)
+
+
+def term_call(own, other, mine, theirs, place, column):
+    features, tokens = own.shape
+    count = mine.shape[1] // column
+    rows = features // 2
+    whole = pl.BlockSpec((rows, tokens), lambda i, j, p: (j, 0))
+    source = pl.BlockSpec((tokens, column), lambda i, j, p: (0, i))
+    return pl.pallas_call(
+        term_kernel,
         grid_spec=pltpu.PrefetchScalarGridSpec(
             num_scalar_prefetch=1,
-            grid=(per,),
-            in_specs=[
-                pl.BlockSpec((tokens, width), lambda i, p: (0, 0)),
-                pl.BlockSpec((features, step), lambda i, p: (0, p[0] * per + i)),
-                spec,
-                spec,
-            ],
-            out_specs=spec,
+            grid=(count, 2),
+            in_specs=[whole, whole, source, source],
+            out_specs=pl.BlockSpec((1, rows, column), lambda i, j, p: (i, j, 0)),
         ),
-        out_shape=jax.ShapeDtypeStruct((tokens, width), F32),
-        compiler_params=pltpu.CompilerParams(vmem_limit_bytes=VMEM_LIMIT),
-        name="mixed_last",
-    )(place.astype(jnp.int32), attn, out_weight, left, right)
-
-
-def term_order(chips):
-    top = chips // 2
-    groups = {(1, 0): [], (1, 1): [], (0, 1): [], (0, 0): []}
-    for i in range(chips):
-        groups[i & 1, int(i & top != 0)].append(i)
-    return [i for key in ((1, 0), (1, 1), (0, 1), (0, 0)) for i in groups[key]]
-
-
-def term_kernel(
-    place_ref, own_ref, other_ref, mine_a, theirs_a, mine_b, theirs_b,
-    a_send, a_keep, b_send, b_keep, turned, both, *, chips, first,
-):
+        out_shape=jax.ShapeDtypeStruct((count, features, column), BF16),
+        compiler_params=pltpu.CompilerParams(vmem_limit_bytes=VMEM_LIMIT),
+        name="weight_terms",
+    )(place, own, other, mine, theirs)
+
+
+def late_kernel(place_ref, own_ref, other_ref, mine_ref, theirs_ref, early_ref, *refs, chips, base, first):
+    a_send, a_keep, b_send, b_keep = refs[-4:]
     step = pl.program_id(0)
-    features, tokens = own_ref.shape
-
-    @pl.when(step == 0)
-    def _():
-        turned[:, pl.ds(0, tokens)] = own_ref[...]
-        turned[:, pl.ds(tokens, tokens)] = other_ref[...]
-
-    is_first = place_ref[step] < first
-
-    @pl.when(is_first)
-    def _():
-        both[pl.ds(0, tokens), :] = mine_a[...]
-        both[pl.ds(tokens, tokens), :] = theirs_a[...]
-
-    @pl.when(jnp.logical_not(is_first))
-    def _():
-        both[pl.ds(0, tokens), :] = mine_b[...]
-        both[pl.ds(tokens, tokens), :] = theirs_b[...]
-
-    half = features // 2
+    half = own_ref.shape[0] // 2
     in_a = step < chips // 2
     in_b = jnp.logical_and(step >= chips // 4, step < 3 * chips // 4)
+    is_early = place_ref[base + step] < first
     for start, flag, send, keep in ((0, in_a, a_send, a_keep), (half, in_b, b_send, b_keep)):
-        rows = dot_nn(turned[pl.ds(start, half), :], both[...]).astype(BF16)
-
-        @pl.when(flag)
+        here = pl.ds(start, half)
+
+        def store(rows):
+            @pl.when(flag)
+            def _():
+                send[0] = rows
+
+            @pl.when(jnp.logical_not(flag))
+            def _():
+                keep[0] = rows
+
+        @pl.when(is_early)
         def _():
-            send[0] = rows
-
-        @pl.when(jnp.logical_not(flag))
+            store(early_ref[0, here, :])
+
+        @pl.when(jnp.logical_not(is_early))
         def _():
-            keep[0] = rows
-
-
-def term_call(own, other, early, late, place, column):
+            rows = dot_nn(own_ref[here, :], mine_ref[...]) + dot_nn(
+                other_ref[here, :], theirs_ref[...]
+            )
+            store(rows.astype(BF16))
+
+
+def late_call(own, other, mine, theirs, early, place, base, chips, column, after):
     features, tokens = own.shape
-    chips = place.shape[0]
+    first = early.shape[0]
     half, quarter = chips // 2, chips // 4
-    first = early[0].shape[1] // column
     whole = pl.BlockSpec((features, tokens), lambda i, p: (0, 0))
-    spec_a = pl.BlockSpec((tokens, column), lambda i, p: (0, jnp.minimum(p[i], first - 1)))
-    spec_b = pl.BlockSpec((tokens, column), lambda i, p: (0, jnp.maximum(p[i] - first, 0)))
+    source = pl.BlockSpec((tokens, column), lambda i, p: (0, jnp.maximum(p[base + i] - first, 0)))
     shape = (1, features // 2, column)
     outs = [
         pl.BlockSpec(shape, lambda i, p: (jnp.minimum(i, half - 1), 0, 0)),
@@ -649,22 +668,22 @@
             lambda i, p: (jnp.where(i < 3 * quarter, jnp.minimum(i, quarter - 1), i - half), 0, 0),
         ),
     ]
-    return pl.pallas_call(
-        functools.partial(term_kernel, chips=chips, first=first),
+    early_spec = pl.BlockSpec(
+        (1, features, column), lambda i, p: (jnp.minimum(p[base + i], first - 1), 0, 0)
+    )
+    return pl.pallas_call(
+        functools.partial(late_kernel, chips=chips, base=base, first=first),
         grid_spec=pltpu.PrefetchScalarGridSpec(
             num_scalar_prefetch=1,
             grid=(chips,),
-            in_specs=[whole, whole, spec_a, spec_a, spec_b, spec_b],
+            in_specs=[whole, whole, source, source, early_spec]
+            + [pl.BlockSpec(memory_space=pl.ANY)] * len(after),
             out_specs=outs,
-            scratch_shapes=[
-                pltpu.VMEM((features, 2 * tokens), BF16),
-                pltpu.VMEM((2 * tokens, column), BF16),
-            ],
         ),
         out_shape=[jax.ShapeDtypeStruct((half, features // 2, column), BF16)] * 4,
         compiler_params=pltpu.CompilerParams(vmem_limit_bytes=VMEM_LIMIT),
-        name="weight_terms",
-    )(place, own, other, *early, *late)
+        name="weight_terms_late",
+    )(place, own, other, mine, theirs, early, *after)
 
 
 def total_kernel(top_a, top_b, bottom_a, bottom_b, out):
@@ -683,22 +702,57 @@
     )(*top, *bottom)
 
 
-def halve(sent, kept, bits):
-    for n, bit in enumerate(bits):
-        arrived = swap(sent[1], "ctx", 2 * bit)
-        names = [i ^ bit for i in sent[0]]
-        if n + 1 == len(bits):
-            return kept[1][0], arrived[0]
-
-        def added(flag):
-            here = [i for i in kept[0] if (i & bits[n + 1] != 0) == flag]
-            parts = [
-                kept[1][kept[0].index(i)].astype(F32) + arrived[names.index(i)].astype(F32)
-                for i in here
-            ]
-            return here, jnp.stack([p.astype(BF16) for p in parts])
-
-        sent, kept = added(True), added(False)
+def term_order(chips):
+    top = chips // 2
+    groups = {(1, 0): [], (1, 1): [], (0, 1): [], (0, 0): []}
+    for i in range(chips):
+        groups[i & 1, int(i & top != 0)].append(i)
+    return [i for key in ((1, 0), (1, 1), (0, 1), (0, 0)) for i in groups[key]]
+
+
+def fold_kernel(*refs, plans):
+    at = 0
+    out_at = 2 * len(plans)
+    for plan in plans:
+        kept, arrived = refs[at : at + 2]
+        for out, pairs in zip(refs[out_at : out_at + 2], plan):
+            for n, (k, m) in enumerate(pairs):
+                out[n] = (kept[k].astype(F32) + arrived[m].astype(F32)).astype(BF16)
+        at += 2
+        out_at += 2
+
+
+def fold_call(sides):
+    plans, operands, names, shapes = [], [], [], []
+    for sent, arrived, keep, kept, bit, following in sides:
+        source = [i ^ bit for i in sent]
+        parts = [[i for i in keep if (i & following != 0) == flag] for flag in (True, False)]
+        plans.append([[(keep.index(i), source.index(i)) for i in part] for part in parts])
+        operands += [kept, arrived]
+        names.append(parts)
+        shapes += [jax.ShapeDtypeStruct((len(p), *kept.shape[1:]), BF16) for p in parts]
+    outs = pl.pallas_call(
+        functools.partial(fold_kernel, plans=plans),
+        out_shape=shapes,
+        compiler_params=pltpu.CompilerParams(vmem_limit_bytes=VMEM_LIMIT),
+        name="fold_terms",
+    )(*operands)
+    return [(names[n], outs[2 * n : 2 * n + 2]) for n in range(len(sides))]
+
+
+def top_kernel(tops_ref, *refs):
+    refs[-1][...] = tops_ref[...]
+
+
+def held_back(value, after):
+    spec = pl.BlockSpec(value.shape, lambda: (0,) * value.ndim)
+    return pl.pallas_call(
+        top_kernel,
+        in_specs=[spec] + [pl.BlockSpec(memory_space=pl.ANY)] * len(after),
+        out_specs=spec,
+        out_shape=jax.ShapeDtypeStruct(value.shape, value.dtype),
+        name="held_back",
+    )(value, *after)
 
 
 def swap(value, axis, mask):
@@ -714,81 +768,149 @@
     me = lax.axis_index("ctx")
     z = lax.axis_index("head")
 
-    right, left = cotangent, cotangent
-    from_left, from_right = [None], [None]
-    for step in range(1, count):
+    core = me % 2
+    chips = ctx_count // 2
+    per_chunk = chips // count
+    early = [s for s in range(count) if s not in (1, count - 1)]
+    late = sorted({1, count - 1})
+    bits = [1 << n for n in range(chips.bit_length() - 1)]
+    order = term_order(chips)
+    slots = {s: n for n, s in enumerate(early + late)}
+    table = np.zeros((count, ctx_count, count + chips), np.int32)
+    for i in range(count):
+        for j in range(ctx_count):
+            table[i, j, :count] = [(i + d) % count for d in range(count)]
+            for n, distance in enumerate(order):
+                chip = (j // 2) ^ distance
+                s = (i - chip // per_chunk) % count
+                table[i, j, count + n] = slots[s] * per_chunk + chip % per_chunk
+    place = lax.dynamic_slice(jnp.asarray(table), (z, me, 0), (1, 1, count + chips)).reshape(-1)
+
+    from_left, from_right = [cotangent], [cotangent]
+
+    def pass_on(step):
+        right, left = from_left[-1], from_right[-1]
         right = lax.ppermute(right, "head", [(i, i + 1) for i in range(step - 1, count - 1)])
         left = lax.ppermute(left, "head", [(i, i - 1) for i in range(1, count - step + 1)])
         from_left.append(right)
         from_right.append(left)
 
-    near, three, four = pool_call(key, value)
+    def send_on(step, left, right):
+        return (
+            lax.ppermute(left, "head", [(i, i - 1) for i in range(count - step, count)]),
+            lax.ppermute(right, "head", [(i, i + 1) for i in range(0, step)]),
+        )
+
+    def chunks_of(group):
+        return [(cotangent,) if s == 0 else (from_left[s], from_right[count - s]) for s in group]
+
+    back_by = lambda group: tuple(-s % count for s in group)
+
+    pass_on(1)
+    if OPT.get("x0"):
+        tiny = swap(key[:16, :128], "ctx", 1)
+        key_in = lax.optimization_barrier((key, tiny))[0]
+    else:
+        key_in = key
+    near, three, four = pool_call(key_in, value)
     three = swap(three, "ctx", 2)
     four_a = swap(four, "ctx", 4)
     four_b = swap(four, "ctx", 6)
-    near = swap(lower_call(near, three, four_a, four_b), "ctx", 1)
+    near = lower_call(near, three, four_a, four_b)
+    if OPT.get("bar"):
+        near, from_left[1], from_right[1] = lax.optimization_barrier((near, from_left[1], from_right[1]))
+    if OPT.get("bar2"):
+        lower, from_left[1], from_right[1] = lax.optimization_barrier((near, from_left[1], from_right[1]))
+        received_after = (lower,)
+    near = swap(near, "ctx", 1)
+    if OPT.get("bar3"):
+        near, from_left[1], from_right[1] = lax.optimization_barrier((near, from_left[1], from_right[1]))
     received = (near, three, four_a, four_b)
 
-    attn, turned, lse, tops = forward_call(query, key, value, received)
+    attn, turned, lse, tops = forward_call(query, key, value, received, after=((place,) if OPT.get("fp") else ()) + ((lower,) if OPT.get("bar2f") else ()) + ((from_left[1], from_right[1]) if OPT.get("f") else ()))
+    if OPT.get("barF"):
+        attn, from_left[1], from_right[1] = lax.optimization_barrier((attn, from_left[1], from_right[1]))
+    pass_on(2)
     turned_other = swap(turned, "ctx", 1)
-
-    def chunk(*distances):
-        return jnp.stack([lax.rem(z + d + count, count) for d in distances])
-
-    sums = ()
-    summed = []
-    for step in range(1, count):
-        left, right = project_call(attn, out_weight, chunk(step, -step), sums)
-        left = lax.ppermute(left, "head", [(i, i - 1) for i in range(count - step, count)])
-        right = lax.ppermute(right, "head", [(i, i + 1) for i in range(0, step)])
-        sums = (left, right)
-        summed.append(sums)
-    mixed = mixed_call(attn, out_weight, chunk(0), *sums)
-
-    core = me % 2
-    early = [s for s in range(count) if s not in (1, count - 1)]
-    late = sorted({1, count - 1})
-    grad_attn = None
-    columns = []
-    for group in (early, late):
-        chunks = [(cotangent,) if s == 0 else (from_left[s], from_right[count - s]) for s in group]
-        mine, send = split_call(chunks, core, column, after=() if group is early else summed[0])
-        columns.append((mine, swap(send, "ctx", 1)))
-        dtype = F32 if group is early else BF16
-        grad_attn = grad_call(chunks, out_weight, chunk(*[-s for s in group]), grad_attn, dtype)
-
-    chips = ctx_count // 2
-    per_chunk = chips // count
-    slots = {s: n for n, s in enumerate(early + late)}
-    slot = jnp.array([slots[s] for s in range(count)], jnp.int32)
-    order = term_order(chips)
-    chip = jnp.bitwise_xor(me // 2, jnp.array(order, jnp.int32))
-    place = slot[lax.rem(z - chip // per_chunk + count, count)] * per_chunk + chip % per_chunk
-    terms = term_call(turned, turned_other, *columns, place.astype(jnp.int32), column)
+    lm = OPT.get("lm")
+    def lmax(after):
+        level_max = jnp.transpose((held_back(tops, after) if after else tops)[:, :LEVELS, 0])
+        mask = 1
+        while mask < ctx_count:
+            level_max = jnp.maximum(level_max, swap(level_max, "ctx", mask))
+            mask *= 2
+        return level_max
+    if lm == 3:
+        level_max = lmax((turned_other,))
+    if lm == 4:
+        level_max = lmax(())
+    products = product_call(attn, out_weight, place, count, after=(turned_other,) if OPT.get("p2") else ())
+    left, right = send_on(1, products[1], products[count - 1])
+    for step in range(3, count):
+        pass_on(step)
+    chunks = chunks_of(early)
+    mine, send = split_call(chunks, core, column, after=(products[1],) if OPT.get("se") else ())
+    theirs = swap(send, "ctx", 1)
+    grad_attn = grad_call(chunks, out_weight, place, back_by(early), None, F32)
+    terms = term_call(turned, turned_other, mine, theirs, place, column)
+
+    chunks = chunks_of(late)
+    if lm == 1:
+        level_max = lmax((terms, grad_attn))
+    first_arrived = (left, right)
+    for step in range(2, count - 1):
+        sums = add_call((products[step], left), (products[count - step], right))
+        left, right = send_on(step, *sums)
+    mine, send = split_call(chunks, core, column, after=((terms, grad_attn) if OPT.get("sl") else ()) + ((level_max,) if lm == 1 else ()) + (first_arrived if OPT.get("slr") else ()) + (tuple(sums) if OPT.get("sa") else ()) + ())
+    theirs = swap(send, "ctx", 1)
+    terms = late_call(turned, turned_other, mine, theirs, terms, place, count, chips, column, sums if OPT.get("t") else ())
+    grad_attn = grad_call(
+        chunks, out_weight, place, back_by(late), grad_attn, BF16, after=terms if OPT.get("g") else ()
+    )
     half, quarter = chips // 2, chips // 4
-    bits = [1 << n for n in range(chips.bit_length() - 1)]
-    top = halve((order[:half], terms[0]), (order[half:], terms[1]), bits)
-    bottom = halve(
-        (order[quarter : 3 * quarter], terms[2]),
-        (order[:quarter] + order[3 * quarter :], terms[3]),
-        bits[::-1],
-    )
-    weight_grad = total_call(top, bottom)
-
-    outs = backward_call(query, key, value, attn, grad_attn, lse, received, after=terms)
+    first = [swap(terms[0], "ctx", 2 * bits[0]), swap(terms[2], "ctx", 2 * bits[-1])]
+    if lm == 2:
+        level_max = lmax((terms[0],))
+    outs = backward_call(query, key, value, attn, grad_attn, lse, received, after=(tuple(terms) if OPT.get("b") else ()) + ((level_max,) if lm == 2 else ()) + ((left, right) if OPT.get("bl") else ()))
+
+    sums = add_call((products[count - 1], left), (products[1], right))
+    if OPT.get("b3"):
+        sums, first = lax.optimization_barrier((tuple(sums), first))
+    left, right = send_on(count - 1, *sums)
+    ways = [bits, bits[::-1]]
+    sent = [order[:half], order[quarter : 3 * quarter]]
+    held = [order[half:], order[:quarter] + order[3 * quarter :]]
+    kept = [terms[1], terms[3]]
+    for n in range(len(bits) - 1):
+        folded = fold_call(
+            [
+                (sent[k], first[k], held[k], kept[k], ways[k][n], ways[k][n + 1])
+                for k in (0, 1)
+            ]
+        )
+        sent, held = [[f[0][k] for f in folded] for k in (0, 1)]
+        kept = [f[1][1] for f in folded]
+        first = [swap(f[1][0], "ctx", 2 * ways[k][n + 1]) for k, f in enumerate(folded)]
+    top, bottom = [(kept[k][0], first[k][0]) for k in (0, 1)]
     grad_q, grad_k, grad_v, far, keep, four = outs
     far = swap(far, "ctx", 1)
     third = BLK + BLK // 2
-    back = swap((keep.astype(F32) + far[2 * BLK : 2 * BLK + third]).astype(BF16), "ctx", 2)
-    four = four.astype(F32) + far[2 * BLK + third :] + back[BLK:]
-    four = swap(four.astype(BF16), "ctx", 4)
+    if OPT.get("ret2"):
+        sums3 = (keep.astype(F32) + far[2 * BLK : 2 * BLK + third]).astype(BF16)
+        sums4 = (four.astype(F32) + far[2 * BLK + third :]).astype(BF16)
+        back = swap(sums3[:BLK], "ctx", 2)
+        four = (swap(sums4, "ctx", 4), swap(sums3[BLK:], "ctx", 6))
+        four = (four[0].astype(F32) + four[1]).astype(BF16)
+    else:
+      back = swap((keep.astype(F32) + far[2 * BLK : 2 * BLK + third]).astype(BF16), "ctx", 2)
+      four = four.astype(F32) + far[2 * BLK + third :] + back[BLK:]
+      four = swap(four.astype(BF16), "ctx", 4)
+    weight_grad = total_call(top, bottom)
+    mixed = last_call(products[0], left, right)
     grad_k, grad_v = finish_call(grad_k, grad_v, far, back, four)
 
-    level_max = jnp.transpose(tops[:, :LEVELS, 0])
-    mask = 1
-    while mask < ctx_count:
-        level_max = jnp.maximum(level_max, swap(level_max, "ctx", mask))
-        mask *= 2
+    if lm == 0:
+        level_max = lmax((terms[0],))
     return mixed, grad_q, grad_k, grad_v, weight_grad, level_max
 
 

time: 204 us -> 181 us (0.89)
  Pallas kernels: 95.6 us -> 71.1 us
  local copies, waits for them, and re-layouts: 6.25 us -> 17.3 us
  other arithmetic: 8.14 us -> 0.19 us
    ppermute x12, waiting for transfers between devices: 21.9 us -> 9.09 us  [the longest x3 5.77 us: pass_on(): lax.ppermute(left, 'head', [(i, i - 1) for i in range(1, count - step + 1)])]
    ppermute x17, waiting for transfers between devices: 20.7 us -> 32.6 us  [swap(): lax.ppermute(value, axis, [(i, i ^ mask) for i in range(lax.axis_size(axi...]
    pallas_call x5 -> x8, Pallas kernels: 37.9 us -> 26.1 us  [the longest x1 8 us: product_call(): pl.pallas_call(functools.partial(product_kernel, count=count), grid_spec=...]
    unnamed x43 -> x66, local copies, waits for them, and re-layouts: 4.97 us -> 15.7 us
    convert_element_type x2 -> x0, other arithmetic: 4.87 us -> none  [added(): return (here, jnp.stack([p.astype(BF16) for p in parts]))]
    pallas_call x2, Pallas kernels: 15.6 us -> 11.1 us  [grad_call(): pl.pallas_call(functools.partial(grad_kernel, pairs=tuple((len(c) for c i...]
    ppermute x17, starting transfers between devices: 16.3 us -> 12.4 us  [swap(): lax.ppermute(value, axis, [(i, i ^ mask) for i in range(lax.axis_size(axi...]
    another operation x5 -> x0, other arithmetic: 3.06 us -> none  [chunk(): return jnp.stack([lax.rem(z + d + count, count) for d in distances])]
  transfers between devices with their start and end apart: 29 -> 29, of which waited for: 9 -> 12; matrix products, arithmetic and copies ran while one was open for 5% -> 1% of each run, Pallas kernels for 45% -> 37%
where the time goes in v3:
time: 181 us; the launch traced here: 180 us
  Pallas kernels  71.1 us (39%)
  starting transfers between devices  48.3 us (27%)
  waiting for transfers between devices  41.7 us (23%)
  local copies, waits for them, and re-layouts  17.3 us (10%)
    ppermute x17, waiting for transfers between devices, swap(): lax.ppermute(value, axis, [(i, i ^ mask) for i in range(lax.axis_size(axi...  32.6 us
    ppermute x3, starting transfers between devices, send_on(): lax.ppermute(right, 'head', [(i, i + 1) for i in range(0, step)])  18.9 us
    unnamed x66, local copies, waits for them, and re-layouts  15.7 us
    ppermute x17, starting transfers between devices, swap(): lax.ppermute(value, axis, [(i, i ^ mask) for i in range(lax.axis_size(axi...  12.4 us
    pallas_call x1, Pallas kernels, backward_call(): pl.pallas_call(functools.partial(backward_kernel, extra=len(after)), grid...  12 us
    pallas_call x2, Pallas kernels, grad_call(): pl.pallas_call(functools.partial(grad_kernel, pairs=tuple((len(c) for c i...  11.1 us
    pallas_call x1, Pallas kernels, forward_call(): pl.pallas_call(functools.partial(forward_kernel, extra=len(after)), grid=...  10.1 us
    ppermute x3, starting transfers between devices, pass_on(): lax.ppermute(right, 'head', [(i, i + 1) for i in range(step - 1, count -...  9.32 us
  transfers between devices with their start and end apart: 29, of which 12 were waited for; matrix products, arithmetic and copies ran while one was open for 1% of the time, Pallas kernels for 37%

profile of v3, /device:TPU:0, one launch (start us, length us, event | category | flops | bytes accessed | tf_op | source)
XLA Modules:
  0.0 179.7 jit_solution(13746997482995926049)
XLA Ops:
  0.6 5.9 %collective-permute-start.3 = (bf16[512,1024]{1,0:T(8,128)(2,1)}, bf16[512,1024]{1,0:T(8,128)(2,1)}, u32[]{:S(2)}, u32[]{:S(2)}) collective-permute-start(bf16[512,1024]{1,0:T(8,128)(2,1)} %refs_0_.5), channel_id=1, source_target_pairs={{0,1},{1,2},{2,3},{4,5},{5,6},{6,7},{8,9},{9,10},{10,11},{12,13},{... | collective-permute-start | bytes 3145736 | tf_op jit(solution)/shard_map/ppermute | solution.py:793
  6.6 1.3 collective-permute-start.4
  9.1 1.2 copy-done.9
  10.3 1.7 pool_keys.1
  12.0 1.5 collective-permute-start
  13.5 1.5 collective-permute-start.1
  15.5 3.0 %collective-permute-done.1.four_a = bf16[64,1024]{1,0:T(8,128)(2,1)S(1)} collective-permute-done((bf16[64,1024]{1,0:T(8,128)(2,1)S(1)}, bf16[64,1024]{1,0:T(8,128)(2,1)S(1)}, u32[]{:S(2)}, u32[]{:S(2)}) %collective-permute-start.1) | collective-permute-done | bytes 131104 | tf_op jit(solution)/shard_map/ppermute | solution.py:759
  18.4 5.1 %collective-permute-done.2.four_b = bf16[64,1024]{1,0:T(8,128)(2,1)S(1)} collective-permute-done((bf16[64,1024]{1,0:T(8,128)(2,1)S(1)}, bf16[64,1024]{1,0:T(8,128)(2,1)S(1)}, u32[]{:S(2)}, u32[]{:S(2)}) %collective-permute-start.2) | collective-permute-done | bytes 131104 | tf_op jit(solution)/shard_map/ppermute | solution.py:759
  25.0 3.3 %collective-permute-done.3.refs_0_ = bf16[512,1024]{1,0:T(8,128)(2,1)} collective-permute-done((bf16[512,1024]{1,0:T(8,128)(2,1)}, bf16[512,1024]{1,0:T(8,128)(2,1)}, u32[]{:S(2)}, u32[]{:S(2)}) %collective-permute-start.3) | collective-permute-done | bytes 1048608 | tf_op jit(solution)/shard_map/ppermute | solution.py:793
  28.3 5.1 %collective-permute-done.4.refs_3_ = bf16[512,1024]{1,0:T(8,128)(2,1)} collective-permute-done((bf16[512,1024]{1,0:T(8,128)(2,1)}, bf16[512,1024]{1,0:T(8,128)(2,1)}, u32[]{:S(2)}, u32[]{:S(2)}) %collective-permute-start.4) | collective-permute-done | bytes 1048608 | tf_op jit(solution)/shard_map/ppermute | solution.py:794
  33.4 1.3 collective-permute-start.11
  34.7 1.7 collective-permute-start.13
  38.0 10.1 %attention_forward.1 = (bf16[512,1024]{1,0:T(8,128)(2,1)S(1)}, bf16[1024,512]{1,0:T(8,128)(2,1)}, f32[512,1024]{1,0:T(8,128)S(1)}, f32[8,8,128]{2,1,0:T(8,128)S(1)}) custom-call(bf16[512,1024]{1,0:T(8,128)(2,1)S(1)} %copy-done.13, bf16[512,1024]{1,0:T(8,128)(2,1)S(1)} %copy-done.8, bf16[512,1024]{1,0:T(8,128)(2,1)S(1)} %copy-done.10, ...), custom_call_target="tpu_custom_call" | custom-call | tf_op jit(solution)/shard_map/attention_forward/pallas_call | solution.py:225
  49.1 1.3 copy-done.22
  51.6 3.4 %copy-done = bf16[1024,4096]{1,0:T(8,128)(2,1)S(1)} copy-done((bf16[1024,4096]{1,0:T(8,128)(2,1)S(1)}, bf16[1024,4096]{1,0:T(8,128)(2,1)}, u32[]{:S(2)}) %copy-start) | copy-done | bytes 8388632
  56.2 8.0 %mixed_products.1 = (bf16[512,1024]{1,0:T(8,128)(2,1)S(1)}, bf16[512,1024]{1,0:T(8,128)(2,1)}, bf16[512,1024]{1,0:T(8,128)(2,1)S(1)}, bf16[512,1024]{1,0:T(8,128)(2,1)}) custom-call(s32[8]{0:T(128)S(1)} %dynamic-slice_bitcast_fusion.rest_0_.place_ref, bf16[512,1024]{1,0:T(8,128)(2,1)S(1)} %copy-done.16, bf16[1024,4096]{1,0:T(8,128)(2,1)S(1)} %copy-done, ...), custom_call_target="tpu_custom_call" | custom-call | tf_op jit(solution)/shard_map/mixed_products/pallas_call | solution.py:542
  64.2 2.4 %split_columns.2 = (bf16[512,1024]{1,0:T(8,128)(2,1)S(1)}, bf16[512,1024]{1,0:T(8,128)(2,1)S(1)}) custom-call(s32[1]{0:T(128)} %bitcast.1.core_ref, bf16[512,1024]{1,0:T(8,128)(2,1)S(1)} %copy-done.12, bf16[512,1024]{1,0:T(8,128)(2,1)} %collective-permute-done.13.refs_1_, bf16[512,1024]{1,0:T(8,128)(2,1)} %collective-permute-done.11.refs_2_, ...), custom_call_target="tpu_custom_call" | custom-call | tf_op jit(solution)/shard_map/split_columns/pallas_call | solution.py:471
  66.7 1.6 collective-permute-start.6
  68.3 8.4 %collective-permute-start.7 = (bf16[512,1024]{1,0:T(8,128)(2,1)}, bf16[512,1024]{1,0:T(8,128)(2,1)}, u32[]{:S(2)}, u32[]{:S(2)}) collective-permute-start(bf16[512,1024]{1,0:T(8,128)(2,1)} %get-tuple-element.54.left_a), channel_id=1, source_target_pairs={{0,1},{4,5},{8,9},{12,13},{16,17},{20,21},{24,25},{28,29}} | collective-permute-start | bytes 3145736 | tf_op jit(solution)/shard_map/ppermute | solution.py:801
  76.7 1.3 collective-permute-start.12
  78.0 1.7 collective-permute-start.14
  79.7 5.0 %grad_products.2.refs_1_.refs_5_.refs_6_ = f32[512,1024]{1,0:T(8,128)S(1)} custom-call(s32[8]{0:T(128)S(1)} %dynamic-slice_bitcast_fusion.rest_0_.place_ref, bf16[512,1024]{1,0:T(8,128)(2,1)S(1)} %copy-done.12, bf16[512,1024]{1,0:T(8,128)(2,1)} %collective-permute-done.13.refs_1_, bf16[512,1024]{1,0:T(8,128)(2,1)} %collective-permute-done.11.refs_2_, ...), custom_call_target="tpu_custom_call" | custom-call | tf_op jit(solution)/shard_map/grad_products/pallas_call | solution.py:512
  84.7 5.1 %weight_terms.1.refs_0_.refs_4_.early_ref = bf16[2,1024,512]{2,1,0:T(8,128)(2,1)S(1)} custom-call(s32[8]{0:T(128)S(1)} %dynamic-slice_bitcast_fusion.rest_0_.place_ref, bf16[1024,512]{1,0:T(8,128)(2,1)} %get-tuple-element.61.own_ref, bf16[1024,512]{1,0:T(8,128)(2,1)S(1)} %collective-permute-done.10.other_ref, ...), custom_call_target="tpu_custom_call" | custom-call | tf_op jit(solution)/shard_map/weight_terms/pallas_call | solution.py:610
  89.8 1.3 copy-done.2
  91.1 1.5 held_back.1
  94.7 1.5 collective-permute-start.17
  96.2 2.1 %collective-permute-done.17 = f32[5,8]{1,0:T(8,128)S(1)} collective-permute-done((f32[5,8]{1,0:T(8,128)S(1)}, f32[5,8]{1,0:T(8,128)S(1)}, u32[]{:S(2)}, u32[]{:S(2)}) %collective-permute-start.17) | collective-permute-done | bytes 192 | tf_op jit(solution)/shard_map/ppermute | solution.py:759
  98.3 1.5 collective-permute-start.18
  101.1 1.9 %mixed_add.2 = (bf16[512,1024]{1,0:T(8,128)(2,1)S(1)}, bf16[512,1024]{1,0:T(8,128)(2,1)S(1)}) custom-call(bf16[512,1024]{1,0:T(8,128)(2,1)S(1)} %copy-done.21, bf16[512,1024]{1,0:T(8,128)(2,1)} %collective-permute-done.6.left_b, bf16[512,1024]{1,0:T(8,128)(2,1)S(1)} %copy-done.21, bf16[512,1024]{1,0:T(8,128)(2,1)} %collective-permute-done.7.right_b), custom_call_target="tpu_custom_call" | custom-call | tf_op jit(solution)/shard_map/mixed_add/pallas_call | solution.py:569
  103.7 1.6 copy-done.5
  105.3 2.4 %split_columns.3 = (bf16[512,1024]{1,0:T(8,128)(2,1)S(1)}, bf16[512,1024]{1,0:T(8,128)(2,1)S(1)}) custom-call(s32[1]{0:T(128)} %bitcast.1.core_ref, bf16[512,1024]{1,0:T(8,128)(2,1)} %collective-permute-done.3.refs_0_, bf16[512,1024]{1,0:T(8,128)(2,1)} %collective-permute-done.12.refs_1_, bf16[512,1024]{1,0:T(8,128)(2,1)} %collective-permute-done.14.refs_2_, ...), custom_call_target="tpu_custom_call" | custom-call | tf_op jit(solution)/shard_map/split_columns/pallas_call | solution.py:471
  108.7 5.6 %collective-permute-start.9 = (bf16[512,1024]{1,0:T(8,128)(2,1)S(1)}, bf16[512,1024]{1,0:T(8,128)(2,1)S(1)}, u32[]{:S(2)}, u32[]{:S(2)}) collective-permute-start(bf16[512,1024]{1,0:T(8,128)(2,1)S(1)} %get-tuple-element.58.refs_8_), channel_id=1, source_target_pairs={{0,1},{1,2},{4,5},{5,6},{8,9},{9,10},{12,13},{13,14},{16,17},{17,1... | collective-permute-start | bytes 3145736 | tf_op jit(solution)/shard_map/ppermute | solution.py:801
  114.4 5.3 %weight_terms_late.1 = (bf16[2,512,512]{2,1,0:T(8,128)(2,1)S(1)}, bf16[2,512,512]{2,1,0:T(8,128)(2,1)S(1)}, bf16[2,512,512]{2,1,0:T(8,128)(2,1)S(1)}, bf16[2,512,512]{2,1,0:T(8,128)(2,1)S(1)}) custom-call(s32[8]{0:T(128)S(1)} %dynamic-slice_bitcast_fusion.rest_0_.place_ref, bf16[1024,512]{1,0:T(8,128)(2,1)} %get-tuple-element.61.own_ref, ...), custom_call_target="tpu_custom_call" | custom-call | tf_op jit(solution)/shard_map/weight_terms_late/pallas_call | solution.py:674
  119.7 1.6 collective-permute-start.20
  122.0 6.1 %grad_products.3.grad_ref = bf16[512,1024]{1,0:T(8,128)(2,1)S(1)} custom-call(s32[8]{0:T(128)S(1)} %dynamic-slice_bitcast_fusion.rest_0_.place_ref, bf16[512,1024]{1,0:T(8,128)(2,1)} %collective-permute-done.3.refs_0_, bf16[512,1024]{1,0:T(8,128)(2,1)} %collective-permute-done.12.refs_1_, bf16[512,1024]{1,0:T(8,128)(2,1)} %collective-permute-done.14.refs_2_, ...), custom_call_target="tpu_custom_call" | custom-call | tf_op jit(solution)/shard_map/grad_products/pallas_call | solution.py:512
  128.1 12.0 %attention_backward.1 = (f32[512,1024]{1,0:T(8,128)}, bf16[512,1024]{1,0:T(8,128)(2,1)S(1)}, bf16[512,1024]{1,0:T(8,128)(2,1)S(1)}, bf16[512,1024]{1,0:T(8,128)(...) custom-call(bf16[512,1024]{1,0:T(8,128)(2,1)S(1)} %copy-done.14, bf16[512,1024]{1,0:T(8,128)(2,1)S(1)} %copy-done.8, ...), custom_call_target="tpu_custom_call" | custom-call | tf_op jit(solution)/shard_map/attention_backward/pallas_call | solution.py:389
  140.2 1.8 mixed_add.3
  142.0 3.0 %collective-permute-done.20.refs_1_ = bf16[2,512,512]{2,1,0:T(8,128)(2,1)S(1)} collective-permute-done((bf16[2,512,512]{2,1,0:T(8,128)(2,1)S(1)}, bf16[2,512,512]{2,1,0:T(8,128)(2,1)S(1)}, u32[]{:S(2)}, u32[]{:S(2)}) %collective-permute-start.20) | collective-permute-done | bytes 1048608 | tf_op jit(solution)/shard_map/ppermute | solution.py:759
  144.9 1.3 collective-permute-done.21.refs_3_
  146.2 1.3 collective-permute-start.22
  147.5 4.9 %collective-permute-start.23 = (bf16[512,1024]{1,0:T(8,128)(2,1)S(1)}, bf16[512,1024]{1,0:T(8,128)(2,1)S(1)}, u32[]{:S(2)}, u32[]{:S(2)}) collective-permute-start(bf16[512,1024]{1,0:T(8,128)(2,1)S(1)} %get-tuple-element.72), channel_id=1, source_target_pairs={{0,1},{1,2},{2,3},{4,5},{5,6},{6,7},{8,9},{9,10},{10,11},{12,13},{... | collective-permute-start | bytes 3145736 | tf_op jit(solution)/shard_map/ppermute | solution.py:801
  154.2 1.4 collective-permute-start.28
  155.6 9.1 %collective-permute-done.25.three = bf16[192,1024]{1,0:T(8,128)(2,1)S(1)} collective-permute-done((bf16[192,1024]{1,0:T(8,128)(2,1)S(1)}, bf16[192,1024]{1,0:T(8,128)(2,1)S(1)}, u32[]{:S(2)}, u32[]{:S(2)}) %collective-permute-start.25) | collective-permute-done | bytes 393248 | tf_op jit(solution)/shard_map/ppermute | solution.py:759
  165.2 1.8 %collective-permute-done.27 = bf16[1,512,512]{2,1,0:T(8,128)(2,1)S(1)} collective-permute-done((bf16[1,512,512]{2,1,0:T(8,128)(2,1)S(1)}, bf16[1,512,512]{2,1,0:T(8,128)(2,1)S(1)}, u32[]{:S(2)}, u32[]{:S(2)}) %collective-permute-start.27) | collective-permute-done | bytes 524320 | tf_op jit(solution)/shard_map/ppermute | solution.py:759
  167.0 6.2 %collective-permute-done.28 = bf16[1,512,512]{2,1,0:T(8,128)(2,1)S(1)} collective-permute-done((bf16[1,512,512]{2,1,0:T(8,128)(2,1)S(1)}, bf16[1,512,512]{2,1,0:T(8,128)(2,1)S(1)}, u32[]{:S(2)}, u32[]{:S(2)}) %collective-permute-start.28) | collective-permute-done | bytes 524320 | tf_op jit(solution)/shard_map/ppermute | solution.py:759
  173.2 1.5 weight_total.1
  174.7 3.0 %add_returned.1 = (f32[512,1024]{1,0:T(8,128)}, f32[512,1024]{1,0:T(8,128)}) custom-call(bf16[512,1024]{1,0:T(8,128)(2,1)S(1)} %get-tuple-element.77.gk_ref, bf16[512,1024]{1,0:T(8,128)(2,1)S(1)} %get-tuple-element.78.gv_ref, bf16[512,1024]{1,0:T(8,128)(2,1)S(1)} %collective-permute-done.24.near, bf16[192,1024]{1,0:T(8,128)(2,1)S(1)} %collective-permute-done.25.three, ...), custom_call_target="tpu_custom_call" | custom-call | tf_op jit(solution)/shard_map/add_returned/pallas_call | solution.py:431
  177.8 2.0 %mixed_last.1 = f32[512,1024]{1,0:T(8,128)} custom-call(bf16[512,1024]{1,0:T(8,128)(2,1)S(1)} %copy-done.28, bf16[512,1024]{1,0:T(8,128)(2,1)S(1)} %collective-permute-done.22.left, bf16[512,1024]{1,0:T(8,128)(2,1)S(1)} %collective-permute-done.23.right), custom_call_target="tpu_custom_call" | custom-call | tf_op jit(solution)/shard_map/mixed_last/pallas_call | solution.py:587
  (102 shorter events, 16.1 us)
Async XLA Ops:
  0.6 27.7 %collective-permute-start.3 = (bf16[512,1024]{1,0:T(8,128)(2,1)}, bf16[512,1024]{1,0:T(8,128)(2,1)}, u32[]{:S(2)}, u32[]{:S(2)}) collective-permute-start(bf16[512,1024]{1,0:T(8,128)(2,1)} %refs_0_.5), channel_id=1, source_target_pairs={{0,1},{1,2},{2,3},{4,5},{5,6},{6,7},{8,9},{9,10},{10,11},{12,13},{... | collective-permute-start | bytes 3145736 | tf_op jit(solution)/shard_map/ppermute | solution.py:793
  6.6 26.8 %collective-permute-start.4 = (bf16[512,1024]{1,0:T(8,128)(2,1)}, bf16[512,1024]{1,0:T(8,128)(2,1)}, u32[]{:S(2)}, u32[]{:S(2)}) collective-permute-start(bf16[512,1024]{1,0:T(8,128)(2,1)} %refs_0_.5), channel_id=1, source_target_pairs={{1,0},{2,1},{3,2},{5,4},{6,5},{7,6},{9,8},{10,9},{11,10},{13,12},{... | collective-permute-start | bytes 3145736 | tf_op jit(solution)/shard_map/ppermute | solution.py:794
  10.3 26.8 %copy-start.8 = (bf16[512,1024]{1,0:T(8,128)(2,1)S(1)}, bf16[512,1024]{1,0:T(8,128)(2,1)}, u32[]{:S(2)}) copy-start(bf16[512,1024]{1,0:T(8,128)(2,1)} %k_ref.5) | copy-start | bytes 3145732
  10.3 26.8 %copy-start.10 = (bf16[512,1024]{1,0:T(8,128)(2,1)S(1)}, bf16[512,1024]{1,0:T(8,128)(2,1)}, u32[]{:S(2)}) copy-start(bf16[512,1024]{1,0:T(8,128)(2,1)} %v_ref.5) | copy-start | bytes 3145732
  10.3 26.8 %copy-start.13 = (bf16[512,1024]{1,0:T(8,128)(2,1)S(1)}, bf16[512,1024]{1,0:T(8,128)(2,1)}, u32[]{:S(2)}) copy-start(bf16[512,1024]{1,0:T(8,128)(2,1)} %q_ref.3) | copy-start | bytes 3145732
  12.0 11.5 %collective-permute-start = (bf16[128,1024]{1,0:T(8,128)(2,1)S(1)}, bf16[128,1024]{1,0:T(8,128)(2,1)S(1)}, u32[]{:S(2)}, u32[]{:S(2)}) collective-permute-start(bf16[128,1024]{1,0:T(8,128)(2,1)S(1)} %get-tuple-element.49), channel_id=1, source_target_pairs={{0,8},{4,12},{8,0},{12,4},{16,24},{20,28},{24,16},{28,20},{1,9},{5... | collective-permute-start | bytes 786440 | tf_op jit(solution)/shard_map/ppermute | solution.py:759
  13.5 5.0 %collective-permute-start.1 = (bf16[64,1024]{1,0:T(8,128)(2,1)S(1)}, bf16[64,1024]{1,0:T(8,128)(2,1)S(1)}, u32[]{:S(2)}, u32[]{:S(2)}) collective-permute-start(bf16[64,1024]{1,0:T(8,128)(2,1)S(1)} %get-tuple-element.50), channel_id=1, source_target_pairs={{0,16},{4,20},{8,24},{12,28},{16,0},{20,4},{24,8},{28,12},{1,17},{... | collective-permute-start | bytes 393224 | tf_op jit(solution)/shard_map/ppermute | solution.py:759
  15.0 8.5 %collective-permute-start.2 = (bf16[64,1024]{1,0:T(8,128)(2,1)S(1)}, bf16[64,1024]{1,0:T(8,128)(2,1)S(1)}, u32[]{:S(2)}, u32[]{:S(2)}) collective-permute-start(bf16[64,1024]{1,0:T(8,128)(2,1)S(1)} %get-tuple-element.50), channel_id=1, source_target_pairs={{0,24},{4,28},{8,16},{12,20},{16,8},{20,12},{24,0},{28,4},{1,25},{... | collective-permute-start | bytes 393224 | tf_op jit(solution)/shard_map/ppermute | solution.py:759
  33.4 3.7 %collective-permute-start.5 = (bf16[512,1024]{1,0:T(8,128)(2,1)}, bf16[512,1024]{1,0:T(8,128)(2,1)}, u32[]{:S(2)}, u32[]{:S(2)}) collective-permute-start(bf16[512,1024]{1,0:T(8,128)(2,1)} %lower_rows.1), channel_id=1, source_target_pairs={{0,4},{4,0},{8,12},{12,8},{16,20},{20,16},{24,28},{28,24},{1,5},{5... | collective-permute-start | bytes 3145736 | tf_op jit(solution)/shard_map/ppermute | solution.py:759
  33.4 30.8 %collective-permute-start.11 = (bf16[512,1024]{1,0:T(8,128)(2,1)}, bf16[512,1024]{1,0:T(8,128)(2,1)}, u32[]{:S(2)}, u32[]{:S(2)}) collective-permute-start(bf16[512,1024]{1,0:T(8,128)(2,1)} %collective-permute-done.4.refs_3_), channel_id=1, source_target_pairs={{1,0},{2,1},{5,4},{6,5},{9,8},{10,9},{13,12},{14,13},{17,16},{18,1... | collective-permute-start | bytes 3145736 | tf_op jit(solution)/shard_map/ppermute | solution.py:794
  34.7 29.5 %collective-permute-start.13 = (bf16[512,1024]{1,0:T(8,128)(2,1)}, bf16[512,1024]{1,0:T(8,128)(2,1)}, u32[]{:S(2)}, u32[]{:S(2)}) collective-permute-start(bf16[512,1024]{1,0:T(8,128)(2,1)} %collective-permute-done.3.refs_0_), channel_id=1, source_target_pairs={{1,2},{2,3},{5,6},{6,7},{9,10},{10,11},{13,14},{14,15},{17,18},{18... | collective-permute-start | bytes 3145736 | tf_op jit(solution)/shard_map/ppermute | solution.py:793
  51.1 26.9 %collective-permute-start.10 = (bf16[1024,512]{1,0:T(8,128)(2,1)}, bf16[1024,512]{1,0:T(8,128)(2,1)S(1)}, u32[]{:S(2)}, u32[]{:S(2)}) collective-permute-start(bf16[1024,512]{1,0:T(8,128)(2,1)} %get-tuple-element.61.own_ref), channel_id=1, source_target_pairs={{0,4},{4,0},{8,12},{12,8},{16,20},{20,16},{24,28},{28,24},{1,5},{5... | collective-permute-start | bytes 3145736 | tf_op jit(solution)/shard_map/ppermute | solution.py:759
  51.6 3.4 %copy-start = (bf16[1024,4096]{1,0:T(8,128)(2,1)S(1)}, bf16[1024,4096]{1,0:T(8,128)(2,1)}, u32[]{:S(2)}) copy-start(bf16[1024,4096]{1,0:T(8,128)(2,1)} %refs_5_.1) | copy-start | bytes 25165828
  56.2 8.0 %copy-start.12 = (bf16[512,1024]{1,0:T(8,128)(2,1)S(1)}, bf16[512,1024]{1,0:T(8,128)(2,1)}, u32[]{:S(2)}) copy-start(bf16[512,1024]{1,0:T(8,128)(2,1)} %refs_0_.5) | copy-start | bytes 3145732
  56.2 23.5 %copy-start.1 = (bf16[1024,4096]{1,0:T(8,128)(2,1)S(1)}, bf16[1024,4096]{1,0:T(8,128)(2,1)}, u32[]{:S(2)}) copy-start(bf16[1024,4096]{1,0:T(8,128)(2,1)} %refs_5_.1) | copy-start | bytes 25165828
  66.6 18.1 %collective-permute-start.15 = (bf16[512,1024]{1,0:T(8,128)(2,1)S(1)}, bf16[512,1024]{1,0:T(8,128)(2,1)S(1)}, u32[]{:S(2)}, u32[]{:S(2)}) collective-permute-start(bf16[512,1024]{1,0:T(8,128)(2,1)S(1)} %get-tuple-element.65), channel_id=1, source_target_pairs={{0,4},{4,0},{8,12},{12,8},{16,20},{20,16},{24,28},{28,24},{1,5},{5... | collective-permute-start | bytes 3145736 | tf_op jit(solution)/shard_map/ppermute | solution.py:759
  66.7 33.1 %collective-permute-start.6 = (bf16[512,1024]{1,0:T(8,128)(2,1)}, bf16[512,1024]{1,0:T(8,128)(2,1)}, u32[]{:S(2)}, u32[]{:S(2)}) collective-permute-start(bf16[512,1024]{1,0:T(8,128)(2,1)} %get-tuple-element.56.right_a.refs_3_), channel_id=1, source_target_pairs={{3,2},{7,6},{11,10},{15,14},{19,18},{23,22},{27,26},{31,30}} | collective-permute-start | bytes 3145736 | tf_op jit(solution)/shard_map/ppermute | solution.py:800
  68.3 31.5 %collective-permute-start.7 = (bf16[512,1024]{1,0:T(8,128)(2,1)}, bf16[512,1024]{1,0:T(8,128)(2,1)}, u32[]{:S(2)}, u32[]{:S(2)}) collective-permute-start(bf16[512,1024]{1,0:T(8,128)(2,1)} %get-tuple-element.54.left_a), channel_id=1, source_target_pairs={{0,1},{4,5},{8,9},{12,13},{16,17},{20,21},{24,25},{28,29}} | collective-permute-start | bytes 3145736 | tf_op jit(solution)/shard_map/ppermute | solution.py:801
  76.7 27.0 %collective-permute-start.12 = (bf16[512,1024]{1,0:T(8,128)(2,1)}, bf16[512,1024]{1,0:T(8,128)(2,1)}, u32[]{:S(2)}, u32[]{:S(2)}) collective-permute-start(bf16[512,1024]{1,0:T(8,128)(2,1)} %collective-permute-done.11.refs_2_), channel_id=1, source_target_pairs={{1,0},{5,4},{9,8},{13,12},{17,16},{21,20},{25,24},{29,28}} | collective-permute-start | bytes 3145736 | tf_op jit(solution)/shard_map/ppermute | solution.py:794
  78.0 6.7 %copy-start.18 = (bf16[1024,512]{1,0:T(8,128)(2,1)}, bf16[1024,512]{1,0:T(8,128)(2,1)S(1)}, u32[]{:S(2)}) copy-start(bf16[1024,512]{1,0:T(8,128)(2,1)S(1)} %collective-permute-done.10.other_ref) | copy-start | bytes 3145732
  78.0 25.7 %collective-permute-start.14 = (bf16[512,1024]{1,0:T(8,128)(2,1)}, bf16[512,1024]{1,0:T(8,128)(2,1)}, u32[]{:S(2)}, u32[]{:S(2)}) collective-permute-start(bf16[512,1024]{1,0:T(8,128)(2,1)} %collective-permute-done.13.refs_1_), channel_id=1, source_target_pairs={{2,3},{6,7},{10,11},{14,15},{18,19},{22,23},{26,27},{30,31}} | collective-permute-start | bytes 3145736 | tf_op jit(solution)/shard_map/ppermute | solution.py:793
  84.7 5.1 %copy-start.4 = (f32[512,1024]{1,0:T(8,128)}, f32[512,1024]{1,0:T(8,128)S(1)}, u32[]{:S(2)}) copy-start(f32[512,1024]{1,0:T(8,128)S(1)} %grad_products.2.refs_1_.refs_5_.refs_6_) | copy-start | bytes 6291460
  91.1 12.6 %copy-start.3 = (bf16[2,1024,512]{2,1,0:T(8,128)(2,1)S(1)}, bf16[2,1024,512]{2,1,0:T(8,128)(2,1)}, u32[]{:S(2)}) copy-start(bf16[2,1024,512]{2,1,0:T(8,128)(2,1)} %copy-done.2) | copy-start | bytes 6291460
  93.5 1.2 collective-permute-start.16
  94.7 3.6 %collective-permute-start.17 = (f32[5,8]{1,0:T(8,128)S(1)}, f32[5,8]{1,0:T(8,128)S(1)}, u32[]{:S(2)}, u32[]{:S(2)}) collective-permute-start(f32[5,8]{1,0:T(8,128)S(1)} %bitcast_maximum_fusion), channel_id=1, source_target_pairs={{0,8},{4,12},{8,0},{12,4},{16,24},{20,28},{24,16},{28,20},{1,9},{5... | collective-permute-start | bytes 488 | tf_op jit(solution)/shard_map/ppermute | solution.py:759
  98.3 4.7 %collective-permute-start.18 = (f32[5,8]{1,0:T(8,128)S(1)}, f32[5,8]{1,0:T(8,128)S(1)}, u32[]{:S(2)}, u32[]{:S(2)}) collective-permute-start(f32[5,8]{1,0:T(8,128)S(1)} %max.10), channel_id=1, source_target_pairs={{0,16},{4,20},{8,24},{12,28},{16,0},{20,4},{24,8},{28,12},{1,17},{... | collective-permute-start | bytes 488 | tf_op jit(solution)/shard_map/ppermute | solution.py:759
  101.1 20.9 %slice-start = ((s8[8388608]{0:T(1024)(128)(4,1)}), s8[4194304]{0:T(1024)(128)(4,1)S(1)}, s32[]{:S(2)}) async-start(s8[8388608]{0:T(1024)(128)(4,1)} %bitcast.12), calls=%async_computation | async-start | bytes 8388608
  103.0 4.7 %copy-start.30 = (f32[5,8]{1,0:T(8,128)}, f32[5,8]{1,0:T(8,128)S(1)}, u32[]{:S(2)}) copy-start(f32[5,8]{1,0:T(8,128)S(1)} %max.11.refs_6_) | copy-start | bytes 484
  105.3 9.1 %copy-start.19 = (bf16[1024,512]{1,0:T(8,128)(2,1)S(1)}, bf16[1024,512]{1,0:T(8,128)(2,1)}, u32[]{:S(2)}) copy-start(bf16[1024,512]{1,0:T(8,128)(2,1)} %copy-done.18) | copy-start | bytes 3145732
  105.3 16.6 %slice-start.1 = ((s8[8388608]{0:T(1024)(128)(4,1)}), s8[4194304]{0:T(1024)(128)(4,1)S(1)}, s32[]{:S(2)}) async-start(s8[8388608]{0:T(1024)(128)(4,1)} %bitcast.12), calls=%async_computation.1 | async-start | bytes 8388608
  107.7 6.6 %collective-permute-start.19 = (bf16[512,1024]{1,0:T(8,128)(2,1)S(1)}, bf16[512,1024]{1,0:T(8,128)(2,1)S(1)}, u32[]{:S(2)}, u32[]{:S(2)}) collective-permute-start(bf16[512,1024]{1,0:T(8,128)(2,1)S(1)} %get-tuple-element.68), channel_id=1, source_target_pairs={{0,4},{4,0},{8,12},{12,8},{16,20},{20,16},{24,28},{28,24},{1,5},{5... | collective-permute-start | bytes 3145736 | tf_op jit(solution)/shard_map/ppermute | solution.py:759
  107.8 32.3 %collective-permute-start.8 = (bf16[512,1024]{1,0:T(8,128)(2,1)S(1)}, bf16[512,1024]{1,0:T(8,128)(2,1)S(1)}, u32[]{:S(2)}, u32[]{:S(2)}) collective-permute-start(bf16[512,1024]{1,0:T(8,128)(2,1)S(1)} %get-tuple-element.57.refs_7_), channel_id=1, source_target_pairs={{2,1},{3,2},{6,5},{7,6},{10,9},{11,10},{14,13},{15,14},{18,17},{19... | collective-permute-start | bytes 3145736 | tf_op jit(solution)/shard_map/ppermute | solution.py:800
  108.7 31.5 %collective-permute-start.9 = (bf16[512,1024]{1,0:T(8,128)(2,1)S(1)}, bf16[512,1024]{1,0:T(8,128)(2,1)S(1)}, u32[]{:S(2)}, u32[]{:S(2)}) collective-permute-start(bf16[512,1024]{1,0:T(8,128)(2,1)S(1)} %get-tuple-element.58.refs_8_), channel_id=1, source_target_pairs={{0,1},{1,2},{4,5},{5,6},{8,9},{9,10},{12,13},{13,14},{16,17},{17,1... | collective-permute-start | bytes 3145736 | tf_op jit(solution)/shard_map/ppermute | solution.py:801
  114.4 7.6 %copy-start.6 = (f32[512,1024]{1,0:T(8,128)S(1)}, f32[512,1024]{1,0:T(8,128)}, u32[]{:S(2)}) copy-start(f32[512,1024]{1,0:T(8,128)} %copy-done.4) | copy-start | bytes 6291460
  119.7 25.2 %collective-permute-start.20 = (bf16[2,512,512]{2,1,0:T(8,128)(2,1)S(1)}, bf16[2,512,512]{2,1,0:T(8,128)(2,1)S(1)}, u32[]{:S(2)}, u32[]{:S(2)}) collective-permute-start(bf16[2,512,512]{2,1,0:T(8,128)(2,1)S(1)} %get-tuple-element.69.refs_7_.rest_0_), channel_id=1, source_target_pairs={{0,8},{4,12},{8,0},{12,4},{16,24},{20,28},{24,16},{28,20},{1,9},{5... | collective-permute-start | bytes 3145736 | tf_op jit(solution)/shard_map/ppermute | solution.py:759
  121.3 24.9 %collective-permute-start.21 = (bf16[2,512,512]{2,1,0:T(8,128)(2,1)S(1)}, bf16[2,512,512]{2,1,0:T(8,128)(2,1)S(1)}, u32[]{:S(2)}, u32[]{:S(2)}) collective-permute-start(bf16[2,512,512]{2,1,0:T(8,128)(2,1)S(1)} %get-tuple-element.70.refs_9_.rest_2_), channel_id=1, source_target_pairs={{0,16},{4,20},{8,24},{12,28},{16,0},{20,4},{24,8},{28,12},{1,17},{... | collective-permute-start | bytes 3145736 | tf_op jit(solution)/shard_map/ppermute | solution.py:759
  121.9 6.2 %copy-start.11 = (bf16[512,1024]{1,0:T(8,128)(2,1)S(1)}, bf16[512,1024]{1,0:T(8,128)(2,1)}, u32[]{:S(2)}) copy-start(bf16[512,1024]{1,0:T(8,128)(2,1)} %v_ref.5) | copy-start | bytes 3145732
  121.9 6.1 %copy-start.14 = (bf16[512,1024]{1,0:T(8,128)(2,1)S(1)}, bf16[512,1024]{1,0:T(8,128)(2,1)}, u32[]{:S(2)}) copy-start(bf16[512,1024]{1,0:T(8,128)(2,1)} %q_ref.3) | copy-start | bytes 3145732
  122.0 6.1 %copy-start.17 = (bf16[512,1024]{1,0:T(8,128)(2,1)S(1)}, bf16[512,1024]{1,0:T(8,128)(2,1)}, u32[]{:S(2)}) copy-start(bf16[512,1024]{1,0:T(8,128)(2,1)} %copy-done.15) | copy-start | bytes 3145732
  122.0 6.1 %copy-start.23 = (f32[512,1024]{1,0:T(8,128)S(1)}, f32[512,1024]{1,0:T(8,128)}, u32[]{:S(2)}) copy-start(f32[512,1024]{1,0:T(8,128)} %copy-done.22) | copy-start | bytes 6291460
  122.0 6.1 %copy-start.26 = (bf16[64,1024]{1,0:T(8,128)(2,1)S(1)}, bf16[64,1024]{1,0:T(8,128)(2,1)}, u32[]{:S(2)}) copy-start(bf16[64,1024]{1,0:T(8,128)(2,1)} %copy-done.24) | copy-start | bytes 393220
  140.2 12.3 %collective-permute-start.24 = (bf16[512,1024]{1,0:T(8,128)(2,1)S(1)}, bf16[512,1024]{1,0:T(8,128)(2,1)S(1)}, u32[]{:S(2)}, u32[]{:S(2)}) collective-permute-start(bf16[512,1024]{1,0:T(8,128)(2,1)S(1)} %get-tuple-element.79), channel_id=1, source_target_pairs={{0,4},{4,0},{8,12},{12,8},{16,20},{20,16},{24,28},{28,24},{1,5},{5... | collective-permute-start | bytes 3145736 | tf_op jit(solution)/shard_map/ppermute | solution.py:759
  146.2 31.6 %collective-permute-start.22 = (bf16[512,1024]{1,0:T(8,128)(2,1)S(1)}, bf16[512,1024]{1,0:T(8,128)(2,1)S(1)}, u32[]{:S(2)}, u32[]{:S(2)}) collective-permute-start(bf16[512,1024]{1,0:T(8,128)(2,1)S(1)} %get-tuple-element.71), channel_id=1, source_target_pairs={{1,0},{2,1},{3,2},{5,4},{6,5},{7,6},{9,8},{10,9},{11,10},{13,12},{... | collective-permute-start | bytes 3145736 | tf_op jit(solution)/shard_map/ppermute | solution.py:800
  147.5 30.3 %collective-permute-start.23 = (bf16[512,1024]{1,0:T(8,128)(2,1)S(1)}, bf16[512,1024]{1,0:T(8,128)(2,1)S(1)}, u32[]{:S(2)}, u32[]{:S(2)}) collective-permute-start(bf16[512,1024]{1,0:T(8,128)(2,1)S(1)} %get-tuple-element.72), channel_id=1, source_target_pairs={{0,1},{1,2},{2,3},{4,5},{5,6},{6,7},{8,9},{9,10},{10,11},{12,13},{... | collective-permute-start | bytes 3145736 | tf_op jit(solution)/shard_map/ppermute | solution.py:801
  152.6 12.1 %collective-permute-start.25 = (bf16[192,1024]{1,0:T(8,128)(2,1)S(1)}, bf16[192,1024]{1,0:T(8,128)(2,1)S(1)}, u32[]{:S(2)}, u32[]{:S(2)}) collective-permute-start(bf16[192,1024]{1,0:T(8,128)(2,1)S(1)} %add_convert_fusion), channel_id=1, source_target_pairs={{0,8},{4,12},{8,0},{12,4},{16,24},{20,28},{24,16},{28,20},{1,9},{5... | collective-permute-start | bytes 1179656 | tf_op jit(solution)/shard_map/ppermute | solution.py:759
  153.7 13.3 %collective-permute-start.27 = (bf16[1,512,512]{2,1,0:T(8,128)(2,1)S(1)}, bf16[1,512,512]{2,1,0:T(8,128)(2,1)S(1)}, u32[]{:S(2)}, u32[]{:S(2)}) collective-permute-start(bf16[1,512,512]{2,1,0:T(8,128)(2,1)S(1)} %get-tuple-element.87), channel_id=1, source_target_pairs={{0,16},{4,20},{8,24},{12,28},{16,0},{20,4},{24,8},{28,12},{1,17},{... | collective-permute-start | bytes 1572872 | tf_op jit(solution)/shard_map/ppermute | solution.py:759
  154.2 19.0 %collective-permute-start.28 = (bf16[1,512,512]{2,1,0:T(8,128)(2,1)S(1)}, bf16[1,512,512]{2,1,0:T(8,128)(2,1)S(1)}, u32[]{:S(2)}, u32[]{:S(2)}) collective-permute-start(bf16[1,512,512]{2,1,0:T(8,128)(2,1)S(1)} %get-tuple-element.89), channel_id=1, source_target_pairs={{0,8},{4,12},{8,0},{12,4},{16,24},{20,28},{24,16},{28,20},{1,9},{5... | collective-permute-start | bytes 1572872 | tf_op jit(solution)/shard_map/ppermute | solution.py:759
  164.7 10.0 %collective-permute-start.26 = (bf16[64,1024]{1,0:T(8,128)(2,1)S(1)}, bf16[64,1024]{1,0:T(8,128)(2,1)S(1)}, u32[]{:S(2)}, u32[]{:S(2)}) collective-permute-start(bf16[64,1024]{1,0:T(8,128)(2,1)S(1)} %add_convert_fusion.1), channel_id=1, source_target_pairs={{0,16},{4,20},{8,24},{12,28},{16,0},{20,4},{24,8},{28,12},{1,17},{... | collective-permute-start | bytes 393224 | tf_op jit(solution)/shard_map/ppermute | solution.py:759
  (14 other events, 20.1 us)

commit v4 on v3

--- a/solution.py
+++ b/solution.py
@@ -17,9 +17,6 @@
 F32 = jnp.float32
 BF16 = jnp.bfloat16
 VMEM_LIMIT = 20 * 1024 * 1024
-
-
-OPT = {'fp': True, 'se': True, 'sl': True, 'g': True, 'b': True, 'lm': 1, 'sa': True, 'b3': True, 'bar': True}
 
 
 def dot_nn(a, b):
@@ -558,23 +555,28 @@
     )(place, attn, *[out_weight] * count, *after)
 
 
-def add_kernel(left_a, left_b, right_a, right_b, left, right):
-    left[...] = (left_a[...].astype(F32) + left_b[...].astype(F32)).astype(left.dtype)
-    right[...] = (right_a[...].astype(F32) + right_b[...].astype(F32)).astype(right.dtype)
-
-
-def add_call(left, right):
-    tokens, width = left[0].shape
+def add_kernel(*refs):
+    half = len(refs) // 3
+    for n in range(half):
+        a, b = refs[2 * n : 2 * n + 2]
+        refs[2 * half + n][...] = (a[...].astype(F32) + b[...].astype(F32)).astype(BF16)
+
+
+def add_call(*pairs):
+    full = [p for p in pairs if p[1] is not None]
+    tokens, width = pairs[0][0].shape
     spec = pl.BlockSpec((tokens // 2, width), lambda i: (i, 0))
-    return pl.pallas_call(
+    sums = pl.pallas_call(
         add_kernel,
         grid=(2,),
-        in_specs=[spec] * 4,
-        out_specs=[spec] * 2,
-        out_shape=[jax.ShapeDtypeStruct((tokens, width), BF16)] * 2,
+        in_specs=[spec] * (2 * len(full)),
+        out_specs=[spec] * len(full),
+        out_shape=[jax.ShapeDtypeStruct((tokens, width), BF16)] * len(full),
         compiler_params=pltpu.CompilerParams(vmem_limit_bytes=VMEM_LIMIT),
         name="mixed_add",
-    )(*left, *right)
+    )(*[x for p in full for x in p])
+    sums = iter(sums)
+    return [p[0] if p[1] is None else next(sums) for p in pairs]
 
 
 def last_kernel(own, left, right, out):
@@ -759,6 +761,16 @@
     return lax.ppermute(value, axis, [(i, i ^ mask) for i in range(lax.axis_size(axis))])
 
 
+def line_pairs(count, rightward, leftward):
+    pairs = [(i, i + 1) for i in rightward] + [(i, i - 1) for i in leftward]
+    even = [p for p in pairs if min(p) % 2 == 0]
+    return even, [p for p in pairs if min(p) % 2 == 1]
+
+
+def along(value, pairs):
+    return lax.ppermute(value, "head", pairs) if pairs else None
+
+
 def per_device(query, key, value, out_weight, cotangent):
     tokens, width = query.shape
     model = out_weight.shape[1]
@@ -771,112 +783,92 @@
     core = me % 2
     chips = ctx_count // 2
     per_chunk = chips // count
-    early = [s for s in range(count) if s not in (1, count - 1)]
     late = sorted({1, count - 1})
+    early = [s for s in range(count) if s not in late]
     bits = [1 << n for n in range(chips.bit_length() - 1)]
     order = term_order(chips)
     slots = {s: n for n, s in enumerate(early + late)}
     table = np.zeros((count, ctx_count, count + chips), np.int32)
     for i in range(count):
+        sign = 1 if i % 2 else -1
         for j in range(ctx_count):
-            table[i, j, :count] = [(i + d) % count for d in range(count)]
+            table[i, j, :count] = [(i + sign * d) % count for d in range(count)]
             for n, distance in enumerate(order):
                 chip = (j // 2) ^ distance
-                s = (i - chip // per_chunk) % count
+                s = sign * (chip // per_chunk - i) % count
                 table[i, j, count + n] = slots[s] * per_chunk + chip % per_chunk
     place = lax.dynamic_slice(jnp.asarray(table), (z, me, 0), (1, 1, count + chips)).reshape(-1)
 
-    from_left, from_right = [cotangent], [cotangent]
+    even, odd = [cotangent], [cotangent]
 
     def pass_on(step):
-        right, left = from_left[-1], from_right[-1]
-        right = lax.ppermute(right, "head", [(i, i + 1) for i in range(step - 1, count - 1)])
-        left = lax.ppermute(left, "head", [(i, i - 1) for i in range(1, count - step + 1)])
-        from_left.append(right)
-        from_right.append(left)
-
-    def send_on(step, left, right):
-        return (
-            lax.ppermute(left, "head", [(i, i - 1) for i in range(count - step, count)]),
-            lax.ppermute(right, "head", [(i, i + 1) for i in range(0, step)]),
-        )
+        pairs = line_pairs(count, range(step - 1, count - 1), range(1, count - step + 1))
+        even_next = along(odd[-1], pairs[0])
+        odd.append(along(even[-1], pairs[1]))
+        even.append(even_next)
+
+    def send_on(step, values):
+        pairs = line_pairs(count, range(0, step), range(count - step, count))
+        return tuple(along(v, p) for v, p in zip(values, pairs))
 
     def chunks_of(group):
-        return [(cotangent,) if s == 0 else (from_left[s], from_right[count - s]) for s in group]
-
-    back_by = lambda group: tuple(-s % count for s in group)
+        found = [(cotangent,) if s == 0 else (odd[s], even[count - s]) for s in group]
+        return [tuple(c for c in chunk if c is not None) for chunk in found]
 
     pass_on(1)
-    if OPT.get("x0"):
-        tiny = swap(key[:16, :128], "ctx", 1)
-        key_in = lax.optimization_barrier((key, tiny))[0]
-    else:
-        key_in = key
-    near, three, four = pool_call(key_in, value)
+    near, three, four = pool_call(key, value)
     three = swap(three, "ctx", 2)
     four_a = swap(four, "ctx", 4)
     four_b = swap(four, "ctx", 6)
     near = lower_call(near, three, four_a, four_b)
-    if OPT.get("bar"):
-        near, from_left[1], from_right[1] = lax.optimization_barrier((near, from_left[1], from_right[1]))
-    if OPT.get("bar2"):
-        lower, from_left[1], from_right[1] = lax.optimization_barrier((near, from_left[1], from_right[1]))
-        received_after = (lower,)
+    near, even[1], odd[1] = lax.optimization_barrier((near, even[1], odd[1]))
     near = swap(near, "ctx", 1)
-    if OPT.get("bar3"):
-        near, from_left[1], from_right[1] = lax.optimization_barrier((near, from_left[1], from_right[1]))
     received = (near, three, four_a, four_b)
 
-    attn, turned, lse, tops = forward_call(query, key, value, received, after=((place,) if OPT.get("fp") else ()) + ((lower,) if OPT.get("bar2f") else ()) + ((from_left[1], from_right[1]) if OPT.get("f") else ()))
-    if OPT.get("barF"):
-        attn, from_left[1], from_right[1] = lax.optimization_barrier((attn, from_left[1], from_right[1]))
     pass_on(2)
+    attn, turned, lse, tops = forward_call(query, key, value, received, after=(place,))
     turned_other = swap(turned, "ctx", 1)
-    lm = OPT.get("lm")
-    def lmax(after):
-        level_max = jnp.transpose((held_back(tops, after) if after else tops)[:, :LEVELS, 0])
-        mask = 1
-        while mask < ctx_count:
-            level_max = jnp.maximum(level_max, swap(level_max, "ctx", mask))
-            mask *= 2
-        return level_max
-    if lm == 3:
-        level_max = lmax((turned_other,))
-    if lm == 4:
-        level_max = lmax(())
-    products = product_call(attn, out_weight, place, count, after=(turned_other,) if OPT.get("p2") else ())
-    left, right = send_on(1, products[1], products[count - 1])
+    products = product_call(attn, out_weight, place, count)
+    arrived = send_on(1, (products[1], products[count - 1]))
     for step in range(3, count):
         pass_on(step)
+
     chunks = chunks_of(early)
-    mine, send = split_call(chunks, core, column, after=(products[1],) if OPT.get("se") else ())
+    mine, send = split_call(chunks, core, column, after=(products[1],))
     theirs = swap(send, "ctx", 1)
-    grad_attn = grad_call(chunks, out_weight, place, back_by(early), None, F32)
+    grad_attn = grad_call(chunks, out_weight, place, early, None, F32)
     terms = term_call(turned, turned_other, mine, theirs, place, column)
 
+    level_max = jnp.transpose(held_back(tops, (terms, grad_attn))[:, :LEVELS, 0])
+    mask = 1
+    while mask < ctx_count:
+        level_max = jnp.maximum(level_max, swap(level_max, "ctx", mask))
+        mask *= 2
+
+    def add_products(step, arrived):
+        return add_call((products[step], arrived[1]), (products[count - step], arrived[0]))
+
+    for step in range(2, count - 1):
+        sums = add_products(step, arrived)
+        arrived = send_on(step, sums)
     chunks = chunks_of(late)
-    if lm == 1:
-        level_max = lmax((terms, grad_attn))
-    first_arrived = (left, right)
-    for step in range(2, count - 1):
-        sums = add_call((products[step], left), (products[count - step], right))
-        left, right = send_on(step, *sums)
-    mine, send = split_call(chunks, core, column, after=((terms, grad_attn) if OPT.get("sl") else ()) + ((level_max,) if lm == 1 else ()) + (first_arrived if OPT.get("slr") else ()) + (tuple(sums) if OPT.get("sa") else ()) + ())
+    mine, send = split_call(
+        chunks, core, column, after=(terms, grad_attn, level_max, *[x for x in sums if x is not None])
+    )
     theirs = swap(send, "ctx", 1)
-    terms = late_call(turned, turned_other, mine, theirs, terms, place, count, chips, column, sums if OPT.get("t") else ())
+    terms = late_call(turned, turned_other, mine, theirs, terms, place, count, chips, column, ())
     grad_attn = grad_call(
-        chunks, out_weight, place, back_by(late), grad_attn, BF16, after=terms if OPT.get("g") else ()
+        chunks, out_weight, place, late, grad_attn, BF16, after=tuple(terms)
     )
     half, quarter = chips // 2, chips // 4
     first = [swap(terms[0], "ctx", 2 * bits[0]), swap(terms[2], "ctx", 2 * bits[-1])]
-    if lm == 2:
-        level_max = lmax((terms[0],))
-    outs = backward_call(query, key, value, attn, grad_attn, lse, received, after=(tuple(terms) if OPT.get("b") else ()) + ((level_max,) if lm == 2 else ()) + ((left, right) if OPT.get("bl") else ()))
-
-    sums = add_call((products[count - 1], left), (products[1], right))
-    if OPT.get("b3"):
-        sums, first = lax.optimization_barrier((tuple(sums), first))
-    left, right = send_on(count - 1, *sums)
+    outs = backward_call(
+        query, key, value, attn, grad_attn, lse, received, after=tuple(terms)
+    )
+
+    sums = add_products(count - 1, arrived)
+    sums, first = lax.optimization_barrier((tuple(sums), first))
+    arrived = send_on(count - 1, sums)
     ways = [bits, bits[::-1]]
     sent = [order[:half], order[quarter : 3 * quarter]]
     held = [order[half:], order[:quarter] + order[3 * quarter :]]
@@ -892,25 +884,16 @@
         kept = [f[1][1] for f in folded]
         first = [swap(f[1][0], "ctx", 2 * ways[k][n + 1]) for k, f in enumerate(folded)]
     top, bottom = [(kept[k][0], first[k][0]) for k in (0, 1)]
+    weight_grad = total_call(top, bottom)
+    mixed = last_call(products[0], *arrived)
+
     grad_q, grad_k, grad_v, far, keep, four = outs
     far = swap(far, "ctx", 1)
     third = BLK + BLK // 2
-    if OPT.get("ret2"):
-        sums3 = (keep.astype(F32) + far[2 * BLK : 2 * BLK + third]).astype(BF16)
-        sums4 = (four.astype(F32) + far[2 * BLK + third :]).astype(BF16)
-        back = swap(sums3[:BLK], "ctx", 2)
-        four = (swap(sums4, "ctx", 4), swap(sums3[BLK:], "ctx", 6))
-        four = (four[0].astype(F32) + four[1]).astype(BF16)
-    else:
-      back = swap((keep.astype(F32) + far[2 * BLK : 2 * BLK + third]).astype(BF16), "ctx", 2)
-      four = four.astype(F32) + far[2 * BLK + third :] + back[BLK:]
-      four = swap(four.astype(BF16), "ctx", 4)
-    weight_grad = total_call(top, bottom)
-    mixed = last_call(products[0], left, right)
+    back = swap((keep.astype(F32) + far[2 * BLK : 2 * BLK + third]).astype(BF16), "ctx", 2)
+    four = four.astype(F32) + far[2 * BLK + third :] + back[BLK:]
+    four = swap(four.astype(BF16), "ctx", 4)
     grad_k, grad_v = finish_call(grad_k, grad_v, far, back, four)
-
-    if lm == 0:
-        level_max = lmax((terms[0],))
     return mixed, grad_q, grad_k, grad_v, weight_grad, level_max
 
 

time: 181 us -> 166 us (0.917)
  starting transfers between devices: 48.3 us -> 34.9 us
  Pallas kernels: 71.1 us -> 66 us
  waiting for transfers between devices: 41.7 us -> 45.9 us
    ppermute x12 -> x10, starting transfers between devices: 35.9 us -> 19.2 us  [along(): return lax.ppermute(value, 'head', pairs) if pairs else None]
    ppermute x12 -> x10, waiting for transfers between devices: 9.09 us -> 15.5 us  [along(): return lax.ppermute(value, 'head', pairs) if pairs else None]
    ppermute x17, starting transfers between devices: 12.4 us -> 15.7 us  [swap(): lax.ppermute(value, axis, [(i, i ^ mask) for i in range(lax.axis_size(axi...]
    ppermute x17, waiting for transfers between devices: 32.6 us -> 30.4 us  [swap(): lax.ppermute(value, axis, [(i, i ^ mask) for i in range(lax.axis_size(axi...]
    unnamed x66 -> x68, local copies, waits for them, and re-layouts: 15.7 us -> 15 us
  transfers between devices with their start and end apart: 29 -> 27, of which waited for: 12 -> 13; matrix products, arithmetic and copies ran while one was open for 1% -> 1% of each run, Pallas kernels for 37% -> 38%
where the time goes in v4:
time: 166 us; the launch traced here: 165 us
  Pallas kernels  66 us (40%)
  waiting for transfers between devices  45.9 us (28%)
  starting transfers between devices  34.9 us (21%)
  local copies, waits for them, and re-layouts  16.7 us (10%)
    ppermute x17, waiting for transfers between devices, swap(): lax.ppermute(value, axis, [(i, i ^ mask) for i in range(lax.axis_size(axi...  30.4 us
    ppermute x10, starting transfers between devices, along(): return lax.ppermute(value, 'head', pairs) if pairs else None  19.2 us
    ppermute x17, starting transfers between devices, swap(): lax.ppermute(value, axis, [(i, i ^ mask) for i in range(lax.axis_size(axi...  15.7 us
    ppermute x10, waiting for transfers between devices, along(): return lax.ppermute(value, 'head', pairs) if pairs else None  15.5 us
    unnamed x68, local copies, waits for them, and re-layouts  15 us
    pallas_call x1, Pallas kernels, backward_call(): pl.pallas_call(functools.partial(backward_kernel, extra=len(after)), grid...  12.1 us
    pallas_call x2, Pallas kernels, grad_call(): pl.pallas_call(functools.partial(grad_kernel, pairs=tuple((len(c) for c i...  10.7 us
    pallas_call x1, Pallas kernels, forward_call(): pl.pallas_call(functools.partial(forward_kernel, extra=len(after)), grid=...  9.44 us
  transfers between devices with their start and end apart: 27, of which 13 were waited for; matrix products, arithmetic and copies ran while one was open for 1% of the time, Pallas kernels for 38%

profile of v4, /device:TPU:0, one launch (start us, length us, event | category | flops | bytes accessed | tf_op | source)
XLA Modules:
  0.0 164.8 jit_solution(9203850049200882163)
XLA Ops:
  0.6 3.1 %collective-permute-start.3 = (bf16[512,1024]{1,0:T(8,128)(2,1)}, bf16[512,1024]{1,0:T(8,128)(2,1)}, u32[]{:S(2)}, u32[]{:S(2)}) collective-permute-start(bf16[512,1024]{1,0:T(8,128)(2,1)} %refs_0_.5), channel_id=1, source_target_pairs={{0,1},{2,3},{1,0},{3,2},{4,5},{6,7},{5,4},{7,6},{8,9},{10,11},{9,8... | collective-permute-start | bytes 3145736 | tf_op jit(solution)/shard_map/ppermute | solution.py:771
  3.7 1.6 collective-permute-start.4
  5.4 1.2 copy-done.7
  7.8 1.7 %pool_keys.1 = (bf16[512,1024]{1,0:T(8,128)(2,1)}, bf16[128,1024]{1,0:T(8,128)(2,1)S(1)}, bf16[64,1024]{1,0:T(8,128)(2,1)S(1)}) custom-call(bf16[512,1024]{1,0:T(8,128)(2,1)S(1)} %copy-done.7, bf16[512,1024]{1,0:T(8,128)(2,1)S(1)} %copy-done.9), custom_call_target="tpu_custom_call" | custom-call | tf_op jit(solution)/shard_map/pool_keys/pallas_call | solution.py:65
  9.5 1.5 collective-permute-start
  11.0 1.5 collective-permute-start.1
  13.0 3.0 %collective-permute-done.1.four_a = bf16[64,1024]{1,0:T(8,128)(2,1)S(1)} collective-permute-done((bf16[64,1024]{1,0:T(8,128)(2,1)S(1)}, bf16[64,1024]{1,0:T(8,128)(2,1)S(1)}, u32[]{:S(2)}, u32[]{:S(2)}) %collective-permute-start.1) | collective-permute-done | bytes 131104 | tf_op jit(solution)/shard_map/ppermute | solution.py:761
  16.0 5.1 %collective-permute-done.2.four_b = bf16[64,1024]{1,0:T(8,128)(2,1)S(1)} collective-permute-done((bf16[64,1024]{1,0:T(8,128)(2,1)S(1)}, bf16[64,1024]{1,0:T(8,128)(2,1)S(1)}, u32[]{:S(2)}, u32[]{:S(2)}) %collective-permute-start.2) | collective-permute-done | bytes 131104 | tf_op jit(solution)/shard_map/ppermute | solution.py:761
  22.5 4.7 %collective-permute-done.3.refs_2_ = bf16[512,1024]{1,0:T(8,128)(2,1)} collective-permute-done((bf16[512,1024]{1,0:T(8,128)(2,1)}, bf16[512,1024]{1,0:T(8,128)(2,1)}, u32[]{:S(2)}, u32[]{:S(2)}) %collective-permute-start.3) | collective-permute-done | bytes 1048608 | tf_op jit(solution)/shard_map/ppermute | solution.py:771
  27.2 1.7 %collective-permute-start.10 = (bf16[512,1024]{1,0:T(8,128)(2,1)}, bf16[512,1024]{1,0:T(8,128)(2,1)}, u32[]{:S(2)}, u32[]{:S(2)}) collective-permute-start(bf16[512,1024]{1,0:T(8,128)(2,1)} %collective-permute-done.3.refs_2_), channel_id=1, source_target_pairs={{1,2},{2,1},{5,6},{6,5},{9,10},{10,9},{13,14},{14,13},{17,18},{18,... | collective-permute-start | bytes 3145736 | tf_op jit(solution)/shard_map/ppermute | solution.py:771
  28.9 1.3 collective-permute-start.12
  31.8 9.4 %attention_forward.1 = (bf16[512,1024]{1,0:T(8,128)(2,1)S(1)}, bf16[1024,512]{1,0:T(8,128)(2,1)S(1)}, f32[512,1024]{1,0:T(8,128)S(1)}, f32[8,8,128]{2,1,0:T(8,128)S(1)}) custom-call(bf16[512,1024]{1,0:T(8,128)(2,1)S(1)} %copy-done.13, bf16[512,1024]{1,0:T(8,128)(2,1)S(1)} %copy-done.8, bf16[512,1024]{1,0:T(8,128)(2,1)S(1)} %copy-done.10, ...), custom_call_target="tpu_custom_call" | custom-call | tf_op jit(solution)/shard_map/attention_forward/pallas_call | solution.py:222
  41.3 1.3 copy-done.21
  43.7 3.6 %copy-done = bf16[1024,4096]{1,0:T(8,128)(2,1)S(1)} copy-done((bf16[1024,4096]{1,0:T(8,128)(2,1)S(1)}, bf16[1024,4096]{1,0:T(8,128)(2,1)}, u32[]{:S(2)}) %copy-start) | copy-done | bytes 8388632
  47.3 8.0 %mixed_products.1 = (bf16[512,1024]{1,0:T(8,128)(2,1)S(1)}, bf16[512,1024]{1,0:T(8,128)(2,1)}, bf16[512,1024]{1,0:T(8,128)(2,1)}, bf16[512,1024]{1,0:T(8,128)(2,1)S(1)}) custom-call(s32[8]{0:T(128)S(1)} %dynamic-slice_bitcast_fusion.rest_0_.place_ref, bf16[512,1024]{1,0:T(8,128)(2,1)S(1)} %get-tuple-element.50.attn_ref, bf16[1024,4096]{1,0:T(8,128)(2,1)S(1)} %copy-done, ...), custom_call_target="tpu_custom_call" | custom-call | tf_op jit(solution)/shard_map/mixed_products/pallas_call | solution.py:539
  55.3 5.5 %collective-permute-done.12.refs_2_ = bf16[512,1024]{1,0:T(8,128)(2,1)} collective-permute-done((bf16[512,1024]{1,0:T(8,128)(2,1)}, bf16[512,1024]{1,0:T(8,128)(2,1)}, u32[]{:S(2)}, u32[]{:S(2)}) %collective-permute-start.12) | collective-permute-done | bytes 1048608 | tf_op jit(solution)/shard_map/ppermute | solution.py:771
  60.7 1.6 split_columns.2
  62.5 6.1 %collective-permute-start.6 = (bf16[512,1024]{1,0:T(8,128)(2,1)}, bf16[512,1024]{1,0:T(8,128)(2,1)}, u32[]{:S(2)}, u32[]{:S(2)}) collective-permute-start(bf16[512,1024]{1,0:T(8,128)(2,1)} %get-tuple-element.54.refs_2_.refs_3_), channel_id=1, source_target_pairs={{0,1},{3,2},{4,5},{7,6},{8,9},{11,10},{12,13},{15,14},{16,17},{19,... | collective-permute-start | bytes 3145736 | tf_op jit(solution)/shard_map/ppermute | solution.py:771
  68.6 1.3 collective-permute-start.11
  69.9 5.0 %grad_products.2.refs_1_.refs_4_.refs_5_ = f32[512,1024]{1,0:T(8,128)S(1)} custom-call(s32[8]{0:T(128)S(1)} %dynamic-slice_bitcast_fusion.rest_0_.place_ref, bf16[512,1024]{1,0:T(8,128)(2,1)S(1)} %copy-done.12, bf16[512,1024]{1,0:T(8,128)(2,1)} %collective-permute-done.10.refs_1_, bf16[512,1024]{1,0:T(8,128)(2,1)} %collective-permute-done.12.refs_2_, ...), custom_call_target="tpu_custom_call" | custom-call | tf_op jit(solution)/shard_map/grad_products/pallas_call | solution.py:509
  74.9 3.6 %weight_terms.1.refs_0_.refs_3_.early_ref = bf16[2,1024,512]{2,1,0:T(8,128)(2,1)S(1)} custom-call(s32[8]{0:T(128)S(1)} %dynamic-slice_bitcast_fusion.rest_0_.place_ref, bf16[1024,512]{1,0:T(8,128)(2,1)S(1)} %get-tuple-element.57.own_ref, bf16[1024,512]{1,0:T(8,128)(2,1)S(1)} %collective-permute-done.9.other_ref, ...), custom_call_target="tpu_custom_call" | custom-call | tf_op jit(solution)/shard_map/weight_terms/pallas_call | solution.py:612
  78.6 1.3 copy-done.4
  79.9 1.4 held_back.1
  83.5 1.5 collective-permute-start.15
  85.0 2.1 %collective-permute-done.15 = f32[5,8]{1,0:T(8,128)S(1)} collective-permute-done((f32[5,8]{1,0:T(8,128)S(1)}, f32[5,8]{1,0:T(8,128)S(1)}, u32[]{:S(2)}, u32[]{:S(2)}) %collective-permute-start.15) | collective-permute-done | bytes 192 | tf_op jit(solution)/shard_map/ppermute | solution.py:761
  87.1 1.5 collective-permute-start.16
  88.6 2.1 %collective-permute-done.6.refs_1_ = bf16[512,1024]{1,0:T(8,128)(2,1)} collective-permute-done((bf16[512,1024]{1,0:T(8,128)(2,1)}, bf16[512,1024]{1,0:T(8,128)(2,1)}, u32[]{:S(2)}, u32[]{:S(2)}) %collective-permute-start.6) | collective-permute-done | bytes 1048608 | tf_op jit(solution)/shard_map/ppermute | solution.py:771
  90.8 1.8 %mixed_add.2.refs_7_ = bf16[512,1024]{1,0:T(8,128)(2,1)S(1)} custom-call(bf16[512,1024]{1,0:T(8,128)(2,1)} %get-tuple-element.53.refs_0_.refs_6_, bf16[512,1024]{1,0:T(8,128)(2,1)} %collective-permute-done.6.refs_1_), custom_call_target="tpu_custom_call" | custom-call | tf_op jit(solution)/shard_map/mixed_add/pallas_call | solution.py:569
  92.6 3.2 %collective-permute-done.11.refs_1_ = bf16[512,1024]{1,0:T(8,128)(2,1)} collective-permute-done((bf16[512,1024]{1,0:T(8,128)(2,1)}, bf16[512,1024]{1,0:T(8,128)(2,1)}, u32[]{:S(2)}, u32[]{:S(2)}) %collective-permute-start.11) | collective-permute-done | bytes 1048608 | tf_op jit(solution)/shard_map/ppermute | solution.py:771
  95.9 1.6 copy-done.5
  97.5 2.1 %split_columns.3 = (bf16[512,1024]{1,0:T(8,128)(2,1)S(1)}, bf16[512,1024]{1,0:T(8,128)(2,1)S(1)}) custom-call(s32[1]{0:T(128)} %bitcast.1.core_ref, bf16[512,1024]{1,0:T(8,128)(2,1)} %collective-permute-done.4.refs_0_, bf16[512,1024]{1,0:T(8,128)(2,1)} %collective-permute-done.11.refs_1_, bf16[512,1024]{1,0:T(8,128)(2,1)} %collective-permute-done.3.refs_2_, ...), custom_call_target="tpu_custom_call" | custom-call | tf_op jit(solution)/shard_map/split_columns/pallas_call | solution.py:468
  99.7 1.7 %collective-permute-start.8 = (bf16[512,1024]{1,0:T(8,128)(2,1)}, bf16[512,1024]{1,0:T(8,128)(2,1)S(1)}, u32[]{:S(2)}, u32[]{:S(2)}) collective-permute-start(bf16[512,1024]{1,0:T(8,128)(2,1)} %get-tuple-element.53.refs_0_.refs_6_), channel_id=1, source_target_pairs={{0,1},{3,2},{4,5},{7,6},{8,9},{11,10},{12,13},{15,14},{16,17},{19,... | collective-permute-start | bytes 3145736 | tf_op jit(solution)/shard_map/ppermute | solution.py:771
  102.3 1.2 copy-done.18
  104.8 4.2 %weight_terms_late.1 = (bf16[2,512,512]{2,1,0:T(8,128)(2,1)S(1)}, bf16[2,512,512]{2,1,0:T(8,128)(2,1)S(1)}, bf16[2,512,512]{2,1,0:T(8,128)(2,1)S(1)}, bf16[2,512,512]{2,1,0:T(8,128)(2,1)S(1)}) custom-call(s32[8]{0:T(128)S(1)} %dynamic-slice_bitcast_fusion.rest_0_.place_ref, bf16[1024,512]{1,0:T(8,128)(2,1)S(1)} %copy-done.18, ...), custom_call_target="tpu_custom_call" | custom-call | tf_op jit(solution)/shard_map/weight_terms_late/pallas_call | solution.py:676
  109.0 1.5 collective-permute-start.18
  110.5 1.6 collective-permute-start.19
  112.2 5.7 %grad_products.3.grad_ref = bf16[512,1024]{1,0:T(8,128)(2,1)S(1)} custom-call(s32[8]{0:T(128)S(1)} %dynamic-slice_bitcast_fusion.rest_0_.place_ref, bf16[512,1024]{1,0:T(8,128)(2,1)} %collective-permute-done.4.refs_0_, bf16[512,1024]{1,0:T(8,128)(2,1)} %collective-permute-done.11.refs_1_, bf16[512,1024]{1,0:T(8,128)(2,1)} %collective-permute-done.3.refs_2_, ...), custom_call_target="tpu_custom_call" | custom-call | tf_op jit(solution)/shard_map/grad_products/pallas_call | solution.py:509
  118.0 12.1 %attention_backward.1 = (f32[512,1024]{1,0:T(8,128)}, bf16[512,1024]{1,0:T(8,128)(2,1)S(1)}, bf16[512,1024]{1,0:T(8,128)(2,1)S(1)}, bf16[512,1024]{1,0:T(8,128)(...) custom-call(bf16[512,1024]{1,0:T(8,128)(2,1)S(1)} %copy-done.14, bf16[512,1024]{1,0:T(8,128)(2,1)S(1)} %copy-done.8, ...), custom_call_target="tpu_custom_call" | custom-call | tf_op jit(solution)/shard_map/attention_backward/pallas_call | solution.py:386
  130.1 1.6 mixed_add.3
  131.6 2.6 %collective-permute-done.18.refs_1_ = bf16[2,512,512]{2,1,0:T(8,128)(2,1)S(1)} collective-permute-done((bf16[2,512,512]{2,1,0:T(8,128)(2,1)S(1)}, bf16[2,512,512]{2,1,0:T(8,128)(2,1)S(1)}, u32[]{:S(2)}, u32[]{:S(2)}) %collective-permute-start.18) | collective-permute-done | bytes 1048608 | tf_op jit(solution)/shard_map/ppermute | solution.py:761
  138.2 1.7 %collective-permute-start.25 = (bf16[1,512,512]{2,1,0:T(8,128)(2,1)S(1)}, bf16[1,512,512]{2,1,0:T(8,128)(2,1)S(1)}, u32[]{:S(2)}, u32[]{:S(2)}) collective-permute-start(bf16[1,512,512]{2,1,0:T(8,128)(2,1)S(1)} %get-tuple-element.83), channel_id=1, source_target_pairs={{0,16},{4,20},{8,24},{12,28},{16,0},{20,4},{24,8},{28,12},{1,17},{... | collective-permute-start | bytes 1572872 | tf_op jit(solution)/shard_map/ppermute | solution.py:761
  139.9 1.5 collective-permute-start.26
  141.4 7.9 %collective-permute-done.23.three = bf16[192,1024]{1,0:T(8,128)(2,1)S(1)} collective-permute-done((bf16[192,1024]{1,0:T(8,128)(2,1)S(1)}, bf16[192,1024]{1,0:T(8,128)(2,1)S(1)}, u32[]{:S(2)}, u32[]{:S(2)}) %collective-permute-start.23) | collective-permute-done | bytes 393248 | tf_op jit(solution)/shard_map/ppermute | solution.py:761
  149.3 1.7 %collective-permute-start.24 = (bf16[64,1024]{1,0:T(8,128)(2,1)S(1)}, bf16[64,1024]{1,0:T(8,128)(2,1)S(1)}, u32[]{:S(2)}, u32[]{:S(2)}) collective-permute-start(bf16[64,1024]{1,0:T(8,128)(2,1)S(1)} %add_convert_fusion.1), channel_id=1, source_target_pairs={{0,16},{4,20},{8,24},{12,28},{16,0},{20,4},{24,8},{28,12},{1,17},{... | collective-permute-start | bytes 393224 | tf_op jit(solution)/shard_map/ppermute | solution.py:761
  152.1 6.2 %collective-permute-done.26 = bf16[1,512,512]{2,1,0:T(8,128)(2,1)S(1)} collective-permute-done((bf16[1,512,512]{2,1,0:T(8,128)(2,1)S(1)}, bf16[1,512,512]{2,1,0:T(8,128)(2,1)S(1)}, u32[]{:S(2)}, u32[]{:S(2)}) %collective-permute-start.26) | collective-permute-done | bytes 524320 | tf_op jit(solution)/shard_map/ppermute | solution.py:761
  158.3 1.5 weight_total.1
  159.8 3.0 %add_returned.1 = (f32[512,1024]{1,0:T(8,128)}, f32[512,1024]{1,0:T(8,128)}) custom-call(bf16[512,1024]{1,0:T(8,128)(2,1)S(1)} %get-tuple-element.73.gk_ref, bf16[512,1024]{1,0:T(8,128)(2,1)S(1)} %get-tuple-element.74.gv_ref, bf16[512,1024]{1,0:T(8,128)(2,1)S(1)} %collective-permute-done.22.near, bf16[192,1024]{1,0:T(8,128)(2,1)S(1)} %collective-permute-done.23.three, ...), custom_call_target="tpu_custom_call" | custom-call | tf_op jit(solution)/shard_map/add_returned/pallas_call | solution.py:428
  162.8 2.0 %mixed_last.1 = f32[512,1024]{1,0:T(8,128)} custom-call(bf16[512,1024]{1,0:T(8,128)(2,1)S(1)} %copy-done.27, bf16[512,1024]{1,0:T(8,128)(2,1)S(1)} %collective-permute-done.20.left, bf16[512,1024]{1,0:T(8,128)(2,1)S(1)} %collective-permute-done.21.right), custom_call_target="tpu_custom_call" | custom-call | tf_op jit(solution)/shard_map/mixed_last/pallas_call | solution.py:589
  (100 shorter events, 15.7 us)
Async XLA Ops:
  0.6 26.6 %collective-permute-start.3 = (bf16[512,1024]{1,0:T(8,128)(2,1)}, bf16[512,1024]{1,0:T(8,128)(2,1)}, u32[]{:S(2)}, u32[]{:S(2)}) collective-permute-start(bf16[512,1024]{1,0:T(8,128)(2,1)} %refs_0_.5), channel_id=1, source_target_pairs={{0,1},{2,3},{1,0},{3,2},{4,5},{6,7},{5,4},{7,6},{8,9},{10,11},{9,8... | collective-permute-start | bytes 3145736 | tf_op jit(solution)/shard_map/ppermute | solution.py:771
  3.7 23.5 %collective-permute-start.4 = (bf16[512,1024]{1,0:T(8,128)(2,1)}, bf16[512,1024]{1,0:T(8,128)(2,1)}, u32[]{:S(2)}, u32[]{:S(2)}) collective-permute-start(bf16[512,1024]{1,0:T(8,128)(2,1)} %refs_0_.5), channel_id=1, source_target_pairs={{1,2},{2,1},{5,6},{6,5},{9,10},{10,9},{13,14},{14,13},{17,18},{18,... | collective-permute-start | bytes 3145736 | tf_op jit(solution)/shard_map/ppermute | solution.py:771
  7.8 23.1 %copy-start.8 = (bf16[512,1024]{1,0:T(8,128)(2,1)S(1)}, bf16[512,1024]{1,0:T(8,128)(2,1)}, u32[]{:S(2)}) copy-start(bf16[512,1024]{1,0:T(8,128)(2,1)} %k_ref.5) | copy-start | bytes 3145732
  7.8 23.1 %copy-start.10 = (bf16[512,1024]{1,0:T(8,128)(2,1)S(1)}, bf16[512,1024]{1,0:T(8,128)(2,1)}, u32[]{:S(2)}) copy-start(bf16[512,1024]{1,0:T(8,128)(2,1)} %v_ref.5) | copy-start | bytes 3145732
  7.8 23.1 %copy-start.13 = (bf16[512,1024]{1,0:T(8,128)(2,1)S(1)}, bf16[512,1024]{1,0:T(8,128)(2,1)}, u32[]{:S(2)}) copy-start(bf16[512,1024]{1,0:T(8,128)(2,1)} %q_ref.3) | copy-start | bytes 3145732
  9.5 11.5 %collective-permute-start = (bf16[128,1024]{1,0:T(8,128)(2,1)S(1)}, bf16[128,1024]{1,0:T(8,128)(2,1)S(1)}, u32[]{:S(2)}, u32[]{:S(2)}) collective-permute-start(bf16[128,1024]{1,0:T(8,128)(2,1)S(1)} %get-tuple-element.47), channel_id=1, source_target_pairs={{0,8},{4,12},{8,0},{12,4},{16,24},{20,28},{24,16},{28,20},{1,9},{5... | collective-permute-start | bytes 786440 | tf_op jit(solution)/shard_map/ppermute | solution.py:761
  11.0 5.0 %collective-permute-start.1 = (bf16[64,1024]{1,0:T(8,128)(2,1)S(1)}, bf16[64,1024]{1,0:T(8,128)(2,1)S(1)}, u32[]{:S(2)}, u32[]{:S(2)}) collective-permute-start(bf16[64,1024]{1,0:T(8,128)(2,1)S(1)} %get-tuple-element.48), channel_id=1, source_target_pairs={{0,16},{4,20},{8,24},{12,28},{16,0},{20,4},{24,8},{28,12},{1,17},{... | collective-permute-start | bytes 393224 | tf_op jit(solution)/shard_map/ppermute | solution.py:761
  12.5 8.5 %collective-permute-start.2 = (bf16[64,1024]{1,0:T(8,128)(2,1)S(1)}, bf16[64,1024]{1,0:T(8,128)(2,1)S(1)}, u32[]{:S(2)}, u32[]{:S(2)}) collective-permute-start(bf16[64,1024]{1,0:T(8,128)(2,1)S(1)} %get-tuple-element.48), channel_id=1, source_target_pairs={{0,24},{4,28},{8,16},{12,20},{16,8},{20,12},{24,0},{28,4},{1,25},{... | collective-permute-start | bytes 393224 | tf_op jit(solution)/shard_map/ppermute | solution.py:761
  27.2 3.7 %collective-permute-start.5 = (bf16[512,1024]{1,0:T(8,128)(2,1)}, bf16[512,1024]{1,0:T(8,128)(2,1)}, u32[]{:S(2)}, u32[]{:S(2)}) collective-permute-start(bf16[512,1024]{1,0:T(8,128)(2,1)} %lower_rows.1), channel_id=1, source_target_pairs={{0,4},{4,0},{8,12},{12,8},{16,20},{20,16},{24,28},{28,24},{1,5},{5... | collective-permute-start | bytes 3145736 | tf_op jit(solution)/shard_map/ppermute | solution.py:761
  27.2 28.1 %collective-permute-start.10 = (bf16[512,1024]{1,0:T(8,128)(2,1)}, bf16[512,1024]{1,0:T(8,128)(2,1)}, u32[]{:S(2)}, u32[]{:S(2)}) collective-permute-start(bf16[512,1024]{1,0:T(8,128)(2,1)} %collective-permute-done.3.refs_2_), channel_id=1, source_target_pairs={{1,2},{2,1},{5,6},{6,5},{9,10},{10,9},{13,14},{14,13},{17,18},{18,... | collective-permute-start | bytes 3145736 | tf_op jit(solution)/shard_map/ppermute | solution.py:771
  28.9 31.9 %collective-permute-start.12 = (bf16[512,1024]{1,0:T(8,128)(2,1)}, bf16[512,1024]{1,0:T(8,128)(2,1)}, u32[]{:S(2)}, u32[]{:S(2)}) collective-permute-start(bf16[512,1024]{1,0:T(8,128)(2,1)} %collective-permute-done.4.refs_0_), channel_id=1, source_target_pairs={{2,3},{1,0},{6,7},{5,4},{10,11},{9,8},{14,15},{13,12},{18,19},{17,... | collective-permute-start | bytes 3145736 | tf_op jit(solution)/shard_map/ppermute | solution.py:771
  43.2 12.1 %copy-start.15 = (bf16[512,1024]{1,0:T(8,128)(2,1)}, bf16[512,1024]{1,0:T(8,128)(2,1)S(1)}, u32[]{:S(2)}) copy-start(bf16[512,1024]{1,0:T(8,128)(2,1)S(1)} %get-tuple-element.50.attn_ref) | copy-start | bytes 3145732
  43.2 31.7 %copy-start.17 = (bf16[1024,512]{1,0:T(8,128)(2,1)}, bf16[1024,512]{1,0:T(8,128)(2,1)S(1)}, u32[]{:S(2)}) copy-start(bf16[1024,512]{1,0:T(8,128)(2,1)S(1)} %get-tuple-element.57.own_ref) | copy-start | bytes 3145732
  43.2 31.7 %collective-permute-start.9 = (bf16[1024,512]{1,0:T(8,128)(2,1)S(1)}, bf16[1024,512]{1,0:T(8,128)(2,1)S(1)}, u32[]{:S(2)}, u32[]{:S(2)}) collective-permute-start(bf16[1024,512]{1,0:T(8,128)(2,1)S(1)} %get-tuple-element.57.own_ref), channel_id=1, source_target_pairs={{0,4},{4,0},{8,12},{12,8},{16,20},{20,16},{24,28},{28,24},{1,5},{5... | collective-permute-start | bytes 3145736 | tf_op jit(solution)/shard_map/ppermute | solution.py:761
  47.3 13.4 %copy-start.12 = (bf16[512,1024]{1,0:T(8,128)(2,1)S(1)}, bf16[512,1024]{1,0:T(8,128)(2,1)}, u32[]{:S(2)}) copy-start(bf16[512,1024]{1,0:T(8,128)(2,1)} %refs_0_.5) | copy-start | bytes 3145732
  47.3 22.6 %copy-start.1 = (bf16[1024,4096]{1,0:T(8,128)(2,1)S(1)}, bf16[1024,4096]{1,0:T(8,128)(2,1)}, u32[]{:S(2)}) copy-start(bf16[1024,4096]{1,0:T(8,128)(2,1)} %refs_4_.3) | copy-start | bytes 25165828
  55.3 7.1 %copy-start.26 = (bf16[512,1024]{1,0:T(8,128)(2,1)}, bf16[512,1024]{1,0:T(8,128)(2,1)S(1)}, u32[]{:S(2)}) copy-start(bf16[512,1024]{1,0:T(8,128)(2,1)S(1)} %get-tuple-element.51.own) | copy-start | bytes 3145732
  55.3 7.1 %copy-start.28 = (bf16[512,1024]{1,0:T(8,128)(2,1)}, bf16[512,1024]{1,0:T(8,128)(2,1)S(1)}, u32[]{:S(2)}) copy-start(bf16[512,1024]{1,0:T(8,128)(2,1)S(1)} %get-tuple-element.52.refs_0_) | copy-start | bytes 3145732
  62.4 12.5 %collective-permute-start.13 = (bf16[512,1024]{1,0:T(8,128)(2,1)S(1)}, bf16[512,1024]{1,0:T(8,128)(2,1)S(1)}, u32[]{:S(2)}, u32[]{:S(2)}) collective-permute-start(bf16[512,1024]{1,0:T(8,128)(2,1)S(1)} %get-tuple-element.61), channel_id=1, source_target_pairs={{0,4},{4,0},{8,12},{12,8},{16,20},{20,16},{24,28},{28,24},{1,5},{5... | collective-permute-start | bytes 3145736 | tf_op jit(solution)/shard_map/ppermute | solution.py:761
  62.5 28.3 %collective-permute-start.6 = (bf16[512,1024]{1,0:T(8,128)(2,1)}, bf16[512,1024]{1,0:T(8,128)(2,1)}, u32[]{:S(2)}, u32[]{:S(2)}) collective-permute-start(bf16[512,1024]{1,0:T(8,128)(2,1)} %get-tuple-element.54.refs_2_.refs_3_), channel_id=1, source_target_pairs={{0,1},{3,2},{4,5},{7,6},{8,9},{11,10},{12,13},{15,14},{16,17},{19,... | collective-permute-start | bytes 3145736 | tf_op jit(solution)/shard_map/ppermute | solution.py:771
  68.6 27.3 %collective-permute-start.11 = (bf16[512,1024]{1,0:T(8,128)(2,1)}, bf16[512,1024]{1,0:T(8,128)(2,1)}, u32[]{:S(2)}, u32[]{:S(2)}) collective-permute-start(bf16[512,1024]{1,0:T(8,128)(2,1)} %collective-permute-done.10.refs_1_), channel_id=1, source_target_pairs={{2,3},{1,0},{6,7},{5,4},{10,11},{9,8},{14,15},{13,12},{18,19},{17,... | collective-permute-start | bytes 3145736 | tf_op jit(solution)/shard_map/ppermute | solution.py:771
  74.9 3.7 %copy-start.2 = (f32[512,1024]{1,0:T(8,128)}, f32[512,1024]{1,0:T(8,128)S(1)}, u32[]{:S(2)}) copy-start(f32[512,1024]{1,0:T(8,128)S(1)} %grad_products.2.refs_1_.refs_4_.refs_5_) | copy-start | bytes 6291460
  81.3 14.6 %copy-start.3 = (f32[512,1024]{1,0:T(8,128)S(1)}, f32[512,1024]{1,0:T(8,128)}, u32[]{:S(2)}) copy-start(f32[512,1024]{1,0:T(8,128)} %copy-done.2) | copy-start | bytes 6291460
  82.3 1.2 collective-permute-start.14
  83.5 3.6 %collective-permute-start.15 = (f32[5,8]{1,0:T(8,128)S(1)}, f32[5,8]{1,0:T(8,128)S(1)}, u32[]{:S(2)}, u32[]{:S(2)}) collective-permute-start(f32[5,8]{1,0:T(8,128)S(1)} %bitcast_maximum_fusion), channel_id=1, source_target_pairs={{0,8},{4,12},{8,0},{12,4},{16,24},{20,28},{24,16},{28,20},{1,9},{5... | collective-permute-start | bytes 488 | tf_op jit(solution)/shard_map/ppermute | solution.py:761
  87.1 5.5 %collective-permute-start.16 = (f32[5,8]{1,0:T(8,128)S(1)}, f32[5,8]{1,0:T(8,128)S(1)}, u32[]{:S(2)}, u32[]{:S(2)}) collective-permute-start(f32[5,8]{1,0:T(8,128)S(1)} %max.10), channel_id=1, source_target_pairs={{0,16},{4,20},{8,24},{12,28},{16,0},{20,4},{24,8},{28,12},{1,17},{... | collective-permute-start | bytes 488 | tf_op jit(solution)/shard_map/ppermute | solution.py:761
  90.8 21.3 %slice-start = ((s8[8388608]{0:T(1024)(128)(4,1)}), s8[4194304]{0:T(1024)(128)(4,1)S(1)}, s32[]{:S(2)}) async-start(s8[8388608]{0:T(1024)(128)(4,1)} %bitcast.12), calls=%async_computation | async-start | bytes 8388608
  92.6 7.0 %copy-start.31 = (f32[5,8]{1,0:T(8,128)}, f32[5,8]{1,0:T(8,128)S(1)}, u32[]{:S(2)}) copy-start(f32[5,8]{1,0:T(8,128)S(1)} %max.11.refs_5_) | copy-start | bytes 484
  92.6 19.5 %slice-start.1 = ((s8[8388608]{0:T(1024)(128)(4,1)}), s8[4194304]{0:T(1024)(128)(4,1)S(1)}, s32[]{:S(2)}) async-start(s8[8388608]{0:T(1024)(128)(4,1)} %bitcast.12), calls=%async_computation.1 | async-start | bytes 8388608
  97.5 4.8 %copy-start.6 = (bf16[2,1024,512]{2,1,0:T(8,128)(2,1)S(1)}, bf16[2,1024,512]{2,1,0:T(8,128)(2,1)}, u32[]{:S(2)}) copy-start(bf16[2,1024,512]{2,1,0:T(8,128)(2,1)} %copy-done.4) | copy-start | bytes 6291460
  99.6 2.7 %collective-permute-start.17 = (bf16[512,1024]{1,0:T(8,128)(2,1)S(1)}, bf16[512,1024]{1,0:T(8,128)(2,1)S(1)}, u32[]{:S(2)}, u32[]{:S(2)}) collective-permute-start(bf16[512,1024]{1,0:T(8,128)(2,1)S(1)} %get-tuple-element.64), channel_id=1, source_target_pairs={{0,4},{4,0},{8,12},{12,8},{16,20},{20,16},{24,28},{28,24},{1,5},{5... | collective-permute-start | bytes 3145736 | tf_op jit(solution)/shard_map/ppermute | solution.py:761
  99.7 30.4 %collective-permute-start.8 = (bf16[512,1024]{1,0:T(8,128)(2,1)}, bf16[512,1024]{1,0:T(8,128)(2,1)S(1)}, u32[]{:S(2)}, u32[]{:S(2)}) collective-permute-start(bf16[512,1024]{1,0:T(8,128)(2,1)} %get-tuple-element.53.refs_0_.refs_6_), channel_id=1, source_target_pairs={{0,1},{3,2},{4,5},{7,6},{8,9},{11,10},{12,13},{15,14},{16,17},{19,... | collective-permute-start | bytes 3145736 | tf_op jit(solution)/shard_map/ppermute | solution.py:771
  101.4 28.7 %collective-permute-start.7 = (bf16[512,1024]{1,0:T(8,128)(2,1)S(1)}, bf16[512,1024]{1,0:T(8,128)(2,1)S(1)}, u32[]{:S(2)}, u32[]{:S(2)}) collective-permute-start(bf16[512,1024]{1,0:T(8,128)(2,1)S(1)} %mixed_add.2.refs_7_), channel_id=1, source_target_pairs={{1,2},{2,1},{5,6},{6,5},{9,10},{10,9},{13,14},{14,13},{17,18},{18,... | collective-permute-start | bytes 3145736 | tf_op jit(solution)/shard_map/ppermute | solution.py:771
  109.0 25.3 %collective-permute-start.18 = (bf16[2,512,512]{2,1,0:T(8,128)(2,1)S(1)}, bf16[2,512,512]{2,1,0:T(8,128)(2,1)S(1)}, u32[]{:S(2)}, u32[]{:S(2)}) collective-permute-start(bf16[2,512,512]{2,1,0:T(8,128)(2,1)S(1)} %get-tuple-element.65.refs_6_.rest_0_), channel_id=1, source_target_pairs={{0,8},{4,12},{8,0},{12,4},{16,24},{20,28},{24,16},{28,20},{1,9},{5... | collective-permute-start | bytes 3145736 | tf_op jit(solution)/shard_map/ppermute | solution.py:761
  110.5 25.0 %collective-permute-start.19 = (bf16[2,512,512]{2,1,0:T(8,128)(2,1)S(1)}, bf16[2,512,512]{2,1,0:T(8,128)(2,1)S(1)}, u32[]{:S(2)}, u32[]{:S(2)}) collective-permute-start(bf16[2,512,512]{2,1,0:T(8,128)(2,1)S(1)} %get-tuple-element.66.refs_8_.rest_2_), channel_id=1, source_target_pairs={{0,16},{4,20},{8,24},{12,28},{16,0},{20,4},{24,8},{28,12},{1,17},{... | collective-permute-start | bytes 3145736 | tf_op jit(solution)/shard_map/ppermute | solution.py:761
  112.1 5.8 %copy-start.11 = (bf16[512,1024]{1,0:T(8,128)(2,1)S(1)}, bf16[512,1024]{1,0:T(8,128)(2,1)}, u32[]{:S(2)}) copy-start(bf16[512,1024]{1,0:T(8,128)(2,1)} %v_ref.5) | copy-start | bytes 3145732
  112.1 5.8 %copy-start.14 = (bf16[512,1024]{1,0:T(8,128)(2,1)S(1)}, bf16[512,1024]{1,0:T(8,128)(2,1)}, u32[]{:S(2)}) copy-start(bf16[512,1024]{1,0:T(8,128)(2,1)} %q_ref.3) | copy-start | bytes 3145732
  112.1 5.8 %copy-start.16 = (bf16[512,1024]{1,0:T(8,128)(2,1)S(1)}, bf16[512,1024]{1,0:T(8,128)(2,1)}, u32[]{:S(2)}) copy-start(bf16[512,1024]{1,0:T(8,128)(2,1)} %copy-done.15) | copy-start | bytes 3145732
  112.1 5.8 %copy-start.22 = (f32[512,1024]{1,0:T(8,128)S(1)}, f32[512,1024]{1,0:T(8,128)}, u32[]{:S(2)}) copy-start(f32[512,1024]{1,0:T(8,128)} %copy-done.21) | copy-start | bytes 6291460
  112.1 5.8 %copy-start.25 = (bf16[64,1024]{1,0:T(8,128)(2,1)S(1)}, bf16[64,1024]{1,0:T(8,128)(2,1)}, u32[]{:S(2)}) copy-start(bf16[64,1024]{1,0:T(8,128)(2,1)} %copy-done.23) | copy-start | bytes 393220
  118.0 12.1 %copy-start.29 = (bf16[512,1024]{1,0:T(8,128)(2,1)S(1)}, bf16[512,1024]{1,0:T(8,128)(2,1)}, u32[]{:S(2)}) copy-start(bf16[512,1024]{1,0:T(8,128)(2,1)} %copy-done.28) | copy-start | bytes 3145732
  130.0 7.0 %collective-permute-start.22 = (bf16[512,1024]{1,0:T(8,128)(2,1)S(1)}, bf16[512,1024]{1,0:T(8,128)(2,1)S(1)}, u32[]{:S(2)}, u32[]{:S(2)}) collective-permute-start(bf16[512,1024]{1,0:T(8,128)(2,1)S(1)} %get-tuple-element.75), channel_id=1, source_target_pairs={{0,4},{4,0},{8,12},{12,8},{16,20},{20,16},{24,28},{28,24},{1,5},{5... | collective-permute-start | bytes 3145736 | tf_op jit(solution)/shard_map/ppermute | solution.py:761
  135.5 27.3 %collective-permute-start.20 = (bf16[512,1024]{1,0:T(8,128)(2,1)S(1)}, bf16[512,1024]{1,0:T(8,128)(2,1)S(1)}, u32[]{:S(2)}, u32[]{:S(2)}) collective-permute-start(bf16[512,1024]{1,0:T(8,128)(2,1)S(1)} %get-tuple-element.67), channel_id=1, source_target_pairs={{0,1},{2,3},{1,0},{3,2},{4,5},{6,7},{5,4},{7,6},{8,9},{10,11},{9,8... | collective-permute-start | bytes 3145736 | tf_op jit(solution)/shard_map/ppermute | solution.py:771
  136.3 26.5 %collective-permute-start.21 = (bf16[512,1024]{1,0:T(8,128)(2,1)S(1)}, bf16[512,1024]{1,0:T(8,128)(2,1)S(1)}, u32[]{:S(2)}, u32[]{:S(2)}) collective-permute-start(bf16[512,1024]{1,0:T(8,128)(2,1)S(1)} %get-tuple-element.68), channel_id=1, source_target_pairs={{1,2},{2,1},{5,6},{6,5},{9,10},{10,9},{13,14},{14,13},{17,18},{18,... | collective-permute-start | bytes 3145736 | tf_op jit(solution)/shard_map/ppermute | solution.py:771
  137.2 12.1 %collective-permute-start.23 = (bf16[192,1024]{1,0:T(8,128)(2,1)S(1)}, bf16[192,1024]{1,0:T(8,128)(2,1)S(1)}, u32[]{:S(2)}, u32[]{:S(2)}) collective-permute-start(bf16[192,1024]{1,0:T(8,128)(2,1)S(1)} %add_convert_fusion), channel_id=1, source_target_pairs={{0,8},{4,12},{8,0},{12,4},{16,24},{20,28},{24,16},{28,20},{1,9},{5... | collective-permute-start | bytes 1179656 | tf_op jit(solution)/shard_map/ppermute | solution.py:761
  138.2 13.9 %collective-permute-start.25 = (bf16[1,512,512]{2,1,0:T(8,128)(2,1)S(1)}, bf16[1,512,512]{2,1,0:T(8,128)(2,1)S(1)}, u32[]{:S(2)}, u32[]{:S(2)}) collective-permute-start(bf16[1,512,512]{2,1,0:T(8,128)(2,1)S(1)} %get-tuple-element.83), channel_id=1, source_target_pairs={{0,16},{4,20},{8,24},{12,28},{16,0},{20,4},{24,8},{28,12},{1,17},{... | collective-permute-start | bytes 1572872 | tf_op jit(solution)/shard_map/ppermute | solution.py:761
  139.9 18.4 %collective-permute-start.26 = (bf16[1,512,512]{2,1,0:T(8,128)(2,1)S(1)}, bf16[1,512,512]{2,1,0:T(8,128)(2,1)S(1)}, u32[]{:S(2)}, u32[]{:S(2)}) collective-permute-start(bf16[1,512,512]{2,1,0:T(8,128)(2,1)S(1)} %get-tuple-element.85), channel_id=1, source_target_pairs={{0,8},{4,12},{8,0},{12,4},{16,24},{20,28},{24,16},{28,20},{1,9},{5... | collective-permute-start | bytes 1572872 | tf_op jit(solution)/shard_map/ppermute | solution.py:761
  149.3 10.5 %collective-permute-start.24 = (bf16[64,1024]{1,0:T(8,128)(2,1)S(1)}, bf16[64,1024]{1,0:T(8,128)(2,1)S(1)}, u32[]{:S(2)}, u32[]{:S(2)}) collective-permute-start(bf16[64,1024]{1,0:T(8,128)(2,1)S(1)} %add_convert_fusion.1), channel_id=1, source_target_pairs={{0,16},{4,20},{8,24},{12,28},{16,0},{20,4},{24,8},{28,12},{1,17},{... | collective-permute-start | bytes 393224 | tf_op jit(solution)/shard_map/ppermute | solution.py:761
  (13 other events, 21.6 us)

commit v5 on v4

--- a/solution.py
+++ b/solution.py
@@ -437,18 +437,31 @@
     )(grad_k, grad_v, near, three, four)
 
 
-def chunk_of(refs, number):
-    return refs[0][...] if number == 1 else refs[0][...] + refs[1][...]
-
-
-def split_kernel(core_ref, *refs, pairs, column, extra):
-    sources = refs[: sum(pairs)]
-    mine_ref, send_ref = refs[sum(pairs) + extra :]
-    first = core_ref[0] == 0
+SUM, PICK = "sum", "pick"
+
+
+def chunk_of(refs, mode, at_end):
+    if mode is None:
+        return refs[0][...]
+    if mode == SUM:
+        return refs[0][...] + refs[1][...]
+    return jnp.where(at_end, refs[1][...], refs[0][...])
+
+
+def used(mode):
+    return 1 if mode is None else 2
+
+
+def split_kernel(place_ref, *refs, modes, column, flags, extra):
+    total = sum(used(m) for m in modes)
+    sources = refs[:total]
+    mine_ref, send_ref = refs[total + extra :]
+    at_end = place_ref[flags] == 1
+    first = place_ref[flags + 1] == 0
     at = 0
-    for index, number in enumerate(pairs):
-        chunk = chunk_of(sources[at:], number)
-        at += number
+    for index, mode in enumerate(modes):
+        chunk = chunk_of(sources[at:], mode, at_end)
+        at += used(mode)
         width = chunk.shape[1]
         for group in range(width // (2 * column)):
             low = chunk[:, 2 * group * column : (2 * group + 1) * column]
@@ -458,8 +471,8 @@
             send_ref[:, here] = jnp.where(first, high, low)
 
 
-def split_call(chunks, core, column, after=()):
-    flat = [array for chunk in chunks for array in chunk]
+def split_call(chunks, place, flags, column, after=()):
+    flat = [array for _, *arrays in chunks for array in arrays]
     tokens, width = flat[0].shape
     count = len(chunks)
     rows = 256
@@ -467,7 +480,8 @@
     half = pl.BlockSpec((rows, count * width // 2), lambda i: (i, 0))
     return pl.pallas_call(
         functools.partial(
-            split_kernel, pairs=tuple(len(c) for c in chunks), column=column, extra=len(after)
+            split_kernel,
+            modes=tuple(c[0] for c in chunks), column=column, flags=flags, extra=len(after),
         ),
         grid=(tokens // rows,),
         in_specs=[pl.BlockSpec(memory_space=pltpu.SMEM)]
@@ -477,26 +491,27 @@
         out_shape=[jax.ShapeDtypeStruct((tokens, count * width // 2), BF16)] * 2,
         compiler_params=pltpu.CompilerParams(vmem_limit_bytes=VMEM_LIMIT),
         name="split_columns",
-    )(core.reshape(1).astype(jnp.int32), *flat, *after)
-
-
-def grad_kernel(place_ref, *refs, pairs, has_sum):
-    total = sum(pairs)
-    count = len(pairs)
+    )(place, *flat, *after)
+
+
+def grad_kernel(place_ref, *refs, modes, flags, has_sum):
+    total = sum(used(m) for m in modes)
+    count = len(modes)
     sources = refs[:total]
     weights = refs[total : total + count]
     out = refs[-1]
+    at_end = place_ref[flags] == 1
     result = refs[total + count][...] if has_sum else None
     at = 0
-    for index, number in enumerate(pairs):
-        part = dot_nt(chunk_of(sources[at:], number), weights[index][...])
+    for index, mode in enumerate(modes):
+        part = dot_nt(chunk_of(sources[at:], mode, at_end), weights[index][...])
         result = part if result is None else result + part
-        at += number
+        at += used(mode)
     out[...] = result.astype(out.dtype)
 
 
-def grad_call(chunks, out_weight, place, distances, partial_sum, dtype, after=()):
-    flat = [array for chunk in chunks for array in chunk]
+def grad_call(chunks, out_weight, place, flags, distances, partial_sum, dtype, after=()):
+    flat = [array for _, *arrays in chunks for array in arrays]
     tokens, width = flat[0].shape
     features = out_weight.shape[0]
     step = min(512, features)
@@ -508,7 +523,8 @@
     sums = () if partial_sum is None else (partial_sum,)
     return pl.pallas_call(
         functools.partial(
-            grad_kernel, pairs=tuple(len(c) for c in chunks), has_sum=partial_sum is not None
+            grad_kernel,
+            modes=tuple(c[0] for c in chunks), flags=flags, has_sum=partial_sum is not None,
         ),
         grid_spec=pltpu.PrefetchScalarGridSpec(
             num_scalar_prefetch=1,
@@ -597,30 +613,26 @@
     )(own, left, right)
 
 
-def term_kernel(place_ref, own_ref, other_ref, mine_ref, theirs_ref, out):
-    out[0] = (
+def term_kernel(own_ref, other_ref, mine_ref, theirs_ref, *refs):
+    refs[-1][0] = (
         dot_nn(own_ref[...], mine_ref[...]) + dot_nn(other_ref[...], theirs_ref[...])
     ).astype(BF16)
 
 
-def term_call(own, other, mine, theirs, place, column):
+def term_call(own, other, mine, theirs, column, after):
     features, tokens = own.shape
     count = mine.shape[1] // column
-    rows = features // 2
-    whole = pl.BlockSpec((rows, tokens), lambda i, j, p: (j, 0))
-    source = pl.BlockSpec((tokens, column), lambda i, j, p: (0, i))
+    whole = pl.BlockSpec((features, tokens), lambda i: (0, 0))
+    source = pl.BlockSpec((tokens, column), lambda i: (0, i))
     return pl.pallas_call(
         term_kernel,
-        grid_spec=pltpu.PrefetchScalarGridSpec(
-            num_scalar_prefetch=1,
-            grid=(count, 2),
-            in_specs=[whole, whole, source, source],
-            out_specs=pl.BlockSpec((1, rows, column), lambda i, j, p: (i, j, 0)),
-        ),
+        grid=(count,),
+        in_specs=[whole, whole, source, source] + [pl.BlockSpec(memory_space=pl.ANY)] * len(after),
+        out_specs=pl.BlockSpec((1, features, column), lambda i: (i, 0, 0)),
         out_shape=jax.ShapeDtypeStruct((count, features, column), BF16),
         compiler_params=pltpu.CompilerParams(vmem_limit_bytes=VMEM_LIMIT),
         name="weight_terms",
-    )(place, own, other, mine, theirs)
+    )(own, other, mine, theirs, *after)
 
 
 def late_kernel(place_ref, own_ref, other_ref, mine_ref, theirs_ref, early_ref, *refs, chips, base, first):
@@ -742,21 +754,6 @@
     return [(names[n], outs[2 * n : 2 * n + 2]) for n in range(len(sides))]
 
 
-def top_kernel(tops_ref, *refs):
-    refs[-1][...] = tops_ref[...]
-
-
-def held_back(value, after):
-    spec = pl.BlockSpec(value.shape, lambda: (0,) * value.ndim)
-    return pl.pallas_call(
-        top_kernel,
-        in_specs=[spec] + [pl.BlockSpec(memory_space=pl.ANY)] * len(after),
-        out_specs=spec,
-        out_shape=jax.ShapeDtypeStruct(value.shape, value.dtype),
-        name="held_back",
-    )(value, *after)
-
-
 def swap(value, axis, mask):
     return lax.ppermute(value, axis, [(i, i ^ mask) for i in range(lax.axis_size(axis))])
 
@@ -780,24 +777,27 @@
     me = lax.axis_index("ctx")
     z = lax.axis_index("head")
 
-    core = me % 2
     chips = ctx_count // 2
     per_chunk = chips // count
-    late = sorted({1, count - 1})
-    early = [s for s in range(count) if s not in late]
+    early = [s for s in range(count) if s != 1]
+    late = [1]
+    grad_early = [s for s in early if s != count - 1]
+    grad_late = sorted({1, count - 1})
     bits = [1 << n for n in range(chips.bit_length() - 1)]
     order = term_order(chips)
     slots = {s: n for n, s in enumerate(early + late)}
-    table = np.zeros((count, ctx_count, count + chips), np.int32)
+    flags = count + chips
+    table = np.zeros((count, ctx_count, flags + 2), np.int32)
     for i in range(count):
         sign = 1 if i % 2 else -1
         for j in range(ctx_count):
+            table[i, j, flags:] = (int(i in (0, count - 1)), j % 2)
             table[i, j, :count] = [(i + sign * d) % count for d in range(count)]
             for n, distance in enumerate(order):
                 chip = (j // 2) ^ distance
                 s = sign * (chip // per_chunk - i) % count
                 table[i, j, count + n] = slots[s] * per_chunk + chip % per_chunk
-    place = lax.dynamic_slice(jnp.asarray(table), (z, me, 0), (1, 1, count + chips)).reshape(-1)
+    place = lax.dynamic_slice(jnp.asarray(table), (z, me, 0), (1, 1, flags + 2)).reshape(-1)
 
     even, odd = [cotangent], [cotangent]
 
@@ -811,9 +811,14 @@
         pairs = line_pairs(count, range(0, step), range(count - step, count))
         return tuple(along(v, p) for v, p in zip(values, pairs))
 
-    def chunks_of(group):
-        found = [(cotangent,) if s == 0 else (odd[s], even[count - s]) for s in group]
-        return [tuple(c for c in chunk if c is not None) for chunk in found]
+    def chunk(s):
+        if s == 0:
+            return None, cotangent
+        if s == 1:
+            return PICK, odd[1], joint
+        if s == count - 1:
+            return None, even[1]
+        return SUM, odd[s], even[count - s]
 
     pass_on(1)
     near, three, four = pool_call(key, value)
@@ -829,18 +834,26 @@
     attn, turned, lse, tops = forward_call(query, key, value, received, after=(place,))
     turned_other = swap(turned, "ctx", 1)
     products = product_call(attn, out_weight, place, count)
-    arrived = send_on(1, (products[1], products[count - 1]))
-    for step in range(3, count):
+    for step in range(3, count - 1):
         pass_on(step)
-
-    chunks = chunks_of(early)
-    mine, send = split_call(chunks, core, column, after=(products[1],))
+    is_end = jnp.logical_or(z == 0, z == count - 1)
+    ends = [(0, 1), (1, 0), (count - 2, count - 1), (count - 1, count - 2)]
+    ends_in = jnp.where(is_end, products[1], odd[-1])
+    joint = along(ends_in, ends)
+    arrived = (joint, None)
+
+    mine, send = split_call([chunk(s) for s in early], place, flags, column, after=(ends_in,))
     theirs = swap(send, "ctx", 1)
-    grad_attn = grad_call(chunks, out_weight, place, early, None, F32)
-    terms = term_call(turned, turned_other, mine, theirs, place, column)
-
-    level_max = jnp.transpose(held_back(tops, (terms, grad_attn))[:, :LEVELS, 0])
-    mask = 1
+    grad_attn = grad_call(
+        [chunk(s) for s in grad_early], out_weight, place, flags, grad_early, None, F32
+    )
+    level_max = jnp.transpose(tops[:, :LEVELS, 0])
+    level_max = jnp.maximum(level_max, swap(level_max, "ctx", 1))
+    terms = term_call(turned, turned_other, mine, theirs, column, (level_max, grad_attn))
+    level_max, terms = lax.optimization_barrier((level_max, terms))
+    level_max = jnp.maximum(level_max, swap(level_max, "ctx", 2))
+    before_split = level_max
+    mask = 4
     while mask < ctx_count:
         level_max = jnp.maximum(level_max, swap(level_max, "ctx", mask))
         mask *= 2
@@ -851,14 +864,14 @@
     for step in range(2, count - 1):
         sums = add_products(step, arrived)
         arrived = send_on(step, sums)
-    chunks = chunks_of(late)
     mine, send = split_call(
-        chunks, core, column, after=(terms, grad_attn, level_max, *[x for x in sums if x is not None])
+        [chunk(s) for s in late], place, flags, column, after=(terms, grad_attn, before_split, *[x for x in sums if x is not None])
     )
     theirs = swap(send, "ctx", 1)
-    terms = late_call(turned, turned_other, mine, theirs, terms, place, count, chips, column, ())
+    terms = late_call(turned, turned_other, mine, theirs, terms, place, count, chips, column, (level_max,))
     grad_attn = grad_call(
-        chunks, out_weight, place, late, grad_attn, BF16, after=tuple(terms)
+        [chunk(s) for s in grad_late], out_weight, place, flags, grad_late, grad_attn, BF16,
+        after=tuple(terms),
     )
     half, quarter = chips // 2, chips // 4
     first = [swap(terms[0], "ctx", 2 * bits[0]), swap(terms[2], "ctx", 2 * bits[-1])]

time: 166 us -> 163 us (0.982)
  starting transfers between devices: 34.9 us -> 31.3 us
  local copies, waits for them, and re-layouts: 16.7 us -> 18.9 us
  Pallas kernels: 66 us -> 64 us
    ppermute x17, starting transfers between devices: 15.7 us -> 12.7 us  [swap(): lax.ppermute(value, axis, [(i, i ^ mask) for i in range(lax.axis_size(axi...]
    pallas_call x2, Pallas kernels: 3.37 us -> 0.81 us  [add_call(): pl.pallas_call(add_kernel, grid=(2,), in_specs=[spec] * (2 * len(full)),...]
    unnamed x68 -> x66, local copies, waits for them, and re-layouts: 15 us -> 17.3 us
    ppermute x10 -> x9, waiting for transfers between devices: 15.5 us -> 14.3 us  [along(): return lax.ppermute(value, 'head', pairs) if pairs else None]
    ppermute x10 -> x9, starting transfers between devices: 19.2 us -> 18.6 us  [along(): return lax.ppermute(value, 'head', pairs) if pairs else None]
    pallas_call x6 -> x5, Pallas kernels: 19.4 us -> 19.9 us  [the longest x2 10.2 us: grad_call(): pl.pallas_call(functools.partial(grad_kernel, modes=tuple((c[0] for c in...]
  transfers between devices with their start and end apart: 27 -> 26, of which waited for: 13 -> 11; matrix products, arithmetic and copies ran while one was open for 1% -> 2% of each run, Pallas kernels for 38% -> 36%
where the time goes in v5:
time: 163 us; the launch traced here: 162 us
  Pallas kernels  64 us (39%)
  waiting for transfers between devices  45.3 us (28%)
  starting transfers between devices  31.3 us (19%)
  local copies, waits for them, and re-layouts  18.9 us (12%)
    ppermute x17, waiting for transfers between devices, swap(): lax.ppermute(value, axis, [(i, i ^ mask) for i in range(lax.axis_size(axi...  31 us
    ppermute x9, starting transfers between devices, along(): return lax.ppermute(value, 'head', pairs) if pairs else None  18.6 us
    unnamed x66, local copies, waits for them, and re-layouts  17.3 us
    ppermute x9, waiting for transfers between devices, along(): return lax.ppermute(value, 'head', pairs) if pairs else None  14.3 us
    ppermute x17, starting transfers between devices, swap(): lax.ppermute(value, axis, [(i, i ^ mask) for i in range(lax.axis_size(axi...  12.7 us
    pallas_call x1, Pallas kernels, backward_call(): pl.pallas_call(functools.partial(backward_kernel, extra=len(after)), grid...  12.2 us
    pallas_call x2, Pallas kernels, grad_call(): pl.pallas_call(functools.partial(grad_kernel, modes=tuple((c[0] for c in...  10.2 us
    pallas_call x1, Pallas kernels, forward_call(): pl.pallas_call(functools.partial(forward_kernel, extra=len(after)), grid=...  10.1 us
  transfers between devices with their start and end apart: 26, of which 11 were waited for; matrix products, arithmetic and copies ran while one was open for 2% of the time, Pallas kernels for 36%

profile of v5, /device:TPU:0, one launch (start us, length us, event | category | flops | bytes accessed | tf_op | source)
XLA Modules:
  0.0 162.0 jit_solution(3228333505881453072)
XLA Ops:
  0.6 3.1 %collective-permute-start.3 = (bf16[512,1024]{1,0:T(8,128)(2,1)}, bf16[512,1024]{1,0:T(8,128)(2,1)}, u32[]{:S(2)}, u32[]{:S(2)}) collective-permute-start(bf16[512,1024]{1,0:T(8,128)(2,1)} %refs_0_.5), channel_id=1, source_target_pairs={{0,1},{2,3},{1,0},{3,2},{4,5},{6,7},{5,4},{7,6},{8,9},{10,11},{9,8... | collective-permute-start | bytes 3145736 | tf_op jit(solution)/shard_map/ppermute | solution.py:768
  3.7 1.7 %collective-permute-start.4 = (bf16[512,1024]{1,0:T(8,128)(2,1)}, bf16[512,1024]{1,0:T(8,128)(2,1)}, u32[]{:S(2)}, u32[]{:S(2)}) collective-permute-start(bf16[512,1024]{1,0:T(8,128)(2,1)} %refs_0_.5), channel_id=1, source_target_pairs={{1,2},{2,1},{5,6},{6,5},{9,10},{10,9},{13,14},{14,13},{17,18},{18,... | collective-permute-start | bytes 3145736 | tf_op jit(solution)/shard_map/ppermute | solution.py:768
  5.4 1.2 copy-done.2
  6.6 1.2 copy-done.4
  7.9 1.7 %pool_keys.1 = (bf16[512,1024]{1,0:T(8,128)(2,1)}, bf16[128,1024]{1,0:T(8,128)(2,1)S(1)}, bf16[64,1024]{1,0:T(8,128)(2,1)S(1)}) custom-call(bf16[512,1024]{1,0:T(8,128)(2,1)S(1)} %copy-done.2, bf16[512,1024]{1,0:T(8,128)(2,1)S(1)} %copy-done.4), custom_call_target="tpu_custom_call" | custom-call | tf_op jit(solution)/shard_map/pool_keys/pallas_call | solution.py:65
  9.5 1.5 collective-permute-start
  11.0 1.5 collective-permute-start.1
  13.0 3.0 %collective-permute-done.1.four_a = bf16[64,1024]{1,0:T(8,128)(2,1)S(1)} collective-permute-done((bf16[64,1024]{1,0:T(8,128)(2,1)S(1)}, bf16[64,1024]{1,0:T(8,128)(2,1)S(1)}, u32[]{:S(2)}, u32[]{:S(2)}) %collective-permute-start.1) | collective-permute-done | bytes 131104 | tf_op jit(solution)/shard_map/ppermute | solution.py:758
  16.0 5.1 %collective-permute-done.2.four_b = bf16[64,1024]{1,0:T(8,128)(2,1)S(1)} collective-permute-done((bf16[64,1024]{1,0:T(8,128)(2,1)S(1)}, bf16[64,1024]{1,0:T(8,128)(2,1)S(1)}, u32[]{:S(2)}, u32[]{:S(2)}) %collective-permute-start.2) | collective-permute-done | bytes 131104 | tf_op jit(solution)/shard_map/ppermute | solution.py:758
  21.1 0.8 lower_rows.1
  21.9 5.3 %collective-permute-done.3.refs_3_.refs_2_ = bf16[512,1024]{1,0:T(8,128)(2,1)} collective-permute-done((bf16[512,1024]{1,0:T(8,128)(2,1)}, bf16[512,1024]{1,0:T(8,128)(2,1)}, u32[]{:S(2)}, u32[]{:S(2)}) %collective-permute-start.3) | collective-permute-done | bytes 1048608 | tf_op jit(solution)/shard_map/ppermute | solution.py:768
  28.0 1.3 collective-permute-start.12
  30.2 1.2 copy-done.8
  31.4 0.9 copy-done.23
  32.3 10.1 %attention_forward.1 = (bf16[512,1024]{1,0:T(8,128)(2,1)S(1)}, bf16[1024,512]{1,0:T(8,128)(2,1)}, f32[512,1024]{1,0:T(8,128)S(1)}, f32[8,8,128]{2,1,0:T(8,128)S(1)}) custom-call(bf16[512,1024]{1,0:T(8,128)(2,1)S(1)} %copy-done.8, bf16[512,1024]{1,0:T(8,128)(2,1)S(1)} %copy-done.3, bf16[512,1024]{1,0:T(8,128)(2,1)S(1)} %copy-done.5, ...), custom_call_target="tpu_custom_call" | custom-call | tf_op jit(solution)/shard_map/attention_forward/pallas_call | solution.py:222
  42.5 1.3 copy-done.18
  44.4 3.8 %copy-done = bf16[1024,4096]{1,0:T(8,128)(2,1)S(1)} copy-done((bf16[1024,4096]{1,0:T(8,128)(2,1)S(1)}, bf16[1024,4096]{1,0:T(8,128)(2,1)}, u32[]{:S(2)}) %copy-start) | copy-done | bytes 8388632
  48.2 7.4 %mixed_products.1 = (bf16[512,1024]{1,0:T(8,128)(2,1)S(1)}, bf16[512,1024]{1,0:T(8,128)(2,1)S(1)}, bf16[512,1024]{1,0:T(8,128)(2,1)S(1)}, bf16[512,1024]{1,0:T(8,128)(2,1)S(1)}) custom-call(s32[10]{0:T(128)S(1)} %dynamic-slice_bitcast_fusion.rest_0_.place_ref, bf16[512,1024]{1,0:T(8,128)(2,1)S(1)} %get-tuple-element.52.attn_ref, ...), custom_call_target="tpu_custom_call" | custom-call | tf_op jit(solution)/shard_map/mixed_products/pallas_call | solution.py:555
  55.7 1.1 broadcast_select_fusion.refs_4_
  56.8 3.9 %collective-permute-done.12.refs_2_ = bf16[512,1024]{1,0:T(8,128)(2,1)} collective-permute-done((bf16[512,1024]{1,0:T(8,128)(2,1)}, bf16[512,1024]{1,0:T(8,128)(2,1)}, u32[]{:S(2)}, u32[]{:S(2)}) %collective-permute-start.12) | collective-permute-done | bytes 1048608 | tf_op jit(solution)/shard_map/ppermute | solution.py:768
  60.7 2.6 %split_columns.2 = (bf16[512,1536]{1,0:T(8,128)(2,1)S(1)}, bf16[512,1536]{1,0:T(8,128)(2,1)}) custom-call(s32[10]{0:T(128)S(1)} %dynamic-slice_bitcast_fusion.rest_0_.place_ref, bf16[512,1024]{1,0:T(8,128)(2,1)S(1)} %copy-done.14, bf16[512,1024]{1,0:T(8,128)(2,1)S(1)} %collective-permute-done.6.refs_1_, bf16[512,1024]{1,0:T(8,128)(2,1)} %collective-permute-done.12.refs_2_, ...), custom_call_target="tpu_custom_call" | custom-call | tf_op jit(solution)/shard_map/split_columns/pallas_call | solution.py:481
  63.4 1.1 copy-done.20
  65.0 5.7 %collective-permute-start.7 = (bf16[512,1024]{1,0:T(8,128)(2,1)}, bf16[512,1024]{1,0:T(8,128)(2,1)S(1)}, u32[]{:S(2)}, u32[]{:S(2)}) collective-permute-start(bf16[512,1024]{1,0:T(8,128)(2,1)} %broadcast_select_fusion.refs_4_), channel_id=1, source_target_pairs={{0,1},{1,0},{2,3},{3,2},{4,5},{5,4},{6,7},{7,6},{8,9},{9,8},{10,11... | collective-permute-start | bytes 3145736 | tf_op jit(solution)/shard_map/ppermute | solution.py:768
  70.7 0.9 copy.15
  71.7 3.4 %copy-done.1 = bf16[1024,4096]{1,0:T(8,128)(2,1)S(1)} copy-done((bf16[1024,4096]{1,0:T(8,128)(2,1)S(1)}, bf16[1024,4096]{1,0:T(8,128)(2,1)}, u32[]{:S(2)}) %copy-start.1) | copy-done | bytes 8388632
  75.0 1.2 copy-done.7
  76.3 1.2 copy-done.15
  77.5 4.7 %grad_products.2.refs_1_.refs_3_.refs_5_ = f32[512,1024]{1,0:T(8,128)S(1)} custom-call(s32[10]{0:T(128)S(1)} %dynamic-slice_bitcast_fusion.rest_0_.place_ref, bf16[512,1024]{1,0:T(8,128)(2,1)S(1)} %copy-done.15, bf16[512,1024]{1,0:T(8,128)(2,1)S(1)} %copy-done.7, bf16[512,1024]{1,0:T(8,128)(2,1)} %collective-permute-done.12.refs_2_, ...), custom_call_target="tpu_custom_call" | custom-call | tf_op jit(solution)/shard_map/grad_products/pallas_call | solution.py:524
  82.3 5.6 %weight_terms.1.refs_2_.early_ref = bf16[3,1024,512]{2,1,0:T(8,128)(2,1)S(1)} custom-call(bf16[1024,512]{1,0:T(8,128)(2,1)} %get-tuple-element.60.own_ref, bf16[1024,512]{1,0:T(8,128)(2,1)} %collective-permute-done.10.other_ref, bf16[512,1536]{1,0:T(8,128)(2,1)S(1)} %copy-done.21, bf16[512,1536]{1,0:T(8,128)(2,1)} %collective-permute-done.13.theirs_ref, ...), custom_call_target="tpu_custom_call" | custom-call | tf_op jit(solution)/shard_map/weight_terms/pallas_call | solution.py:627
  87.9 1.6 collective-permute-start.14
  89.5 5.0 %collective-permute-done.7.refs_1_ = bf16[512,1024]{1,0:T(8,128)(2,1)S(1)} collective-permute-done((bf16[512,1024]{1,0:T(8,128)(2,1)}, bf16[512,1024]{1,0:T(8,128)(2,1)S(1)}, u32[]{:S(2)}, u32[]{:S(2)}) %collective-permute-start.7) | collective-permute-done | bytes 1048608 | tf_op jit(solution)/shard_map/ppermute | solution.py:768
  94.8 1.5 split_columns.3
  96.4 1.6 collective-permute-start.16
  98.0 3.7 %collective-permute-start.9 = (bf16[512,1024]{1,0:T(8,128)(2,1)S(1)}, bf16[512,1024]{1,0:T(8,128)(2,1)S(1)}, u32[]{:S(2)}, u32[]{:S(2)}) collective-permute-start(bf16[512,1024]{1,0:T(8,128)(2,1)S(1)} %copy-done.11), channel_id=1, source_target_pairs={{0,1},{3,2},{4,5},{7,6},{8,9},{11,10},{12,13},{15,14},{16,17},{19,... | collective-permute-start | bytes 3145736 | tf_op jit(solution)/shard_map/ppermute | solution.py:768
  101.7 0.9 collective-permute-start.8
  102.7 4.1 %weight_terms_late.1 = (bf16[2,512,512]{2,1,0:T(8,128)(2,1)S(1)}, bf16[2,512,512]{2,1,0:T(8,128)(2,1)S(1)}, bf16[2,512,512]{2,1,0:T(8,128)(2,1)S(1)}, bf16[2,512,512]{2,1,0:T(8,128)(2,1)S(1)}) custom-call(s32[10]{0:T(128)S(1)} %dynamic-slice_bitcast_fusion.rest_0_.place_ref, bf16[1024,512]{1,0:T(8,128)(2,1)} %get-tuple-element.60.own_ref, ...), custom_call_target="tpu_custom_call" | custom-call | tf_op jit(solution)/shard_map/weight_terms_late/pallas_call | solution.py:688
  106.8 1.5 collective-permute-start.17
  109.0 5.4 %grad_products.3.grad_ref = bf16[512,1024]{1,0:T(8,128)(2,1)S(1)} custom-call(s32[10]{0:T(128)S(1)} %dynamic-slice_bitcast_fusion.rest_0_.place_ref, bf16[512,1024]{1,0:T(8,128)(2,1)} %collective-permute-done.4.refs_0_, bf16[512,1024]{1,0:T(8,128)(2,1)S(1)} %collective-permute-done.7.refs_1_, bf16[512,1024]{1,0:T(8,128)(2,1)} %collective-permute-done.3.refs_3_.refs_2_, ...), custom_call_target="tpu_custom_call" | custom-call | tf_op jit(solution)/shard_map/grad_products/pallas_call | solution.py:524
  114.5 12.2 %attention_backward.1 = (f32[512,1024]{1,0:T(8,128)}, bf16[512,1024]{1,0:T(8,128)(2,1)S(1)}, bf16[512,1024]{1,0:T(8,128)(2,1)S(1)}, bf16[512,1024]{1,0:T(8,128)(...) custom-call(bf16[512,1024]{1,0:T(8,128)(2,1)S(1)} %copy-done.9, bf16[512,1024]{1,0:T(8,128)(2,1)S(1)} %copy-done.3, ...), custom_call_target="tpu_custom_call" | custom-call | tf_op jit(solution)/shard_map/attention_backward/pallas_call | solution.py:386
  127.3 4.5 %collective-permute-done.17.refs_1_ = bf16[2,512,512]{2,1,0:T(8,128)(2,1)S(1)} collective-permute-done((bf16[2,512,512]{2,1,0:T(8,128)(2,1)S(1)}, bf16[2,512,512]{2,1,0:T(8,128)(2,1)S(1)}, u32[]{:S(2)}, u32[]{:S(2)}) %collective-permute-start.17) | collective-permute-done | bytes 1048608 | tf_op jit(solution)/shard_map/ppermute | solution.py:758
  131.8 1.2 collective-permute-done.18.refs_3_
  136.3 1.5 collective-permute-start.25
  137.8 9.0 %collective-permute-done.22.three = bf16[192,1024]{1,0:T(8,128)(2,1)S(1)} collective-permute-done((bf16[192,1024]{1,0:T(8,128)(2,1)S(1)}, bf16[192,1024]{1,0:T(8,128)(2,1)S(1)}, u32[]{:S(2)}, u32[]{:S(2)}) %collective-permute-start.22) | collective-permute-done | bytes 393248 | tf_op jit(solution)/shard_map/ppermute | solution.py:758
  147.4 1.8 %collective-permute-done.24 = bf16[1,512,512]{2,1,0:T(8,128)(2,1)S(1)} collective-permute-done((bf16[1,512,512]{2,1,0:T(8,128)(2,1)S(1)}, bf16[1,512,512]{2,1,0:T(8,128)(2,1)S(1)}, u32[]{:S(2)}, u32[]{:S(2)}) %collective-permute-start.24) | collective-permute-done | bytes 524320 | tf_op jit(solution)/shard_map/ppermute | solution.py:758
  149.3 6.2 %collective-permute-done.25 = bf16[1,512,512]{2,1,0:T(8,128)(2,1)S(1)} collective-permute-done((bf16[1,512,512]{2,1,0:T(8,128)(2,1)S(1)}, bf16[1,512,512]{2,1,0:T(8,128)(2,1)S(1)}, u32[]{:S(2)}, u32[]{:S(2)}) %collective-permute-start.25) | collective-permute-done | bytes 524320 | tf_op jit(solution)/shard_map/ppermute | solution.py:758
  155.4 1.5 weight_total.1
  157.0 3.0 %add_returned.1 = (f32[512,1024]{1,0:T(8,128)}, f32[512,1024]{1,0:T(8,128)}) custom-call(bf16[512,1024]{1,0:T(8,128)(2,1)S(1)} %get-tuple-element.77.gk_ref, bf16[512,1024]{1,0:T(8,128)(2,1)S(1)} %get-tuple-element.78.gv_ref, bf16[512,1024]{1,0:T(8,128)(2,1)S(1)} %collective-permute-done.21.near, bf16[192,1024]{1,0:T(8,128)(2,1)S(1)} %collective-permute-done.22.three, ...), custom_call_target="tpu_custom_call" | custom-call | tf_op jit(solution)/shard_map/add_returned/pallas_call | solution.py:428
  160.0 2.0 %mixed_last.1 = f32[512,1024]{1,0:T(8,128)} custom-call(bf16[512,1024]{1,0:T(8,128)(2,1)S(1)} %copy-done.26, bf16[512,1024]{1,0:T(8,128)(2,1)S(1)} %collective-permute-done.19.left, bf16[512,1024]{1,0:T(8,128)(2,1)S(1)} %collective-permute-done.20.right), custom_call_target="tpu_custom_call" | custom-call | tf_op jit(solution)/shard_map/mixed_last/pallas_call | solution.py:605
  (96 shorter events, 9.0 us)
Async XLA Ops:
  0.6 26.6 %collective-permute-start.3 = (bf16[512,1024]{1,0:T(8,128)(2,1)}, bf16[512,1024]{1,0:T(8,128)(2,1)}, u32[]{:S(2)}, u32[]{:S(2)}) collective-permute-start(bf16[512,1024]{1,0:T(8,128)(2,1)} %refs_0_.5), channel_id=1, source_target_pairs={{0,1},{2,3},{1,0},{3,2},{4,5},{6,7},{5,4},{7,6},{8,9},{10,11},{9,8... | collective-permute-start | bytes 3145736 | tf_op jit(solution)/shard_map/ppermute | solution.py:768
  3.7 23.5 %collective-permute-start.4 = (bf16[512,1024]{1,0:T(8,128)(2,1)}, bf16[512,1024]{1,0:T(8,128)(2,1)}, u32[]{:S(2)}, u32[]{:S(2)}) collective-permute-start(bf16[512,1024]{1,0:T(8,128)(2,1)} %refs_0_.5), channel_id=1, source_target_pairs={{1,2},{2,1},{5,6},{6,5},{9,10},{10,9},{13,14},{14,13},{17,18},{18,... | collective-permute-start | bytes 3145736 | tf_op jit(solution)/shard_map/ppermute | solution.py:768
  7.8 22.4 %copy-start.3 = (bf16[512,1024]{1,0:T(8,128)(2,1)S(1)}, bf16[512,1024]{1,0:T(8,128)(2,1)}, u32[]{:S(2)}) copy-start(bf16[512,1024]{1,0:T(8,128)(2,1)} %k_ref.5) | copy-start | bytes 3145732
  7.9 22.4 %copy-start.5 = (bf16[512,1024]{1,0:T(8,128)(2,1)S(1)}, bf16[512,1024]{1,0:T(8,128)(2,1)}, u32[]{:S(2)}) copy-start(bf16[512,1024]{1,0:T(8,128)(2,1)} %v_ref.5) | copy-start | bytes 3145732
  9.5 11.5 %collective-permute-start = (bf16[128,1024]{1,0:T(8,128)(2,1)S(1)}, bf16[128,1024]{1,0:T(8,128)(2,1)S(1)}, u32[]{:S(2)}, u32[]{:S(2)}) collective-permute-start(bf16[128,1024]{1,0:T(8,128)(2,1)S(1)} %get-tuple-element.49), channel_id=1, source_target_pairs={{0,8},{4,12},{8,0},{12,4},{16,24},{20,28},{24,16},{28,20},{1,9},{5... | collective-permute-start | bytes 786440 | tf_op jit(solution)/shard_map/ppermute | solution.py:758
  11.0 5.0 %collective-permute-start.1 = (bf16[64,1024]{1,0:T(8,128)(2,1)S(1)}, bf16[64,1024]{1,0:T(8,128)(2,1)S(1)}, u32[]{:S(2)}, u32[]{:S(2)}) collective-permute-start(bf16[64,1024]{1,0:T(8,128)(2,1)S(1)} %get-tuple-element.50), channel_id=1, source_target_pairs={{0,16},{4,20},{8,24},{12,28},{16,0},{20,4},{24,8},{28,12},{1,17},{... | collective-permute-start | bytes 393224 | tf_op jit(solution)/shard_map/ppermute | solution.py:758
  12.5 8.5 %collective-permute-start.2 = (bf16[64,1024]{1,0:T(8,128)(2,1)S(1)}, bf16[64,1024]{1,0:T(8,128)(2,1)S(1)}, u32[]{:S(2)}, u32[]{:S(2)}) collective-permute-start(bf16[64,1024]{1,0:T(8,128)(2,1)S(1)} %get-tuple-element.50), channel_id=1, source_target_pairs={{0,24},{4,28},{8,16},{12,20},{16,8},{20,12},{24,0},{28,4},{1,25},{... | collective-permute-start | bytes 393224 | tf_op jit(solution)/shard_map/ppermute | solution.py:758
  21.1 6.1 %copy-start.22 = (bf16[64,1024]{1,0:T(8,128)(2,1)}, bf16[64,1024]{1,0:T(8,128)(2,1)S(1)}, u32[]{:S(2)}) copy-start(bf16[64,1024]{1,0:T(8,128)(2,1)S(1)} %collective-permute-done.2.four_b) | copy-start | bytes 393220
  27.2 3.0 %collective-permute-start.5 = (bf16[512,1024]{1,0:T(8,128)(2,1)}, bf16[512,1024]{1,0:T(8,128)(2,1)}, u32[]{:S(2)}, u32[]{:S(2)}) collective-permute-start(bf16[512,1024]{1,0:T(8,128)(2,1)} %lower_rows.1), channel_id=1, source_target_pairs={{0,4},{4,0},{8,12},{12,8},{16,20},{20,16},{24,28},{28,24},{1,5},{5... | collective-permute-start | bytes 3145736 | tf_op jit(solution)/shard_map/ppermute | solution.py:758
  27.2 28.4 %collective-permute-start.6 = (bf16[512,1024]{1,0:T(8,128)(2,1)}, bf16[512,1024]{1,0:T(8,128)(2,1)S(1)}, u32[]{:S(2)}, u32[]{:S(2)}) collective-permute-start(bf16[512,1024]{1,0:T(8,128)(2,1)} %collective-permute-done.3.refs_3_.refs_2_), channel_id=1, source_target_pairs={{1,2},{2,1},{5,6},{6,5},{9,10},{10,9},{13,14},{14,13},{17,18},{18,... | collective-permute-start | bytes 3145736 | tf_op jit(solution)/shard_map/ppermute | solution.py:768
  28.0 32.8 %collective-permute-start.12 = (bf16[512,1024]{1,0:T(8,128)(2,1)}, bf16[512,1024]{1,0:T(8,128)(2,1)}, u32[]{:S(2)}, u32[]{:S(2)}) collective-permute-start(bf16[512,1024]{1,0:T(8,128)(2,1)} %collective-permute-done.4.refs_0_), channel_id=1, source_target_pairs={{2,3},{1,0},{6,7},{5,4},{10,11},{9,8},{14,15},{13,12},{18,19},{17,... | collective-permute-start | bytes 3145736 | tf_op jit(solution)/shard_map/ppermute | solution.py:768
  44.4 11.2 %copy-start.12 = (bf16[512,1024]{1,0:T(8,128)(2,1)}, bf16[512,1024]{1,0:T(8,128)(2,1)S(1)}, u32[]{:S(2)}) copy-start(bf16[512,1024]{1,0:T(8,128)(2,1)S(1)} %get-tuple-element.52.attn_ref) | copy-start | bytes 3145732
  44.4 3.8 %copy-start = (bf16[1024,4096]{1,0:T(8,128)(2,1)S(1)}, bf16[1024,4096]{1,0:T(8,128)(2,1)}, u32[]{:S(2)}) copy-start(bf16[1024,4096]{1,0:T(8,128)(2,1)} %refs_4_.3) | copy-start | bytes 25165828
  55.6 7.7 %copy-start.10 = (bf16[512,1024]{1,0:T(8,128)(2,1)}, bf16[512,1024]{1,0:T(8,128)(2,1)S(1)}, u32[]{:S(2)}) copy-start(bf16[512,1024]{1,0:T(8,128)(2,1)S(1)} %get-tuple-element.55.refs_0_.refs_5_) | copy-start | bytes 3145732
  55.6 7.7 %copy-start.16 = (bf16[512,1024]{1,0:T(8,128)(2,1)}, bf16[512,1024]{1,0:T(8,128)(2,1)S(1)}, u32[]{:S(2)}) copy-start(bf16[512,1024]{1,0:T(8,128)(2,1)S(1)} %get-tuple-element.56.refs_2_) | copy-start | bytes 3145732
  55.6 7.7 %copy-start.25 = (bf16[512,1024]{1,0:T(8,128)(2,1)}, bf16[512,1024]{1,0:T(8,128)(2,1)S(1)}, u32[]{:S(2)}) copy-start(bf16[512,1024]{1,0:T(8,128)(2,1)S(1)} %get-tuple-element.53.own) | copy-start | bytes 3145732
  55.6 7.7 %copy-start.27 = (bf16[512,1024]{1,0:T(8,128)(2,1)}, bf16[512,1024]{1,0:T(8,128)(2,1)S(1)}, u32[]{:S(2)}) copy-start(bf16[512,1024]{1,0:T(8,128)(2,1)S(1)} %get-tuple-element.54.refs_0_) | copy-start | bytes 3145732
  55.6 5.1 %copy-start.14 = (bf16[512,1024]{1,0:T(8,128)(2,1)S(1)}, bf16[512,1024]{1,0:T(8,128)(2,1)}, u32[]{:S(2)}) copy-start(bf16[512,1024]{1,0:T(8,128)(2,1)} %refs_0_.5) | copy-start | bytes 3145732
  55.7 7.7 %copy-start.6 = (bf16[512,1024]{1,0:T(8,128)(2,1)}, bf16[512,1024]{1,0:T(8,128)(2,1)S(1)}, u32[]{:S(2)}) copy-start(bf16[512,1024]{1,0:T(8,128)(2,1)S(1)} %collective-permute-done.6.refs_1_) | copy-start | bytes 3145732
  64.5 17.7 %collective-permute-start.13 = (bf16[512,1536]{1,0:T(8,128)(2,1)}, bf16[512,1536]{1,0:T(8,128)(2,1)}, u32[]{:S(2)}, u32[]{:S(2)}) collective-permute-start(bf16[512,1536]{1,0:T(8,128)(2,1)} %get-tuple-element.64), channel_id=1, source_target_pairs={{0,4},{4,0},{8,12},{12,8},{16,20},{20,16},{24,28},{28,24},{1,5},{5... | collective-permute-start | bytes 4718600 | tf_op jit(solution)/shard_map/ppermute | solution.py:758
  64.5 17.7 %collective-permute-start.10 = (bf16[1024,512]{1,0:T(8,128)(2,1)}, bf16[1024,512]{1,0:T(8,128)(2,1)}, u32[]{:S(2)}, u32[]{:S(2)}) collective-permute-start(bf16[1024,512]{1,0:T(8,128)(2,1)} %get-tuple-element.60.own_ref), channel_id=1, source_target_pairs={{0,4},{4,0},{8,12},{12,8},{16,20},{20,16},{24,28},{28,24},{1,5},{5... | collective-permute-start | bytes 3145736 | tf_op jit(solution)/shard_map/ppermute | solution.py:758
  65.0 29.5 %collective-permute-start.7 = (bf16[512,1024]{1,0:T(8,128)(2,1)}, bf16[512,1024]{1,0:T(8,128)(2,1)S(1)}, u32[]{:S(2)}, u32[]{:S(2)}) collective-permute-start(bf16[512,1024]{1,0:T(8,128)(2,1)} %broadcast_select_fusion.refs_4_), channel_id=1, source_target_pairs={{0,1},{1,0},{2,3},{3,2},{4,5},{5,4},{6,7},{7,6},{8,9},{9,8},{10,11... | collective-permute-start | bytes 3145736 | tf_op jit(solution)/shard_map/ppermute | solution.py:768
  71.6 10.6 %collective-permute-start.11 = (f32[5,8]{1,0:T(8,128)S(1)}, f32[5,8]{1,0:T(8,128)S(1)}, u32[]{:S(2)}, u32[]{:S(2)}) collective-permute-start(f32[5,8]{1,0:T(8,128)S(1)} %bitcast.18), channel_id=1, source_target_pairs={{0,4},{4,0},{8,12},{12,8},{16,20},{20,16},{24,28},{28,24},{1,5},{5... | collective-permute-start | bytes 488 | tf_op jit(solution)/shard_map/ppermute | solution.py:758
  77.5 4.8 %copy-start.21 = (bf16[512,1536]{1,0:T(8,128)(2,1)S(1)}, bf16[512,1536]{1,0:T(8,128)(2,1)}, u32[]{:S(2)}) copy-start(bf16[512,1536]{1,0:T(8,128)(2,1)} %copy-done.20) | copy-start | bytes 4718596
  82.3 12.2 %copy-start.11 = (bf16[512,1024]{1,0:T(8,128)(2,1)S(1)}, bf16[512,1024]{1,0:T(8,128)(2,1)}, u32[]{:S(2)}) copy-start(bf16[512,1024]{1,0:T(8,128)(2,1)} %copy-done.10) | copy-start | bytes 3145732
  87.9 6.9 %collective-permute-start.14 = (f32[5,8]{1,0:T(8,128)S(1)}, f32[5,8]{1,0:T(8,128)S(1)}, u32[]{:S(2)}, u32[]{:S(2)}) collective-permute-start(f32[5,8]{1,0:T(8,128)S(1)} %bitcast_maximum_fusion.refs_0_), channel_id=1, source_target_pairs={{0,8},{4,12},{8,0},{12,4},{16,24},{20,28},{24,16},{28,20},{1,9},{5... | collective-permute-start | bytes 488 | tf_op jit(solution)/shard_map/ppermute | solution.py:758
  94.5 14.5 %slice-start = ((s8[8388608]{0:T(1024)(128)(4,1)}), s8[4194304]{0:T(1024)(128)(4,1)S(1)}, s32[]{:S(2)}) async-start(s8[8388608]{0:T(1024)(128)(4,1)} %bitcast.11), calls=%async_computation | async-start | bytes 8388608
  94.8 14.2 %slice-start.1 = ((s8[8388608]{0:T(1024)(128)(4,1)}), s8[4194304]{0:T(1024)(128)(4,1)S(1)}, s32[]{:S(2)}) async-start(s8[8388608]{0:T(1024)(128)(4,1)} %bitcast.11), calls=%async_computation.1 | async-start | bytes 8388608
  96.3 6.3 %collective-permute-start.15 = (bf16[512,512]{1,0:T(8,128)(2,1)S(1)}, bf16[512,512]{1,0:T(8,128)(2,1)S(1)}, u32[]{:S(2)}, u32[]{:S(2)}) collective-permute-start(bf16[512,512]{1,0:T(8,128)(2,1)S(1)} %get-tuple-element.68), channel_id=1, source_target_pairs={{0,4},{4,0},{8,12},{12,8},{16,20},{20,16},{24,28},{28,24},{1,5},{5... | collective-permute-start | bytes 1572872 | tf_op jit(solution)/shard_map/ppermute | solution.py:758
  96.4 6.2 %collective-permute-start.16 = (f32[5,8]{1,0:T(8,128)S(1)}, f32[5,8]{1,0:T(8,128)S(1)}, u32[]{:S(2)}, u32[]{:S(2)}) collective-permute-start(f32[5,8]{1,0:T(8,128)S(1)} %max.10.refs_4_), channel_id=1, source_target_pairs={{0,16},{4,20},{8,24},{12,28},{16,0},{20,4},{24,8},{28,12},{1,17},{... | collective-permute-start | bytes 488 | tf_op jit(solution)/shard_map/ppermute | solution.py:758
  98.0 28.7 %collective-permute-start.9 = (bf16[512,1024]{1,0:T(8,128)(2,1)S(1)}, bf16[512,1024]{1,0:T(8,128)(2,1)S(1)}, u32[]{:S(2)}, u32[]{:S(2)}) collective-permute-start(bf16[512,1024]{1,0:T(8,128)(2,1)S(1)} %copy-done.11), channel_id=1, source_target_pairs={{0,1},{3,2},{4,5},{7,6},{8,9},{11,10},{12,13},{15,14},{16,17},{19,... | collective-permute-start | bytes 3145736 | tf_op jit(solution)/shard_map/ppermute | solution.py:768
  101.7 25.0 %collective-permute-start.8 = (bf16[512,1024]{1,0:T(8,128)(2,1)S(1)}, bf16[512,1024]{1,0:T(8,128)(2,1)S(1)}, u32[]{:S(2)}, u32[]{:S(2)}) collective-permute-start(bf16[512,1024]{1,0:T(8,128)(2,1)S(1)} %mixed_add.2.refs_6_), channel_id=1, source_target_pairs={{1,2},{2,1},{5,6},{6,5},{9,10},{10,9},{13,14},{14,13},{17,18},{18,... | collective-permute-start | bytes 3145736 | tf_op jit(solution)/shard_map/ppermute | solution.py:768
  102.6 4.2 %copy-start.30 = (f32[5,8]{1,0:T(8,128)}, f32[5,8]{1,0:T(8,128)S(1)}, u32[]{:S(2)}) copy-start(f32[5,8]{1,0:T(8,128)S(1)} %max.11.refs_0_) | copy-start | bytes 484
  106.8 25.0 %collective-permute-start.17 = (bf16[2,512,512]{2,1,0:T(8,128)(2,1)S(1)}, bf16[2,512,512]{2,1,0:T(8,128)(2,1)S(1)}, u32[]{:S(2)}, u32[]{:S(2)}) collective-permute-start(bf16[2,512,512]{2,1,0:T(8,128)(2,1)S(1)} %get-tuple-element.69.refs_6_.rest_0_), channel_id=1, source_target_pairs={{0,8},{4,12},{8,0},{12,4},{16,24},{20,28},{24,16},{28,20},{1,9},{5... | collective-permute-start | bytes 3145736 | tf_op jit(solution)/shard_map/ppermute | solution.py:758
  108.3 24.7 %collective-permute-start.18 = (bf16[2,512,512]{2,1,0:T(8,128)(2,1)S(1)}, bf16[2,512,512]{2,1,0:T(8,128)(2,1)S(1)}, u32[]{:S(2)}, u32[]{:S(2)}) collective-permute-start(bf16[2,512,512]{2,1,0:T(8,128)(2,1)S(1)} %get-tuple-element.70.refs_8_.rest_2_), channel_id=1, source_target_pairs={{0,16},{4,20},{8,24},{12,28},{16,0},{20,4},{24,8},{28,12},{1,17},{... | collective-permute-start | bytes 3145736 | tf_op jit(solution)/shard_map/ppermute | solution.py:758
  109.0 5.5 %copy-start.9 = (bf16[512,1024]{1,0:T(8,128)(2,1)S(1)}, bf16[512,1024]{1,0:T(8,128)(2,1)}, u32[]{:S(2)}) copy-start(bf16[512,1024]{1,0:T(8,128)(2,1)} %q_ref.3) | copy-start | bytes 3145732
  109.0 5.5 %copy-start.13 = (bf16[512,1024]{1,0:T(8,128)(2,1)S(1)}, bf16[512,1024]{1,0:T(8,128)(2,1)}, u32[]{:S(2)}) copy-start(bf16[512,1024]{1,0:T(8,128)(2,1)} %copy-done.12) | copy-start | bytes 3145732
  109.0 5.5 %copy-start.19 = (f32[512,1024]{1,0:T(8,128)S(1)}, f32[512,1024]{1,0:T(8,128)}, u32[]{:S(2)}) copy-start(f32[512,1024]{1,0:T(8,128)} %copy-done.18) | copy-start | bytes 6291460
  109.0 5.5 %copy-start.24 = (bf16[64,1024]{1,0:T(8,128)(2,1)S(1)}, bf16[64,1024]{1,0:T(8,128)(2,1)}, u32[]{:S(2)}) copy-start(bf16[64,1024]{1,0:T(8,128)(2,1)} %copy-done.22) | copy-start | bytes 393220
  114.5 12.2 %copy-start.17 = (bf16[512,1024]{1,0:T(8,128)(2,1)S(1)}, bf16[512,1024]{1,0:T(8,128)(2,1)}, u32[]{:S(2)}) copy-start(bf16[512,1024]{1,0:T(8,128)(2,1)} %copy-done.16) | copy-start | bytes 3145732
  114.5 12.2 %copy-start.28 = (bf16[512,1024]{1,0:T(8,128)(2,1)S(1)}, bf16[512,1024]{1,0:T(8,128)(2,1)}, u32[]{:S(2)}) copy-start(bf16[512,1024]{1,0:T(8,128)(2,1)} %copy-done.27) | copy-start | bytes 3145732
  126.7 7.8 %collective-permute-start.21 = (bf16[512,1024]{1,0:T(8,128)(2,1)S(1)}, bf16[512,1024]{1,0:T(8,128)(2,1)S(1)}, u32[]{:S(2)}, u32[]{:S(2)}) collective-permute-start(bf16[512,1024]{1,0:T(8,128)(2,1)S(1)} %get-tuple-element.79), channel_id=1, source_target_pairs={{0,4},{4,0},{8,12},{12,8},{16,20},{20,16},{24,28},{28,24},{1,5},{5... | collective-permute-start | bytes 3145736 | tf_op jit(solution)/shard_map/ppermute | solution.py:758
  133.0 27.0 %collective-permute-start.19 = (bf16[512,1024]{1,0:T(8,128)(2,1)S(1)}, bf16[512,1024]{1,0:T(8,128)(2,1)S(1)}, u32[]{:S(2)}, u32[]{:S(2)}) collective-permute-start(bf16[512,1024]{1,0:T(8,128)(2,1)S(1)} %get-tuple-element.71), channel_id=1, source_target_pairs={{0,1},{2,3},{1,0},{3,2},{4,5},{6,7},{5,4},{7,6},{8,9},{10,11},{9,8... | collective-permute-start | bytes 3145736 | tf_op jit(solution)/shard_map/ppermute | solution.py:768
  133.8 26.2 %collective-permute-start.20 = (bf16[512,1024]{1,0:T(8,128)(2,1)S(1)}, bf16[512,1024]{1,0:T(8,128)(2,1)S(1)}, u32[]{:S(2)}, u32[]{:S(2)}) collective-permute-start(bf16[512,1024]{1,0:T(8,128)(2,1)S(1)} %get-tuple-element.72), channel_id=1, source_target_pairs={{1,2},{2,1},{5,6},{6,5},{9,10},{10,9},{13,14},{14,13},{17,18},{18,... | collective-permute-start | bytes 3145736 | tf_op jit(solution)/shard_map/ppermute | solution.py:768
  134.7 12.1 %collective-permute-start.22 = (bf16[192,1024]{1,0:T(8,128)(2,1)S(1)}, bf16[192,1024]{1,0:T(8,128)(2,1)S(1)}, u32[]{:S(2)}, u32[]{:S(2)}) collective-permute-start(bf16[192,1024]{1,0:T(8,128)(2,1)S(1)} %add_convert_fusion), channel_id=1, source_target_pairs={{0,8},{4,12},{8,0},{12,4},{16,24},{20,28},{24,16},{28,20},{1,9},{5... | collective-permute-start | bytes 1179656 | tf_op jit(solution)/shard_map/ppermute | solution.py:758
  135.8 13.5 %collective-permute-start.24 = (bf16[1,512,512]{2,1,0:T(8,128)(2,1)S(1)}, bf16[1,512,512]{2,1,0:T(8,128)(2,1)S(1)}, u32[]{:S(2)}, u32[]{:S(2)}) collective-permute-start(bf16[1,512,512]{2,1,0:T(8,128)(2,1)S(1)} %get-tuple-element.87), channel_id=1, source_target_pairs={{0,16},{4,20},{8,24},{12,28},{16,0},{20,4},{24,8},{28,12},{1,17},{... | collective-permute-start | bytes 1572872 | tf_op jit(solution)/shard_map/ppermute | solution.py:758
  136.3 19.1 %collective-permute-start.25 = (bf16[1,512,512]{2,1,0:T(8,128)(2,1)S(1)}, bf16[1,512,512]{2,1,0:T(8,128)(2,1)S(1)}, u32[]{:S(2)}, u32[]{:S(2)}) collective-permute-start(bf16[1,512,512]{2,1,0:T(8,128)(2,1)S(1)} %get-tuple-element.89), channel_id=1, source_target_pairs={{0,8},{4,12},{8,0},{12,4},{16,24},{20,28},{24,16},{28,20},{1,9},{5... | collective-permute-start | bytes 1572872 | tf_op jit(solution)/shard_map/ppermute | solution.py:758
  146.9 10.1 %collective-permute-start.23 = (bf16[64,1024]{1,0:T(8,128)(2,1)S(1)}, bf16[64,1024]{1,0:T(8,128)(2,1)S(1)}, u32[]{:S(2)}, u32[]{:S(2)}) collective-permute-start(bf16[64,1024]{1,0:T(8,128)(2,1)S(1)} %add_convert_fusion.1), channel_id=1, source_target_pairs={{0,16},{4,20},{8,24},{12,28},{16,0},{20,4},{24,8},{28,12},{1,17},{... | collective-permute-start | bytes 393224 | tf_op jit(solution)/shard_map/ppermute | solution.py:758
  (11 other events, 16.5 us)

commit v6 on v5

--- a/solution.py
+++ b/solution.py
@@ -566,7 +566,7 @@
             out_specs=[spec] * count,
         ),
         out_shape=[jax.ShapeDtypeStruct((tokens, width), BF16)] * count,
-        compiler_params=pltpu.CompilerParams(vmem_limit_bytes=VMEM_LIMIT),
+        compiler_params=pltpu.CompilerParams(vmem_limit_bytes=50 * 1024 * 1024),
         name="mixed_products",
     )(place, attn, *[out_weight] * count, *after)
 
@@ -700,20 +700,24 @@
     )(place, own, other, mine, theirs, early, *after)
 
 
-def total_kernel(top_a, top_b, bottom_a, bottom_b, out):
+def total_kernel(top_a, top_b, bottom_a, bottom_b, *refs):
+    out = refs[-1]
     half = top_a.shape[0]
     out[pl.ds(0, half), :] = top_a[...].astype(F32) + top_b[...].astype(F32)
     out[pl.ds(half, half), :] = bottom_a[...].astype(F32) + bottom_b[...].astype(F32)
 
 
-def total_call(top, bottom):
+def total_call(top, bottom, after):
     rows, column = top[0].shape
+    spec = pl.BlockSpec((rows, column), lambda: (0, 0))
     return pl.pallas_call(
         total_kernel,
+        in_specs=[spec] * 4 + [pl.BlockSpec(memory_space=pl.ANY)] * len(after),
+        out_specs=pl.BlockSpec((2 * rows, column), lambda: (0, 0)),
         out_shape=jax.ShapeDtypeStruct((2 * rows, column), F32),
         compiler_params=pltpu.CompilerParams(vmem_limit_bytes=VMEM_LIMIT),
         name="weight_total",
-    )(*top, *bottom)
+    )(*top, *bottom, *after)
 
 
 def term_order(chips):
@@ -842,18 +846,21 @@
     joint = along(ends_in, ends)
     arrived = (joint, None)
 
-    mine, send = split_call([chunk(s) for s in early], place, flags, column, after=(ends_in,))
+    level_max = jnp.transpose(tops[:, :LEVELS, 0])
+    level_max = jnp.maximum(level_max, swap(level_max, "ctx", 1))
+
+    mine, send = split_call([chunk(s) for s in early], place, flags, column, after=(ends_in, level_max))
     theirs = swap(send, "ctx", 1)
     grad_attn = grad_call(
         [chunk(s) for s in grad_early], out_weight, place, flags, grad_early, None, F32
     )
-    level_max = jnp.transpose(tops[:, :LEVELS, 0])
-    level_max = jnp.maximum(level_max, swap(level_max, "ctx", 1))
-    terms = term_call(turned, turned_other, mine, theirs, column, (level_max, grad_attn))
+    level_max, theirs = lax.optimization_barrier((level_max, theirs))
+    level_max = jnp.maximum(level_max, swap(level_max, "ctx", 2))
+    terms = term_call(turned, turned_other, mine, theirs, column, (grad_attn, level_max))
     level_max, terms = lax.optimization_barrier((level_max, terms))
-    level_max = jnp.maximum(level_max, swap(level_max, "ctx", 2))
+    level_max = jnp.maximum(level_max, swap(level_max, "ctx", 4))
     before_split = level_max
-    mask = 4
+    mask = 8
     while mask < ctx_count:
         level_max = jnp.maximum(level_max, swap(level_max, "ctx", mask))
         mask *= 2
@@ -897,7 +904,6 @@
         kept = [f[1][1] for f in folded]
         first = [swap(f[1][0], "ctx", 2 * ways[k][n + 1]) for k, f in enumerate(folded)]
     top, bottom = [(kept[k][0], first[k][0]) for k in (0, 1)]
-    weight_grad = total_call(top, bottom)
     mixed = last_call(products[0], *arrived)
 
     grad_q, grad_k, grad_v, far, keep, four = outs
@@ -907,6 +913,7 @@
     four = four.astype(F32) + far[2 * BLK + third :] + back[BLK:]
     four = swap(four.astype(BF16), "ctx", 4)
     grad_k, grad_v = finish_call(grad_k, grad_v, far, back, four)
+    weight_grad = total_call(top, bottom, (grad_k,))
     return mixed, grad_q, grad_k, grad_v, weight_grad, level_max
 
 

time: 163 us -> 154 us (0.945)
  local copies, waits for them, and re-layouts: 18.9 us -> 9.39 us
  waiting for transfers between devices: 45.3 us -> 48.3 us
  Pallas kernels: 64 us -> 61.4 us
  starting transfers between devices: 31.3 us -> 33 us
    unnamed x66 -> x36, local copies, waits for them, and re-layouts: 17.3 us -> 8.56 us
    ppermute x9, waiting for transfers between devices: 14.3 us -> 22.6 us  [along(): return lax.ppermute(value, 'head', pairs) if pairs else None]
    ppermute x17, waiting for transfers between devices: 31 us -> 25.7 us  [swap(): lax.ppermute(value, axis, [(i, i ^ mask) for i in range(lax.axis_size(axi...]
    ppermute x17, starting transfers between devices: 12.7 us -> 16.1 us  [swap(): lax.ppermute(value, axis, [(i, i ^ mask) for i in range(lax.axis_size(axi...]
    pallas_call x1, Pallas kernels: 7.42 us -> 9.38 us  [product_call(): pl.pallas_call(functools.partial(product_kernel, count=count), grid_spec=...]
    ppermute x9, starting transfers between devices: 18.6 us -> 17 us  [along(): return lax.ppermute(value, 'head', pairs) if pairs else None]
    pallas_call x1, Pallas kernels: 5.65 us -> 4.01 us  [term_call(): pl.pallas_call(term_kernel, grid=(count,), in_specs=[whole, whole, source...]
  transfers between devices with their start and end apart: 26 -> 26, of which waited for: 11 -> 10; matrix products, arithmetic and copies ran while one was open for 2% -> 1% of each run, Pallas kernels for 36% -> 37%
where the time goes in v6:
time: 154 us; the launch traced here: 153 us
  Pallas kernels  61.4 us (40%)
  waiting for transfers between devices  48.3 us (31%)
  starting transfers between devices  33 us (21%)
  local copies, waits for them, and re-layouts  9.39 us (6%)
    ppermute x17, waiting for transfers between devices, swap(): lax.ppermute(value, axis, [(i, i ^ mask) for i in range(lax.axis_size(axi...  25.7 us
    ppermute x9, waiting for transfers between devices, along(): return lax.ppermute(value, 'head', pairs) if pairs else None  22.6 us
    ppermute x9, starting transfers between devices, along(): return lax.ppermute(value, 'head', pairs) if pairs else None  17 us
    ppermute x17, starting transfers between devices, swap(): lax.ppermute(value, axis, [(i, i ^ mask) for i in range(lax.axis_size(axi...  16.1 us
    pallas_call x1, Pallas kernels, backward_call(): pl.pallas_call(functools.partial(backward_kernel, extra=len(after)), grid...  12 us
    pallas_call x2, Pallas kernels, grad_call(): pl.pallas_call(functools.partial(grad_kernel, modes=tuple((c[0] for c in...  10.4 us
    pallas_call x1, Pallas kernels, forward_call(): pl.pallas_call(functools.partial(forward_kernel, extra=len(after)), grid=...  9.44 us
    pallas_call x1, Pallas kernels, product_call(): pl.pallas_call(functools.partial(product_kernel, count=count), grid_spec=...  9.38 us
  transfers between devices with their start and end apart: 26, of which 10 were waited for; matrix products, arithmetic and copies ran while one was open for 1% of the time, Pallas kernels for 37%

profile of v6, /device:TPU:0, one launch (start us, length us, event | category | flops | bytes accessed | tf_op | source)
XLA Modules:
  0.0 153.5 jit_solution(7357903112491027574)
XLA Ops:
  0.6 3.1 %collective-permute-start.3 = (bf16[512,1024]{1,0:T(8,128)(2,1)}, bf16[512,1024]{1,0:T(8,128)(2,1)}, u32[]{:S(2)}, u32[]{:S(2)}) collective-permute-start(bf16[512,1024]{1,0:T(8,128)(2,1)} %refs_0_.5), channel_id=1, source_target_pairs={{0,1},{2,3},{1,0},{3,2},{4,5},{6,7},{5,4},{7,6},{8,9},{10,11},{9,8... | collective-permute-start | bytes 3145736 | tf_op jit(solution)/shard_map/ppermute | solution.py:772
  3.7 1.6 %collective-permute-start.4 = (bf16[512,1024]{1,0:T(8,128)(2,1)}, bf16[512,1024]{1,0:T(8,128)(2,1)}, u32[]{:S(2)}, u32[]{:S(2)}) collective-permute-start(bf16[512,1024]{1,0:T(8,128)(2,1)} %refs_0_.5), channel_id=1, source_target_pairs={{1,2},{2,1},{5,6},{6,5},{9,10},{10,9},{13,14},{14,13},{17,18},{18,... | collective-permute-start | bytes 3145736 | tf_op jit(solution)/shard_map/ppermute | solution.py:772
  5.4 1.2 copy-done
  6.6 1.2 copy-done.2
  7.8 1.7 %pool_keys.1 = (bf16[512,1024]{1,0:T(8,128)(2,1)}, bf16[128,1024]{1,0:T(8,128)(2,1)S(1)}, bf16[64,1024]{1,0:T(8,128)(2,1)S(1)}) custom-call(bf16[512,1024]{1,0:T(8,128)(2,1)S(1)} %copy-done, bf16[512,1024]{1,0:T(8,128)(2,1)S(1)} %copy-done.2), custom_call_target="tpu_custom_call" | custom-call | tf_op jit(solution)/shard_map/pool_keys/pallas_call | solution.py:65
  9.5 1.5 collective-permute-start
  11.0 1.5 collective-permute-start.1
  13.0 3.0 %collective-permute-done.1.four_a = bf16[64,1024]{1,0:T(8,128)(2,1)S(1)} collective-permute-done((bf16[64,1024]{1,0:T(8,128)(2,1)S(1)}, bf16[64,1024]{1,0:T(8,128)(2,1)S(1)}, u32[]{:S(2)}, u32[]{:S(2)}) %collective-permute-start.1) | collective-permute-done | bytes 131104 | tf_op jit(solution)/shard_map/ppermute | solution.py:762
  15.9 5.1 %collective-permute-done.2.four_b = bf16[64,1024]{1,0:T(8,128)(2,1)S(1)} collective-permute-done((bf16[64,1024]{1,0:T(8,128)(2,1)S(1)}, bf16[64,1024]{1,0:T(8,128)(2,1)S(1)}, u32[]{:S(2)}, u32[]{:S(2)}) %collective-permute-start.2) | collective-permute-done | bytes 131104 | tf_op jit(solution)/shard_map/ppermute | solution.py:762
  21.0 0.8 lower_rows.1
  21.8 5.4 %collective-permute-done.3.refs_3_.refs_2_ = bf16[512,1024]{1,0:T(8,128)(2,1)} collective-permute-done((bf16[512,1024]{1,0:T(8,128)(2,1)}, bf16[512,1024]{1,0:T(8,128)(2,1)}, u32[]{:S(2)}, u32[]{:S(2)}) %collective-permute-start.3) | collective-permute-done | bytes 1048608 | tf_op jit(solution)/shard_map/ppermute | solution.py:772
  27.2 1.6 %collective-permute-start.6 = (bf16[512,1024]{1,0:T(8,128)(2,1)}, bf16[512,1024]{1,0:T(8,128)(2,1)}, u32[]{:S(2)}, u32[]{:S(2)}) collective-permute-start(bf16[512,1024]{1,0:T(8,128)(2,1)} %collective-permute-done.3.refs_3_.refs_2_), channel_id=1, source_target_pairs={{1,2},{2,1},{5,6},{6,5},{9,10},{10,9},{13,14},{14,13},{17,18},{18,... | collective-permute-start | bytes 3145736 | tf_op jit(solution)/shard_map/ppermute | solution.py:772
  28.8 1.3 collective-permute-start.12
  30.9 1.2 copy-done.4
  32.1 9.4 %attention_forward.1 = (bf16[512,1024]{1,0:T(8,128)(2,1)S(1)}, bf16[1024,512]{1,0:T(8,128)(2,1)S(1)}, f32[512,1024]{1,0:T(8,128)S(1)}, f32[8,8,128]{2,1,0:T(8,128)S(1)}) custom-call(bf16[512,1024]{1,0:T(8,128)(2,1)S(1)} %copy-done.4, bf16[512,1024]{1,0:T(8,128)(2,1)S(1)} %copy-done.1, bf16[512,1024]{1,0:T(8,128)(2,1)S(1)} %copy-done.3, ...), custom_call_target="tpu_custom_call" | custom-call | tf_op jit(solution)/shard_map/attention_forward/pallas_call | solution.py:222
  41.6 1.0 copy-done.6
  42.5 1.0 copy-done.9
  43.5 1.3 copy-done.11
  45.5 9.4 %mixed_products.1 = (bf16[512,1024]{1,0:T(8,128)(2,1)S(1)}, bf16[512,1024]{1,0:T(8,128)(2,1)S(1)}, bf16[512,1024]{1,0:T(8,128)(2,1)S(1)}, bf16[512,1024]{1,0:T(8,128)(2,1)}) custom-call(s32[10]{0:T(128)S(1)} %dynamic-slice_bitcast_fusion.rest_0_.place_ref, bf16[512,1024]{1,0:T(8,128)(2,1)} %copy-done.6, bf16[1024,4096]{1,0:T(8,128)(2,1)} %refs_4_.3, ...), custom_call_target="tpu_custom_call" | custom-call | tf_op jit(solution)/shard_map/mixed_products/pallas_call | solution.py:555
  55.0 5.7 %collective-permute-done.12.refs_2_ = bf16[512,1024]{1,0:T(8,128)(2,1)} collective-permute-done((bf16[512,1024]{1,0:T(8,128)(2,1)}, bf16[512,1024]{1,0:T(8,128)(2,1)}, u32[]{:S(2)}, u32[]{:S(2)}) %collective-permute-start.12) | collective-permute-done | bytes 1048608 | tf_op jit(solution)/shard_map/ppermute | solution.py:772
  60.7 2.0 %split_columns.2 = (bf16[512,1536]{1,0:T(8,128)(2,1)S(1)}, bf16[512,1536]{1,0:T(8,128)(2,1)S(1)}) custom-call(s32[10]{0:T(128)S(1)} %dynamic-slice_bitcast_fusion.rest_0_.place_ref, bf16[512,1024]{1,0:T(8,128)(2,1)S(1)} %copy-done.8, bf16[512,1024]{1,0:T(8,128)(2,1)} %collective-permute-done.6.refs_1_, bf16[512,1024]{1,0:T(8,128)(2,1)} %collective-permute-done.12.refs_2_, ...), custom_call_target="tpu_custom_call" | custom-call | tf_op jit(solution)/shard_map/split_columns/pallas_call | solution.py:481
  63.3 3.2 %collective-permute-start.7 = (bf16[512,1024]{1,0:T(8,128)(2,1)S(1)}, bf16[512,1024]{1,0:T(8,128)(2,1)S(1)}, u32[]{:S(2)}, u32[]{:S(2)}) collective-permute-start(bf16[512,1024]{1,0:T(8,128)(2,1)S(1)} %broadcast_select_fusion.refs_4_), channel_id=1, source_target_pairs={{0,1},{1,0},{2,3},{3,2},{4,5},{5,4},{6,7},{7,6},{8,9},{9,8},{10,11... | collective-permute-start | bytes 3145736 | tf_op jit(solution)/shard_map/ppermute | solution.py:772
  66.5 1.5 collective-permute-start.14
  68.0 5.0 %grad_products.2.refs_0_.refs_3_.refs_5_ = f32[512,1024]{1,0:T(8,128)S(1)} custom-call(s32[10]{0:T(128)S(1)} %dynamic-slice_bitcast_fusion.rest_0_.place_ref, bf16[512,1024]{1,0:T(8,128)(2,1)S(1)} %copy-done.8, bf16[512,1024]{1,0:T(8,128)(2,1)} %collective-permute-done.6.refs_1_, bf16[512,1024]{1,0:T(8,128)(2,1)} %collective-permute-done.12.refs_2_, ...), custom_call_target="tpu_custom_call" | custom-call | tf_op jit(solution)/shard_map/grad_products/pallas_call | solution.py:524
  73.0 4.0 %weight_terms.1.refs_2_.early_ref = bf16[3,1024,512]{2,1,0:T(8,128)(2,1)S(1)} custom-call(bf16[1024,512]{1,0:T(8,128)(2,1)S(1)} %copy-done.10, bf16[1024,512]{1,0:T(8,128)(2,1)S(1)} %collective-permute-done.10.other_ref, bf16[512,1536]{1,0:T(8,128)(2,1)S(1)} %get-tuple-element.67.mine_ref, bf16[512,1536]{1,0:T(8,128)(2,1)S(1)} %collective-permute-done.13.theirs_ref, ...), custom_call_target="tpu_custom_call" | custom-call | tf_op jit(solution)/shard_map/weight_terms/pallas_call | solution.py:627
  77.0 1.6 %collective-permute-start.15 = (f32[5,8]{1,0:T(8,128)S(1)}, f32[5,8]{1,0:T(8,128)S(1)}, u32[]{:S(2)}, u32[]{:S(2)}) collective-permute-start(f32[5,8]{1,0:T(8,128)S(1)} %max.10.refs_1_), channel_id=1, source_target_pairs={{0,16},{4,20},{8,24},{12,28},{16,0},{20,4},{24,8},{28,12},{1,17},{... | collective-permute-start | bytes 488 | tf_op jit(solution)/shard_map/ppermute | solution.py:762
  78.6 11.5 %collective-permute-done.7.refs_1_ = bf16[512,1024]{1,0:T(8,128)(2,1)S(1)} collective-permute-done((bf16[512,1024]{1,0:T(8,128)(2,1)S(1)}, bf16[512,1024]{1,0:T(8,128)(2,1)S(1)}, u32[]{:S(2)}, u32[]{:S(2)}) %collective-permute-start.7) | collective-permute-done | bytes 1048608 | tf_op jit(solution)/shard_map/ppermute | solution.py:772
  90.4 1.3 split_columns.3
  91.8 3.7 %collective-permute-start.9 = (bf16[512,1024]{1,0:T(8,128)(2,1)S(1)}, bf16[512,1024]{1,0:T(8,128)(2,1)S(1)}, u32[]{:S(2)}, u32[]{:S(2)}) collective-permute-start(bf16[512,1024]{1,0:T(8,128)(2,1)S(1)} %get-tuple-element.57.refs_0_.refs_5_), channel_id=1, source_target_pairs={{0,1},{3,2},{4,5},{7,6},{8,9},{11,10},{12,13},{15,14},{16,17},{19,... | collective-permute-start | bytes 3145736 | tf_op jit(solution)/shard_map/ppermute | solution.py:772
  95.5 0.9 collective-permute-start.8
  96.5 2.6 %weight_terms_late.1 = (bf16[2,512,512]{2,1,0:T(8,128)(2,1)S(1)}, bf16[2,512,512]{2,1,0:T(8,128)(2,1)S(1)}, bf16[2,512,512]{2,1,0:T(8,128)(2,1)S(1)}, bf16[2,512,512]{2,1,0:T(8,128)(2,1)S(1)}) custom-call(s32[10]{0:T(128)S(1)} %dynamic-slice_bitcast_fusion.rest_0_.place_ref, bf16[1024,512]{1,0:T(8,128)(2,1)S(1)} %copy-done.10, ...), custom_call_target="tpu_custom_call" | custom-call | tf_op jit(solution)/shard_map/weight_terms_late/pallas_call | solution.py:688
  99.1 1.6 %collective-permute-start.17 = (bf16[2,512,512]{2,1,0:T(8,128)(2,1)S(1)}, bf16[2,512,512]{2,1,0:T(8,128)(2,1)S(1)}, u32[]{:S(2)}, u32[]{:S(2)}) collective-permute-start(bf16[2,512,512]{2,1,0:T(8,128)(2,1)S(1)} %get-tuple-element.73.refs_6_.rest_0_), channel_id=1, source_target_pairs={{0,8},{4,12},{8,0},{12,4},{16,24},{20,28},{24,16},{28,20},{1,9},{5... | collective-permute-start | bytes 3145736 | tf_op jit(solution)/shard_map/ppermute | solution.py:762
  100.6 1.5 collective-permute-start.18
  102.2 5.4 %grad_products.3.grad_ref = bf16[512,1024]{1,0:T(8,128)(2,1)S(1)} custom-call(s32[10]{0:T(128)S(1)} %dynamic-slice_bitcast_fusion.rest_0_.place_ref, bf16[512,1024]{1,0:T(8,128)(2,1)} %collective-permute-done.4.refs_0_, bf16[512,1024]{1,0:T(8,128)(2,1)S(1)} %collective-permute-done.7.refs_1_, bf16[512,1024]{1,0:T(8,128)(2,1)} %collective-permute-done.3.refs_3_.refs_2_, ...), custom_call_target="tpu_custom_call" | custom-call | tf_op jit(solution)/shard_map/grad_products/pallas_call | solution.py:524
  107.6 12.0 %attention_backward.1 = (f32[512,1024]{1,0:T(8,128)}, bf16[512,1024]{1,0:T(8,128)(2,1)S(1)}, bf16[512,1024]{1,0:T(8,128)(2,1)S(1)}, bf16[512,1024]{1,0:T(8,128)(...) custom-call(bf16[512,1024]{1,0:T(8,128)(2,1)S(1)} %copy-done.5, bf16[512,1024]{1,0:T(8,128)(2,1)S(1)} %copy-done.1, ...), custom_call_target="tpu_custom_call" | custom-call | tf_op jit(solution)/shard_map/attention_backward/pallas_call | solution.py:386
  120.2 4.2 %collective-permute-done.17.refs_1_ = bf16[2,512,512]{2,1,0:T(8,128)(2,1)S(1)} collective-permute-done((bf16[2,512,512]{2,1,0:T(8,128)(2,1)S(1)}, bf16[2,512,512]{2,1,0:T(8,128)(2,1)S(1)}, u32[]{:S(2)}, u32[]{:S(2)}) %collective-permute-start.17) | collective-permute-done | bytes 1048608 | tf_op jit(solution)/shard_map/ppermute | solution.py:762
  124.4 1.2 collective-permute-done.18.refs_3_
  125.6 0.8 collective-permute-start.19
  128.4 1.6 %collective-permute-start.24 = (bf16[1,512,512]{2,1,0:T(8,128)(2,1)S(1)}, bf16[1,512,512]{2,1,0:T(8,128)(2,1)S(1)}, u32[]{:S(2)}, u32[]{:S(2)}) collective-permute-start(bf16[1,512,512]{2,1,0:T(8,128)(2,1)S(1)} %get-tuple-element.91), channel_id=1, source_target_pairs={{0,16},{4,20},{8,24},{12,28},{16,0},{20,4},{24,8},{28,12},{1,17},{... | collective-permute-start | bytes 1572872 | tf_op jit(solution)/shard_map/ppermute | solution.py:762
  129.9 1.5 collective-permute-start.25
  131.4 8.0 %collective-permute-done.22.three = bf16[192,1024]{1,0:T(8,128)(2,1)S(1)} collective-permute-done((bf16[192,1024]{1,0:T(8,128)(2,1)S(1)}, bf16[192,1024]{1,0:T(8,128)(2,1)S(1)}, u32[]{:S(2)}, u32[]{:S(2)}) %collective-permute-start.22) | collective-permute-done | bytes 393248 | tf_op jit(solution)/shard_map/ppermute | solution.py:762
  139.5 1.6 %collective-permute-start.23 = (bf16[64,1024]{1,0:T(8,128)(2,1)S(1)}, bf16[64,1024]{1,0:T(8,128)(2,1)S(1)}, u32[]{:S(2)}, u32[]{:S(2)}) collective-permute-start(bf16[64,1024]{1,0:T(8,128)(2,1)S(1)} %add_convert_fusion.1), channel_id=1, source_target_pairs={{0,16},{4,20},{8,24},{12,28},{16,0},{20,4},{24,8},{28,12},{1,17},{... | collective-permute-start | bytes 393224 | tf_op jit(solution)/shard_map/ppermute | solution.py:762
  141.0 3.5 %collective-permute-done.23.four = bf16[64,1024]{1,0:T(8,128)(2,1)S(1)} collective-permute-done((bf16[64,1024]{1,0:T(8,128)(2,1)S(1)}, bf16[64,1024]{1,0:T(8,128)(2,1)S(1)}, u32[]{:S(2)}, u32[]{:S(2)}) %collective-permute-start.23) | collective-permute-done | bytes 131104 | tf_op jit(solution)/shard_map/ppermute | solution.py:762
  144.5 3.0 %add_returned.1 = (f32[512,1024]{1,0:T(8,128)}, f32[512,1024]{1,0:T(8,128)}) custom-call(bf16[512,1024]{1,0:T(8,128)(2,1)S(1)} %get-tuple-element.81.gk_ref, bf16[512,1024]{1,0:T(8,128)(2,1)S(1)} %get-tuple-element.82.gv_ref, bf16[512,1024]{1,0:T(8,128)(2,1)S(1)} %collective-permute-done.21.near, bf16[192,1024]{1,0:T(8,128)(2,1)S(1)} %collective-permute-done.22.three, ...), custom_call_target="tpu_custom_call" | custom-call | tf_op jit(solution)/shard_map/add_returned/pallas_call | solution.py:428
  147.5 0.9 collective-permute-done.25
  148.4 1.6 %copy-done.13 = f32[512,1024]{1,0:T(8,128)S(1)} copy-done((f32[512,1024]{1,0:T(8,128)S(1)}, f32[512,1024]{1,0:T(8,128)}, u32[]{:S(2)}) %copy-start.13) | copy-done | bytes 2097176
  150.0 1.5 weight_total.1
  151.5 1.9 %mixed_last.1 = f32[512,1024]{1,0:T(8,128)} custom-call(bf16[512,1024]{1,0:T(8,128)(2,1)S(1)} %get-tuple-element.55.own, bf16[512,1024]{1,0:T(8,128)(2,1)S(1)} %collective-permute-done.19.left, bf16[512,1024]{1,0:T(8,128)(2,1)S(1)} %collective-permute-done.20.right), custom_call_target="tpu_custom_call" | custom-call | tf_op jit(solution)/shard_map/mixed_last/pallas_call | solution.py:605
  (66 shorter events, 5.5 us)
Async XLA Ops:
  0.6 26.6 %collective-permute-start.3 = (bf16[512,1024]{1,0:T(8,128)(2,1)}, bf16[512,1024]{1,0:T(8,128)(2,1)}, u32[]{:S(2)}, u32[]{:S(2)}) collective-permute-start(bf16[512,1024]{1,0:T(8,128)(2,1)} %refs_0_.5), channel_id=1, source_target_pairs={{0,1},{2,3},{1,0},{3,2},{4,5},{6,7},{5,4},{7,6},{8,9},{10,11},{9,8... | collective-permute-start | bytes 3145736 | tf_op jit(solution)/shard_map/ppermute | solution.py:772
  3.7 23.5 %collective-permute-start.4 = (bf16[512,1024]{1,0:T(8,128)(2,1)}, bf16[512,1024]{1,0:T(8,128)(2,1)}, u32[]{:S(2)}, u32[]{:S(2)}) collective-permute-start(bf16[512,1024]{1,0:T(8,128)(2,1)} %refs_0_.5), channel_id=1, source_target_pairs={{1,2},{2,1},{5,6},{6,5},{9,10},{10,9},{13,14},{14,13},{17,18},{18,... | collective-permute-start | bytes 3145736 | tf_op jit(solution)/shard_map/ppermute | solution.py:772
  5.4 1.2 copy-start
  6.6 1.2 copy-start.2
  7.8 23.0 %copy-start.1 = (bf16[512,1024]{1,0:T(8,128)(2,1)S(1)}, bf16[512,1024]{1,0:T(8,128)(2,1)}, u32[]{:S(2)}) copy-start(bf16[512,1024]{1,0:T(8,128)(2,1)} %k_ref.5) | copy-start | bytes 3145732
  7.8 23.1 %copy-start.3 = (bf16[512,1024]{1,0:T(8,128)(2,1)S(1)}, bf16[512,1024]{1,0:T(8,128)(2,1)}, u32[]{:S(2)}) copy-start(bf16[512,1024]{1,0:T(8,128)(2,1)} %v_ref.5) | copy-start | bytes 3145732
  9.5 11.5 %collective-permute-start = (bf16[128,1024]{1,0:T(8,128)(2,1)S(1)}, bf16[128,1024]{1,0:T(8,128)(2,1)S(1)}, u32[]{:S(2)}, u32[]{:S(2)}) collective-permute-start(bf16[128,1024]{1,0:T(8,128)(2,1)S(1)} %get-tuple-element.51), channel_id=1, source_target_pairs={{0,8},{4,12},{8,0},{12,4},{16,24},{20,28},{24,16},{28,20},{1,9},{5... | collective-permute-start | bytes 786440 | tf_op jit(solution)/shard_map/ppermute | solution.py:762
  11.0 5.0 %collective-permute-start.1 = (bf16[64,1024]{1,0:T(8,128)(2,1)S(1)}, bf16[64,1024]{1,0:T(8,128)(2,1)S(1)}, u32[]{:S(2)}, u32[]{:S(2)}) collective-permute-start(bf16[64,1024]{1,0:T(8,128)(2,1)S(1)} %get-tuple-element.52), channel_id=1, source_target_pairs={{0,16},{4,20},{8,24},{12,28},{16,0},{20,4},{24,8},{28,12},{1,17},{... | collective-permute-start | bytes 393224 | tf_op jit(solution)/shard_map/ppermute | solution.py:762
  12.5 8.5 %collective-permute-start.2 = (bf16[64,1024]{1,0:T(8,128)(2,1)S(1)}, bf16[64,1024]{1,0:T(8,128)(2,1)S(1)}, u32[]{:S(2)}, u32[]{:S(2)}) collective-permute-start(bf16[64,1024]{1,0:T(8,128)(2,1)S(1)} %get-tuple-element.52), channel_id=1, source_target_pairs={{0,24},{4,28},{8,16},{12,20},{16,8},{20,12},{24,0},{28,4},{1,25},{... | collective-permute-start | bytes 393224 | tf_op jit(solution)/shard_map/ppermute | solution.py:762
  27.2 3.6 %collective-permute-start.5 = (bf16[512,1024]{1,0:T(8,128)(2,1)}, bf16[512,1024]{1,0:T(8,128)(2,1)}, u32[]{:S(2)}, u32[]{:S(2)}) collective-permute-start(bf16[512,1024]{1,0:T(8,128)(2,1)} %lower_rows.1), channel_id=1, source_target_pairs={{0,4},{4,0},{8,12},{12,8},{16,20},{20,16},{24,28},{28,24},{1,5},{5... | collective-permute-start | bytes 3145736 | tf_op jit(solution)/shard_map/ppermute | solution.py:762
  27.2 27.7 %collective-permute-start.6 = (bf16[512,1024]{1,0:T(8,128)(2,1)}, bf16[512,1024]{1,0:T(8,128)(2,1)}, u32[]{:S(2)}, u32[]{:S(2)}) collective-permute-start(bf16[512,1024]{1,0:T(8,128)(2,1)} %collective-permute-done.3.refs_3_.refs_2_), channel_id=1, source_target_pairs={{1,2},{2,1},{5,6},{6,5},{9,10},{10,9},{13,14},{14,13},{17,18},{18,... | collective-permute-start | bytes 3145736 | tf_op jit(solution)/shard_map/ppermute | solution.py:772
  28.8 31.9 %collective-permute-start.12 = (bf16[512,1024]{1,0:T(8,128)(2,1)}, bf16[512,1024]{1,0:T(8,128)(2,1)}, u32[]{:S(2)}, u32[]{:S(2)}) collective-permute-start(bf16[512,1024]{1,0:T(8,128)(2,1)} %collective-permute-done.4.refs_0_), channel_id=1, source_target_pairs={{2,3},{1,0},{6,7},{5,4},{10,11},{9,8},{14,15},{13,12},{18,19},{17,... | collective-permute-start | bytes 3145736 | tf_op jit(solution)/shard_map/ppermute | solution.py:772
  30.9 1.2 copy-start.4
  41.5 1.0 copy-start.6
  42.5 1.0 copy-start.9
  43.5 1.3 copy-start.11
  44.9 10.1 %collective-permute-start.11 = (f32[5,8]{1,0:T(8,128)S(1)}, f32[5,8]{1,0:T(8,128)S(1)}, u32[]{:S(2)}, u32[]{:S(2)}) collective-permute-start(f32[5,8]{1,0:T(8,128)S(1)} %bitcast.18), channel_id=1, source_target_pairs={{0,4},{4,0},{8,12},{12,8},{16,20},{20,16},{24,28},{28,24},{1,5},{5... | collective-permute-start | bytes 488 | tf_op jit(solution)/shard_map/ppermute | solution.py:762
  45.5 22.5 %slice-start = ((s8[8388608]{0:T(1024)(128)(4,1)}), s8[4194304]{0:T(1024)(128)(4,1)S(1)}, s32[]{:S(2)}) async-start(s8[8388608]{0:T(1024)(128)(4,1)} %bitcast.11), calls=%async_computation | async-start | bytes 8388608
  45.5 22.5 %slice-start.1 = ((s8[8388608]{0:T(1024)(128)(4,1)}), s8[4194304]{0:T(1024)(128)(4,1)S(1)}, s32[]{:S(2)}) async-start(s8[8388608]{0:T(1024)(128)(4,1)} %bitcast.11), calls=%async_computation.1 | async-start | bytes 8388608
  54.9 5.9 %copy-start.8 = (bf16[512,1024]{1,0:T(8,128)(2,1)S(1)}, bf16[512,1024]{1,0:T(8,128)(2,1)}, u32[]{:S(2)}) copy-start(bf16[512,1024]{1,0:T(8,128)(2,1)} %refs_0_.5) | copy-start | bytes 3145732
  55.0 7.8 %copy-start.10 = (bf16[1024,512]{1,0:T(8,128)(2,1)S(1)}, bf16[1024,512]{1,0:T(8,128)(2,1)}, u32[]{:S(2)}) copy-start(bf16[1024,512]{1,0:T(8,128)(2,1)} %copy-done.9) | copy-start | bytes 3145732
  62.7 3.8 %collective-permute-start.13 = (bf16[512,1536]{1,0:T(8,128)(2,1)S(1)}, bf16[512,1536]{1,0:T(8,128)(2,1)S(1)}, u32[]{:S(2)}, u32[]{:S(2)}) collective-permute-start(bf16[512,1536]{1,0:T(8,128)(2,1)S(1)} %get-tuple-element.65), channel_id=1, source_target_pairs={{0,4},{4,0},{8,12},{12,8},{16,20},{20,16},{24,28},{28,24},{1,5},{5... | collective-permute-start | bytes 4718600 | tf_op jit(solution)/shard_map/ppermute | solution.py:762
  62.8 10.2 %collective-permute-start.10 = (bf16[1024,512]{1,0:T(8,128)(2,1)S(1)}, bf16[1024,512]{1,0:T(8,128)(2,1)S(1)}, u32[]{:S(2)}, u32[]{:S(2)}) collective-permute-start(bf16[1024,512]{1,0:T(8,128)(2,1)S(1)} %copy-done.10), channel_id=1, source_target_pairs={{0,4},{4,0},{8,12},{12,8},{16,20},{20,16},{24,28},{28,24},{1,5},{5... | collective-permute-start | bytes 3145736 | tf_op jit(solution)/shard_map/ppermute | solution.py:762
  63.3 26.8 %collective-permute-start.7 = (bf16[512,1024]{1,0:T(8,128)(2,1)S(1)}, bf16[512,1024]{1,0:T(8,128)(2,1)S(1)}, u32[]{:S(2)}, u32[]{:S(2)}) collective-permute-start(bf16[512,1024]{1,0:T(8,128)(2,1)S(1)} %broadcast_select_fusion.refs_4_), channel_id=1, source_target_pairs={{0,1},{1,0},{2,3},{3,2},{4,5},{5,4},{6,7},{7,6},{8,9},{9,8},{10,11... | collective-permute-start | bytes 3145736 | tf_op jit(solution)/shard_map/ppermute | solution.py:772
  66.5 6.5 %collective-permute-start.14 = (f32[5,8]{1,0:T(8,128)S(1)}, f32[5,8]{1,0:T(8,128)S(1)}, u32[]{:S(2)}, u32[]{:S(2)}) collective-permute-start(f32[5,8]{1,0:T(8,128)S(1)} %bitcast_maximum_fusion.refs_5_), channel_id=1, source_target_pairs={{0,8},{4,12},{8,0},{12,4},{16,24},{20,28},{24,16},{28,20},{1,9},{5... | collective-permute-start | bytes 488 | tf_op jit(solution)/shard_map/ppermute | solution.py:762
  77.0 13.3 %collective-permute-start.15 = (f32[5,8]{1,0:T(8,128)S(1)}, f32[5,8]{1,0:T(8,128)S(1)}, u32[]{:S(2)}, u32[]{:S(2)}) collective-permute-start(f32[5,8]{1,0:T(8,128)S(1)} %max.10.refs_1_), channel_id=1, source_target_pairs={{0,16},{4,20},{8,24},{12,28},{16,0},{20,4},{24,8},{28,12},{1,17},{... | collective-permute-start | bytes 488 | tf_op jit(solution)/shard_map/ppermute | solution.py:762
  90.4 6.1 %copy-start.15 = (f32[5,8]{1,0:T(8,128)}, f32[5,8]{1,0:T(8,128)S(1)}, u32[]{:S(2)}) copy-start(f32[5,8]{1,0:T(8,128)S(1)} %max.11.refs_4_.refs_0_) | copy-start | bytes 484
  91.7 4.7 %collective-permute-start.16 = (bf16[512,512]{1,0:T(8,128)(2,1)S(1)}, bf16[512,512]{1,0:T(8,128)(2,1)S(1)}, u32[]{:S(2)}, u32[]{:S(2)}) collective-permute-start(bf16[512,512]{1,0:T(8,128)(2,1)S(1)} %get-tuple-element.72), channel_id=1, source_target_pairs={{0,4},{4,0},{8,12},{12,8},{16,20},{20,16},{24,28},{28,24},{1,5},{5... | collective-permute-start | bytes 1572872 | tf_op jit(solution)/shard_map/ppermute | solution.py:762
  91.8 27.8 %collective-permute-start.9 = (bf16[512,1024]{1,0:T(8,128)(2,1)S(1)}, bf16[512,1024]{1,0:T(8,128)(2,1)S(1)}, u32[]{:S(2)}, u32[]{:S(2)}) collective-permute-start(bf16[512,1024]{1,0:T(8,128)(2,1)S(1)} %get-tuple-element.57.refs_0_.refs_5_), channel_id=1, source_target_pairs={{0,1},{3,2},{4,5},{7,6},{8,9},{11,10},{12,13},{15,14},{16,17},{19,... | collective-permute-start | bytes 3145736 | tf_op jit(solution)/shard_map/ppermute | solution.py:772
  95.5 24.1 %collective-permute-start.8 = (bf16[512,1024]{1,0:T(8,128)(2,1)S(1)}, bf16[512,1024]{1,0:T(8,128)(2,1)S(1)}, u32[]{:S(2)}, u32[]{:S(2)}) collective-permute-start(bf16[512,1024]{1,0:T(8,128)(2,1)S(1)} %mixed_add.2.refs_6_), channel_id=1, source_target_pairs={{1,2},{2,1},{5,6},{6,5},{9,10},{10,9},{13,14},{14,13},{17,18},{18,... | collective-permute-start | bytes 3145736 | tf_op jit(solution)/shard_map/ppermute | solution.py:772
  99.1 25.3 %collective-permute-start.17 = (bf16[2,512,512]{2,1,0:T(8,128)(2,1)S(1)}, bf16[2,512,512]{2,1,0:T(8,128)(2,1)S(1)}, u32[]{:S(2)}, u32[]{:S(2)}) collective-permute-start(bf16[2,512,512]{2,1,0:T(8,128)(2,1)S(1)} %get-tuple-element.73.refs_6_.rest_0_), channel_id=1, source_target_pairs={{0,8},{4,12},{8,0},{12,4},{16,24},{20,28},{24,16},{28,20},{1,9},{5... | collective-permute-start | bytes 3145736 | tf_op jit(solution)/shard_map/ppermute | solution.py:762
  100.6 25.0 %collective-permute-start.18 = (bf16[2,512,512]{2,1,0:T(8,128)(2,1)S(1)}, bf16[2,512,512]{2,1,0:T(8,128)(2,1)S(1)}, u32[]{:S(2)}, u32[]{:S(2)}) collective-permute-start(bf16[2,512,512]{2,1,0:T(8,128)(2,1)S(1)} %get-tuple-element.74.refs_8_.rest_2_), channel_id=1, source_target_pairs={{0,16},{4,20},{8,24},{12,28},{16,0},{20,4},{24,8},{28,12},{1,17},{... | collective-permute-start | bytes 3145736 | tf_op jit(solution)/shard_map/ppermute | solution.py:762
  102.1 5.5 %copy-start.5 = (bf16[512,1024]{1,0:T(8,128)(2,1)S(1)}, bf16[512,1024]{1,0:T(8,128)(2,1)}, u32[]{:S(2)}) copy-start(bf16[512,1024]{1,0:T(8,128)(2,1)} %q_ref.3) | copy-start | bytes 3145732
  102.1 5.5 %copy-start.7 = (bf16[512,1024]{1,0:T(8,128)(2,1)S(1)}, bf16[512,1024]{1,0:T(8,128)(2,1)}, u32[]{:S(2)}) copy-start(bf16[512,1024]{1,0:T(8,128)(2,1)} %copy-done.6) | copy-start | bytes 3145732
  102.2 5.5 %copy-start.12 = (f32[512,1024]{1,0:T(8,128)S(1)}, f32[512,1024]{1,0:T(8,128)}, u32[]{:S(2)}) copy-start(f32[512,1024]{1,0:T(8,128)} %copy-done.11) | copy-start | bytes 6291460
  107.6 12.0 %copy-start.14 = (bf16[512,1024]{1,0:T(8,128)(2,1)S(1)}, bf16[512,1024]{1,0:T(8,128)(2,1)}, u32[]{:S(2)}) copy-start(bf16[512,1024]{1,0:T(8,128)(2,1)} %get-tuple-element.56.refs_0_) | copy-start | bytes 3145732
  119.6 7.5 %collective-permute-start.21 = (bf16[512,1024]{1,0:T(8,128)(2,1)S(1)}, bf16[512,1024]{1,0:T(8,128)(2,1)S(1)}, u32[]{:S(2)}, u32[]{:S(2)}) collective-permute-start(bf16[512,1024]{1,0:T(8,128)(2,1)S(1)} %get-tuple-element.83), channel_id=1, source_target_pairs={{0,4},{4,0},{8,12},{12,8},{16,20},{20,16},{24,28},{28,24},{1,5},{5... | collective-permute-start | bytes 3145736 | tf_op jit(solution)/shard_map/ppermute | solution.py:762
  125.6 25.9 %collective-permute-start.19 = (bf16[512,1024]{1,0:T(8,128)(2,1)S(1)}, bf16[512,1024]{1,0:T(8,128)(2,1)S(1)}, u32[]{:S(2)}, u32[]{:S(2)}) collective-permute-start(bf16[512,1024]{1,0:T(8,128)(2,1)S(1)} %get-tuple-element.75), channel_id=1, source_target_pairs={{0,1},{2,3},{1,0},{3,2},{4,5},{6,7},{5,4},{7,6},{8,9},{10,11},{9,8... | collective-permute-start | bytes 3145736 | tf_op jit(solution)/shard_map/ppermute | solution.py:772
  126.4 25.1 %collective-permute-start.20 = (bf16[512,1024]{1,0:T(8,128)(2,1)S(1)}, bf16[512,1024]{1,0:T(8,128)(2,1)S(1)}, u32[]{:S(2)}, u32[]{:S(2)}) collective-permute-start(bf16[512,1024]{1,0:T(8,128)(2,1)S(1)} %get-tuple-element.76), channel_id=1, source_target_pairs={{1,2},{2,1},{5,6},{6,5},{9,10},{10,9},{13,14},{14,13},{17,18},{18,... | collective-permute-start | bytes 3145736 | tf_op jit(solution)/shard_map/ppermute | solution.py:772
  127.3 12.1 %collective-permute-start.22 = (bf16[192,1024]{1,0:T(8,128)(2,1)S(1)}, bf16[192,1024]{1,0:T(8,128)(2,1)S(1)}, u32[]{:S(2)}, u32[]{:S(2)}) collective-permute-start(bf16[192,1024]{1,0:T(8,128)(2,1)S(1)} %add_convert_fusion), channel_id=1, source_target_pairs={{0,8},{4,12},{8,0},{12,4},{16,24},{20,28},{24,16},{28,20},{1,9},{5... | collective-permute-start | bytes 1179656 | tf_op jit(solution)/shard_map/ppermute | solution.py:762
  128.4 19.2 %collective-permute-start.24 = (bf16[1,512,512]{2,1,0:T(8,128)(2,1)S(1)}, bf16[1,512,512]{2,1,0:T(8,128)(2,1)S(1)}, u32[]{:S(2)}, u32[]{:S(2)}) collective-permute-start(bf16[1,512,512]{2,1,0:T(8,128)(2,1)S(1)} %get-tuple-element.91), channel_id=1, source_target_pairs={{0,16},{4,20},{8,24},{12,28},{16,0},{20,4},{24,8},{28,12},{1,17},{... | collective-permute-start | bytes 1572872 | tf_op jit(solution)/shard_map/ppermute | solution.py:762
  129.9 18.4 %collective-permute-start.25 = (bf16[1,512,512]{2,1,0:T(8,128)(2,1)S(1)}, bf16[1,512,512]{2,1,0:T(8,128)(2,1)S(1)}, u32[]{:S(2)}, u32[]{:S(2)}) collective-permute-start(bf16[1,512,512]{2,1,0:T(8,128)(2,1)S(1)} %get-tuple-element.93), channel_id=1, source_target_pairs={{0,8},{4,12},{8,0},{12,4},{16,24},{20,28},{24,16},{28,20},{1,9},{5... | collective-permute-start | bytes 1572872 | tf_op jit(solution)/shard_map/ppermute | solution.py:762
  139.5 5.0 %collective-permute-start.23 = (bf16[64,1024]{1,0:T(8,128)(2,1)S(1)}, bf16[64,1024]{1,0:T(8,128)(2,1)S(1)}, u32[]{:S(2)}, u32[]{:S(2)}) collective-permute-start(bf16[64,1024]{1,0:T(8,128)(2,1)S(1)} %add_convert_fusion.1), channel_id=1, source_target_pairs={{0,16},{4,20},{8,24},{12,28},{16,0},{20,4},{24,8},{28,12},{1,17},{... | collective-permute-start | bytes 393224 | tf_op jit(solution)/shard_map/ppermute | solution.py:762
  148.4 1.6 %copy-start.13 = (f32[512,1024]{1,0:T(8,128)S(1)}, f32[512,1024]{1,0:T(8,128)}, u32[]{:S(2)}) copy-start(f32[512,1024]{1,0:T(8,128)} %get-tuple-element.46.refs_0_) | copy-start | bytes 6291460

commit v7 on v6

--- a/solution.py
+++ b/solution.py
@@ -68,7 +68,7 @@
         in_specs=[spec, spec],
         out_specs=[pl.BlockSpec((r, step), lambda i: (0, i)) for r in rows],
         out_shape=[jax.ShapeDtypeStruct((r, width), BF16) for r in (tokens, *rows[1:])],
-        compiler_params=pltpu.CompilerParams(vmem_limit_bytes=VMEM_LIMIT),
+        compiler_params=pltpu.CompilerParams(vmem_limit_bytes=56 * 1024 * 1024),
         name="pool_keys",
     )(key, value)
 
@@ -241,7 +241,7 @@
             pltpu.VMEM((step * 2 * tokens, 128), F32),
             pltpu.VMEM((step * 2 * tokens, 128), F32),
         ],
-        compiler_params=pltpu.CompilerParams(vmem_limit_bytes=VMEM_LIMIT),
+        compiler_params=pltpu.CompilerParams(vmem_limit_bytes=50 * 1024 * 1024),
         name="attention_forward",
     )(query, key, value, *received, *after)
 
@@ -432,7 +432,7 @@
         out_specs=[spec, spec],
         out_shape=[full, full],
         scratch_shapes=[scratch, scratch],
-        compiler_params=pltpu.CompilerParams(vmem_limit_bytes=VMEM_LIMIT),
+        compiler_params=pltpu.CompilerParams(vmem_limit_bytes=50 * 1024 * 1024),
         name="add_returned",
     )(grad_k, grad_v, near, three, four)
 
@@ -715,7 +715,7 @@
         in_specs=[spec] * 4 + [pl.BlockSpec(memory_space=pl.ANY)] * len(after),
         out_specs=pl.BlockSpec((2 * rows, column), lambda: (0, 0)),
         out_shape=jax.ShapeDtypeStruct((2 * rows, column), F32),
-        compiler_params=pltpu.CompilerParams(vmem_limit_bytes=VMEM_LIMIT),
+        compiler_params=pltpu.CompilerParams(vmem_limit_bytes=50 * 1024 * 1024),
         name="weight_total",
     )(*top, *bottom, *after)
 

time: 154 us -> 151 us (0.981)
  local copies, waits for them, and re-layouts: 9.39 us -> 2.82 us
  waiting for transfers between devices: 48.3 us -> 52.6 us
  starting transfers between devices: 33 us -> 30.4 us
  Pallas kernels: 61.4 us -> 63 us
    unnamed x36 -> x30, local copies, waits for them, and re-layouts: 8.56 us -> 1.99 us
    ppermute x9, waiting for transfers between devices: 22.6 us -> 25.1 us  [along(): return lax.ppermute(value, 'head', pairs) if pairs else None]
    ppermute x9, starting transfers between devices: 17 us -> 14.5 us  [along(): return lax.ppermute(value, 'head', pairs) if pairs else None]
    ppermute x17, waiting for transfers between devices: 25.7 us -> 27.4 us  [swap(): lax.ppermute(value, axis, [(i, i ^ mask) for i in range(lax.axis_size(axi...]
  transfers between devices with their start and end apart: 26 -> 26, of which waited for: 10 -> 12; matrix products, arithmetic and copies ran while one was open for 1% -> 1% of each run, Pallas kernels for 37% -> 39%
where the time goes in v7:
time: 151 us; the launch traced here: 150 us
  Pallas kernels  63 us (42%)
  waiting for transfers between devices  52.6 us (35%)
  starting transfers between devices  30.4 us (20%)
  local copies, waits for them, and re-layouts  2.82 us (2%)
    ppermute x17, waiting for transfers between devices, swap(): lax.ppermute(value, axis, [(i, i ^ mask) for i in range(lax.axis_size(axi...  27.4 us
    ppermute x9, waiting for transfers between devices, along(): return lax.ppermute(value, 'head', pairs) if pairs else None  25.1 us
    ppermute x17, starting transfers between devices, swap(): lax.ppermute(value, axis, [(i, i ^ mask) for i in range(lax.axis_size(axi...  15.8 us
    ppermute x9, starting transfers between devices, along(): return lax.ppermute(value, 'head', pairs) if pairs else None  14.5 us
    pallas_call x1, Pallas kernels, backward_call(): pl.pallas_call(functools.partial(backward_kernel, extra=len(after)), grid...  12 us
    pallas_call x1, Pallas kernels, forward_call(): pl.pallas_call(functools.partial(forward_kernel, extra=len(after)), grid=...  10.5 us
    pallas_call x2, Pallas kernels, grad_call(): pl.pallas_call(functools.partial(grad_kernel, modes=tuple((c[0] for c in...  10.1 us
    pallas_call x1, Pallas kernels, product_call(): pl.pallas_call(functools.partial(product_kernel, count=count), grid_spec=...  9.38 us
  transfers between devices with their start and end apart: 26, of which 12 were waited for; matrix products, arithmetic and copies ran while one was open for 1% of the time, Pallas kernels for 39%

profile of v7, /device:TPU:0, one launch (start us, length us, event | category | flops | bytes accessed | tf_op | source)
XLA Modules:
  0.0 150.1 jit_solution(8583051451332296642)
XLA Ops:
  0.6 3.1 %collective-permute-start.3 = (bf16[512,1024]{1,0:T(8,128)(2,1)}, bf16[512,1024]{1,0:T(8,128)(2,1)}, u32[]{:S(2)}, u32[]{:S(2)}) collective-permute-start(bf16[512,1024]{1,0:T(8,128)(2,1)} %refs_0_.5), channel_id=1, source_target_pairs={{0,1},{2,3},{1,0},{3,2},{4,5},{6,7},{5,4},{7,6},{8,9},{10,11},{9,8... | collective-permute-start | bytes 3145736 | tf_op jit(solution)/shard_map/ppermute | solution.py:772
  3.7 1.6 %collective-permute-start.4 = (bf16[512,1024]{1,0:T(8,128)(2,1)}, bf16[512,1024]{1,0:T(8,128)(2,1)}, u32[]{:S(2)}, u32[]{:S(2)}) collective-permute-start(bf16[512,1024]{1,0:T(8,128)(2,1)} %refs_0_.5), channel_id=1, source_target_pairs={{1,2},{2,1},{5,6},{6,5},{9,10},{10,9},{13,14},{14,13},{17,18},{18,... | collective-permute-start | bytes 3145736 | tf_op jit(solution)/shard_map/ppermute | solution.py:772
  5.4 2.8 %pool_keys.1 = (bf16[512,1024]{1,0:T(8,128)(2,1)}, bf16[128,1024]{1,0:T(8,128)(2,1)}, bf16[64,1024]{1,0:T(8,128)(2,1)}) custom-call(bf16[512,1024]{1,0:T(8,128)(2,1)} %k_ref.5, bf16[512,1024]{1,0:T(8,128)(2,1)} %v_ref.5), custom_call_target="tpu_custom_call" | custom-call | tf_op jit(solution)/shard_map/pool_keys/pallas_call | solution.py:65
  8.1 1.5 collective-permute-start
  9.6 1.5 %collective-permute-start.1 = (bf16[64,1024]{1,0:T(8,128)(2,1)}, bf16[64,1024]{1,0:T(8,128)(2,1)S(1)}, u32[]{:S(2)}, u32[]{:S(2)}) collective-permute-start(bf16[64,1024]{1,0:T(8,128)(2,1)} %get-tuple-element.52), channel_id=1, source_target_pairs={{0,16},{4,20},{8,24},{12,28},{16,0},{20,4},{24,8},{28,12},{1,17},{... | collective-permute-start | bytes 393224 | tf_op jit(solution)/shard_map/ppermute | solution.py:762
  11.6 3.2 %collective-permute-done.1.four_a = bf16[64,1024]{1,0:T(8,128)(2,1)S(1)} collective-permute-done((bf16[64,1024]{1,0:T(8,128)(2,1)}, bf16[64,1024]{1,0:T(8,128)(2,1)S(1)}, u32[]{:S(2)}, u32[]{:S(2)}) %collective-permute-start.1) | collective-permute-done | bytes 131104 | tf_op jit(solution)/shard_map/ppermute | solution.py:762
  14.8 5.1 %collective-permute-done.2.four_b = bf16[64,1024]{1,0:T(8,128)(2,1)S(1)} collective-permute-done((bf16[64,1024]{1,0:T(8,128)(2,1)}, bf16[64,1024]{1,0:T(8,128)(2,1)S(1)}, u32[]{:S(2)}, u32[]{:S(2)}) %collective-permute-start.2) | collective-permute-done | bytes 131104 | tf_op jit(solution)/shard_map/ppermute | solution.py:762
  19.9 0.8 lower_rows.1
  20.7 6.5 %collective-permute-done.3.refs_3_.refs_2_ = bf16[512,1024]{1,0:T(8,128)(2,1)} collective-permute-done((bf16[512,1024]{1,0:T(8,128)(2,1)}, bf16[512,1024]{1,0:T(8,128)(2,1)}, u32[]{:S(2)}, u32[]{:S(2)}) %collective-permute-start.3) | collective-permute-done | bytes 1048608 | tf_op jit(solution)/shard_map/ppermute | solution.py:772
  27.2 0.7 collective-permute-start.6
  27.9 1.3 collective-permute-start.12
  29.2 0.7 dynamic-slice_bitcast_fusion.rest_0_.place_ref
  30.2 10.5 %attention_forward.1 = (bf16[512,1024]{1,0:T(8,128)(2,1)S(1)}, bf16[1024,512]{1,0:T(8,128)(2,1)S(1)}, f32[512,1024]{1,0:T(8,128)}, f32[8,8,128]{2,1,0:T(8,128)S(1)}) custom-call(bf16[512,1024]{1,0:T(8,128)(2,1)S(1)} %copy-done.2, bf16[512,1024]{1,0:T(8,128)(2,1)} %k_ref.5, bf16[512,1024]{1,0:T(8,128)(2,1)} %v_ref.5, ...), custom_call_target="tpu_custom_call" | custom-call | tf_op jit(solution)/shard_map/attention_forward/pallas_call | solution.py:222
  40.7 1.0 copy-done.3
  41.7 1.0 copy-done.6
  43.1 9.4 %mixed_products.1 = (bf16[512,1024]{1,0:T(8,128)(2,1)S(1)}, bf16[512,1024]{1,0:T(8,128)(2,1)S(1)}, bf16[512,1024]{1,0:T(8,128)(2,1)S(1)}, bf16[512,1024]{1,0:T(8,128)(2,1)}) custom-call(s32[10]{0:T(128)S(1)} %dynamic-slice_bitcast_fusion.rest_0_.place_ref, bf16[512,1024]{1,0:T(8,128)(2,1)} %copy-done.3, bf16[1024,4096]{1,0:T(8,128)(2,1)} %refs_4_.3, ...), custom_call_target="tpu_custom_call" | custom-call | tf_op jit(solution)/shard_map/mixed_products/pallas_call | solution.py:555
  52.6 8.1 %collective-permute-done.12.refs_2_ = bf16[512,1024]{1,0:T(8,128)(2,1)} collective-permute-done((bf16[512,1024]{1,0:T(8,128)(2,1)}, bf16[512,1024]{1,0:T(8,128)(2,1)}, u32[]{:S(2)}, u32[]{:S(2)}) %collective-permute-start.12) | collective-permute-done | bytes 1048608 | tf_op jit(solution)/shard_map/ppermute | solution.py:772
  60.8 1.7 %split_columns.2 = (bf16[512,1536]{1,0:T(8,128)(2,1)S(1)}, bf16[512,1536]{1,0:T(8,128)(2,1)S(1)}) custom-call(s32[10]{0:T(128)S(1)} %dynamic-slice_bitcast_fusion.rest_0_.place_ref, bf16[512,1024]{1,0:T(8,128)(2,1)S(1)} %copy-done.5, bf16[512,1024]{1,0:T(8,128)(2,1)S(1)} %collective-permute-done.6.refs_1_, ...), custom_call_target="tpu_custom_call" | custom-call | tf_op jit(solution)/shard_map/split_columns/pallas_call | solution.py:481
  63.1 1.6 %collective-permute-start.7 = (bf16[512,1024]{1,0:T(8,128)(2,1)S(1)}, bf16[512,1024]{1,0:T(8,128)(2,1)S(1)}, u32[]{:S(2)}, u32[]{:S(2)}) collective-permute-start(bf16[512,1024]{1,0:T(8,128)(2,1)S(1)} %broadcast_select_fusion.refs_4_), channel_id=1, source_target_pairs={{0,1},{1,0},{2,3},{3,2},{4,5},{5,4},{6,7},{7,6},{8,9},{9,8},{10,11... | collective-permute-start | bytes 3145736 | tf_op jit(solution)/shard_map/ppermute | solution.py:772
  64.7 1.3 collective-permute-done.13.theirs_ref
  65.9 1.5 collective-permute-start.14
  67.4 4.7 %grad_products.2.refs_0_.refs_3_.refs_5_ = f32[512,1024]{1,0:T(8,128)S(1)} custom-call(s32[10]{0:T(128)S(1)} %dynamic-slice_bitcast_fusion.rest_0_.place_ref, bf16[512,1024]{1,0:T(8,128)(2,1)S(1)} %copy-done.5, bf16[512,1024]{1,0:T(8,128)(2,1)S(1)} %collective-permute-done.6.refs_1_, bf16[512,1024]{1,0:T(8,128)(2,1)} %collective-permute-done.12.refs_2_, ...), custom_call_target="tpu_custom_call" | custom-call | tf_op jit(solution)/shard_map/grad_products/pallas_call | solution.py:524
  72.2 4.0 %weight_terms.1.refs_2_.early_ref = bf16[3,1024,512]{2,1,0:T(8,128)(2,1)S(1)} custom-call(bf16[1024,512]{1,0:T(8,128)(2,1)S(1)} %copy-done.7, bf16[1024,512]{1,0:T(8,128)(2,1)S(1)} %collective-permute-done.10.other_ref, bf16[512,1536]{1,0:T(8,128)(2,1)S(1)} %get-tuple-element.67.mine_ref, bf16[512,1536]{1,0:T(8,128)(2,1)S(1)} %collective-permute-done.13.theirs_ref, ...), custom_call_target="tpu_custom_call" | custom-call | tf_op jit(solution)/shard_map/weight_terms/pallas_call | solution.py:627
  76.2 1.6 %collective-permute-start.15 = (f32[5,8]{1,0:T(8,128)S(1)}, f32[5,8]{1,0:T(8,128)S(1)}, u32[]{:S(2)}, u32[]{:S(2)}) collective-permute-start(f32[5,8]{1,0:T(8,128)S(1)} %max.10.refs_1_), channel_id=1, source_target_pairs={{0,16},{4,20},{8,24},{12,28},{16,0},{20,4},{24,8},{28,12},{1,17},{... | collective-permute-start | bytes 488 | tf_op jit(solution)/shard_map/ppermute | solution.py:762
  77.8 10.5 %collective-permute-done.7.refs_1_ = bf16[512,1024]{1,0:T(8,128)(2,1)S(1)} collective-permute-done((bf16[512,1024]{1,0:T(8,128)(2,1)S(1)}, bf16[512,1024]{1,0:T(8,128)(2,1)S(1)}, u32[]{:S(2)}, u32[]{:S(2)}) %collective-permute-start.7) | collective-permute-done | bytes 1048608 | tf_op jit(solution)/shard_map/ppermute | solution.py:772
  88.6 1.3 split_columns.3
  90.0 3.7 %collective-permute-start.9 = (bf16[512,1024]{1,0:T(8,128)(2,1)S(1)}, bf16[512,1024]{1,0:T(8,128)(2,1)S(1)}, u32[]{:S(2)}, u32[]{:S(2)}) collective-permute-start(bf16[512,1024]{1,0:T(8,128)(2,1)S(1)} %get-tuple-element.57.refs_0_.refs_5_), channel_id=1, source_target_pairs={{0,1},{3,2},{4,5},{7,6},{8,9},{11,10},{12,13},{15,14},{16,17},{19,... | collective-permute-start | bytes 3145736 | tf_op jit(solution)/shard_map/ppermute | solution.py:772
  93.7 0.9 collective-permute-start.8
  94.7 2.6 %weight_terms_late.1 = (bf16[2,512,512]{2,1,0:T(8,128)(2,1)S(1)}, bf16[2,512,512]{2,1,0:T(8,128)(2,1)S(1)}, bf16[2,512,512]{2,1,0:T(8,128)(2,1)S(1)}, bf16[2,512,512]{2,1,0:T(8,128)(2,1)S(1)}) custom-call(s32[10]{0:T(128)S(1)} %dynamic-slice_bitcast_fusion.rest_0_.place_ref, bf16[1024,512]{1,0:T(8,128)(2,1)S(1)} %copy-done.7, ...), custom_call_target="tpu_custom_call" | custom-call | tf_op jit(solution)/shard_map/weight_terms_late/pallas_call | solution.py:688
  97.3 1.6 %collective-permute-start.17 = (bf16[2,512,512]{2,1,0:T(8,128)(2,1)S(1)}, bf16[2,512,512]{2,1,0:T(8,128)(2,1)S(1)}, u32[]{:S(2)}, u32[]{:S(2)}) collective-permute-start(bf16[2,512,512]{2,1,0:T(8,128)(2,1)S(1)} %get-tuple-element.73.refs_6_.rest_0_), channel_id=1, source_target_pairs={{0,8},{4,12},{8,0},{12,4},{16,24},{20,28},{24,16},{28,20},{1,9},{5... | collective-permute-start | bytes 3145736 | tf_op jit(solution)/shard_map/ppermute | solution.py:762
  98.8 1.5 %collective-permute-start.18 = (bf16[2,512,512]{2,1,0:T(8,128)(2,1)S(1)}, bf16[2,512,512]{2,1,0:T(8,128)(2,1)S(1)}, u32[]{:S(2)}, u32[]{:S(2)}) collective-permute-start(bf16[2,512,512]{2,1,0:T(8,128)(2,1)S(1)} %get-tuple-element.74.refs_8_.rest_2_), channel_id=1, source_target_pairs={{0,16},{4,20},{8,24},{12,28},{16,0},{20,4},{24,8},{28,12},{1,17},{... | collective-permute-start | bytes 3145736 | tf_op jit(solution)/shard_map/ppermute | solution.py:762
  100.4 5.4 %grad_products.3.grad_ref = bf16[512,1024]{1,0:T(8,128)(2,1)S(1)} custom-call(s32[10]{0:T(128)S(1)} %dynamic-slice_bitcast_fusion.rest_0_.place_ref, bf16[512,1024]{1,0:T(8,128)(2,1)} %collective-permute-done.4.refs_0_, bf16[512,1024]{1,0:T(8,128)(2,1)S(1)} %collective-permute-done.7.refs_1_, bf16[512,1024]{1,0:T(8,128)(2,1)} %collective-permute-done.3.refs_3_.refs_2_, ...), custom_call_target="tpu_custom_call" | custom-call | tf_op jit(solution)/shard_map/grad_products/pallas_call | solution.py:524
  105.9 12.0 %attention_backward.1 = (f32[512,1024]{1,0:T(8,128)}, bf16[512,1024]{1,0:T(8,128)(2,1)S(1)}, bf16[512,1024]{1,0:T(8,128)(2,1)S(1)}, bf16[512,1024]{1,0:T(8,128)(...) custom-call(bf16[512,1024]{1,0:T(8,128)(2,1)S(1)} %copy-done.2, bf16[512,1024]{1,0:T(8,128)(2,1)S(1)} %copy-done, ...), custom_call_target="tpu_custom_call" | custom-call | tf_op jit(solution)/shard_map/attention_backward/pallas_call | solution.py:386
  117.9 0.5 mixed_add.3
  118.4 4.2 %collective-permute-done.17.refs_1_ = bf16[2,512,512]{2,1,0:T(8,128)(2,1)S(1)} collective-permute-done((bf16[2,512,512]{2,1,0:T(8,128)(2,1)S(1)}, bf16[2,512,512]{2,1,0:T(8,128)(2,1)S(1)}, u32[]{:S(2)}, u32[]{:S(2)}) %collective-permute-start.17) | collective-permute-done | bytes 1048608 | tf_op jit(solution)/shard_map/ppermute | solution.py:762
  122.6 1.2 collective-permute-done.18.refs_3_
  123.8 0.8 collective-permute-start.19
  124.6 0.7 collective-permute-start.20
  125.5 0.6 collective-permute-start.22
  126.6 1.6 %collective-permute-start.24 = (bf16[1,512,512]{2,1,0:T(8,128)(2,1)S(1)}, bf16[1,512,512]{2,1,0:T(8,128)(2,1)S(1)}, u32[]{:S(2)}, u32[]{:S(2)}) collective-permute-start(bf16[1,512,512]{2,1,0:T(8,128)(2,1)S(1)} %get-tuple-element.91), channel_id=1, source_target_pairs={{0,16},{4,20},{8,24},{12,28},{16,0},{20,4},{24,8},{28,12},{1,17},{... | collective-permute-start | bytes 1572872 | tf_op jit(solution)/shard_map/ppermute | solution.py:762
  128.2 1.5 collective-permute-start.25
  129.6 8.0 %collective-permute-done.22.three = bf16[192,1024]{1,0:T(8,128)(2,1)S(1)} collective-permute-done((bf16[192,1024]{1,0:T(8,128)(2,1)S(1)}, bf16[192,1024]{1,0:T(8,128)(2,1)S(1)}, u32[]{:S(2)}, u32[]{:S(2)}) %collective-permute-start.22) | collective-permute-done | bytes 393248 | tf_op jit(solution)/shard_map/ppermute | solution.py:762
  137.7 1.6 %collective-permute-start.23 = (bf16[64,1024]{1,0:T(8,128)(2,1)S(1)}, bf16[64,1024]{1,0:T(8,128)(2,1)S(1)}, u32[]{:S(2)}, u32[]{:S(2)}) collective-permute-start(bf16[64,1024]{1,0:T(8,128)(2,1)S(1)} %add_convert_fusion.1), channel_id=1, source_target_pairs={{0,16},{4,20},{8,24},{12,28},{16,0},{20,4},{24,8},{28,12},{1,17},{... | collective-permute-start | bytes 393224 | tf_op jit(solution)/shard_map/ppermute | solution.py:762
  139.3 3.4 %collective-permute-done.23.four = bf16[64,1024]{1,0:T(8,128)(2,1)S(1)} collective-permute-done((bf16[64,1024]{1,0:T(8,128)(2,1)S(1)}, bf16[64,1024]{1,0:T(8,128)(2,1)S(1)}, u32[]{:S(2)}, u32[]{:S(2)}) %collective-permute-start.23) | collective-permute-done | bytes 131104 | tf_op jit(solution)/shard_map/ppermute | solution.py:762
  142.7 3.0 %add_returned.1 = (f32[512,1024]{1,0:T(8,128)}, f32[512,1024]{1,0:T(8,128)}) custom-call(bf16[512,1024]{1,0:T(8,128)(2,1)S(1)} %get-tuple-element.81.gk_ref, bf16[512,1024]{1,0:T(8,128)(2,1)S(1)} %get-tuple-element.82.gv_ref, bf16[512,1024]{1,0:T(8,128)(2,1)S(1)} %collective-permute-done.21.near, bf16[192,1024]{1,0:T(8,128)(2,1)S(1)} %collective-permute-done.22.three, ...), custom_call_target="tpu_custom_call" | custom-call | tf_op jit(solution)/shard_map/add_returned/pallas_call | solution.py:428
  145.7 0.9 collective-permute-done.25
  146.6 1.5 %weight_total.1 = f32[1024,512]{1,0:T(8,128)} custom-call(bf16[512,512]{1,0:T(8,128)(2,1)S(1)} %bitcast.13, bf16[512,512]{1,0:T(8,128)(2,1)S(1)} %bitcast.15, bf16[512,512]{1,0:T(8,128)(2,1)S(1)} %bitcast.14, bf16[512,512]{1,0:T(8,128)(2,1)S(1)} %bitcast.16, f32[512,1024]{1,0:T(8,128)} %get-tuple-element.46.refs_0_), custom_call_target="tpu_custom_call" | custom-call | tf_op jit(solution)/shard_map/weight_total/pallas_call | solution.py:713
  148.1 2.0 %mixed_last.1 = f32[512,1024]{1,0:T(8,128)} custom-call(bf16[512,1024]{1,0:T(8,128)(2,1)S(1)} %copy-done.10, bf16[512,1024]{1,0:T(8,128)(2,1)S(1)} %collective-permute-done.19.left, bf16[512,1024]{1,0:T(8,128)(2,1)S(1)} %collective-permute-done.20.right), custom_call_target="tpu_custom_call" | custom-call | tf_op jit(solution)/shard_map/mixed_last/pallas_call | solution.py:605
  (60 shorter events, 3.0 us)
Async XLA Ops:
  0.6 29.6 %copy-start.2 = (bf16[512,1024]{1,0:T(8,128)(2,1)S(1)}, bf16[512,1024]{1,0:T(8,128)(2,1)}, u32[]{:S(2)}) copy-start(bf16[512,1024]{1,0:T(8,128)(2,1)} %q_ref.3) | copy-start | bytes 3145732
  0.6 26.6 %collective-permute-start.3 = (bf16[512,1024]{1,0:T(8,128)(2,1)}, bf16[512,1024]{1,0:T(8,128)(2,1)}, u32[]{:S(2)}, u32[]{:S(2)}) collective-permute-start(bf16[512,1024]{1,0:T(8,128)(2,1)} %refs_0_.5), channel_id=1, source_target_pairs={{0,1},{2,3},{1,0},{3,2},{4,5},{6,7},{5,4},{7,6},{8,9},{10,11},{9,8... | collective-permute-start | bytes 3145736 | tf_op jit(solution)/shard_map/ppermute | solution.py:772
  3.7 23.5 %collective-permute-start.4 = (bf16[512,1024]{1,0:T(8,128)(2,1)}, bf16[512,1024]{1,0:T(8,128)(2,1)}, u32[]{:S(2)}, u32[]{:S(2)}) collective-permute-start(bf16[512,1024]{1,0:T(8,128)(2,1)} %refs_0_.5), channel_id=1, source_target_pairs={{1,2},{2,1},{5,6},{6,5},{9,10},{10,9},{13,14},{14,13},{17,18},{18,... | collective-permute-start | bytes 3145736 | tf_op jit(solution)/shard_map/ppermute | solution.py:772
  8.1 11.7 %collective-permute-start = (bf16[128,1024]{1,0:T(8,128)(2,1)}, bf16[128,1024]{1,0:T(8,128)(2,1)S(1)}, u32[]{:S(2)}, u32[]{:S(2)}) collective-permute-start(bf16[128,1024]{1,0:T(8,128)(2,1)} %get-tuple-element.51), channel_id=1, source_target_pairs={{0,8},{4,12},{8,0},{12,4},{16,24},{20,28},{24,16},{28,20},{1,9},{5... | collective-permute-start | bytes 786440 | tf_op jit(solution)/shard_map/ppermute | solution.py:762
  9.6 5.2 %collective-permute-start.1 = (bf16[64,1024]{1,0:T(8,128)(2,1)}, bf16[64,1024]{1,0:T(8,128)(2,1)S(1)}, u32[]{:S(2)}, u32[]{:S(2)}) collective-permute-start(bf16[64,1024]{1,0:T(8,128)(2,1)} %get-tuple-element.52), channel_id=1, source_target_pairs={{0,16},{4,20},{8,24},{12,28},{16,0},{20,4},{24,8},{28,12},{1,17},{... | collective-permute-start | bytes 393224 | tf_op jit(solution)/shard_map/ppermute | solution.py:762
  11.1 8.7 %collective-permute-start.2 = (bf16[64,1024]{1,0:T(8,128)(2,1)}, bf16[64,1024]{1,0:T(8,128)(2,1)S(1)}, u32[]{:S(2)}, u32[]{:S(2)}) collective-permute-start(bf16[64,1024]{1,0:T(8,128)(2,1)} %get-tuple-element.52), channel_id=1, source_target_pairs={{0,24},{4,28},{8,16},{12,20},{16,8},{20,12},{24,0},{28,4},{1,25},{... | collective-permute-start | bytes 393224 | tf_op jit(solution)/shard_map/ppermute | solution.py:762
  27.2 3.0 %collective-permute-start.5 = (bf16[512,1024]{1,0:T(8,128)(2,1)}, bf16[512,1024]{1,0:T(8,128)(2,1)}, u32[]{:S(2)}, u32[]{:S(2)}) collective-permute-start(bf16[512,1024]{1,0:T(8,128)(2,1)} %lower_rows.1), channel_id=1, source_target_pairs={{0,4},{4,0},{8,12},{12,8},{16,20},{20,16},{24,28},{28,24},{1,5},{5... | collective-permute-start | bytes 3145736 | tf_op jit(solution)/shard_map/ppermute | solution.py:762
  27.2 25.2 %collective-permute-start.6 = (bf16[512,1024]{1,0:T(8,128)(2,1)}, bf16[512,1024]{1,0:T(8,128)(2,1)S(1)}, u32[]{:S(2)}, u32[]{:S(2)}) collective-permute-start(bf16[512,1024]{1,0:T(8,128)(2,1)} %collective-permute-done.3.refs_3_.refs_2_), channel_id=1, source_target_pairs={{1,2},{2,1},{5,6},{6,5},{9,10},{10,9},{13,14},{14,13},{17,18},{18,... | collective-permute-start | bytes 3145736 | tf_op jit(solution)/shard_map/ppermute | solution.py:772
  27.9 32.8 %collective-permute-start.12 = (bf16[512,1024]{1,0:T(8,128)(2,1)}, bf16[512,1024]{1,0:T(8,128)(2,1)}, u32[]{:S(2)}, u32[]{:S(2)}) collective-permute-start(bf16[512,1024]{1,0:T(8,128)(2,1)} %collective-permute-done.4.refs_0_), channel_id=1, source_target_pairs={{2,3},{1,0},{6,7},{5,4},{10,11},{9,8},{14,15},{13,12},{18,19},{17,... | collective-permute-start | bytes 3145736 | tf_op jit(solution)/shard_map/ppermute | solution.py:772
  40.7 1.0 copy-start.3
  41.7 1.0 copy-start.6
  42.8 9.8 %collective-permute-start.11 = (f32[5,8]{1,0:T(8,128)S(1)}, f32[5,8]{1,0:T(8,128)S(1)}, u32[]{:S(2)}, u32[]{:S(2)}) collective-permute-start(f32[5,8]{1,0:T(8,128)S(1)} %bitcast.18), channel_id=1, source_target_pairs={{0,4},{4,0},{8,12},{12,8},{16,20},{20,16},{24,28},{28,24},{1,5},{5... | collective-permute-start | bytes 488 | tf_op jit(solution)/shard_map/ppermute | solution.py:762
  43.1 24.4 %slice-start = ((s8[8388608]{0:T(1024)(128)(4,1)}), s8[4194304]{0:T(1024)(128)(4,1)S(1)}, s32[]{:S(2)}) async-start(s8[8388608]{0:T(1024)(128)(4,1)} %bitcast.11), calls=%async_computation | async-start | bytes 8388608
  43.1 24.4 %slice-start.1 = ((s8[8388608]{0:T(1024)(128)(4,1)}), s8[4194304]{0:T(1024)(128)(4,1)S(1)}, s32[]{:S(2)}) async-start(s8[8388608]{0:T(1024)(128)(4,1)} %bitcast.11), calls=%async_computation.1 | async-start | bytes 8388608
  52.5 10.0 %copy-start.9 = (bf16[512,1024]{1,0:T(8,128)(2,1)}, bf16[512,1024]{1,0:T(8,128)(2,1)S(1)}, u32[]{:S(2)}) copy-start(bf16[512,1024]{1,0:T(8,128)(2,1)S(1)} %get-tuple-element.55.own) | copy-start | bytes 3145732
  52.5 8.3 %copy-start.5 = (bf16[512,1024]{1,0:T(8,128)(2,1)S(1)}, bf16[512,1024]{1,0:T(8,128)(2,1)}, u32[]{:S(2)}) copy-start(bf16[512,1024]{1,0:T(8,128)(2,1)} %refs_0_.5) | copy-start | bytes 3145732
  52.6 9.9 %copy-start.7 = (bf16[1024,512]{1,0:T(8,128)(2,1)S(1)}, bf16[1024,512]{1,0:T(8,128)(2,1)}, u32[]{:S(2)}) copy-start(bf16[1024,512]{1,0:T(8,128)(2,1)} %copy-done.6) | copy-start | bytes 3145732
  62.5 3.5 %collective-permute-start.13 = (bf16[512,1536]{1,0:T(8,128)(2,1)S(1)}, bf16[512,1536]{1,0:T(8,128)(2,1)S(1)}, u32[]{:S(2)}, u32[]{:S(2)}) collective-permute-start(bf16[512,1536]{1,0:T(8,128)(2,1)S(1)} %get-tuple-element.65), channel_id=1, source_target_pairs={{0,4},{4,0},{8,12},{12,8},{16,20},{20,16},{24,28},{28,24},{1,5},{5... | collective-permute-start | bytes 4718600 | tf_op jit(solution)/shard_map/ppermute | solution.py:762
  62.6 9.6 %collective-permute-start.10 = (bf16[1024,512]{1,0:T(8,128)(2,1)S(1)}, bf16[1024,512]{1,0:T(8,128)(2,1)S(1)}, u32[]{:S(2)}, u32[]{:S(2)}) collective-permute-start(bf16[1024,512]{1,0:T(8,128)(2,1)S(1)} %copy-done.7), channel_id=1, source_target_pairs={{0,4},{4,0},{8,12},{12,8},{16,20},{20,16},{24,28},{28,24},{1,5},{5... | collective-permute-start | bytes 3145736 | tf_op jit(solution)/shard_map/ppermute | solution.py:762
  63.1 25.2 %collective-permute-start.7 = (bf16[512,1024]{1,0:T(8,128)(2,1)S(1)}, bf16[512,1024]{1,0:T(8,128)(2,1)S(1)}, u32[]{:S(2)}, u32[]{:S(2)}) collective-permute-start(bf16[512,1024]{1,0:T(8,128)(2,1)S(1)} %broadcast_select_fusion.refs_4_), channel_id=1, source_target_pairs={{0,1},{1,0},{2,3},{3,2},{4,5},{5,4},{6,7},{7,6},{8,9},{9,8},{10,11... | collective-permute-start | bytes 3145736 | tf_op jit(solution)/shard_map/ppermute | solution.py:772
  65.9 6.2 %collective-permute-start.14 = (f32[5,8]{1,0:T(8,128)S(1)}, f32[5,8]{1,0:T(8,128)S(1)}, u32[]{:S(2)}, u32[]{:S(2)}) collective-permute-start(f32[5,8]{1,0:T(8,128)S(1)} %bitcast_maximum_fusion.refs_5_), channel_id=1, source_target_pairs={{0,8},{4,12},{8,0},{12,4},{16,24},{20,28},{24,16},{28,20},{1,9},{5... | collective-permute-start | bytes 488 | tf_op jit(solution)/shard_map/ppermute | solution.py:762
  76.2 12.4 %collective-permute-start.15 = (f32[5,8]{1,0:T(8,128)S(1)}, f32[5,8]{1,0:T(8,128)S(1)}, u32[]{:S(2)}, u32[]{:S(2)}) collective-permute-start(f32[5,8]{1,0:T(8,128)S(1)} %max.10.refs_1_), channel_id=1, source_target_pairs={{0,16},{4,20},{8,24},{12,28},{16,0},{20,4},{24,8},{28,12},{1,17},{... | collective-permute-start | bytes 488 | tf_op jit(solution)/shard_map/ppermute | solution.py:762
  88.6 6.1 %copy-start.12 = (f32[5,8]{1,0:T(8,128)}, f32[5,8]{1,0:T(8,128)S(1)}, u32[]{:S(2)}) copy-start(f32[5,8]{1,0:T(8,128)S(1)} %max.11.refs_4_.refs_0_) | copy-start | bytes 484
  89.9 4.7 %collective-permute-start.16 = (bf16[512,512]{1,0:T(8,128)(2,1)S(1)}, bf16[512,512]{1,0:T(8,128)(2,1)S(1)}, u32[]{:S(2)}, u32[]{:S(2)}) collective-permute-start(bf16[512,512]{1,0:T(8,128)(2,1)S(1)} %get-tuple-element.72), channel_id=1, source_target_pairs={{0,4},{4,0},{8,12},{12,8},{16,20},{20,16},{24,28},{28,24},{1,5},{5... | collective-permute-start | bytes 1572872 | tf_op jit(solution)/shard_map/ppermute | solution.py:762
  90.0 27.9 %collective-permute-start.9 = (bf16[512,1024]{1,0:T(8,128)(2,1)S(1)}, bf16[512,1024]{1,0:T(8,128)(2,1)S(1)}, u32[]{:S(2)}, u32[]{:S(2)}) collective-permute-start(bf16[512,1024]{1,0:T(8,128)(2,1)S(1)} %get-tuple-element.57.refs_0_.refs_5_), channel_id=1, source_target_pairs={{0,1},{3,2},{4,5},{7,6},{8,9},{11,10},{12,13},{15,14},{16,17},{19,... | collective-permute-start | bytes 3145736 | tf_op jit(solution)/shard_map/ppermute | solution.py:772
  93.7 24.1 %collective-permute-start.8 = (bf16[512,1024]{1,0:T(8,128)(2,1)S(1)}, bf16[512,1024]{1,0:T(8,128)(2,1)S(1)}, u32[]{:S(2)}, u32[]{:S(2)}) collective-permute-start(bf16[512,1024]{1,0:T(8,128)(2,1)S(1)} %mixed_add.2.refs_6_), channel_id=1, source_target_pairs={{1,2},{2,1},{5,6},{6,5},{9,10},{10,9},{13,14},{14,13},{17,18},{18,... | collective-permute-start | bytes 3145736 | tf_op jit(solution)/shard_map/ppermute | solution.py:772
  97.3 25.3 %collective-permute-start.17 = (bf16[2,512,512]{2,1,0:T(8,128)(2,1)S(1)}, bf16[2,512,512]{2,1,0:T(8,128)(2,1)S(1)}, u32[]{:S(2)}, u32[]{:S(2)}) collective-permute-start(bf16[2,512,512]{2,1,0:T(8,128)(2,1)S(1)} %get-tuple-element.73.refs_6_.rest_0_), channel_id=1, source_target_pairs={{0,8},{4,12},{8,0},{12,4},{16,24},{20,28},{24,16},{28,20},{1,9},{5... | collective-permute-start | bytes 3145736 | tf_op jit(solution)/shard_map/ppermute | solution.py:762
  98.8 25.0 %collective-permute-start.18 = (bf16[2,512,512]{2,1,0:T(8,128)(2,1)S(1)}, bf16[2,512,512]{2,1,0:T(8,128)(2,1)S(1)}, u32[]{:S(2)}, u32[]{:S(2)}) collective-permute-start(bf16[2,512,512]{2,1,0:T(8,128)(2,1)S(1)} %get-tuple-element.74.refs_8_.rest_2_), channel_id=1, source_target_pairs={{0,16},{4,20},{8,24},{12,28},{16,0},{20,4},{24,8},{28,12},{1,17},{... | collective-permute-start | bytes 3145736 | tf_op jit(solution)/shard_map/ppermute | solution.py:762
  100.4 5.5 %copy-start = (bf16[512,1024]{1,0:T(8,128)(2,1)S(1)}, bf16[512,1024]{1,0:T(8,128)(2,1)}, u32[]{:S(2)}) copy-start(bf16[512,1024]{1,0:T(8,128)(2,1)} %k_ref.5) | copy-start | bytes 3145732
  100.4 5.5 %copy-start.1 = (bf16[512,1024]{1,0:T(8,128)(2,1)S(1)}, bf16[512,1024]{1,0:T(8,128)(2,1)}, u32[]{:S(2)}) copy-start(bf16[512,1024]{1,0:T(8,128)(2,1)} %v_ref.5) | copy-start | bytes 3145732
  100.4 5.5 %copy-start.4 = (bf16[512,1024]{1,0:T(8,128)(2,1)S(1)}, bf16[512,1024]{1,0:T(8,128)(2,1)}, u32[]{:S(2)}) copy-start(bf16[512,1024]{1,0:T(8,128)(2,1)} %copy-done.3) | copy-start | bytes 3145732
  100.4 5.5 %copy-start.8 = (f32[512,1024]{1,0:T(8,128)S(1)}, f32[512,1024]{1,0:T(8,128)}, u32[]{:S(2)}) copy-start(f32[512,1024]{1,0:T(8,128)} %get-tuple-element.79.lse_ref) | copy-start | bytes 6291460
  105.8 12.0 %copy-start.11 = (bf16[512,1024]{1,0:T(8,128)(2,1)S(1)}, bf16[512,1024]{1,0:T(8,128)(2,1)}, u32[]{:S(2)}) copy-start(bf16[512,1024]{1,0:T(8,128)(2,1)} %get-tuple-element.56.refs_0_) | copy-start | bytes 3145732
  117.9 7.5 %collective-permute-start.21 = (bf16[512,1024]{1,0:T(8,128)(2,1)S(1)}, bf16[512,1024]{1,0:T(8,128)(2,1)S(1)}, u32[]{:S(2)}, u32[]{:S(2)}) collective-permute-start(bf16[512,1024]{1,0:T(8,128)(2,1)S(1)} %get-tuple-element.83), channel_id=1, source_target_pairs={{0,4},{4,0},{8,12},{12,8},{16,20},{20,16},{24,28},{28,24},{1,5},{5... | collective-permute-start | bytes 3145736 | tf_op jit(solution)/shard_map/ppermute | solution.py:762
  123.8 24.3 %collective-permute-start.19 = (bf16[512,1024]{1,0:T(8,128)(2,1)S(1)}, bf16[512,1024]{1,0:T(8,128)(2,1)S(1)}, u32[]{:S(2)}, u32[]{:S(2)}) collective-permute-start(bf16[512,1024]{1,0:T(8,128)(2,1)S(1)} %get-tuple-element.75), channel_id=1, source_target_pairs={{0,1},{2,3},{1,0},{3,2},{4,5},{6,7},{5,4},{7,6},{8,9},{10,11},{9,8... | collective-permute-start | bytes 3145736 | tf_op jit(solution)/shard_map/ppermute | solution.py:772
  124.6 23.5 %collective-permute-start.20 = (bf16[512,1024]{1,0:T(8,128)(2,1)S(1)}, bf16[512,1024]{1,0:T(8,128)(2,1)S(1)}, u32[]{:S(2)}, u32[]{:S(2)}) collective-permute-start(bf16[512,1024]{1,0:T(8,128)(2,1)S(1)} %get-tuple-element.76), channel_id=1, source_target_pairs={{1,2},{2,1},{5,6},{6,5},{9,10},{10,9},{13,14},{14,13},{17,18},{18,... | collective-permute-start | bytes 3145736 | tf_op jit(solution)/shard_map/ppermute | solution.py:772
  125.5 12.1 %collective-permute-start.22 = (bf16[192,1024]{1,0:T(8,128)(2,1)S(1)}, bf16[192,1024]{1,0:T(8,128)(2,1)S(1)}, u32[]{:S(2)}, u32[]{:S(2)}) collective-permute-start(bf16[192,1024]{1,0:T(8,128)(2,1)S(1)} %add_convert_fusion), channel_id=1, source_target_pairs={{0,8},{4,12},{8,0},{12,4},{16,24},{20,28},{24,16},{28,20},{1,9},{5... | collective-permute-start | bytes 1179656 | tf_op jit(solution)/shard_map/ppermute | solution.py:762
  126.6 19.2 %collective-permute-start.24 = (bf16[1,512,512]{2,1,0:T(8,128)(2,1)S(1)}, bf16[1,512,512]{2,1,0:T(8,128)(2,1)S(1)}, u32[]{:S(2)}, u32[]{:S(2)}) collective-permute-start(bf16[1,512,512]{2,1,0:T(8,128)(2,1)S(1)} %get-tuple-element.91), channel_id=1, source_target_pairs={{0,16},{4,20},{8,24},{12,28},{16,0},{20,4},{24,8},{28,12},{1,17},{... | collective-permute-start | bytes 1572872 | tf_op jit(solution)/shard_map/ppermute | solution.py:762
  128.2 18.4 %collective-permute-start.25 = (bf16[1,512,512]{2,1,0:T(8,128)(2,1)S(1)}, bf16[1,512,512]{2,1,0:T(8,128)(2,1)S(1)}, u32[]{:S(2)}, u32[]{:S(2)}) collective-permute-start(bf16[1,512,512]{2,1,0:T(8,128)(2,1)S(1)} %get-tuple-element.93), channel_id=1, source_target_pairs={{0,8},{4,12},{8,0},{12,4},{16,24},{20,28},{24,16},{28,20},{1,9},{5... | collective-permute-start | bytes 1572872 | tf_op jit(solution)/shard_map/ppermute | solution.py:762
  137.7 5.0 %collective-permute-start.23 = (bf16[64,1024]{1,0:T(8,128)(2,1)S(1)}, bf16[64,1024]{1,0:T(8,128)(2,1)S(1)}, u32[]{:S(2)}, u32[]{:S(2)}) collective-permute-start(bf16[64,1024]{1,0:T(8,128)(2,1)S(1)} %add_convert_fusion.1), channel_id=1, source_target_pairs={{0,16},{4,20},{8,24},{12,28},{16,0},{20,4},{24,8},{28,12},{1,17},{... | collective-permute-start | bytes 393224 | tf_op jit(solution)/shard_map/ppermute | solution.py:762
  146.6 1.5 %copy-start.10 = (bf16[512,1024]{1,0:T(8,128)(2,1)S(1)}, bf16[512,1024]{1,0:T(8,128)(2,1)}, u32[]{:S(2)}) copy-start(bf16[512,1024]{1,0:T(8,128)(2,1)} %copy-done.9) | copy-start | bytes 3145732
